TPU v7x, 32 devices: a whole 2x2x4 slice. The times are simulated.
32 devices in a mesh: rep: 2 (over x), fsdp: 16 (over z, y, core).
Axes of the slice: x: 2, y: 2, z: 4, core: 2. Of those that a mesh axis runs over, the one named last changes fastest.
Arguments:
- tokens: bfloat16 [8192, 768], P(('rep', 'fsdp')), may hold values from -6 to 6
- cotangent: bfloat16 [8192, 768], P(('rep', 'fsdp')), may hold values from -6 to 6
- clip_index: int32 [8192], P(('rep', 'fsdp')), may hold values from 0 to 3, as said below
- key_valid: int32 [8192], P(('rep', 'fsdp')), may hold values from 0 to 1, as said below
- patch_masked: int32 [8192], P(('rep', 'fsdp')), may hold values 0 or 1
- attn_weight: float32 [768, 3072], P('fsdp')
- mlp_weight: float32 [768, 6144], P('fsdp')
- gain_vector: float32 [1536], P('fsdp'), may hold values from 0.25 to 1.75
- offset_vector: float32 [8448], P('fsdp'), may hold values from -1.8 to 1.8
- attn_moment: float32 [768, 3072], P('fsdp')
- mlp_moment: float32 [768, 6144], P('fsdp')
- gain_moment: float32 [1536], P('fsdp')
- offset_moment: float32 [8448], P('fsdp')
- attn_average: float32 [768, 3072], P('fsdp')
- mlp_average: float32 [768, 6144], P('fsdp')
- gain_average: float32 [1536], P('fsdp'), may hold values from 0.25 to 1.75
- offset_average: float32 [8448], P('fsdp'), may hold values from -1.8 to 1.8
Outputs:
- activations: bfloat16 [8192, 768], P(('rep', 'fsdp'))
- input_grad: bfloat16 [8192, 768], P(('rep', 'fsdp'))
- attn_new: float32 [768, 3072], P('fsdp')
- attn_momentum: float32 [768, 3072], P('fsdp')
- attn_ema: float32 [768, 3072], P('fsdp')
- attn_copy: bfloat16 [768, 3072], P('fsdp')
- mlp_new: float32 [768, 6144], P('fsdp')
- mlp_momentum: float32 [768, 6144], P('fsdp')
- mlp_ema: float32 [768, 6144], P('fsdp')
- mlp_copy: bfloat16 [768, 6144], P('fsdp')
- gain_new: float32 [1536], P('fsdp')
- gain_momentum: float32 [1536], P('fsdp')
- gain_ema: float32 [1536], P('fsdp')
- gain_copy: bfloat16 [1536], P('fsdp')
- offset_new: float32 [8448], P('fsdp')
- offset_momentum: float32 [8448], P('fsdp')
- offset_ema: float32 [8448], P('fsdp')
- offset_copy: bfloat16 [8448], P('fsdp')
Inputs may be any that keep to these rules, and one draw needn't show every extreme that they name: `clip_index`: each aligned block of 256 slots holds whole clips of consecutive slots, numbered from 0 in order within the block; every clip has a multiple of 64 slots, from 64 to 256; some block holds a single clip, and some block holds clips of 64 slots only. `key_valid`: padded slots lie only at the end of a clip, at most 32 of them in one clip.
All inputs are finite; a program needn't handle non-finite values. No bound on the sum of `patch_masked` on one device may be relied on, other than what follows from the above.
Results may differ from a plain program's by a relative error of at most 0.013.
The roundings to bfloat16 on the way count: a program that leaves them out, or rounds other values in their place, can miss the bound.
Values may be sent and summed in bfloat16 or wider, within the bound.
No kernel may reach another device: no remote copies, remote signals or barrier semaphores. Data moves between devices by JAX's collectives and lax.ppermute only.
A program may use at most 128 MiB of HBM per device.

v0:
```python
import math

import jax
import jax.numpy as jnp
from jax import lax
from jax.sharding import PartitionSpec as P

D = 768
HEADS = 12
HEAD_DIM = 64
FF = 3072


momentum_decay = 0.9
average_decay = 0.8
base_rate = 0.02
norm_eps = 1e-06
mask_fill = -1e30


def normalize(inputs):
    mean_val = jnp.mean(inputs, axis=-1, keepdims=True)
    centred = inputs - mean_val
    variance = jnp.mean(centred * centred, axis=-1, keepdims=True)
    return centred * lax.rsqrt(variance + norm_eps)


def norm_affine(inputs, gain_part, shift_part):
    return normalize(inputs) * gain_part + shift_part


def gelu_exact(inputs):
    return jax.nn.gelu(inputs, approximate=False)


def over_tokens(left_mat, right_mat):
    return lax.dot_general(
        left_mat, right_mat, (((0,), (0,)), ((), ())), preferred_element_type=jnp.float32
    )


def against_rows(left_mat, right_mat):
    return lax.dot_general(
        left_mat, right_mat, (((1,), (1,)), ((), ())), preferred_element_type=jnp.float32
    )


def block_mask(clip_ids, key_ok):
    return (clip_ids[:, None] == clip_ids[None, :]) & (key_ok[None, :] == 1)


def forward(inputs, params, clip_ids, key_ok, masked):
    attn_full = params[0]
    mlp_full = params[1]
    gain_f = params[2].astype(jnp.float32)
    shift_f = params[3].astype(jnp.float32)
    tok_rows = inputs.shape[0]
    score_scale = HEAD_DIM ** (-0.5)
    is_masked = masked[:, None] == 1
    embedded = jnp.where(is_masked, shift_f[6 * D : 7 * D][None, :], inputs)
    normed_one = norm_affine(embedded, gain_f[:D], shift_f[:D]).astype(jnp.bfloat16)
    qkv_bias = jnp.concatenate(
        [shift_f[D : 2 * D], jnp.zeros((D,), jnp.float32), shift_f[2 * D : 3 * D]]
    )
    projected = (
        jnp.dot(normed_one, attn_full[:, : 3 * D], preferred_element_type=jnp.float32) + qkv_bias
    )
    projected = projected.astype(jnp.bfloat16)
    queries = projected[:, :D].reshape(tok_rows, HEADS, HEAD_DIM)
    key_heads = projected[:, D : 2 * D].reshape(tok_rows, HEADS, HEAD_DIM)
    value_heads = projected[:, 2 * D :].reshape(tok_rows, HEADS, HEAD_DIM)
    allowed = block_mask(clip_ids, key_ok)
    scores = (
        jnp.einsum("qhd,khd->hqk", queries, key_heads, preferred_element_type=jnp.float32)
        * score_scale
    )
    scores = jnp.where(allowed[None], scores, mask_fill)
    row_peak = jnp.max(scores, axis=-1, keepdims=True)
    exponent = jnp.exp(scores - row_peak)
    summed = jnp.sum(exponent, axis=-1, keepdims=True)
    attn_prob = (exponent / summed).astype(jnp.bfloat16)
    mixed_parts = jnp.einsum(
        "hqk,khd->qhd", attn_prob, value_heads, preferred_element_type=jnp.float32
    )
    lse_parts = [row_peak + jnp.log(summed)]
    mixed_out = mixed_parts.reshape(tok_rows, D).astype(jnp.bfloat16)
    after_attn = embedded + against_rows(mixed_out, attn_full[:, 3 * D :]) + shift_f[3 * D : 4 * D]
    normed_two = norm_affine(after_attn, gain_f[D:], shift_f[4 * D : 5 * D]).astype(jnp.bfloat16)
    hidden_pre = (
        jnp.dot(normed_two, mlp_full[:, :FF], preferred_element_type=jnp.float32) + shift_f[7 * D :]
    )
    hidden_act = gelu_exact(hidden_pre).astype(jnp.bfloat16)
    output = after_attn + against_rows(hidden_act, mlp_full[:, FF:]) + shift_f[5 * D : 6 * D]
    kept_values = (
        embedded,
        normed_one,
        queries,
        key_heads,
        value_heads,
        lse_parts,
        mixed_out,
        after_attn,
        normed_two,
        hidden_pre,
        hidden_act,
        gain_f,
        shift_f,
    )
    return (output, kept_values)


def backward(cotangent, params, kept_values, clip_ids, key_ok, masked):
    attn_full = params[0]
    mlp_full = params[1]
    (
        embedded,
        normed_one,
        queries,
        key_heads,
        value_heads,
        lse_parts,
        mixed_out,
        after_attn,
        normed_two,
        hidden_pre,
        hidden_act,
        gain_f,
        shift_f,
    ) = kept_values
    tok_rows = cotangent.shape[0]
    score_scale = HEAD_DIM ** (-0.5)
    d_out = cotangent.astype(jnp.float32)
    d_bias_two = jnp.sum(d_out, axis=0)
    d_down = over_tokens(cotangent, hidden_act)
    d_act = jnp.dot(cotangent, mlp_full[:, FF:], preferred_element_type=jnp.float32)
    gelu_value, gelu_pull = jax.vjp(gelu_exact, hidden_pre)
    d_pre_low = gelu_pull(d_act)[0].astype(jnp.bfloat16)
    d_bias_one = jnp.sum(d_pre_low.astype(jnp.float32), axis=0)
    d_up = over_tokens(normed_two, d_pre_low)
    mlp_grad = jnp.concatenate([d_up, d_down], axis=1)
    d_normed_two = against_rows(d_pre_low, mlp_full[:, :FF])
    norm_value, norm_pull = jax.vjp(norm_affine, after_attn, gain_f[D:], shift_f[4 * D : 5 * D])
    d_after_norm, d_gain_two, d_shift_two = norm_pull(d_normed_two)
    d_after = d_out + d_after_norm
    d_after_low = d_after.astype(jnp.bfloat16)
    d_bias_out = jnp.sum(d_after, axis=0)
    d_outproj = over_tokens(d_after_low, mixed_out)
    d_mixed = jnp.dot(d_after_low, attn_full[:, 3 * D :], preferred_element_type=jnp.float32)
    d_mixed_low = d_mixed.astype(jnp.bfloat16).reshape(tok_rows, HEADS, HEAD_DIM)
    block_rows = min(512, tok_rows)
    d_query_parts = []
    d_keys = jnp.zeros((tok_rows, HEADS, HEAD_DIM), jnp.float32)
    d_values = jnp.zeros((tok_rows, HEADS, HEAD_DIM), jnp.float32)
    for block_number, offset in enumerate(range(0, tok_rows, block_rows)):
        allowed = block_mask(clip_ids, key_ok)
        scores = (
            jnp.einsum("qhd,khd->hqk", queries, key_heads, preferred_element_type=jnp.float32)
            * score_scale
        )
        scores = jnp.where(allowed[None], scores, mask_fill)
        attn_prob = jnp.exp(scores - lse_parts[block_number])
        prob_low = attn_prob.astype(jnp.bfloat16)
        d_prob = jnp.einsum(
            "qhd,khd->hqk", d_mixed_low, value_heads, preferred_element_type=jnp.float32
        )
        row_delta = jnp.sum(d_prob * attn_prob, axis=-1, keepdims=True)
        d_scores = (attn_prob * (d_prob - row_delta)).astype(jnp.bfloat16)
        d_query_parts.append(
            jnp.einsum("hqk,khd->qhd", d_scores, key_heads, preferred_element_type=jnp.float32)
            * score_scale
        )
        d_keys = (
            jnp.einsum("hqk,qhd->khd", d_scores, queries, preferred_element_type=jnp.float32)
            * score_scale
        )
        d_values = jnp.einsum(
            "hqk,qhd->khd", prob_low, d_mixed_low, preferred_element_type=jnp.float32
        )
    d_queries = d_query_parts[0]
    d_proj_low = jnp.concatenate(
        [
            d_queries.reshape(tok_rows, D),
            d_keys.reshape(tok_rows, D),
            d_values.reshape(tok_rows, D),
        ],
        axis=1,
    ).astype(jnp.bfloat16)
    d_bias_q = jnp.sum(d_proj_low[:, :D].astype(jnp.float32), axis=0)
    d_bias_v = jnp.sum(d_proj_low[:, 2 * D :].astype(jnp.float32), axis=0)
    d_qkv = over_tokens(normed_one, d_proj_low)
    d_normed_one = against_rows(d_proj_low, attn_full[:, : 3 * D])
    first_value, first_pull = jax.vjp(norm_affine, embedded, gain_f[:D], shift_f[:D])
    d_embed_norm, d_gain_one, d_shift_one = first_pull(d_normed_one)
    d_embedded = d_after + d_embed_norm
    is_masked = masked[:, None] == 1
    d_mask_vec = jnp.sum(jnp.where(is_masked, d_embedded, 0.0), axis=0)
    input_grad = jnp.where(is_masked, 0.0, d_embedded).astype(jnp.bfloat16)
    attn_grad = jnp.concatenate([d_qkv, d_outproj], axis=1)
    gain_grad = jnp.concatenate([d_gain_one, d_gain_two])
    offset_grad = jnp.concatenate(
        [
            d_shift_one,
            d_bias_q,
            d_bias_v,
            d_bias_out,
            d_shift_two,
            d_bias_two,
            d_mask_vec,
            d_bias_one,
        ]
    )
    return (input_grad, (attn_grad, mlp_grad, gain_grad, offset_grad))


def advance(gradient, weight, moment, average, learn_rate):
    moment_new = momentum_decay * moment + gradient
    weight_new = weight - learn_rate * (gradient + momentum_decay * moment_new)
    average_new = average_decay * average + (1.0 - average_decay) * weight_new
    return (weight_new, moment_new, average_new, weight_new.astype(jnp.bfloat16))


def per_device(
    tokens,
    cotangent,
    clip_index,
    key_valid,
    patch_masked,
    attn_weight,
    mlp_weight,
    gain_vector,
    offset_vector,
    attn_moment,
    mlp_moment,
    gain_moment,
    offset_moment,
    attn_average,
    mlp_average,
    gain_average,
    offset_average,
):
    attn_shard = attn_weight.astype(jnp.bfloat16)
    mlp_shard = mlp_weight.astype(jnp.bfloat16)
    gain_shard = gain_vector.astype(jnp.bfloat16)
    offset_shard = offset_vector.astype(jnp.bfloat16)
    params = (
        lax.all_gather(attn_shard, "fsdp", axis=0, tiled=True),
        lax.all_gather(mlp_shard, "fsdp", axis=0, tiled=True),
        lax.all_gather(gain_shard, "fsdp", axis=0, tiled=True),
        lax.all_gather(offset_shard, "fsdp", axis=0, tiled=True),
    )
    inputs = tokens.astype(jnp.float32)
    output, first_kept = forward(inputs, params, clip_index, key_valid, patch_masked)
    again = (
        lax.all_gather(attn_shard, "fsdp", axis=0, tiled=True),
        lax.all_gather(mlp_shard, "fsdp", axis=0, tiled=True),
        lax.all_gather(gain_shard, "fsdp", axis=0, tiled=True),
        lax.all_gather(offset_shard, "fsdp", axis=0, tiled=True),
    )
    output_again, kept_values = forward(inputs, again, clip_index, key_valid, patch_masked)
    input_grad, gradients = backward(
        cotangent, again, kept_values, clip_index, key_valid, patch_masked
    )
    owned = (
        lax.psum_scatter(gradients[0], "fsdp", scatter_dimension=0, tiled=True),
        lax.psum_scatter(gradients[1], "fsdp", scatter_dimension=0, tiled=True),
        lax.psum_scatter(gradients[2], "fsdp", scatter_dimension=0, tiled=True),
        lax.psum_scatter(gradients[3], "fsdp", scatter_dimension=0, tiled=True),
    )
    shares = (
        lax.psum_scatter(
            owned[0].astype(jnp.bfloat16), "rep", scatter_dimension=1, tiled=True
        ).astype(jnp.float32),
        lax.psum_scatter(
            owned[1].astype(jnp.bfloat16), "rep", scatter_dimension=1, tiled=True
        ).astype(jnp.float32),
        lax.psum_scatter(
            owned[2].astype(jnp.bfloat16), "rep", scatter_dimension=0, tiled=True
        ).astype(jnp.float32),
        lax.psum_scatter(
            owned[3].astype(jnp.bfloat16), "rep", scatter_dimension=0, tiled=True
        ).astype(jnp.float32),
    )
    reduced = (
        lax.all_gather(shares[0].astype(jnp.bfloat16), "rep", axis=1, tiled=True).astype(
            jnp.float32
        ),
        lax.all_gather(shares[1].astype(jnp.bfloat16), "rep", axis=1, tiled=True).astype(
            jnp.float32
        ),
        lax.all_gather(shares[2].astype(jnp.bfloat16), "rep", axis=0, tiled=True).astype(
            jnp.float32
        ),
        lax.all_gather(shares[3].astype(jnp.bfloat16), "rep", axis=0, tiled=True).astype(
            jnp.float32
        ),
    )
    learn_rate = base_rate / math.sqrt(
        tokens.shape[0] * lax.axis_size("rep") * lax.axis_size("fsdp")
    )
    attn_new, attn_momentum, attn_ema, attn_copy = advance(
        reduced[0], attn_weight, attn_moment, attn_average, learn_rate
    )
    mlp_new, mlp_momentum, mlp_ema, mlp_copy = advance(
        reduced[1], mlp_weight, mlp_moment, mlp_average, learn_rate
    )
    gain_new, gain_momentum, gain_ema, gain_copy = advance(
        reduced[2], gain_vector, gain_moment, gain_average, learn_rate
    )
    offset_new, offset_momentum, offset_ema, offset_copy = advance(
        reduced[3], offset_vector, offset_moment, offset_average, learn_rate
    )
    return (
        output.astype(jnp.bfloat16),
        input_grad,
        attn_new,
        attn_momentum,
        attn_ema,
        attn_copy,
        mlp_new,
        mlp_momentum,
        mlp_ema,
        mlp_copy,
        gain_new,
        gain_momentum,
        gain_ema,
        gain_copy,
        offset_new,
        offset_momentum,
        offset_ema,
        offset_copy,
    )


def solution(mesh):
    placed = (
        P(("rep", "fsdp"), None),
        P(("rep", "fsdp"), None),
        P(("rep", "fsdp")),
        P(("rep", "fsdp")),
        P(("rep", "fsdp")),
        P("fsdp", None),
        P("fsdp", None),
        P("fsdp"),
        P("fsdp"),
        P("fsdp", None),
        P("fsdp", None),
        P("fsdp"),
        P("fsdp"),
        P("fsdp", None),
        P("fsdp", None),
        P("fsdp"),
        P("fsdp"),
    )
    return jax.shard_map(
        per_device,
        mesh=mesh,
        in_specs=placed,
        out_specs=(
            P(("rep", "fsdp"), None),
            P(("rep", "fsdp"), None),
            P("fsdp", None),
            P("fsdp", None),
            P("fsdp", None),
            P("fsdp", None),
            P("fsdp", None),
            P("fsdp", None),
            P("fsdp", None),
            P("fsdp", None),
            P("fsdp"),
            P("fsdp"),
            P("fsdp"),
            P("fsdp"),
            P("fsdp"),
            P("fsdp"),
            P("fsdp"),
            P("fsdp"),
        ),
        check_vma=False,
    )
```

profile of v0, /device:TPU:0, one launch (start us, length us, event | category | flops | bytes accessed | tf_op | source)
XLA Modules:
  0.0 553.7 jit_solution(1085969406303026644)
XLA Ops:
  7.3 1.9 convert_element_type.137
  9.3 2.1 convert_element_type.144
  14.0 63.7 %all-reduce.9 = (bf16[8448]{0:T(1024)(128)(2,1)S(1)}, bf16[1536]{0:T(1024)(128)(2,1)S(1)}) all-reduce(bf16[8448]{0:T(1024)(128)(2,1)S(1)} %dynamic-update-slice, bf16[1536]{0:T(1024)(128)(2,1)S(1)} %dynamic-update-slice.1), channel_id=1, replica_groups=mesh['rep'=2,'fsdp'=16] {'fsdp'}, use_global_device_ids=true, to_apply=%add | all-reduce | flops 9984 | bytes 39936
  80.8 3.2 fusion.11
  86.9 1.9 fusion.80
  89.9 2.0 fusion.81
  94.3 56.2 %all-gather.5.cloned.1.call-done = bf16[768,6144]{1,0:T(8,128)(2,1)} async-done(((bf16[48,6144]{1,0:T(8,128)(2,1)}), bf16[768,6144]{1,0:T(8,128)(2,1)}) %all-gather.5.cloned.1.call-update) | async-done | bytes 9437200 | tf_op jit(solution)/shard_map/all_gather | solution.py:247
  150.5 11.0 %multiply_convert_fusion.1 = (bf16[256,3072]{1,0:T(8,128)(2,1)}, f32[256,3072]{1,0:T(8,128)S(1)}, f32[256,3072]{1,0:T(8,128)S(1)}) fusion(f32[3072]{0:T(1024)} %slice.105, bf16[768,6144]{1,0:T(8,128)(2,1)} %all-gather.5.cloned.1.call-done, f32[256,768]{1,0:T(8,128)} %copy-done.3, f32[768]{0:T(1024)S(1)} %get-tuple-element.59, ...), kind=kOutput, calls=%fused_computation.21 | convolution fusion | flops 1260847104 | bytes 13389824 | tf_op jit(solution)/shard_map/dot_general | solution.py:90
  161.5 3.2 convert_reduce_fusion
  164.8 2.2 multiply_reduce_fusion.1
  168.0 1.9 fusion.55
  170.0 2.5 convolution_convert_fusion
  172.5 1.9 copy.63
  174.4 1.7 fusion.40
  179.7 4.2 fusion.54
  184.0 8.0 %pad_maximum_fusion.1 = f32[768,3072]{1,0:T(8,128)} fusion(f32[768,768]{1,0:T(8,128)S(1)} %copy-done.2, f32[768,2304]{1,0:T(8,128)} %fusion.54), kind=kLoop, calls=%fused_computation.1 | loop fusion | flops 2359296 | bytes 18874368 | tf_op jit(solution)/shard_map/concatenate | solution.py:198
  192.1 1.3 copy-done.16
  193.5 5.5 convolution_bitcast_fusion
  199.0 5.9 %fusion.64 = f32[768,3072]{1,0:T(8,128)} fusion(bf16[256,3072]{1,0:T(8,128)(2,1)S(1)} %copy-done.23, f32[256,768]{1,0:T(8,128)S(1)} %copy-done.5, f32[768]{0:T(1024)S(1)} %get-tuple-element.59, f32[768]{0:T(1024)S(1)} %get-tuple-element.65, f32[256]{0:T(256)S(1)} %copy-done.48, f32[256]{0:T(256)S(1)} %copy-done.36), kind=kOutput, calls=%fused_computation.132 | convolution fusion | flops 1208942592 | bytes 11804672 | tf_op jit(solution)/shard_map/dot_general | solution.py:37
  204.9 96.8 %reduce-scatter.5.cloned.1.call-done = f32[48,3072]{1,0:T(8,128)} async-done(((f32[768,3072]{1,0:T(8,128)}), f32[48,3072]{1,0:T(8,128)}) %reduce-scatter.5.cloned.1.call-update) | async-done | bytes 589840 | tf_op jit(solution)/shard_map/reduce_scatter | solution.py:264
  301.6 1.8 convert_element_type.154
  303.5 14.6 %pad_maximum_fusion = f32[768,6144]{1,0:T(8,128)} fusion(f32[768,3072]{1,0:T(8,128)} %convolution_bitcast_fusion, f32[768,3072]{1,0:T(8,128)} %fusion.64), kind=kLoop, calls=%fused_computation | loop fusion | flops 4718592 | bytes 37748736 | tf_op jit(solution)/shard_map/concatenate | solution.py:140
  322.4 3.4 multiply_reduce_fusion.2
  325.9 1.4 constant_dynamic-update-slice_fusion.7
  327.5 1.3 constant_dynamic-update-slice_fusion.6
  329.0 1.3 constant_dynamic-update-slice_fusion.5
  331.7 1.3 constant_dynamic-update-slice_fusion.4
  333.0 1.3 constant_dynamic-update-slice_fusion.3
  334.3 1.3 constant_dynamic-update-slice_fusion.2
  335.7 1.3 constant_dynamic-update-slice_fusion.1
  337.0 1.3 constant_dynamic-update-slice_fusion
  338.3 64.1 %all-reduce.8 = (bf16[1536]{0:T(1024)(128)(2,1)S(1)}, bf16[8448]{0:T(1024)(128)(2,1)S(1)}) all-reduce(f32[1536]{0:T(1024)S(1)} %pad_maximum_fusion.6, f32[8448]{0:T(1024)} %constant_dynamic-update-slice_fusion), channel_id=6, replica_groups=mesh['rep'=2,'fsdp'=16] {'fsdp'}, use_global_device_ids=true, to_apply=%region_17.18.clone | all-reduce | flops 9984 | bytes 59904
  402.5 4.9 all-reduce.11
  408.0 4.9 all-reduce.10
  412.9 1.2 fusion.67
  414.1 1.2 multiply_add_fusion.5
  415.3 1.3 fusion.65
  416.6 1.3 multiply_add_fusion.2
  417.9 4.5 fusion.36
  422.5 6.2 %all_gather.32 = bf16[48,3072]{1,0:T(8,128)(2,1)S(1)} all-gather(bf16[48,1536]{1,0:T(8,128)(2,1)} %reduce-scatter.7.cloned.1.call-done), channel_id=1, replica_groups=mesh['rep'=2,'fsdp'=16] {'rep'}, dimensions={1}, use_global_device_ids=true | all-gather | bytes 442368 | tf_op jit(solution)/shard_map/all_gather | solution.py:284
  428.6 87.1 %reduce-scatter.9.cloned.1.call-done = f32[48,6144]{1,0:T(8,128)} async-done(((f32[768,6144]{1,0:T(8,128)}), f32[48,6144]{1,0:T(8,128)}) %reduce-scatter.9.cloned.1.call-update) | async-done | bytes 1179664 | tf_op jit(solution)/shard_map/reduce_scatter | solution.py:265
  515.8 2.1 convert_element_type.157
  518.0 2.2 fusion.70
  520.2 1.0 multiply_add_fusion.1
  521.2 11.8 %reduce-scatter.11.cloned.1.call-done = bf16[48,3072]{1,0:T(8,128)(2,1)} async-done(((bf16[48,6144]{1,0:T(8,128)(2,1)}), bf16[48,3072]{1,0:T(8,128)(2,1)}) %reduce-scatter.11.cloned.1.call-update) | async-done | bytes 294928 | tf_op jit(solution)/shard_map/reduce_scatter | solution.py:273
  533.0 9.6 %all_gather.33 = bf16[48,6144]{1,0:T(8,128)(2,1)S(1)} all-gather(bf16[48,3072]{1,0:T(8,128)(2,1)} %reduce-scatter.11.cloned.1.call-done), channel_id=1, replica_groups=mesh['rep'=2,'fsdp'=16] {'rep'}, dimensions={1}, use_global_device_ids=true | all-gather | bytes 884736 | tf_op jit(solution)/shard_map/all_gather | solution.py:287
  542.6 2.9 fusion.68
  545.5 1.4 multiply_add_fusion
  (196 shorter events, 18.4 us)
Async XLA Ops:
  7.2 4.4 copy-start.58
  7.2 4.4 copy-start.59
  7.2 4.3 copy-start.60
  7.2 6.2 %copy-start.43 = (f32[528]{0:T(1024)S(1)}, f32[528]{0:T(1024)}, u32[]{:S(2)}) copy-start(f32[528]{0:T(1024)} %param.25) | copy-start | bytes 6340
  7.2 71.7 %copy-start.63 = (s32[256]{0:T(256)S(1)}, s32[256]{0:T(256)}, u32[]{:S(2)}) copy-start(s32[256]{0:T(256)} %param.21) | copy-start | bytes 3076
  7.2 71.7 %copy-start.6 = (bf16[256,768]{1,0:T(8,128)(2,1)S(1)}, bf16[256,768]{1,0:T(8,128)(2,1)}, u32[]{:S(2)}) copy-start(bf16[256,768]{1,0:T(8,128)(2,1)} %param.17) | copy-start | bytes 1179652
  7.3 72.2 %copy-start.64 = (s32[256]{0:T(256)S(1)}, s32[256]{0:T(256)}, u32[]{:S(2)}) copy-start(s32[256]{0:T(256)} %param.20) | copy-start | bytes 3076
  7.3 72.7 %copy-start.55 = (s32[256]{0:T(256)S(1)}, s32[256]{0:T(256)}, u32[]{:S(2)}) copy-start(s32[256]{0:T(256)} %param.19) | copy-start | bytes 3076
  7.3 73.5 %all-gather.3.cloned.1.call-start = ((), (), s32[]{:S(2)}) async-start(), calls=%async_computation.4 | async-start | bytes 5013504 | tf_op jit(solution)/shard_map/all_gather | solution.py:246
  9.2 141.3 %all-gather.5.cloned.1.call-start = ((), (), s32[]{:S(2)}) async-start(), calls=%async_computation.5 | async-start | bytes 10027008 | tf_op jit(solution)/shard_map/all_gather | solution.py:247
  11.4 290.2 %reduce-scatter.5.cloned.1.call-start = ((), (), s32[]{:S(2)}) async-start(), calls=%async_computation.6 | async-start | bytes 10027008 | tf_op jit(solution)/shard_map/reduce_scatter | solution.py:264
  78.9 5.1 copy-start.29
  78.9 5.1 copy-start.37
  79.2 4.8 copy-start.31
  80.0 4.0 copy-start.44
  86.9 2.3 copy-start.20
  89.9 3.2 copy-start.26
  150.5 11.0 %copy-start.17 = (bf16[256,768]{1,0:T(8,128)(2,1)S(1)}, bf16[256,768]{1,0:T(8,128)(2,1)}, u32[]{:S(2)}) copy-start(bf16[256,768]{1,0:T(8,128)(2,1)} %param.18) | copy-start | bytes 1179652
  150.5 11.0 %copy-start.62 = (bf16[768,6144]{1,0:T(8,128)(2,1)S(1)}, bf16[768,6144]{1,0:T(8,128)(2,1)}, u32[]{:S(2)}) copy-start(bf16[768,6144]{1,0:T(8,128)(2,1)} %all-gather.5.cloned.1.call-done) | copy-start | bytes 28311556
  161.5 3.3 copy-start.4
  161.5 3.3 copy-start.35
  161.5 3.3 copy-start.47
  176.1 2.9 copy-start.9
  179.7 4.2 copy-start.2
  192.0 230.5 %reduce-scatter.7.cloned.1.call-start = ((), (), s32[]{:S(2)}) async-start(), calls=%async_computation.7 | async-start | bytes 442368 | tf_op jit(solution)/shard_map/reduce_scatter | solution.py:270
  193.5 5.5 copy-start.5
  193.5 5.5 copy-start.23
  193.5 5.5 copy-start.36
  193.5 5.5 copy-start.48
  303.5 212.3 %reduce-scatter.9.cloned.1.call-start = ((), (), s32[]{:S(2)}) async-start(), calls=%async_computation.8 | async-start | bytes 20054016 | tf_op jit(solution)/shard_map/reduce_scatter | solution.py:265
  318.2 4.2 copy-start.10
  318.2 4.2 copy-start.33
  318.2 4.2 copy-start.40
  318.2 214.8 %reduce-scatter.11.cloned.1.call-start = ((), (), s32[]{:S(2)}) async-start(), calls=%async_computation.9 | async-start | bytes 884736 | tf_op jit(solution)/shard_map/reduce_scatter | solution.py:273
  322.4 7.9 %copy-start.51 = (f32[256]{0:T(256)S(1)}, f32[256]{0:T(256)}, u32[]{:S(2)}) copy-start(f32[256]{0:T(256)} %copy-done.50) | copy-start | bytes 3076
  322.4 7.9 %copy-start.46 = (f32[256]{0:T(256)S(1)}, f32[256]{0:T(256)}, u32[]{:S(2)}) copy-start(f32[256]{0:T(256)} %copy-done.44) | copy-start | bytes 3076
  325.8 4.9 copy-start.1
  325.8 7.2 %copy-start.56 = (f32[768]{0:T(1024)S(1)}, f32[768]{0:T(1024)}, u32[]{:S(2)}) copy-start(f32[768]{0:T(1024)} %get-tuple-element.24) | copy-start | bytes 9220
  325.8 8.5 %copy-start.41 = (f32[768]{0:T(1024)S(1)}, f32[768]{0:T(1024)}, u32[]{:S(2)}) copy-start(f32[768]{0:T(1024)} %get-tuple-element.56) | copy-start | bytes 9220
  325.9 11.1 %copy-start.57 = (f32[768]{0:T(1024)S(1)}, f32[768]{0:T(1024)}, u32[]{:S(2)}) copy-start(f32[768]{0:T(1024)} %get-tuple-element.18) | copy-start | bytes 9220
  325.9 11.1 %copy-start.49 = (f32[3072]{0:T(1024)S(1)}, f32[3072]{0:T(1024)}, u32[]{:S(2)}) copy-start(f32[3072]{0:T(1024)} %get-tuple-element.80) | copy-start | bytes 36868
  414.1 8.3 %copy-start.61 = (f32[96]{0:T(128)}, f32[96]{0:T(128)S(1)}, u32[]{:S(2)}) copy-start(f32[96]{0:T(128)S(1)} %get-tuple-element.38) | copy-start | bytes 1156
  416.6 5.8 %copy-start.42 = (f32[528]{0:T(1024)}, f32[528]{0:T(1024)S(1)}, u32[]{:S(2)}) copy-start(f32[528]{0:T(1024)S(1)} %get-tuple-element.35) | copy-start | bytes 6340
  422.4 95.5 %copy-start.15 = (f32[48,3072]{1,0:T(8,128)S(1)}, f32[48,3072]{1,0:T(8,128)}, u32[]{:S(2)}) copy-start(f32[48,3072]{1,0:T(8,128)} %param.22) | copy-start | bytes 1769476
  422.4 97.7 %copy-start.25 = (f32[48,3072]{1,0:T(8,128)S(1)}, f32[48,3072]{1,0:T(8,128)}, u32[]{:S(2)}) copy-start(f32[48,3072]{1,0:T(8,128)} %param.30) | copy-start | bytes 1769476
  517.9 24.7 %copy-start.8 = (f32[48,6144]{1,0:T(8,128)S(1)}, f32[48,6144]{1,0:T(8,128)}, u32[]{:S(2)}) copy-start(f32[48,6144]{1,0:T(8,128)} %param.23) | copy-start | bytes 3538948
  520.2 25.3 %copy-start.14 = (f32[48,3072]{1,0:T(8,128)}, f32[48,3072]{1,0:T(8,128)S(1)}, u32[]{:S(2)}) copy-start(f32[48,3072]{1,0:T(8,128)S(1)} %get-tuple-element.44) | copy-start | bytes 1769476
  542.6 2.9 copy-start.24
  (23 other events, 32.1 us)
Sparse Core Ops, SparseCore 0:
  11.0 56.4 all-gather.2
  70.3 80.1 all-gather.4
  192.1 109.4 reduce-scatter.4
  304.4 11.7 reduce-scatter.6
  320.7 194.9 reduce-scatter.8
  518.6 14.3 reduce-scatter.10
where the time goes:
time: 555 us; the launch traced here: 554 us
  waiting for transfers between devices  252 us (45%)
  blocking collectives  153 us (28%)
  matrix products  55.7 us (10%)
  other arithmetic  49.7 us (9%)
  local copies, waits for them, and re-layouts  22.4 us (4%)
  between operations  20.1 us (4%)
    unnamed x4, blocking collectives  138 us
    reduce_scatter x1, waiting for transfers between devices, per_device(): lax.psum_scatter(gradients[0], 'fsdp', scatter_dimension=0, tiled=True)  96.8 us
    reduce_scatter x1, waiting for transfers between devices, per_device(): lax.psum_scatter(gradients[1], 'fsdp', scatter_dimension=0, tiled=True)  87.1 us
    all_gather x1, waiting for transfers between devices, per_device(): lax.all_gather(mlp_shard, 'fsdp', axis=0, tiled=True)  56.2 us
    dot_general x4, matrix products, over_tokens(): lax.dot_general(left_mat, right_mat, (((0,), (0,)), ((), ())), preferred_...  17.5 us
    unnamed x150, local copies, waits for them, and re-layouts  15.1 us
    concatenate x1, other arithmetic, backward(): mlp_grad = jnp.concatenate([d_up, d_down], axis=1)  14.6 us
    dot_general x4, matrix products, against_rows(): lax.dot_general(left_mat, right_mat, (((1,), (1,)), ((), ())), preferred_...  12.2 us
  transfers between devices with their start and end apart: 6, of which 4 were waited for; matrix products, arithmetic and copies ran while one was open for 13% of the time, Pallas kernels for 0%

commit v1 on v0

--- a/solution.py
+++ b/solution.py
@@ -1,14 +1,19 @@
+import functools
 import math
 
 import jax
 import jax.numpy as jnp
 from jax import lax
+from jax.experimental import pallas as pl
+from jax.experimental.pallas import tpu as pltpu
 from jax.sharding import PartitionSpec as P
 
 D = 768
 HEADS = 12
 HEAD_DIM = 64
 FF = 3072
+BF = jnp.bfloat16
+F32 = jnp.float32
 
 
 momentum_decay = 0.9
@@ -331,6 +336,487 @@
     )
 
 
+def scalars(co):
+    return co[0], co[1], co[2], co[3]
+
+
+def call(kernel, outs, args, flops=0, limit=24):
+    specs = []
+    total = 0
+    for arg in args:
+        if arg.dtype == jnp.int32 and arg.ndim == 1:
+            specs.append(pl.BlockSpec(memory_space=pltpu.SMEM))
+        else:
+            specs.append(pl.BlockSpec(memory_space=pltpu.VMEM))
+        total += arg.size * arg.dtype.itemsize
+    for shape, dtype in outs:
+        total += math.prod(shape) * jnp.dtype(dtype).itemsize
+    return pl.pallas_call(
+        kernel,
+        out_shape=[jax.ShapeDtypeStruct(shape, dtype) for shape, dtype in outs],
+        in_specs=specs,
+        out_specs=[pl.BlockSpec(memory_space=pltpu.VMEM)] * len(outs),
+        compiler_params=pltpu.CompilerParams(vmem_limit_bytes=limit * 2**20),
+        cost_estimate=pl.CostEstimate(flops=flops, bytes_accessed=total, transcendentals=0),
+    )
+
+
+def lanes(offset, size):
+    return pl.ds(pl.multiple_of(offset, 128), size)
+
+
+def nn(left, right):
+    return lax.dot_general(left, right, (((1,), (0,)), ((), ())), preferred_element_type=jnp.float32)
+
+
+def nt(left, right):
+    return lax.dot_general(left, right, (((1,), (1,)), ((), ())), preferred_element_type=jnp.float32)
+
+
+def row_norm(values):
+    mean = jnp.mean(values, axis=-1, keepdims=True)
+    centred = values - mean
+    var = jnp.mean(centred * centred, axis=-1, keepdims=True)
+    rstd = lax.rsqrt(var + norm_eps)
+    return centred * rstd, rstd
+
+
+def prep_kernel(co, attn, mlp, s0, s1, s2, w2):
+    r = co[0]
+    for part in range(3):
+        s0[:, part * 384 : part * 384 + 384] = attn[:, lanes(part * D + 384 * r, 384)].astype(BF)
+    s1[:, :384] = attn[:, lanes(3 * D + 384 * r, 384)].astype(BF)
+    s1[:, 384:] = mlp[:, lanes(1536 * r, 768)].astype(BF)
+    s2[...] = mlp[:, lanes(1536 * r + 768, 768)].astype(BF)
+    w2[...] = mlp[:, FF:].astype(BF)
+
+
+def assemble_kernel(maps, co, *refs):
+    r, z, y, c = scalars(co)
+    pieces = refs[:8]
+    outs = refs[8:]
+    for number in range(8):
+        a, b, i = number // 4, (number // 2) % 2, number % 2
+        half = lax.bitwise_xor(r, b)
+        for k in range(4):
+            zi, yi, ci = lax.bitwise_xor(z, k), lax.bitwise_xor(y, i), lax.bitwise_xor(c, a)
+            for out, src, size, base, stride in maps:
+                outs[out][zi, yi, ci, :, lanes(base + stride * half, size)] = pieces[number][
+                    k * 48 : k * 48 + 48, src : src + size
+                ]
+
+
+def first_norm_kernel(tokens, masked, vec, h1, h1t):
+    x0 = jnp.where(masked[...] == 1, vec[8:9, :], tokens[...].astype(F32))
+    xh, rstd = row_norm(x0)
+    h = xh * vec[0:1, :] + vec[2:3, :]
+    h1[...] = h.astype(BF)
+    h1t[...] = h.T.astype(BF)
+
+
+def allowed_pairs(clip_col, clip_row, valid_col):
+    return (clip_col[...] == clip_row[...]) & (valid_col[...] == 1)
+
+
+def attention_kernel(h1, weight, vec, clip_col, clip_row, valid_col, qkv, att, lse):
+    for part in range(3):
+        out = nn(h1[...], weight[:, part * D : part * D + D])
+        if part != 1:
+            out = out + vec[3:4, :] if part == 0 else out + vec[4:5, :]
+        qkv[:, part * D : part * D + D] = out.astype(BF)
+    allowed = allowed_pairs(clip_col, clip_row, valid_col)
+    low = lax.broadcasted_iota(jnp.int32, (256, 128), 1) < 64
+    for pair in range(6):
+        q2 = qkv[:, pair * 128 : pair * 128 + 128]
+        k2 = qkv[:, D + pair * 128 : D + pair * 128 + 128]
+        v2 = qkv[:, 2 * D + pair * 128 : 2 * D + pair * 128 + 128]
+        mixed = []
+        for side in range(2):
+            qm = jnp.where(low if side == 0 else ~low, q2, jnp.zeros_like(q2))
+            s = jnp.where(allowed, nt(k2, qm) * 0.125, mask_fill)
+            peak = jnp.max(s, axis=0, keepdims=True)
+            e = jnp.exp(s - peak)
+            total = jnp.sum(e, axis=0, keepdims=True)
+            prob = (e * (1.0 / total)).astype(BF)
+            lse[2 * pair + side : 2 * pair + side + 1, :] = peak + jnp.log(total)
+            mixed.append(over_tokens(prob, v2))
+        att[:, pair * 128 : pair * 128 + 128] = jnp.where(low, mixed[0], mixed[1]).astype(BF)
+
+
+def second_norm_kernel(tokens, masked, att, weight, vec, y1, h2, h2t):
+    x0 = jnp.where(masked[...] == 1, vec[8:9, :], tokens[...].astype(F32))
+    y = x0 + nt(att[...], weight[...]) + vec[5:6, :]
+    y1[...] = y
+    xh, rstd = row_norm(y)
+    h = xh * vec[1:2, :] + vec[6:7, :]
+    h2[...] = h.astype(BF)
+    h2t[...] = h.T.astype(BF)
+
+
+def hidden_kernel(part, h2, weight, vec, g, slope):
+    for half in range(2):
+        for sub in range(0, D, 256):
+            u = nn(h2[...], weight[:, half * D + sub : half * D + sub + 256])
+            u = u + vec[9 + 2 * half + part : 10 + 2 * half + part, sub : sub + 256]
+            phi = 0.5 * (1.0 + lax.erf(u * math.sqrt(0.5)))
+            g[:, half * D + sub : half * D + sub + 256] = (u * phi).astype(BF)
+            slope[:, half * D + sub : half * D + sub + 256] = phi + u * (
+                jnp.exp(-0.5 * u * u) * (1.0 / math.sqrt(2.0 * math.pi))
+            )
+
+
+def down_grad_kernel(dz, g0, g1, out, dzt):
+    dzt[...] = dz[...].astype(F32).T.astype(BF)
+    for half in range(2):
+        for part, g in ((0, g0), (1, g1)):
+            for sub in range(0, D, 384):
+                res = nn(dzt[...], g[:, half * D + sub : half * D + sub + 384])
+                start = half * 2 * D + part * D + sub
+                out[:, start : start + 384] = res.astype(BF)
+
+
+def hidden_grad_kernel(dz, weight, y1, g0, g1, slope0, slope1, vec, du0, du1, db1, act):
+    acc = y1[...] + vec[7:8, :]
+    for half in range(2):
+        for part, g, slope, du in ((0, g0, slope0, du0), (1, g1, slope1, du1)):
+            start = half * 2 * D + part * D
+            w = weight[:, start : start + D]
+            da = nn(dz[...], w)
+            d = (da * slope[:, half * D : half * D + D]).astype(BF)
+            du[:, half * D : half * D + D] = d
+            row = 2 * half + part
+            db1[row : row + 1, :] = jnp.sum(d.astype(F32), axis=0, keepdims=True)
+            acc = acc + nt(g[:, half * D : half * D + D], w)
+    act[...] = acc.astype(BF)
+
+
+def weight_grad_kernel(groups, width, co, left, right, send, keep, scratch):
+    r, z, y, c = scalars(co)
+    for b in range(2):
+        half = lax.bitwise_xor(r, b)
+        for col, size, base, stride in groups:
+            for sub in range(0, size, 384):
+                scratch[...] = nn(left[...], right[:, lanes(base + stride * half + sub, 384)])
+                dst = b * width + col + sub
+                for k in range(4):
+                    for i in range(2):
+                        row = k * 192 + i * 96
+                        send[k, i, :, dst : dst + 384] = scratch[
+                            pl.ds(pl.multiple_of(row + 48 * (1 - c), 16), 48), :
+                        ].astype(BF)
+                        keep[k, i, :, dst : dst + 384] = scratch[
+                            pl.ds(pl.multiple_of(row + 48 * c, 16), 48), :
+                        ]
+
+
+def second_back_kernel(dz, du0, du1, w0, w1, y1, weight_o, vec, dy1, datt, dpt, small):
+    dh = nt(du0[...], w0[...]) + nt(du1[...], w1[...])
+    yh, rstd = row_norm(y1[...])
+    dy = dz[...].astype(F32)
+    small[0:1, :] = jnp.sum(dh * yh, axis=0, keepdims=True)
+    small[1:2, :] = jnp.sum(dh, axis=0, keepdims=True)
+    small[3:4, :] = jnp.sum(dy, axis=0, keepdims=True)
+    e = dh * vec[1:2, :]
+    d = dy + rstd * (
+        e - jnp.mean(e, axis=-1, keepdims=True) - yh * jnp.mean(e * yh, axis=-1, keepdims=True)
+    )
+    dy1[...] = d
+    small[2:3, :] = jnp.sum(d, axis=0, keepdims=True)
+    dp = d.astype(BF)
+    dpt[...] = d.T.astype(BF)
+    datt[...] = nn(dp, weight_o[...]).astype(BF)
+
+
+def attention_back_kernel(qkv, datt, lse, clip_col, clip_row, valid_col, dqkv, small):
+    allowed = allowed_pairs(clip_col, clip_row, valid_col)
+    low = lax.broadcasted_iota(jnp.int32, (256, 128), 1) < 64
+    for pair in range(6):
+        cols = slice(pair * 128, pair * 128 + 128)
+        q2 = qkv[:, pair * 128 : pair * 128 + 128]
+        k2 = qkv[:, D + pair * 128 : D + pair * 128 + 128]
+        v2 = qkv[:, 2 * D + pair * 128 : 2 * D + pair * 128 + 128]
+        o2 = datt[:, cols]
+        dqs, dks, dvs = [], [], []
+        for side in range(2):
+            mine = low if side == 0 else ~low
+            qm = jnp.where(mine, q2, jnp.zeros_like(q2))
+            om = jnp.where(mine, o2, jnp.zeros_like(o2))
+            s = jnp.where(allowed, nt(k2, qm) * 0.125, mask_fill)
+            prob = jnp.exp(s - lse[2 * pair + side : 2 * pair + side + 1, :])
+            dprob = nt(v2, om)
+            delta = jnp.sum(dprob * prob, axis=0, keepdims=True)
+            ds = (prob * (dprob - delta)).astype(BF)
+            dqs.append(over_tokens(ds, k2))
+            dks.append(nn(ds, q2))
+            dvs.append(nn(prob.astype(BF), o2))
+        dq = (jnp.where(low, dqs[0], dqs[1]) * 0.125).astype(BF)
+        dk = (jnp.where(low, dks[0], dks[1]) * 0.125).astype(BF)
+        dv = jnp.where(low, dvs[0], dvs[1]).astype(BF)
+        dqkv[:, cols] = dq
+        dqkv[:, D + pair * 128 : D + pair * 128 + 128] = dk
+        dqkv[:, 2 * D + pair * 128 : 2 * D + pair * 128 + 128] = dv
+        small[0:1, cols] = jnp.sum(dq.astype(F32), axis=0, keepdims=True)
+        small[1:2, cols] = jnp.sum(dv.astype(F32), axis=0, keepdims=True)
+
+
+def first_back_kernel(
+    dqkv, weight, tokens, masked, dy1, vec, db1, small2, small_a, input_grad, total
+):
+    dh = nt(dqkv[...], weight[...])
+    hidden = masked[...] == 1
+    x0 = jnp.where(hidden, vec[8:9, :], tokens[...].astype(F32))
+    xh, rstd = row_norm(x0)
+    e = dh * vec[0:1, :]
+    dx = dy1[...] + rstd * (
+        e - jnp.mean(e, axis=-1, keepdims=True) - xh * jnp.mean(e * xh, axis=-1, keepdims=True)
+    )
+    input_grad[...] = jnp.where(hidden, 0.0, dx).astype(BF)
+    total[0:1, :] = jnp.sum(dh * xh, axis=0, keepdims=True)
+    total[1:2, :] = small2[0:1, :]
+    total[2:3, :] = jnp.sum(dh, axis=0, keepdims=True)
+    total[3:5, :] = small_a[0:2, :]
+    total[5:6, :] = small2[2:3, :]
+    total[6:7, :] = small2[1:2, :]
+    total[7:8, :] = small2[3:4, :]
+    total[8:9, :] = jnp.sum(jnp.where(hidden, dx, 0.0), axis=0, keepdims=True)
+    total[9:13, :] = db1[0:4, :]
+    total[13:16, :] = jnp.zeros((3, D), F32)
+
+
+def sum_cores_kernel(width, keep, got, x_send, x_keep):
+    x_keep[...] = keep[:, :width] + got[:, :width].astype(F32)
+    x_send[...] = (keep[:, width:] + got[:, width:].astype(F32)).astype(BF)
+
+
+def sum_reps_kernel(co, keep, got, y_send, y_keep):
+    y = co[2]
+    for k in range(4):
+        y_send[k] = (keep[k, 1 - y] + got[k, 1 - y].astype(F32)).astype(BF)
+        y_keep[k] = keep[k, y] + got[k, y].astype(F32)
+
+
+def sum_y_kernel(co, keep, got, z1, z2, z3, z_keep):
+    z = co[1]
+    for k, out in ((1, z1), (2, z2), (3, z3)):
+        at = lax.bitwise_xor(z, k)
+        out[...] = (keep[at] + got[at].astype(F32)).astype(BF)
+    z_keep[...] = keep[z] + got[z].astype(F32)
+
+
+def sum_z_kernel(keep, g1, g2, g3, out):
+    out[...] = (
+        keep[...] + g1[...].astype(F32) + g2[...].astype(F32) + g3[...].astype(F32)
+    ).astype(BF)
+
+
+def update_kernel(rate, co, *refs):
+    ins, outs = refs[:16], refs[16:]
+    attn, mlp = ins[0:3], ins[3:6]
+    qkv_g, out_g, up0_g, up1_g = ins[6:8], ins[8:10], ins[10:12], ins[12:14]
+    down_g = ins[14:16]
+    r = co[0]
+
+    def step(state, new, start, size, grad):
+        cols = lanes(start, size)
+        w, m, a = (ref[:, cols] for ref in state)
+        m_new = momentum_decay * m + grad
+        w_new = w - rate * (grad + momentum_decay * m_new)
+        new[0][:, cols] = w_new
+        new[1][:, cols] = m_new
+        new[2][:, cols] = average_decay * a + (1.0 - average_decay) * w_new
+        new[3][:, cols] = w_new.astype(BF)
+
+    for b in range(2):
+        half = lax.bitwise_xor(r, b)
+        for part in range(3):
+            grad = qkv_g[b][:, part * 384 : part * 384 + 384].astype(F32)
+            step(attn, outs[:4], part * D + 384 * half, 384, grad)
+        step(attn, outs[:4], 3 * D + 384 * half, 384, out_g[b][...].astype(F32))
+        step(mlp, outs[4:], 1536 * half, 768, up0_g[b][...].astype(F32))
+        step(mlp, outs[4:], 1536 * half + 768, 768, up1_g[b][...].astype(F32))
+    for start in range(0, FF, 768):
+        grad = down_g[0][:, start : start + 768].astype(F32) + down_g[1][
+            :, start : start + 768
+        ].astype(F32)
+        step(mlp, outs[4:], FF + start, 768, grad)
+
+
+def fast_device(
+    tokens,
+    cotangent,
+    clip_index,
+    key_valid,
+    patch_masked,
+    attn_weight,
+    mlp_weight,
+    gain_vector,
+    offset_vector,
+    attn_moment,
+    mlp_moment,
+    gain_moment,
+    offset_moment,
+    attn_average,
+    mlp_average,
+    gain_average,
+    offset_average,
+):
+    r, f = lax.axis_index("rep"), lax.axis_index("fsdp")
+    co = jnp.stack([r, f // 4, (f // 2) % 2, f % 2]).astype(jnp.int32)
+
+    def swap(array, mask):
+        return lax.ppermute(array, ("rep", "fsdp"), [(i, i ^ mask) for i in range(32)])
+
+    CORE, Y, Z, X = 1, 2, 4, 16
+
+    s0, s1, s2, w2_shard = call(
+        prep_kernel,
+        [((48, 1152), BF), ((48, 1152), BF), ((48, 768), BF), ((48, FF), BF)],
+        [co, attn_weight, mlp_weight],
+    )(co, attn_weight, mlp_weight)
+    flat = jnp.zeros((16 * D,), F32)
+    flat = lax.dynamic_update_slice(flat, gain_vector.astype(BF).astype(F32), (96 * f,))
+    flat = lax.dynamic_update_slice(flat, offset_vector.astype(BF).astype(F32), (2 * D + 528 * f,))
+    vec = flat.reshape(16, D)
+    for mask in (CORE, Y, Z, 2 * Z):
+        vec = vec + swap(vec, mask)
+    w2 = lax.all_gather(w2_shard, "fsdp", axis=0, tiled=True)
+
+    def gather(shard, maps, widths):
+        stack = jnp.concatenate([shard] + [swap(shard, Z * k) for k in (1, 2, 3)], axis=0)
+        across = swap(stack, Y)
+        mine = [stack, across, swap(stack, X), swap(across, X)]
+        pieces = mine + [swap(piece, CORE) for piece in mine]
+        outs = [((4, 2, 2, 48, width), BF) for width in widths]
+        args = [co] + pieces
+        full = call(functools.partial(assemble_kernel, maps), outs, args)(*args)
+        return [w.reshape(D, -1) for w in full]
+
+    (w_qkv,) = gather(s0, [(0, part * 384, 384, part * D, 384) for part in range(3)], [3 * D])
+    w_out, w_up0 = gather(s1, [(0, 0, 384, 0, 384), (1, 384, 768, 0, 768)], [D, 2 * D])
+    (w_up1,) = gather(s2, [(0, 0, 768, 0, 768)], [2 * D])
+
+    masked = patch_masked[:, None]
+    clip_col, clip_row, valid_col = clip_index[:, None], clip_index[None, :], key_valid[:, None]
+    args = [tokens, masked, vec]
+    h1, h1t = call(first_norm_kernel, [((256, D), BF), ((D, 256), BF)], args)(*args)
+    args = [h1, w_qkv, vec, clip_col, clip_row, valid_col]
+    qkv, att, lse = call(
+        attention_kernel,
+        [((256, 3 * D), BF), ((256, D), BF), ((16, 256), F32)],
+        args,
+        flops=2_000_000_000,
+    )(*args)
+    args = [tokens, masked, att, w_out, vec]
+    y1, h2, h2t = call(
+        second_norm_kernel, [((256, D), F32), ((256, D), BF), ((D, 256), BF)], args, flops=10**9
+    )(*args)
+    hidden = []
+    for part, weight in ((0, w_up0), (1, w_up1)):
+        args = [h2, weight, vec]
+        hidden.append(
+            call(
+                functools.partial(hidden_kernel, part),
+                [((256, 2 * D), BF), ((256, 2 * D), F32)],
+                args,
+                flops=10**9,
+            )(*args)
+        )
+    (g0, slope0), (g1, slope1) = hidden
+
+    args = [cotangent, g0, g1]
+    down_local, _ = call(down_grad_kernel, [((D, FF), BF), ((D, 256), BF)], args, flops=10**9)(*args)
+    down_mine = lax.psum_scatter(down_local, "fsdp", scatter_dimension=0, tiled=True)
+    args = [cotangent, w2, y1, g0, g1, slope0, slope1, vec]
+    du0, du1, db1, activations = call(
+        hidden_grad_kernel,
+        [((256, 2 * D), BF), ((256, 2 * D), BF), ((8, D), F32), ((256, D), BF)],
+        args,
+        flops=3 * 10**9,
+        limit=30,
+    )(*args)
+
+    def weight_grad(left, right, groups, width):
+        args = [co, left, right]
+        specs = [pl.BlockSpec(memory_space=pltpu.SMEM)] + [pl.BlockSpec(memory_space=pltpu.VMEM)] * 2
+        return pl.pallas_call(
+            functools.partial(weight_grad_kernel, groups, width),
+            out_shape=[
+                jax.ShapeDtypeStruct((4, 2, 48, 2 * width), BF),
+                jax.ShapeDtypeStruct((4, 2, 48, 2 * width), F32),
+            ],
+            in_specs=specs,
+            out_specs=[pl.BlockSpec(memory_space=pltpu.VMEM)] * 2,
+            scratch_shapes=[pltpu.VMEM((D, 384), F32)],
+            compiler_params=pltpu.CompilerParams(vmem_limit_bytes=20 * 2**20),
+            cost_estimate=pl.CostEstimate(
+                flops=2 * 256 * D * 2 * width, bytes_accessed=10 * 384 * width, transcendentals=0
+            ),
+        )(*args)
+
+    def reduce(local, width):
+        send, keep = local
+        got = swap(send.reshape(384, 2 * width), CORE)
+        args = [keep.reshape(384, 2 * width), got]
+        x_send, x_keep = call(
+            functools.partial(sum_cores_kernel, width), [((384, width), BF), ((384, width), F32)], args
+        )(*args)
+        got = swap(x_send, X)
+        args = [co, x_keep.reshape(4, 2, 48, width), got.reshape(4, 2, 48, width)]
+        y_send, y_keep = call(
+            sum_reps_kernel, [((4, 48, width), BF), ((4, 48, width), F32)], args
+        )(*args)
+        got = swap(y_send, Y)
+        args = [co, y_keep, got]
+        *z_send, z_keep = call(
+            sum_y_kernel, [((48, width), BF)] * 3 + [((48, width), F32)], args
+        )(*args)
+        args = [z_keep] + [swap(z_send[k - 1], Z * k) for k in (1, 2, 3)]
+        (mine,) = call(sum_z_kernel, [((48, width), BF)], args)(*args)
+        return mine, swap(mine, X)
+
+    up_groups = [(0, 768, 0, 768)]
+    up0_g = reduce(weight_grad(h2t, du0, up_groups, 768), 768)
+    up1_g = reduce(weight_grad(h2t, du1, up_groups, 768), 768)
+    args = [cotangent, du0, du1, w_up0, w_up1, y1, w_out, vec]
+    dy1, datt, dpt, small2 = call(
+        second_back_kernel,
+        [((256, D), F32), ((256, D), BF), ((D, 256), BF), ((8, D), F32)],
+        args,
+        flops=3 * 10**9,
+    )(*args)
+    out_g = reduce(weight_grad(dpt, att, [(0, 384, 0, 384)], 384), 384)
+    args = [qkv, datt, lse, clip_col, clip_row, valid_col]
+    dqkv, small_a = call(
+        attention_back_kernel, [((256, 3 * D), BF), ((8, D), F32)], args, flops=3 * 10**9
+    )(*args)
+    qkv_groups = [(part * 384, 384, part * D, 384) for part in range(3)]
+    qkv_g = reduce(weight_grad(h1t, dqkv, qkv_groups, 1152), 1152)
+    args = [dqkv, w_qkv, tokens, masked, dy1, vec, db1, small2, small_a]
+    input_grad, total = call(
+        first_back_kernel, [((256, D), BF), ((16, D), F32)], args, flops=10**9
+    )(*args)
+    for mask in (CORE, Y, Z, 2 * Z, X):
+        total = total + swap(total, mask)
+    flat = total.reshape(-1)
+    gain_g = lax.dynamic_slice(flat, (96 * f,), (96,))
+    offset_g = lax.dynamic_slice(flat, (2 * D + 528 * f,), (528,))
+
+    rate = base_rate / math.sqrt(tokens.shape[0] * 32)
+    args = [co, attn_weight, attn_moment, attn_average, mlp_weight, mlp_moment, mlp_average]
+    args += [*qkv_g, *out_g, *up0_g, *up1_g, down_mine, swap(down_mine, X)]
+    updated = call(
+        functools.partial(update_kernel, rate),
+        [((48, 4 * D), F32)] * 3
+        + [((48, 4 * D), BF)]
+        + [((48, 2 * FF), F32)] * 3
+        + [((48, 2 * FF), BF)],
+        args,
+    )(*args)
+    gains = advance(gain_g, gain_vector, gain_moment, gain_average, rate)
+    offsets = advance(offset_g, offset_vector, offset_moment, offset_average, rate)
+    return (activations, input_grad, *updated, *gains, *offsets)
+
+
 def solution(mesh):
     placed = (
         P(("rep", "fsdp"), None),
@@ -351,8 +837,9 @@
         P("fsdp"),
         P("fsdp"),
     )
+    small = mesh.shape["rep"] == 2 and mesh.shape["fsdp"] == 16
     return jax.shard_map(
-        per_device,
+        fast_device if small else per_device,
         mesh=mesh,
         in_specs=placed,
         out_specs=(

time: 555 us -> 305 us (0.55)
  blocking collectives: 153 us -> 0 us
  waiting for transfers between devices: 252 us -> 107 us
  starting transfers between devices: 0.47 us -> 70.2 us
  matrix products: 55.7 us -> 0 us
  Pallas kernels: 0 us -> 50 us
  other arithmetic: 49.7 us -> 4.89 us
  local copies, waits for them, and re-layouts: 22.4 us -> 56.4 us
    reduce_scatter x4 -> x1, waiting for transfers between devices: 196 us -> 0.01 us  [fast_device(): lax.psum_scatter(down_local, 'fsdp', scatter_dimension=0, tiled=True)]
    unnamed x4 -> x0, blocking collectives: 138 us -> none
    ppermute x0 -> x68, waiting for transfers between devices: none -> 107 us  [swap(): lax.ppermute(array, ('rep', 'fsdp'), [(i, i ^ mask) for i in range(32)])]
    ppermute x0 -> x68, starting transfers between devices: none -> 70.1 us  [swap(): lax.ppermute(array, ('rep', 'fsdp'), [(i, i ^ mask) for i in range(32)])]
    all_gather x2 -> x1, waiting for transfers between devices: 56.2 us -> 0.02 us  [fast_device(): w2 = lax.all_gather(w2_shard, 'fsdp', axis=0, tiled=True)]
    dot_general x18 -> x0, matrix products: 55.7 us -> none  [the longest x4 17.5 us: over_tokens(): lax.dot_general(left_mat, right_mat, (((0,), (0,)), ((), ())), preferred_...]
    pallas_call x0 -> x35, Pallas kernels: none -> 50 us  [the longest x4 7.23 us: weight_grad(): pl.pallas_call(functools.partial(weight_grad_kernel, groups, width), out_...]
    unnamed x150 -> x249, local copies, waits for them, and re-layouts: 15.1 us -> 54.6 us
  transfers between devices with their start and end apart: 6 -> 70, of which waited for: 4 -> 20; matrix products, arithmetic and copies ran while one was open for 13% -> 2% of each run, Pallas kernels for 0% -> 15%
where the time goes in v1:
time: 305 us; the launch traced here: 304 us
  waiting for transfers between devices  107 us (35%)
  starting transfers between devices  70.2 us (23%)
  local copies, waits for them, and re-layouts  56.4 us (18%)
  Pallas kernels  50 us (16%)
  between operations  15.2 us (5%)
  other arithmetic  4.89 us (2%)
    ppermute x68, waiting for transfers between devices, swap(): lax.ppermute(array, ('rep', 'fsdp'), [(i, i ^ mask) for i in range(32)])  107 us
    ppermute x68, starting transfers between devices, swap(): lax.ppermute(array, ('rep', 'fsdp'), [(i, i ^ mask) for i in range(32)])  70.1 us
    unnamed x249, local copies, waits for them, and re-layouts  54.6 us
    pallas_call x4, Pallas kernels, weight_grad(): pl.pallas_call(functools.partial(weight_grad_kernel, groups, width), out_...  7.23 us
  transfers between devices with their start and end apart: 70, of which 20 were waited for; matrix products, arithmetic and copies ran while one was open for 2% of the time, Pallas kernels for 15%

profile of v1, /device:TPU:0, one launch (start us, length us, event | category | flops | bytes accessed | tf_op | source)
XLA Modules:
  0.0 303.6 jit_solution(85830448580802294)
XLA Ops:
  11.1 5.1 %collective-permute-start.26 = (bf16[48,768]{1,0:T(8,128)(2,1)S(1)}, bf16[48,768]{1,0:T(8,128)(2,1)S(1)}, u32[]{:S(2)}, u32[]{:S(2)}) collective-permute-start(bf16[48,768]{1,0:T(8,128)(2,1)S(1)} %get-tuple-element.107), channel_id=1, source_target_pairs={{0,12},{1,13},{2,14},{3,15},{4,8},{5,9},{6,10},{7,11},{8,4},{9,5},... | collective-permute-start | bytes 221192 | tf_op jit(solution)/shard_map/ppermute | solution.py:667
  17.2 3.8 %collective-permute-start.6 = (bf16[48,1152]{1,0:T(8,128)(2,1)S(1)}, bf16[48,1152]{1,0:T(8,128)(2,1)S(1)}, u32[]{:S(2)}, u32[]{:S(2)}) collective-permute-start(bf16[48,1152]{1,0:T(8,128)(2,1)S(1)} %get-tuple-element.99), channel_id=1, source_target_pairs={{0,12},{1,13},{2,14},{3,15},{4,8},{5,9},{6,10},{7,11},{8,4},{9,5},... | collective-permute-start | bytes 331784 | tf_op jit(solution)/shard_map/ppermute | solution.py:667
  21.2 2.3 collective-permute-start.4
  23.4 4.2 %collective-permute-done.25 = bf16[48,768]{1,0:T(8,128)(2,1)S(1)} collective-permute-done((bf16[48,768]{1,0:T(8,128)(2,1)S(1)}, bf16[48,768]{1,0:T(8,128)(2,1)S(1)}, u32[]{:S(2)}, u32[]{:S(2)}) %collective-permute-start.25) | collective-permute-done | bytes 73760 | tf_op jit(solution)/shard_map/ppermute | solution.py:667
  27.9 1.7 collective-permute-start.1
  29.6 2.5 collective-permute-done.1
  32.1 3.0 collective-permute-done.4
  35.0 2.5 collective-permute-start.14
  37.5 7.7 %collective-permute-done.14 = bf16[48,1152]{1,0:T(8,128)(2,1)S(1)} collective-permute-done((bf16[48,1152]{1,0:T(8,128)(2,1)S(1)}, bf16[48,1152]{1,0:T(8,128)(2,1)S(1)}, u32[]{:S(2)}, u32[]{:S(2)}) %collective-permute-start.14) | collective-permute-done | bytes 110624 | tf_op jit(solution)/shard_map/ppermute | solution.py:667
  45.3 5.6 %collective-permute-done.15 = bf16[48,1152]{1,0:T(8,128)(2,1)S(1)} collective-permute-done((bf16[48,1152]{1,0:T(8,128)(2,1)S(1)}, bf16[48,1152]{1,0:T(8,128)(2,1)S(1)}, u32[]{:S(2)}, u32[]{:S(2)}) %collective-permute-start.15) | collective-permute-done | bytes 110624 | tf_op jit(solution)/shard_map/ppermute | solution.py:667
  50.9 4.1 %collective-permute-done.2 = f32[16,768]{1,0:T(8,128)S(1)} collective-permute-done((f32[16,768]{1,0:T(8,128)S(1)}, f32[16,768]{1,0:T(8,128)S(1)}, u32[]{:S(2)}, u32[]{:S(2)}) %collective-permute-start.2) | collective-permute-done | bytes 49184 | tf_op jit(solution)/shard_map/ppermute | solution.py:667
  55.0 1.5 collective-permute-start.28
  57.8 1.6 collective-permute-start.27
  59.4 5.6 %collective-permute-done.3 = f32[16,768]{1,0:T(8,128)S(1)} collective-permute-done((f32[16,768]{1,0:T(8,128)S(1)}, f32[16,768]{1,0:T(8,128)S(1)}, u32[]{:S(2)}, u32[]{:S(2)}) %collective-permute-start.3) | collective-permute-done | bytes 49184 | tf_op jit(solution)/shard_map/ppermute | solution.py:667
  66.1 1.5 collective-permute-start.17
  67.6 1.8 collective-permute-start.8
  69.4 4.6 %collective-permute-done.27.refs_1_ = bf16[192,768]{1,0:T(8,128)(2,1)S(1)} collective-permute-done((bf16[192,768]{1,0:T(8,128)(2,1)S(1)}, bf16[192,768]{1,0:T(8,128)(2,1)S(1)}, u32[]{:S(2)}, u32[]{:S(2)}) %collective-permute-start.27) | collective-permute-done | bytes 294944 | tf_op jit(solution)/shard_map/ppermute | solution.py:667
  78.2 6.5 %collective-permute-done.17.refs_1_ = bf16[192,1152]{1,0:T(8,128)(2,1)S(1)} collective-permute-done((bf16[192,1152]{1,0:T(8,128)(2,1)S(1)}, bf16[192,1152]{1,0:T(8,128)(2,1)S(1)}, u32[]{:S(2)}, u32[]{:S(2)}) %collective-permute-start.17) | collective-permute-done | bytes 442400 | tf_op jit(solution)/shard_map/ppermute | solution.py:667
  87.4 5.7 %collective-permute-done.7.refs_1_ = bf16[192,1152]{1,0:T(8,128)(2,1)S(1)} collective-permute-done((bf16[192,1152]{1,0:T(8,128)(2,1)S(1)}, bf16[192,1152]{1,0:T(8,128)(2,1)S(1)}, u32[]{:S(2)}, u32[]{:S(2)}) %collective-permute-start.7) | collective-permute-done | bytes 442400 | tf_op jit(solution)/shard_map/ppermute | solution.py:667
  96.6 1.5 collective-permute-start.9
  100.5 2.8 collective-permute-done.19.refs_3_
  105.4 5.3 %collective-permute-done.9.refs_3_ = bf16[192,1152]{1,0:T(8,128)(2,1)S(1)} collective-permute-done((bf16[192,1152]{1,0:T(8,128)(2,1)S(1)}, bf16[192,1152]{1,0:T(8,128)(2,1)S(1)}, u32[]{:S(2)}, u32[]{:S(2)}) %collective-permute-start.9) | collective-permute-done | bytes 442400 | tf_op jit(solution)/shard_map/ppermute | solution.py:667
  122.2 1.6 shard_map.308
  125.6 1.6 shard_map.306
  127.3 2.9 shard_map.307
  137.3 1.9 shard_map.337
  139.2 2.1 copy-done.2
  142.2 2.3 copy-done.78
  151.9 3.5 %shard_map.313 = (bf16[256,1536]{1,0:T(8,128)(2,1)S(1)}, bf16[256,1536]{1,0:T(8,128)(2,1)S(1)}, f32[8,768]{1,0:T(8,128)S(1)}, bf16[256,768]{1,0:T(8,128)(2,1)}) custom-call(bf16[256,768]{1,0:T(8,128)(2,1)S(1)} %copy-done.84, bf16[768,3072]{1,0:T(8,128)(2,1)S(1)} %copy-done.78, f32[256,768]{1,0:T(8,128)S(1)} %copy-done.96, bf16[256,1536]{1,0:T(8,128)(2,1)S(1)} %copy-done.100, ...), custom_call_target="tpu_custom_call" | custom-call | flops 3000000000 | bytes 12656640 | tf_op jit(solution)/shard_map/pallas_call | solution.py:730
  155.5 2.7 shard_map.314
  158.3 5.0 %shard_map.315 = (bf16[256,2304]{1,0:T(8,128)(2,1)S(1)}, f32[8,768]{1,0:T(8,128)S(1)}) custom-call(bf16[256,2304]{1,0:T(8,128)(2,1)S(1)} %copy-done.106, bf16[256,768]{1,0:T(8,128)(2,1)S(1)} %get-tuple-element.115.datt, f32[16,256]{1,0:T(8,128)S(1)} %copy-done.108, s32[256,1]{1,0:T(8,128)S(1)} %copy-done.68, s32[1,256]{1,0:T(1,128)S(1)} %bitcast.46, ...), custom_call_target="tpu_custom_call" | custom-call | flops 3000000000 | bytes 2796544 | tf_op jit(solution)/shard_map/pallas_call | solution.py:789
  163.3 2.3 shard_map.317
  166.4 1.7 shard_map.327
  168.2 2.0 shard_map.332
  177.4 29.0 %collective-permute-done.49 = bf16[384,768]{1,0:T(8,128)(2,1)S(1)} collective-permute-done((bf16[384,768]{1,0:T(8,128)(2,1)S(1)}, bf16[384,768]{1,0:T(8,128)(2,1)S(1)}, u32[]{:S(2)}, u32[]{:S(2)}) %collective-permute-start.49) | collective-permute-done | bytes 589856 | tf_op jit(solution)/shard_map/ppermute | solution.py:667
  208.0 2.3 shard_map.316
  211.7 1.8 collective-permute-start.36
  213.8 11.8 %collective-permute-done.64 = f32[16,768]{1,0:T(8,128)S(1)} collective-permute-done((f32[16,768]{1,0:T(8,128)S(1)}, f32[16,768]{1,0:T(8,128)S(1)}, u32[]{:S(2)}, u32[]{:S(2)}) %collective-permute-start.64) | collective-permute-done | bytes 49184 | tf_op jit(solution)/shard_map/ppermute | solution.py:667
  225.6 1.5 collective-permute-start.65
  229.8 2.6 collective-permute-start.66
  236.6 2.7 collective-permute-done.67
  241.3 2.9 collective-permute-start.45
  245.7 1.7 shard_map.330
  251.7 3.8 %collective-permute-start.52 = (bf16[48,768]{1,0:T(8,128)(2,1)}, bf16[48,768]{1,0:T(8,128)(2,1)}, u32[]{:S(2)}, u32[]{:S(2)}) collective-permute-start(bf16[48,768]{1,0:T(8,128)(2,1)} %get-tuple-element.154), channel_id=1, source_target_pairs={{0,8},{1,9},{2,10},{3,11},{4,12},{5,13},{6,14},{7,15},{8,0},{9,1},... | collective-permute-start | bytes 221192 | tf_op jit(solution)/shard_map/ppermute | solution.py:667
  258.0 3.8 %collective-permute-start.59 = (bf16[48,768]{1,0:T(8,128)(2,1)}, bf16[48,768]{1,0:T(8,128)(2,1)}, u32[]{:S(2)}, u32[]{:S(2)}) collective-permute-start(bf16[48,768]{1,0:T(8,128)(2,1)} %get-tuple-element.164), channel_id=1, source_target_pairs={{0,8},{1,9},{2,10},{3,11},{4,12},{5,13},{6,14},{7,15},{8,0},{9,1},... | collective-permute-start | bytes 221192 | tf_op jit(solution)/shard_map/ppermute | solution.py:667
  268.8 3.8 %collective-permute-start.38 = (bf16[48,1152]{1,0:T(8,128)(2,1)}, bf16[48,1152]{1,0:T(8,128)(2,1)S(1)}, u32[]{:S(2)}, u32[]{:S(2)}) collective-permute-start(bf16[48,1152]{1,0:T(8,128)(2,1)} %copy-done.88), channel_id=1, source_target_pairs={{0,8},{1,9},{2,10},{3,11},{4,12},{5,13},{6,14},{7,15},{8,0},{9,1},... | collective-permute-start | bytes 331784 | tf_op jit(solution)/shard_map/ppermute | solution.py:667
  287.6 2.1 collective-permute-done.40.refs_7_
  293.0 3.8 %shard_map.338 = (f32[48,3072]{1,0:T(8,128)}, f32[48,3072]{1,0:T(8,128)}, f32[48,3072]{1,0:T(8,128)}, bf16[48,3072]{1,0:T(8,128)(2,1)}, f32[48,6144]{1,0:T(8,128...) custom-call(s32[4]{0:T(128)S(1)} %pad_add_fusion.co, f32[48,3072]{1,0:T(8,128)S(1)} %copy-done.4, ...), custom_call_target="tpu_custom_call" | custom-call | bytes 12681232 | tf_op jit(solution)/shard_map/pallas_call | solution.py:807
  (403 shorter events, 104.3 us)
Async XLA Ops:
  7.2 134.2 %all-gather.2.cloned.1.call-start = ((), (), s32[]{:S(2)}) async-start(), calls=%async_computation.1 | async-start | bytes 5013504 | tf_op jit(solution)/shard_map/all_gather | solution.py:682
  11.1 255.7 %reduce-scatter.2.cloned.1.call-start = ((), (), s32[]{:S(2)}) async-start(), calls=%async_computation.2 | async-start | bytes 5013504 | tf_op jit(solution)/shard_map/reduce_scatter | solution.py:728
  11.1 16.8 %collective-permute-start.26 = (bf16[48,768]{1,0:T(8,128)(2,1)S(1)}, bf16[48,768]{1,0:T(8,128)(2,1)S(1)}, u32[]{:S(2)}, u32[]{:S(2)}) collective-permute-start(bf16[48,768]{1,0:T(8,128)(2,1)S(1)} %get-tuple-element.107), channel_id=1, source_target_pairs={{0,12},{1,13},{2,14},{3,15},{4,8},{5,9},{6,10},{7,11},{8,4},{9,5},... | collective-permute-start | bytes 221192 | tf_op jit(solution)/shard_map/ppermute | solution.py:667
  16.2 11.4 %collective-permute-start.25 = (bf16[48,768]{1,0:T(8,128)(2,1)S(1)}, bf16[48,768]{1,0:T(8,128)(2,1)S(1)}, u32[]{:S(2)}, u32[]{:S(2)}) collective-permute-start(bf16[48,768]{1,0:T(8,128)(2,1)S(1)} %get-tuple-element.107), channel_id=1, source_target_pairs={{0,8},{1,9},{2,10},{3,11},{4,12},{5,13},{6,14},{7,15},{8,0},{9,1},... | collective-permute-start | bytes 221192 | tf_op jit(solution)/shard_map/ppermute | solution.py:667
  17.2 40.7 %collective-permute-start.6 = (bf16[48,1152]{1,0:T(8,128)(2,1)S(1)}, bf16[48,1152]{1,0:T(8,128)(2,1)S(1)}, u32[]{:S(2)}, u32[]{:S(2)}) collective-permute-start(bf16[48,1152]{1,0:T(8,128)(2,1)S(1)} %get-tuple-element.99), channel_id=1, source_target_pairs={{0,12},{1,13},{2,14},{3,15},{4,8},{5,9},{6,10},{7,11},{8,4},{9,5},... | collective-permute-start | bytes 331784 | tf_op jit(solution)/shard_map/ppermute | solution.py:667
  21.1 38.4 %collective-permute-start.5 = (bf16[48,1152]{1,0:T(8,128)(2,1)S(1)}, bf16[48,1152]{1,0:T(8,128)(2,1)S(1)}, u32[]{:S(2)}, u32[]{:S(2)}) collective-permute-start(bf16[48,1152]{1,0:T(8,128)(2,1)S(1)} %get-tuple-element.99), channel_id=1, source_target_pairs={{0,8},{1,9},{2,10},{3,11},{4,12},{5,13},{6,14},{7,15},{8,0},{9,1},... | collective-permute-start | bytes 331784 | tf_op jit(solution)/shard_map/ppermute | solution.py:667
  21.2 13.9 %collective-permute-start.4 = (bf16[48,1152]{1,0:T(8,128)(2,1)S(1)}, bf16[48,1152]{1,0:T(8,128)(2,1)S(1)}, u32[]{:S(2)}, u32[]{:S(2)}) collective-permute-start(bf16[48,1152]{1,0:T(8,128)(2,1)S(1)} %get-tuple-element.99), channel_id=1, source_target_pairs={{0,4},{1,5},{2,6},{3,7},{4,0},{5,1},{6,2},{7,3},{8,12},{9,13},{10,... | collective-permute-start | bytes 331784 | tf_op jit(solution)/shard_map/ppermute | solution.py:667
  27.6 28.8 %collective-permute-start.16 = (bf16[48,1152]{1,0:T(8,128)(2,1)S(1)}, bf16[48,1152]{1,0:T(8,128)(2,1)S(1)}, u32[]{:S(2)}, u32[]{:S(2)}) collective-permute-start(bf16[48,1152]{1,0:T(8,128)(2,1)S(1)} %get-tuple-element.101), channel_id=1, source_target_pairs={{0,12},{1,13},{2,14},{3,15},{4,8},{5,9},{6,10},{7,11},{8,4},{9,5},... | collective-permute-start | bytes 331784 | tf_op jit(solution)/shard_map/ppermute | solution.py:667
  32.1 18.8 %collective-permute-start.15 = (bf16[48,1152]{1,0:T(8,128)(2,1)S(1)}, bf16[48,1152]{1,0:T(8,128)(2,1)S(1)}, u32[]{:S(2)}, u32[]{:S(2)}) collective-permute-start(bf16[48,1152]{1,0:T(8,128)(2,1)S(1)} %get-tuple-element.101), channel_id=1, source_target_pairs={{0,8},{1,9},{2,10},{3,11},{4,12},{5,13},{6,14},{7,15},{8,0},{9,1},... | collective-permute-start | bytes 331784 | tf_op jit(solution)/shard_map/ppermute | solution.py:667
  45.3 20.1 %collective-permute-start.30 = (bf16[192,768]{1,0:T(8,128)(2,1)S(1)}, bf16[192,768]{1,0:T(8,128)(2,1)S(1)}, u32[]{:S(2)}, u32[]{:S(2)}) collective-permute-start(bf16[192,768]{1,0:T(8,128)(2,1)S(1)} %constant_dynamic-update-slice_fusion.8.refs_0_), channel_id=1, source_target_pairs={{0,1},{1,0},{2,3},{3,2},{4,5},{5,4},{6,7},{7,6},{8,9},{9,8},{10,11... | collective-permute-start | bytes 884744 | tf_op jit(solution)/shard_map/ppermute | solution.py:667
  55.0 12.7 %collective-permute-start.28 = (bf16[192,768]{1,0:T(8,128)(2,1)S(1)}, bf16[192,768]{1,0:T(8,128)(2,1)S(1)}, u32[]{:S(2)}, u32[]{:S(2)}) collective-permute-start(bf16[192,768]{1,0:T(8,128)(2,1)S(1)} %constant_dynamic-update-slice_fusion.8.refs_0_), channel_id=1, source_target_pairs={{0,16},{1,17},{2,18},{3,19},{4,20},{5,21},{6,22},{7,23},{8,24},{9,... | collective-permute-start | bytes 884744 | tf_op jit(solution)/shard_map/ppermute | solution.py:667
  57.8 16.2 %collective-permute-start.27 = (bf16[192,768]{1,0:T(8,128)(2,1)S(1)}, bf16[192,768]{1,0:T(8,128)(2,1)S(1)}, u32[]{:S(2)}, u32[]{:S(2)}) collective-permute-start(bf16[192,768]{1,0:T(8,128)(2,1)S(1)} %constant_dynamic-update-slice_fusion.8.refs_0_), channel_id=1, source_target_pairs={{0,2},{1,3},{2,0},{3,1},{4,6},{5,7},{6,4},{7,5},{8,10},{9,11},{10,... | collective-permute-start | bytes 884744 | tf_op jit(solution)/shard_map/ppermute | solution.py:667
  59.4 16.1 %collective-permute-start.20 = (bf16[192,1152]{1,0:T(8,128)(2,1)S(1)}, bf16[192,1152]{1,0:T(8,128)(2,1)S(1)}, u32[]{:S(2)}, u32[]{:S(2)}) collective-permute-start(bf16[192,1152]{1,0:T(8,128)(2,1)S(1)} %constant_dynamic-update-slice_fusion.4.refs_0_), channel_id=1, source_target_pairs={{0,1},{1,0},{2,3},{3,2},{4,5},{5,4},{6,7},{7,6},{8,9},{9,8},{10,11... | collective-permute-start | bytes 1327112 | tf_op jit(solution)/shard_map/ppermute | solution.py:667
  65.0 13.1 %collective-permute-start.18 = (bf16[192,1152]{1,0:T(8,128)(2,1)S(1)}, bf16[192,1152]{1,0:T(8,128)(2,1)S(1)}, u32[]{:S(2)}, u32[]{:S(2)}) collective-permute-start(bf16[192,1152]{1,0:T(8,128)(2,1)S(1)} %constant_dynamic-update-slice_fusion.4.refs_0_), channel_id=1, source_target_pairs={{0,16},{1,17},{2,18},{3,19},{4,20},{5,21},{6,22},{7,23},{8,24},{9,... | collective-permute-start | bytes 1327112 | tf_op jit(solution)/shard_map/ppermute | solution.py:667
  66.1 18.6 %collective-permute-start.17 = (bf16[192,1152]{1,0:T(8,128)(2,1)S(1)}, bf16[192,1152]{1,0:T(8,128)(2,1)S(1)}, u32[]{:S(2)}, u32[]{:S(2)}) collective-permute-start(bf16[192,1152]{1,0:T(8,128)(2,1)S(1)} %constant_dynamic-update-slice_fusion.4.refs_0_), channel_id=1, source_target_pairs={{0,2},{1,3},{2,0},{3,1},{4,6},{5,7},{6,4},{7,5},{8,10},{9,11},{10,... | collective-permute-start | bytes 1327112 | tf_op jit(solution)/shard_map/ppermute | solution.py:667
  67.6 19.2 %collective-permute-start.8 = (bf16[192,1152]{1,0:T(8,128)(2,1)S(1)}, bf16[192,1152]{1,0:T(8,128)(2,1)S(1)}, u32[]{:S(2)}, u32[]{:S(2)}) collective-permute-start(bf16[192,1152]{1,0:T(8,128)(2,1)S(1)} %constant_dynamic-update-slice_fusion.refs_0_), channel_id=1, source_target_pairs={{0,16},{1,17},{2,18},{3,19},{4,20},{5,21},{6,22},{7,23},{8,24},{9,... | collective-permute-start | bytes 1327112 | tf_op jit(solution)/shard_map/ppermute | solution.py:667
  74.1 19.1 %collective-permute-start.7 = (bf16[192,1152]{1,0:T(8,128)(2,1)S(1)}, bf16[192,1152]{1,0:T(8,128)(2,1)S(1)}, u32[]{:S(2)}, u32[]{:S(2)}) collective-permute-start(bf16[192,1152]{1,0:T(8,128)(2,1)S(1)} %constant_dynamic-update-slice_fusion.refs_0_), channel_id=1, source_target_pairs={{0,2},{1,3},{2,0},{3,1},{4,6},{5,7},{6,4},{7,5},{8,10},{9,11},{10,... | collective-permute-start | bytes 1327112 | tf_op jit(solution)/shard_map/ppermute | solution.py:667
  76.3 17.7 %collective-permute-start.32 = (bf16[192,768]{1,0:T(8,128)(2,1)S(1)}, bf16[192,768]{1,0:T(8,128)(2,1)S(1)}, u32[]{:S(2)}, u32[]{:S(2)}) collective-permute-start(bf16[192,768]{1,0:T(8,128)(2,1)S(1)} %collective-permute-done.28.refs_2_), channel_id=1, source_target_pairs={{0,1},{1,0},{2,3},{3,2},{4,5},{5,4},{6,7},{7,6},{8,9},{9,8},{10,11... | collective-permute-start | bytes 884744 | tf_op jit(solution)/shard_map/ppermute | solution.py:667
  78.2 17.7 %collective-permute-start.31 = (bf16[192,768]{1,0:T(8,128)(2,1)S(1)}, bf16[192,768]{1,0:T(8,128)(2,1)S(1)}, u32[]{:S(2)}, u32[]{:S(2)}) collective-permute-start(bf16[192,768]{1,0:T(8,128)(2,1)S(1)} %collective-permute-done.27.refs_1_), channel_id=1, source_target_pairs={{0,1},{1,0},{2,3},{3,2},{4,5},{5,4},{6,7},{7,6},{8,9},{9,8},{10,11... | collective-permute-start | bytes 884744 | tf_op jit(solution)/shard_map/ppermute | solution.py:667
  84.7 13.4 %collective-permute-start.29 = (bf16[192,768]{1,0:T(8,128)(2,1)S(1)}, bf16[192,768]{1,0:T(8,128)(2,1)S(1)}, u32[]{:S(2)}, u32[]{:S(2)}) collective-permute-start(bf16[192,768]{1,0:T(8,128)(2,1)S(1)} %collective-permute-done.27.refs_1_), channel_id=1, source_target_pairs={{0,16},{1,17},{2,18},{3,19},{4,20},{5,21},{6,22},{7,23},{8,24},{9,... | collective-permute-start | bytes 884744 | tf_op jit(solution)/shard_map/ppermute | solution.py:667
  86.9 16.4 %collective-permute-start.19 = (bf16[192,1152]{1,0:T(8,128)(2,1)S(1)}, bf16[192,1152]{1,0:T(8,128)(2,1)}, u32[]{:S(2)}, u32[]{:S(2)}) collective-permute-start(bf16[192,1152]{1,0:T(8,128)(2,1)S(1)} %collective-permute-done.17.refs_1_), channel_id=1, source_target_pairs={{0,16},{1,17},{2,18},{3,19},{4,20},{5,21},{6,22},{7,23},{8,24},{9,... | collective-permute-start | bytes 1327112 | tf_op jit(solution)/shard_map/ppermute | solution.py:667
  96.6 14.1 %collective-permute-start.9 = (bf16[192,1152]{1,0:T(8,128)(2,1)S(1)}, bf16[192,1152]{1,0:T(8,128)(2,1)S(1)}, u32[]{:S(2)}, u32[]{:S(2)}) collective-permute-start(bf16[192,1152]{1,0:T(8,128)(2,1)S(1)} %collective-permute-done.7.refs_1_), channel_id=1, source_target_pairs={{0,16},{1,17},{2,18},{3,19},{4,20},{5,21},{6,22},{7,23},{8,24},{9,... | collective-permute-start | bytes 1327112 | tf_op jit(solution)/shard_map/ppermute | solution.py:667
  100.4 23.4 %collective-permute-start.10 = (bf16[192,1152]{1,0:T(8,128)(2,1)S(1)}, bf16[192,1152]{1,0:T(8,128)(2,1)S(1)}, u32[]{:S(2)}, u32[]{:S(2)}) collective-permute-start(bf16[192,1152]{1,0:T(8,128)(2,1)S(1)} %constant_dynamic-update-slice_fusion.refs_0_), channel_id=1, source_target_pairs={{0,1},{1,0},{2,3},{3,2},{4,5},{5,4},{6,7},{7,6},{8,9},{9,8},{10,11... | collective-permute-start | bytes 1327112 | tf_op jit(solution)/shard_map/ppermute | solution.py:667
  103.3 18.0 %collective-permute-start.23 = (bf16[192,1152]{1,0:T(8,128)(2,1)}, bf16[192,1152]{1,0:T(8,128)(2,1)}, u32[]{:S(2)}, u32[]{:S(2)}) collective-permute-start(bf16[192,1152]{1,0:T(8,128)(2,1)} %collective-permute-done.19.refs_3_), channel_id=1, source_target_pairs={{0,1},{1,0},{2,3},{3,2},{4,5},{5,4},{6,7},{7,6},{8,9},{9,8},{10,11... | collective-permute-start | bytes 1327112 | tf_op jit(solution)/shard_map/ppermute | solution.py:667
  104.1 20.5 %collective-permute-start.11 = (bf16[192,1152]{1,0:T(8,128)(2,1)S(1)}, bf16[192,1152]{1,0:T(8,128)(2,1)}, u32[]{:S(2)}, u32[]{:S(2)}) collective-permute-start(bf16[192,1152]{1,0:T(8,128)(2,1)S(1)} %collective-permute-done.7.refs_1_), channel_id=1, source_target_pairs={{0,1},{1,0},{2,3},{3,2},{4,5},{5,4},{6,7},{7,6},{8,9},{9,8},{10,11... | collective-permute-start | bytes 1327112 | tf_op jit(solution)/shard_map/ppermute | solution.py:667
  105.4 19.2 %collective-permute-start.12 = (bf16[192,1152]{1,0:T(8,128)(2,1)S(1)}, bf16[192,1152]{1,0:T(8,128)(2,1)}, u32[]{:S(2)}, u32[]{:S(2)}) collective-permute-start(bf16[192,1152]{1,0:T(8,128)(2,1)S(1)} %collective-permute-done.8.refs_2_), channel_id=1, source_target_pairs={{0,1},{1,0},{2,3},{3,2},{4,5},{5,4},{6,7},{7,6},{8,9},{9,8},{10,11... | collective-permute-start | bytes 1327112 | tf_op jit(solution)/shard_map/ppermute | solution.py:667
  110.7 13.9 %collective-permute-start.13 = (bf16[192,1152]{1,0:T(8,128)(2,1)S(1)}, bf16[192,1152]{1,0:T(8,128)(2,1)}, u32[]{:S(2)}, u32[]{:S(2)}) collective-permute-start(bf16[192,1152]{1,0:T(8,128)(2,1)S(1)} %collective-permute-done.9.refs_3_), channel_id=1, source_target_pairs={{0,1},{1,0},{2,3},{3,2},{4,5},{5,4},{6,7},{7,6},{8,9},{9,8},{10,11... | collective-permute-start | bytes 1327112 | tf_op jit(solution)/shard_map/ppermute | solution.py:667
  171.2 39.1 %collective-permute-start.35 = (bf16[384,1152]{1,0:T(8,128)(2,1)S(1)}, bf16[384,1152]{1,0:T(8,128)(2,1)S(1)}, u32[]{:S(2)}, u32[]{:S(2)}) collective-permute-start(bf16[384,1152]{1,0:T(8,128)(2,1)S(1)} %get-tuple-element.127), channel_id=1, source_target_pairs={{0,16},{1,17},{2,18},{3,19},{4,20},{5,21},{6,22},{7,23},{8,24},{9,... | collective-permute-start | bytes 2654216 | tf_op jit(solution)/shard_map/ppermute | solution.py:667
  174.0 32.4 %collective-permute-start.49 = (bf16[384,768]{1,0:T(8,128)(2,1)S(1)}, bf16[384,768]{1,0:T(8,128)(2,1)S(1)}, u32[]{:S(2)}, u32[]{:S(2)}) collective-permute-start(bf16[384,768]{1,0:T(8,128)(2,1)S(1)} %get-tuple-element.149), channel_id=1, source_target_pairs={{0,16},{1,17},{2,18},{3,19},{4,20},{5,21},{6,22},{7,23},{8,24},{9,... | collective-permute-start | bytes 1769480 | tf_op jit(solution)/shard_map/ppermute | solution.py:667
  175.1 57.4 %collective-permute-start.56 = (bf16[384,768]{1,0:T(8,128)(2,1)S(1)}, bf16[384,768]{1,0:T(8,128)(2,1)S(1)}, u32[]{:S(2)}, u32[]{:S(2)}) collective-permute-start(bf16[384,768]{1,0:T(8,128)(2,1)S(1)} %get-tuple-element.159), channel_id=1, source_target_pairs={{0,16},{1,17},{2,18},{3,19},{4,20},{5,21},{6,22},{7,23},{8,24},{9,... | collective-permute-start | bytes 1769480 | tf_op jit(solution)/shard_map/ppermute | solution.py:667
  176.5 50.7 %collective-permute-start.42 = (bf16[384,384]{1,0:T(8,128)(2,1)S(1)}, bf16[384,384]{1,0:T(8,128)(2,1)S(1)}, u32[]{:S(2)}, u32[]{:S(2)}) collective-permute-start(bf16[384,384]{1,0:T(8,128)(2,1)S(1)} %get-tuple-element.138), channel_id=1, source_target_pairs={{0,16},{1,17},{2,18},{3,19},{4,20},{5,21},{6,22},{7,23},{8,24},{9,... | collective-permute-start | bytes 884744 | tf_op jit(solution)/shard_map/ppermute | solution.py:667
  207.7 36.5 %collective-permute-start.50 = (bf16[4,48,768]{2,1,0:T(8,128)(2,1)}, bf16[4,48,768]{2,1,0:T(8,128)(2,1)}, u32[]{:S(2)}, u32[]{:S(2)}) collective-permute-start(bf16[4,48,768]{2,1,0:T(8,128)(2,1)} %get-tuple-element.151), channel_id=1, source_target_pairs={{0,2},{1,3},{2,0},{3,1},{4,6},{5,7},{6,4},{7,5},{8,10},{9,11},{10,... | collective-permute-start | bytes 884744 | tf_op jit(solution)/shard_map/ppermute | solution.py:667
  211.7 45.6 %collective-permute-start.36 = (bf16[4,48,1152]{2,1,0:T(8,128)(2,1)}, bf16[4,48,1152]{2,1,0:T(8,128)(2,1)S(1)}, u32[]{:S(2)}, u32[]{:S(2)}) collective-permute-start(bf16[4,48,1152]{2,1,0:T(8,128)(2,1)} %get-tuple-element.129), channel_id=1, source_target_pairs={{0,2},{1,3},{2,0},{3,1},{4,6},{5,7},{6,4},{7,5},{8,10},{9,11},{10,... | collective-permute-start | bytes 1327112 | tf_op jit(solution)/shard_map/ppermute | solution.py:667
  213.5 12.1 %collective-permute-start.64 = (f32[16,768]{1,0:T(8,128)S(1)}, f32[16,768]{1,0:T(8,128)S(1)}, u32[]{:S(2)}, u32[]{:S(2)}) collective-permute-start(f32[16,768]{1,0:T(8,128)S(1)} %add.79), channel_id=1, source_target_pairs={{0,2},{1,3},{2,0},{3,1},{4,6},{5,7},{6,4},{7,5},{8,10},{9,11},{10,... | collective-permute-start | bytes 147464 | tf_op jit(solution)/shard_map/ppermute | solution.py:667
  227.8 11.5 %collective-permute-start.43 = (bf16[4,48,384]{2,1,0:T(8,128)(2,1)S(1)}, bf16[4,48,384]{2,1,0:T(8,128)(2,1)S(1)}, u32[]{:S(2)}, u32[]{:S(2)}) collective-permute-start(bf16[4,48,384]{2,1,0:T(8,128)(2,1)S(1)} %get-tuple-element.140), channel_id=1, source_target_pairs={{0,2},{1,3},{2,0},{3,1},{4,6},{5,7},{6,4},{7,5},{8,10},{9,11},{10,... | collective-permute-start | bytes 442376 | tf_op jit(solution)/shard_map/ppermute | solution.py:667
  233.8 14.3 %collective-permute-start.57 = (bf16[4,48,768]{2,1,0:T(8,128)(2,1)}, bf16[4,48,768]{2,1,0:T(8,128)(2,1)S(1)}, u32[]{:S(2)}, u32[]{:S(2)}) collective-permute-start(bf16[4,48,768]{2,1,0:T(8,128)(2,1)} %get-tuple-element.161), channel_id=1, source_target_pairs={{0,2},{1,3},{2,0},{3,1},{4,6},{5,7},{6,4},{7,5},{8,10},{9,11},{10,... | collective-permute-start | bytes 884744 | tf_op jit(solution)/shard_map/ppermute | solution.py:667
  239.9 11.1 %collective-permute-start.44 = (bf16[48,384]{1,0:T(8,128)(2,1)S(1)}, bf16[48,384]{1,0:T(8,128)(2,1)S(1)}, u32[]{:S(2)}, u32[]{:S(2)}) collective-permute-start(bf16[48,384]{1,0:T(8,128)(2,1)S(1)} %get-tuple-element.142), channel_id=1, source_target_pairs={{0,4},{1,5},{2,6},{3,7},{4,0},{5,1},{6,2},{7,3},{8,12},{9,13},{10,... | collective-permute-start | bytes 110600 | tf_op jit(solution)/shard_map/ppermute | solution.py:667
  241.3 14.2 %collective-permute-start.45 = (bf16[48,384]{1,0:T(8,128)(2,1)S(1)}, bf16[48,384]{1,0:T(8,128)(2,1)S(1)}, u32[]{:S(2)}, u32[]{:S(2)}) collective-permute-start(bf16[48,384]{1,0:T(8,128)(2,1)S(1)} %get-tuple-element.143), channel_id=1, source_target_pairs={{0,8},{1,9},{2,10},{3,11},{4,12},{5,13},{6,14},{7,15},{8,0},{9,1},... | collective-permute-start | bytes 110600 | tf_op jit(solution)/shard_map/ppermute | solution.py:667
  244.2 12.1 %collective-permute-start.46 = (bf16[48,384]{1,0:T(8,128)(2,1)S(1)}, bf16[48,384]{1,0:T(8,128)(2,1)S(1)}, u32[]{:S(2)}, u32[]{:S(2)}) collective-permute-start(bf16[48,384]{1,0:T(8,128)(2,1)S(1)} %get-tuple-element.144), channel_id=1, source_target_pairs={{0,12},{1,13},{2,14},{3,15},{4,8},{5,9},{6,10},{7,11},{8,4},{9,5},... | collective-permute-start | bytes 110600 | tf_op jit(solution)/shard_map/ppermute | solution.py:667
  248.1 18.6 %collective-permute-start.51 = (bf16[48,768]{1,0:T(8,128)(2,1)}, bf16[48,768]{1,0:T(8,128)(2,1)}, u32[]{:S(2)}, u32[]{:S(2)}) collective-permute-start(bf16[48,768]{1,0:T(8,128)(2,1)} %get-tuple-element.153), channel_id=1, source_target_pairs={{0,4},{1,5},{2,6},{3,7},{4,0},{5,1},{6,2},{7,3},{8,12},{9,13},{10,... | collective-permute-start | bytes 221192 | tf_op jit(solution)/shard_map/ppermute | solution.py:667
  251.7 16.5 %collective-permute-start.52 = (bf16[48,768]{1,0:T(8,128)(2,1)}, bf16[48,768]{1,0:T(8,128)(2,1)}, u32[]{:S(2)}, u32[]{:S(2)}) collective-permute-start(bf16[48,768]{1,0:T(8,128)(2,1)} %get-tuple-element.154), channel_id=1, source_target_pairs={{0,8},{1,9},{2,10},{3,11},{4,12},{5,13},{6,14},{7,15},{8,0},{9,1},... | collective-permute-start | bytes 221192 | tf_op jit(solution)/shard_map/ppermute | solution.py:667
  256.1 12.3 %collective-permute-start.53 = (bf16[48,768]{1,0:T(8,128)(2,1)}, bf16[48,768]{1,0:T(8,128)(2,1)}, u32[]{:S(2)}, u32[]{:S(2)}) collective-permute-start(bf16[48,768]{1,0:T(8,128)(2,1)} %get-tuple-element.155), channel_id=1, source_target_pairs={{0,12},{1,13},{2,14},{3,15},{4,8},{5,9},{6,10},{7,11},{8,4},{9,5},... | collective-permute-start | bytes 221192 | tf_op jit(solution)/shard_map/ppermute | solution.py:667
  256.9 11.9 %collective-permute-start.58 = (bf16[48,768]{1,0:T(8,128)(2,1)}, bf16[48,768]{1,0:T(8,128)(2,1)}, u32[]{:S(2)}, u32[]{:S(2)}) collective-permute-start(bf16[48,768]{1,0:T(8,128)(2,1)} %get-tuple-element.163), channel_id=1, source_target_pairs={{0,4},{1,5},{2,6},{3,7},{4,0},{5,1},{6,2},{7,3},{8,12},{9,13},{10,... | collective-permute-start | bytes 221192 | tf_op jit(solution)/shard_map/ppermute | solution.py:667
  258.0 14.6 %collective-permute-start.59 = (bf16[48,768]{1,0:T(8,128)(2,1)}, bf16[48,768]{1,0:T(8,128)(2,1)}, u32[]{:S(2)}, u32[]{:S(2)}) collective-permute-start(bf16[48,768]{1,0:T(8,128)(2,1)} %get-tuple-element.164), channel_id=1, source_target_pairs={{0,8},{1,9},{2,10},{3,11},{4,12},{5,13},{6,14},{7,15},{8,0},{9,1},... | collective-permute-start | bytes 221192 | tf_op jit(solution)/shard_map/ppermute | solution.py:667
  266.8 20.1 %collective-permute-start.62 = (bf16[48,3072]{1,0:T(8,128)(2,1)}, bf16[48,3072]{1,0:T(8,128)(2,1)S(1)}, u32[]{:S(2)}, u32[]{:S(2)}) collective-permute-start(bf16[48,3072]{1,0:T(8,128)(2,1)} %reduce-scatter.2.cloned.1.call-done.refs_14_), channel_id=1, source_target_pairs={{0,16},{1,17},{2,18},{3,19},{4,20},{5,21},{6,22},{7,23},{8,24},{9,... | collective-permute-start | bytes 884744 | tf_op jit(solution)/shard_map/ppermute | solution.py:667
  268.4 13.4 %collective-permute-start.37 = (bf16[48,1152]{1,0:T(8,128)(2,1)}, bf16[48,1152]{1,0:T(8,128)(2,1)S(1)}, u32[]{:S(2)}, u32[]{:S(2)}) collective-permute-start(bf16[48,1152]{1,0:T(8,128)(2,1)} %copy-done.89), channel_id=1, source_target_pairs={{0,4},{1,5},{2,6},{3,7},{4,0},{5,1},{6,2},{7,3},{8,12},{9,13},{10,... | collective-permute-start | bytes 331784 | tf_op jit(solution)/shard_map/ppermute | solution.py:667
  268.8 14.5 %collective-permute-start.38 = (bf16[48,1152]{1,0:T(8,128)(2,1)}, bf16[48,1152]{1,0:T(8,128)(2,1)S(1)}, u32[]{:S(2)}, u32[]{:S(2)}) collective-permute-start(bf16[48,1152]{1,0:T(8,128)(2,1)} %copy-done.88), channel_id=1, source_target_pairs={{0,8},{1,9},{2,10},{3,11},{4,12},{5,13},{6,14},{7,15},{8,0},{9,1},... | collective-permute-start | bytes 331784 | tf_op jit(solution)/shard_map/ppermute | solution.py:667
  272.6 11.3 %collective-permute-start.39 = (bf16[48,1152]{1,0:T(8,128)(2,1)}, bf16[48,1152]{1,0:T(8,128)(2,1)S(1)}, u32[]{:S(2)}, u32[]{:S(2)}) collective-permute-start(bf16[48,1152]{1,0:T(8,128)(2,1)} %copy-done.87), channel_id=1, source_target_pairs={{0,12},{1,13},{2,14},{3,15},{4,8},{5,9},{6,10},{7,11},{8,4},{9,5},... | collective-permute-start | bytes 331784 | tf_op jit(solution)/shard_map/ppermute | solution.py:667
  (142 other events, 1158.8 us)
Sparse Core Ops, SparseCore 0:
  11.2 75.5 all-gather.1
  141.5 75.5 reduce-scatter.1

commit v2 on v0

--- a/solution.py
+++ b/solution.py
@@ -1,14 +1,19 @@
+import functools
 import math
 
 import jax
 import jax.numpy as jnp
 from jax import lax
+from jax.experimental import pallas as pl
+from jax.experimental.pallas import tpu as pltpu
 from jax.sharding import PartitionSpec as P
 
 D = 768
 HEADS = 12
 HEAD_DIM = 64
 FF = 3072
+BF = jnp.bfloat16
+F32 = jnp.float32
 
 
 momentum_decay = 0.9
@@ -331,6 +336,653 @@
     )
 
 
+class Operand:
+    def __init__(self, ref):
+        self.ref = ref
+
+    def __getitem__(self, index):
+        return self.ref[index]
+
+
+def call(kernel, outs, args, scratch=(), name=None, limit=8):
+    def body(co_ref, *refs):
+        operands = [Operand(ref) for ref in refs[: len(args) - 1]]
+        kernel(co_ref, *operands, *refs[len(args) - 1 :])
+
+    return pl.pallas_call(
+        body,
+        out_shape=[jax.ShapeDtypeStruct(shape, dtype) for shape, dtype in outs],
+        in_specs=[pl.BlockSpec(memory_space=pltpu.SMEM)]
+        + [pl.BlockSpec(memory_space=pltpu.VMEM)] * (len(args) - 1),
+        out_specs=[pl.BlockSpec(memory_space=pltpu.VMEM)] * len(outs),
+        scratch_shapes=list(scratch),
+        compiler_params=pltpu.CompilerParams(vmem_limit_bytes=limit * 2**20),
+        cost_estimate=pl.CostEstimate(flops=2**20, bytes_accessed=2**20, transcendentals=0),
+        name=name,
+    )(*args)
+
+
+def assemble_kernel(ranges, co, *refs):
+    count = len(refs) - len(ranges)
+    for number in range(count):
+        a, i = (number // 4, number % 2) if count == 8 else (number // 2, number % 2)
+        b = (number // 2) % 2 if count == 8 else 0
+        for k in range(4):
+            row = lax.bitwise_xor(co[1], k) * 192
+            row = row + lax.bitwise_xor(co[2], i) * 96 + lax.bitwise_xor(co[3], a) * 48
+            rows = pl.ds(pl.multiple_of(row, 16), 48)
+            for (start, size), out in zip(ranges, refs[count:]):
+                out[rows, b * size : b * size + size] = refs[number][
+                    k * 48 : k * 48 + 48, start : start + size
+                ]
+
+
+def assemble(co, pieces, *ranges):
+    widths = [size * (2 if len(pieces) == 8 else 1) for start, size in ranges]
+    return call(
+        functools.partial(assemble_kernel, ranges),
+        [((D, width), BF) for width in widths],
+        [co, *pieces],
+        name="assemble",
+    )
+
+
+def lanes(offset, size):
+    return pl.ds(pl.multiple_of(offset, 128), size)
+
+
+def nn(left, right):
+    return lax.dot_general(left, right, (((1,), (0,)), ((), ())), preferred_element_type=jnp.float32)
+
+
+def nt(left, right):
+    return lax.dot_general(left, right, (((1,), (1,)), ((), ())), preferred_element_type=jnp.float32)
+
+
+def whole(weight, start, size):
+    return weight[:, start : start + size]
+
+
+def row_norm(values):
+    mean = jnp.mean(values, axis=-1, keepdims=True)
+    centred = values - mean
+    var = jnp.mean(centred * centred, axis=-1, keepdims=True)
+    rstd = lax.rsqrt(var + norm_eps)
+    return centred * rstd, rstd
+
+
+def prep_kernel(co, attn, mlp, s0, s1, s2, s3, s4):
+    r = co[0]
+    for part in range(3):
+        cols = lanes(part * D + 384 * r, 384)
+        s0[:, part * 384 : part * 384 + 384] = attn[:, cols].astype(BF)
+    s1[:, :384] = attn[:, lanes(3 * D + 384 * r, 384)].astype(BF)
+    s1[:, 384:] = mlp[:, lanes(1536 * r, 768)].astype(BF)
+    for b, out in ((0, s3), (1, s4)):
+        half = lax.bitwise_xor(r, b)
+        s2[:, b * 768 : b * 768 + 768] = mlp[:, lanes(1536 * half + 768, 768)].astype(BF)
+        out[...] = mlp[:, lanes(FF + 1536 * half, 1536)].astype(BF)
+
+
+def first_norm_kernel(co, tokens, info, vec, h1, h1t, cols):
+    turned = jnp.transpose(info[...])
+    cols[:, 0:8] = turned
+    x0 = jnp.where(turned[:, 2:3] == 1.0, vec[8:9, :], tokens[...].astype(F32))
+    xh, rstd = row_norm(x0)
+    h = xh * vec[0:1, :] + vec[2:3, :]
+    h1[...] = h.astype(BF)
+    h1t[...] = h.T.astype(BF)
+
+
+def allowed_pairs(info, cols):
+    return (cols[:, 0:1] == info[0:1, :]) & (cols[:, 1:2] == 1.0)
+
+
+def attention_kernel(co, h1, vec, info, cols, weight, qkv, att, lse):
+    for b in range(2):
+        half = lax.bitwise_xor(co[0], b)
+        for part in range(3):
+            out = nn(h1[...], whole(weight, b * 1152 + part * 384, 384))
+            if part != 1:
+                row = 3 if part == 0 else 4
+                out = out + vec.ref[row : row + 1, lanes(384 * half, 384)]
+            qkv[:, b * 1152 + part * 384 : b * 1152 + part * 384 + 384] = out.astype(BF)
+    allowed = allowed_pairs(info, cols)
+    low = lax.broadcasted_iota(jnp.int32, (256, 128), 1) < 64
+    for pair in range(6):
+        base = (pair // 3) * 1152 + (pair % 3) * 128
+        q2 = qkv[:, base : base + 128]
+        k2 = qkv[:, base + 384 : base + 512]
+        v2 = qkv[:, base + 768 : base + 896]
+        mixed = []
+        for side in range(2):
+            qm = jnp.where(low if side == 0 else ~low, q2, jnp.zeros_like(q2))
+            s = jnp.where(allowed, nt(k2, qm) * 0.125, mask_fill)
+            peak = jnp.max(s, axis=0, keepdims=True)
+            e = jnp.exp(s - peak)
+            total = jnp.sum(e, axis=0, keepdims=True)
+            prob = (e * (1.0 / total)).astype(BF)
+            lse[2 * pair + side : 2 * pair + side + 1, :] = peak + jnp.log(total)
+            mixed.append(over_tokens(prob, v2))
+        att[:, pair * 128 : pair * 128 + 128] = jnp.where(low, mixed[0], mixed[1]).astype(BF)
+
+
+def second_norm_kernel(co, tokens, cols, vec, att, weight, y1, h2, h2t):
+    x0 = jnp.where(cols[:, 2:3] == 1.0, vec[8:9, :], tokens[...].astype(F32))
+    y = x0 + nt(att[...], whole(weight, 0, D)) + vec[5:6, :]
+    y1[...] = y
+    xh, rstd = row_norm(y)
+    h = xh * vec[1:2, :] + vec[6:7, :]
+    h2[...] = h.astype(BF)
+    h2t[...] = h.T.astype(BF)
+
+
+def hidden_kernel(co, h2, vec, dz, w0, w1, g0, g1, slope0, slope1, send, keep, dzt, scratch):
+    dzt[...] = dz[...].astype(F32).T.astype(BF)
+    for part, weight, g, slope in ((0, w0, g0, slope0), (1, w1, g1, slope1)):
+        for b in range(2):
+            half = lax.bitwise_xor(co[0], b)
+            for sub in range(0, D, 384):
+                at = slice(b * D + sub, b * D + sub + 384)
+                u = nn(h2[...], weight[:, at])
+                u = u + vec[pl.ds(9 + 2 * half + part, 1), sub : sub + 384]
+                phi = 0.5 * (1.0 + lax.erf(u * math.sqrt(0.5)))
+                act = (u * phi).astype(BF)
+                g[:, at] = act
+                slope[:, at] = phi + u * (
+                    jnp.exp(-0.5 * u * u) * (1.0 / math.sqrt(2.0 * math.pi))
+                )
+                scratch[...] = nn(dzt[...], act)
+                dst = lanes(half * D + sub, 384) if part == 0 else lanes((2 + b) * D + sub, 384)
+                share_rows(co[3], scratch, send, keep, dst)
+
+
+def hidden_grad_kernel(
+    co, dz, slope0, slope1, w0, w1, left, du0, du1, db1, send, keep, scratch
+):
+    for part, slope, du in ((0, slope0, du0), (1, slope1, du1)):
+        for b, weight in ((0, w0), (1, w1)):
+            half = lax.bitwise_xor(co[0], b)
+            for sub in range(0, D, 384):
+                at = slice(b * D + sub, b * D + sub + 384)
+                da = nn(dz[...], weight[:, part * D + sub : part * D + sub + 384])
+                d = (da * slope[:, at]).astype(BF)
+                du[:, at] = d
+                db1[pl.ds(2 * half + part, 1), sub : sub + 384] = jnp.sum(
+                    d.astype(F32), axis=0, keepdims=True
+                )
+                scratch[...] = nn(left[...], d)
+                dst = lanes(half * D + sub, 384) if part == 0 else lanes((2 + b) * D + sub, 384)
+                share_rows(co[3], scratch, send, keep, dst)
+
+
+def output_kernel(co, y1, vec, g0, g1, w0, w1, act):
+    acc = y1[...] + vec[7:8, :]
+    for part, g in ((0, g0), (1, g1)):
+        for b, weight in ((0, w0), (1, w1)):
+            w = weight[:, part * D : part * D + D]
+            acc = acc + nt(g[:, b * D : b * D + D], w)
+    act[...] = acc.astype(BF)
+
+
+def share_rows(c, scratch, send, keep, dst):
+    for k in range(4):
+        for i in range(2):
+            row = k * 192 + i * 96
+            theirs = scratch[pl.ds(pl.multiple_of(row + 48 * (1 - c), 16), 48), :]
+            mine = scratch[pl.ds(pl.multiple_of(row + 48 * c, 16), 48), :]
+            send[k, i, :, dst] = theirs.astype(BF)
+            keep[k, i, :, dst] = mine
+
+
+def attention_grad_kernel(co, h1t, dqkv, dpt, att, send, keep, scratch):
+    moves = [(h1t, dqkv, b * 1152 + 384 + n * 384, b * D + n * 384) for b in (0, 1) for n in (0, 1)]
+    for b in range(2):
+        place = 384 * lax.bitwise_xor(co[0], b)
+        moves.append((h1t, dqkv, b * 1152, 2 * D + place))
+        moves.append((dpt, att, b * 384, 3 * D + place))
+    for left, right, src, dst in moves:
+        scratch[...] = nn(left[...], right[:, src : src + 384])
+        share_rows(co[3], scratch, send, keep, lanes(dst, 384))
+
+
+def second_back_kernel(co, dz, y1, vec, du0, du1, w0, w1, weight_o, dy1, datt, dpt, small):
+    yh, rstd = row_norm(y1[...])
+    dy = dz[...].astype(F32)
+    dh = nt(du0[...], whole(w0, 0, 2 * D)) + nt(du1[...], whole(w1, 0, 2 * D))
+    small[0:1, :] = jnp.sum(dh * yh, axis=0, keepdims=True)
+    small[1:2, :] = jnp.sum(dh, axis=0, keepdims=True)
+    small[3:4, :] = jnp.sum(dy, axis=0, keepdims=True)
+    e = dh * vec[1:2, :]
+    d = dy + rstd * (
+        e - jnp.mean(e, axis=-1, keepdims=True) - yh * jnp.mean(e * yh, axis=-1, keepdims=True)
+    )
+    dy1[...] = d
+    small[2:3, :] = jnp.sum(d, axis=0, keepdims=True)
+    dpt[...] = d.T.astype(BF)
+    datt[...] = nn(d.astype(BF), whole(weight_o, 0, D)).astype(BF)
+
+
+def attention_back_kernel(co, info, cols, lse, qkv, datt, dqkv, small):
+    allowed = allowed_pairs(info, cols)
+    low = lax.broadcasted_iota(jnp.int32, (256, 128), 1) < 64
+    for pair in range(6):
+        half = lax.bitwise_xor(co[0], pair // 3)
+        base = (pair // 3) * 1152 + (pair % 3) * 128
+        q2 = qkv[:, base : base + 128]
+        k2 = qkv[:, base + 384 : base + 512]
+        v2 = qkv[:, base + 768 : base + 896]
+        o2 = datt[:, pair * 128 : pair * 128 + 128]
+        dqs, dks, dvs = [], [], []
+        for side in range(2):
+            mine = low if side == 0 else ~low
+            qm = jnp.where(mine, q2, jnp.zeros_like(q2))
+            om = jnp.where(mine, o2, jnp.zeros_like(o2))
+            s = jnp.where(allowed, nt(k2, qm) * 0.125, mask_fill)
+            prob = jnp.exp(s - lse[2 * pair + side : 2 * pair + side + 1, :])
+            dprob = nt(v2, om)
+            delta = jnp.sum(dprob * prob, axis=0, keepdims=True)
+            ds = (prob * (dprob - delta)).astype(BF)
+            dqs.append(over_tokens(ds, k2))
+            dks.append(nn(ds, q2))
+            dvs.append(nn(prob.astype(BF), o2))
+        dq = (jnp.where(low, dqs[0], dqs[1]) * 0.125).astype(BF)
+        dk = (jnp.where(low, dks[0], dks[1]) * 0.125).astype(BF)
+        dv = jnp.where(low, dvs[0], dvs[1]).astype(BF)
+        dqkv[:, base : base + 128] = dq
+        dqkv[:, base + 384 : base + 512] = dk
+        dqkv[:, base + 768 : base + 896] = dv
+        place = lanes(384 * half + (pair % 3) * 128, 128)
+        small[0:1, place] = jnp.sum(dq.astype(F32), axis=0, keepdims=True)
+        small[1:2, place] = jnp.sum(dv.astype(F32), axis=0, keepdims=True)
+
+
+def first_back_kernel(
+    co, dqkv, tokens, cols, vec, dy1, db1, small2, small_a, weight, input_grad, total
+):
+    hidden = cols[:, 2:3] == 1.0
+    x0 = jnp.where(hidden, vec[8:9, :], tokens[...].astype(F32))
+    xh, rstd = row_norm(x0)
+    dh = nt(dqkv[...], whole(weight, 0, 3 * D))
+    e = dh * vec[0:1, :]
+    dx = dy1[...] + rstd * (
+        e - jnp.mean(e, axis=-1, keepdims=True) - xh * jnp.mean(e * xh, axis=-1, keepdims=True)
+    )
+    input_grad[...] = jnp.where(hidden, 0.0, dx).astype(BF)
+    total[0:1, :] = jnp.sum(dh * xh, axis=0, keepdims=True)
+    total[1:2, :] = small2[0:1, :]
+    total[2:3, :] = jnp.sum(dh, axis=0, keepdims=True)
+    total[3:5, :] = small_a[0:2, :]
+    total[5:6, :] = small2[2:3, :]
+    total[6:7, :] = small2[1:2, :]
+    total[7:8, :] = small2[3:4, :]
+    total[8:9, :] = jnp.sum(jnp.where(hidden, dx, 0.0), axis=0, keepdims=True)
+    total[9:13, :] = db1[0:4, :]
+    total[13:16, :] = jnp.zeros((3, D), F32)
+
+
+def both(keep, got, *at):
+    return keep[at] + got[at].astype(F32)
+
+
+def split_first_kernel(co, keep, got, y_send, y_keep, x_send, x_keep):
+    y = co[2]
+    every = slice(None)
+    for k in range(4):
+        for out, i in ((y_send, 1 - y), (y_keep, y)):
+            out[k] = both(keep, got, k, i, every, slice(0, 2 * D)).astype(out.dtype)
+    x_keep[...] = both(keep, got, every, every, every, slice(2 * D, 3 * D))
+    x_send[...] = both(keep, got, every, every, every, slice(3 * D, 4 * D)).astype(BF)
+
+
+def split_second_kernel(co, x_keep, x_got, keep, got, y_send, y_keep, x_send, x_next, rest):
+    y = co[2]
+    every = slice(None)
+    for k in range(4):
+        for out, i in ((y_send, 1 - y), (y_keep, y)):
+            out[k, :, :D] = both(x_keep, x_got, k, i).astype(out.dtype)
+            out[k, :, D:] = both(keep, got, k, i, every, slice(0, D)).astype(out.dtype)
+    rest[...] = both(keep, got, every, every, every, slice(D, 2 * D))
+    x_next[...] = both(keep, got, every, every, every, slice(2 * D, 3 * D))
+    x_send[...] = both(keep, got, every, every, every, slice(3 * D, 4 * D)).astype(BF)
+
+
+def split_third_kernel(co, x_keep, x_got, rest, keep, got, y_send, y_keep, x_send, x_next, last):
+    y = co[2]
+    every = slice(None)
+    for k in range(4):
+        for out, i in ((y_send, 1 - y), (y_keep, y)):
+            out[k, :, :D] = both(x_keep, x_got, k, i).astype(out.dtype)
+            out[k, :, D:] = rest[k, i].astype(out.dtype)
+    x_next[...] = both(keep, got, every, every, every, slice(0, D))
+    x_send[...] = both(keep, got, every, every, every, slice(D, 2 * D)).astype(BF)
+    last[...] = both(keep, got, every, every, every, slice(2 * D, 4 * D))
+
+
+def split_fourth_kernel(co, x_keep, x_got, rest, y_send, y_keep):
+    y = co[2]
+    for k in range(4):
+        for out, i in ((y_send, 1 - y), (y_keep, y)):
+            out[k, :, :D] = both(x_keep, x_got, k, i).astype(out.dtype)
+            out[k, :, D:] = rest[k, i].astype(out.dtype)
+
+
+def split_z_kernel(co, keep, got, z1, z2, z3, z_keep):
+    z = co[1]
+    for k, out in ((1, z1), (2, z2), (3, z3)):
+        out[...] = both(keep, got, lax.bitwise_xor(z, k)).astype(BF)
+    z_keep[...] = both(keep, got, z)
+
+
+def sum_z_kernel(co, keep, g1, g2, g3, out):
+    out[...] = (
+        keep[...] + g1[...].astype(F32) + g2[...].astype(F32) + g3[...].astype(F32)
+    ).astype(BF)
+
+
+def update_kernel(rate, moves, co, *refs):
+    state, grads, new = refs[:3], refs[3:-4], refs[-4:]
+    for numbers, src, size, b, col, stride in moves:
+        grad = grads[numbers[0]][:, src : src + size].astype(F32)
+        if len(numbers) == 2:
+            grad = grad + grads[numbers[1]][:, src : src + size].astype(F32)
+        place = col if b is None else col + stride * lax.bitwise_xor(co[0], b)
+        at = lanes(place, size)
+        w, m, a = (ref.ref[:, at] for ref in state)
+        m_new = momentum_decay * m + grad
+        w_new = w - rate * (grad + momentum_decay * m_new)
+        new[0][:, at] = w_new
+        new[1][:, at] = m_new
+        new[2][:, at] = average_decay * a + (1.0 - average_decay) * w_new
+        new[3][:, at] = w_new.astype(BF)
+
+
+def hold(arrays):
+    return lax.optimization_barrier(arrays)
+
+
+def fast_device(
+    tokens,
+    cotangent,
+    clip_index,
+    key_valid,
+    patch_masked,
+    attn_weight,
+    mlp_weight,
+    gain_vector,
+    offset_vector,
+    attn_moment,
+    mlp_moment,
+    gain_moment,
+    offset_moment,
+    attn_average,
+    mlp_average,
+    gain_average,
+    offset_average,
+):
+    r, f = lax.axis_index("rep"), lax.axis_index("fsdp")
+    co = jnp.stack([r, f // 4, (f // 2) % 2, f % 2]).astype(jnp.int32)
+
+    def swap(array, mask):
+        return lax.ppermute(array, ("rep", "fsdp"), [(i, i ^ mask) for i in range(32)])
+
+    CORE, Y, Z, X = 1, 2, 4, 16
+
+    s0, s1, s2, s3, s4 = call(
+        prep_kernel,
+        [((48, 1152), BF)] * 2 + [((48, 1536), BF)] * 3,
+        [co, attn_weight, mlp_weight],
+        name="prep",
+    )
+    info = jnp.zeros((8, 256), F32).at[0:3].set(
+        jnp.stack([clip_index, key_valid, patch_masked]).astype(F32)
+    )
+    flat = jnp.zeros((16 * D,), F32)
+    flat = lax.dynamic_update_slice(flat, gain_vector.astype(BF).astype(F32), (96 * f,))
+    flat = lax.dynamic_update_slice(flat, offset_vector.astype(BF).astype(F32), (2 * D + 528 * f,))
+    vec = flat.reshape(16, D)
+
+    def along_z(shard):
+        return [swap(shard, Z * k) for k in (1, 2, 3)]
+
+    def rows(shard, others):
+        return jnp.concatenate([shard] + others, axis=0)
+
+    def core_pair(pieces):
+        return pieces + [swap(piece, CORE) for piece in pieces]
+
+    z0 = along_z(s0)
+    vec = vec + swap(vec, CORE)
+    vec = vec + swap(vec, Y)
+    stack0, s1, vec = hold((rows(s0, z0), s1, vec))
+    across0 = swap(stack0, Y)
+    far0 = swap(stack0, X)
+    z1 = along_z(s1)
+    vec = vec + swap(vec, Z)
+    stack1, across0, far0, s2, vec = hold((rows(s1, z1), across0, far0, s2, vec))
+    far_across0 = swap(across0, X)
+    across1 = swap(stack1, Y)
+    z2 = along_z(s2)
+    vec = vec + swap(vec, 2 * Z)
+    pieces0 = core_pair([stack0, across0, far0])
+    stack2, stack1, across1, far_across0, vec, s3 = hold(
+        (rows(s2, z2), stack1, across1, far_across0, vec, s3)
+    )
+    far1 = swap(stack1, X)
+    across2 = swap(stack2, Y)
+    z3 = along_z(s3)
+    pieces0 = pieces0[:3] + [far_across0] + pieces0[3:] + [swap(far_across0, CORE)]
+    pieces1 = core_pair([stack1, across1])
+    h1, h1t, cols = call(
+        first_norm_kernel,
+        [((256, D), BF), ((D, 256), BF), ((256, 128), F32)],
+        [co, tokens, info, vec],
+        name="norm1",
+    )
+    stack3, far1, across1, across2, pieces0, h1, s4 = hold(
+        (rows(s3, z3), far1, across1, across2, pieces0, h1, s4)
+    )
+    far_across1 = swap(across1, X)
+    across3 = swap(stack3, Y)
+    z4 = along_z(s4)
+    pieces1 = [*pieces1[:2], far1, *pieces1[2:], swap(far1, CORE)]
+    pieces2 = core_pair([stack2, across2])
+    (w_qkv,) = assemble(co, pieces0, (0, 1152))
+    qkv, att, lse = call(
+        attention_kernel,
+        [((256, 3 * D), BF), ((256, D), BF), ((16, 256), F32)],
+        [co, h1, vec, info, cols, w_qkv],
+        name="attention",
+    )
+    stack4, far_across1, across3, pieces1, pieces2, att = hold(
+        (rows(s4, z4), far_across1, across3, pieces1, pieces2, att)
+    )
+    across4 = swap(stack4, Y)
+    pieces1 = [*pieces1[:3], far_across1, *pieces1[3:], swap(far_across1, CORE)]
+    pieces3 = core_pair([stack3, across3])
+    (w_up1,) = assemble(co, pieces2, (0, 1536))
+    w_out, w_up0 = assemble(co, pieces1, (0, 384), (384, 768))
+
+    y1, h2, h2t = call(
+        second_norm_kernel,
+        [((256, D), F32), ((256, D), BF), ((D, 256), BF)],
+        [co, tokens, cols, vec, att, w_out],
+        name="norm2",
+    )
+    shares = [((4, 2, 48, 4 * D), BF), ((4, 2, 48, 4 * D), F32)]
+    g0, g1, slope0, slope1, down_send, down_keep = call(
+        hidden_kernel,
+        [((256, 2 * D), BF)] * 2 + [((256, 2 * D), F32)] * 2 + shares,
+        [co, h2, vec, cotangent, w_up0, w_up1],
+        scratch=[pltpu.VMEM((D, 256), BF), pltpu.VMEM((D, 384), F32)],
+        name="hidden",
+    )
+    pieces4 = core_pair([stack4, across4])
+
+    down_got = swap(down_send, CORE)
+    (w_down0,) = assemble(co, pieces3, (0, 1536))
+    (w_down1,) = assemble(co, pieces4, (0, 1536))
+    du0, du1, db1, up_send, up_keep = call(
+        hidden_grad_kernel,
+        [((256, 2 * D), BF), ((256, 2 * D), BF), ((8, D), F32)] + shares,
+        [co, cotangent, slope0, slope1, w_down0, w_down1, h2t],
+        scratch=[pltpu.VMEM((D, 384), F32)],
+        name="hidden_grad",
+    )
+    down_got, up_send = hold((down_got, up_send))
+    y_shares = [((4, 48, 2 * D), BF), ((4, 48, 2 * D), F32)]
+    x_shares = [((4, 2, 48, D), BF), ((4, 2, 48, D), F32)]
+    y_send0, y_keep0, x_send1, x_keep1 = call(
+        split_first_kernel, y_shares + x_shares, [co, down_keep, down_got], name="split_first"
+    )
+    y_send0, x_send1, up_send, du0 = hold((y_send0, x_send1, up_send, du0))
+    y_got0 = swap(y_send0, Y)
+    x_got1 = swap(x_send1, X)
+    up_got = swap(up_send, CORE)
+    dy1, datt, dpt, small2 = call(
+        second_back_kernel,
+        [((256, D), F32), ((256, D), BF), ((D, 256), BF), ((8, D), F32)],
+        [co, cotangent, y1, vec, du0, du1, w_up0, w_up1, w_out],
+        name="norm2_back",
+    )
+    dqkv, small_a = call(
+        attention_back_kernel,
+        [((256, 3 * D), BF), ((8, D), F32)],
+        [co, info, cols, lse, qkv, datt],
+        name="attention_back",
+    )
+    attn_send, attn_keep = call(
+        attention_grad_kernel,
+        shares,
+        [co, h1t, dqkv, dpt, att],
+        scratch=[pltpu.VMEM((D, 384), F32)],
+        name="attention_grad",
+    )
+
+    def split_z(keep, got):
+        width = keep.shape[2]
+        *sends, z_keep = call(
+            split_z_kernel,
+            [((48, width), BF)] * 3 + [((48, width), F32)],
+            [co, keep, got],
+            name="split_z",
+        )
+        return sends, z_keep
+
+    def swap_z(sends):
+        return [swap(send, Z * k) for send, k in zip(sends, (1, 2, 3))]
+
+    def sum_z(z_keep, z_got):
+        return call(sum_z_kernel, [(z_keep.shape, BF)], [co, z_keep, *z_got], name="sum_z")[0]
+
+    y_got0, x_got1, up_got, attn_send = hold((y_got0, x_got1, up_got, attn_send))
+    z_send0, z_keep0 = split_z(y_keep0, y_got0)
+    y_send1, y_keep1, x_send2, x_keep2, rest2 = call(
+        split_second_kernel,
+        y_shares + x_shares + x_shares[1:],
+        [co, x_keep1, x_got1, up_keep, up_got],
+        name="split_second",
+    )
+    z_send0, y_send1, x_send2, attn_send, dqkv = hold((z_send0, y_send1, x_send2, attn_send, dqkv))
+    x_got2 = swap(x_send2, X)
+    y_got1 = swap(y_send1, Y)
+    z_got0 = swap_z(z_send0)
+    attn_got = swap(attn_send, CORE)
+    input_grad, total = call(
+        first_back_kernel,
+        [((256, D), BF), ((16, D), F32)],
+        [co, dqkv, tokens, cols, vec, dy1, db1, small2, small_a, w_qkv],
+        name="norm1_back",
+    )
+    z_got0, y_got1, x_got2, attn_got, total = hold((z_got0, y_got1, x_got2, attn_got, total))
+    z_send1, z_keep1 = split_z(y_keep1, y_got1)
+    y_send2, y_keep2, x_send3, x_keep3, rest3 = call(
+        split_third_kernel,
+        y_shares + x_shares + [((4, 2, 48, 2 * D), F32)],
+        [co, x_keep2, x_got2, rest2, attn_keep, attn_got],
+        name="split_third",
+    )
+    mine0 = sum_z(z_keep0, z_got0)
+    z_send1, y_send2, x_send3, mine0, total, y1 = hold(
+        (z_send1, y_send2, x_send3, mine0, total, y1)
+    )
+    x_got3 = swap(x_send3, X)
+    y_got2 = swap(y_send2, Y)
+    z_got1 = swap_z(z_send1)
+    got0 = swap(mine0, X)
+    total = total + swap(total, CORE)
+    total = total + swap(total, Y)
+    (activations,) = call(
+        output_kernel, [((256, D), BF)], [co, y1, vec, g0, g1, w_down0, w_down1], name="output"
+    )
+    z_got1, y_got2, x_got3, got0, total, activations = hold(
+        (z_got1, y_got2, x_got3, got0, total, activations)
+    )
+    z_send2, z_keep2 = split_z(y_keep2, y_got2)
+    y_send3, y_keep3 = call(
+        split_fourth_kernel,
+        [((4, 48, 3 * D), BF), ((4, 48, 3 * D), F32)],
+        [co, x_keep3, x_got3, rest3],
+        name="split_fourth",
+    )
+    mine1 = sum_z(z_keep1, z_got1)
+    z_send2, y_send3, mine1, total = hold((z_send2, y_send3, mine1, total))
+    y_got3 = swap(y_send3, Y)
+    z_got2 = swap_z(z_send2)
+    got1 = swap(mine1, X)
+    total = total + swap(total, X)
+    z_got2, y_got3, got1, total = hold((z_got2, y_got3, got1, total))
+    z_send3, z_keep3 = split_z(y_keep3, y_got3)
+    mine2 = sum_z(z_keep2, z_got2)
+    z_send3, mine2, total = hold((z_send3, mine2, total))
+    z_got3 = swap_z(z_send3)
+    got2 = swap(mine2, X)
+    total = total + swap(total, Z)
+    z_got3, got2, total = hold((z_got3, got2, total))
+    mine3 = sum_z(z_keep3, z_got3)
+    got3 = swap(mine3, X)
+    total = total + swap(total, 2 * Z)
+    flat = total.reshape(-1)
+    gain_g = lax.dynamic_slice(flat, (96 * f,), (96,))
+    offset_g = lax.dynamic_slice(flat, (2 * D + 528 * f,), (528,))
+
+    rate = base_rate / math.sqrt(tokens.shape[0] * 32)
+
+    def update(moves, state, grads, width, name):
+        return call(
+            functools.partial(update_kernel, rate, moves),
+            [((48, width), F32)] * 3 + [((48, width), BF)],
+            [co, *state, *grads],
+            name=name,
+        )
+
+    mlp_moves = [((0, 1), h * D, D, None, FF + h * 2 * D, 0) for h in range(2)]
+    mlp_moves += [((2 + b,), 0, D, b, FF + D, 2 * D) for b in range(2)]
+    mlp_moves += [((2, 3), D, D, None, 0, 0), ((4, 5), D, D, None, 2 * D, 0)]
+    mlp_moves += [((4 + b,), 0, D, b, D, 2 * D) for b in range(2)]
+    mlp = update(
+        mlp_moves,
+        [mlp_weight, mlp_moment, mlp_average],
+        [mine0, got0, mine1, got1, mine2, got2],
+        2 * FF,
+        "update_mlp",
+    )
+    attn_moves = [((0, 1), D, D, None, 0, 0)]
+    attn_moves += [((b,), 0, 384, b, D, 384) for b in range(2)]
+    attn_moves += [((b,), 384, 384, b, 2 * D, 384) for b in range(2)]
+    attn_moves += [((0, 1), 2 * D, D, None, 3 * D, 0)]
+    attn = update(
+        attn_moves,
+        [attn_weight, attn_moment, attn_average],
+        [mine3, got3],
+        4 * D,
+        "update_attn",
+    )
+    gains = advance(gain_g, gain_vector, gain_moment, gain_average, rate)
+    offsets = advance(offset_g, offset_vector, offset_moment, offset_average, rate)
+    return (activations, input_grad, *attn, *mlp, *gains, *offsets)
+
+
 def solution(mesh):
     placed = (
         P(("rep", "fsdp"), None),
@@ -351,8 +1003,9 @@
         P("fsdp"),
         P("fsdp"),
     )
+    small = mesh.shape["rep"] == 2 and mesh.shape["fsdp"] == 16
     return jax.shard_map(
-        per_device,
+        fast_device if small else per_device,
         mesh=mesh,
         in_specs=placed,
         out_specs=(

time: 555 us -> 250 us (0.45)
  blocking collectives: 153 us -> 0 us
  waiting for transfers between devices: 252 us -> 120 us
  starting transfers between devices: 0.47 us -> 69.3 us
  matrix products: 55.7 us -> 0 us
  Pallas kernels: 0 us -> 53.5 us
  other arithmetic: 49.7 us -> 2.92 us
  local copies, waits for them, and re-layouts: 22.4 us -> 2.47 us
  between operations: 20.1 us -> 1.38 us
    reduce_scatter x4 -> x0, waiting for transfers between devices: 196 us -> none  [the longest x1 96.8 us: per_device(): lax.psum_scatter(gradients[0], 'fsdp', scatter_dimension=0, tiled=True)]
    unnamed x4 -> x0, blocking collectives: 138 us -> none
    ppermute x0 -> x73, waiting for transfers between devices: none -> 120 us  [swap(): lax.ppermute(array, ('rep', 'fsdp'), [(i, i ^ mask) for i in range(32)])]
    ppermute x0 -> x73, starting transfers between devices: none -> 69.3 us  [swap(): lax.ppermute(array, ('rep', 'fsdp'), [(i, i ^ mask) for i in range(32)])]
    all_gather x2 -> x0, waiting for transfers between devices: 56.2 us -> none  [the longest x1 56.2 us: per_device(): lax.all_gather(mlp_shard, 'fsdp', axis=0, tiled=True)]
    dot_general x18 -> x0, matrix products: 55.7 us -> none  [the longest x4 17.5 us: over_tokens(): lax.dot_general(left_mat, right_mat, (((0,), (0,)), ((), ())), preferred_...]
    pallas_call x0 -> x30, Pallas kernels: none -> 53.5 us  [call(): pl.pallas_call(body, out_shape=[jax.ShapeDtypeStruct(shape, dtype) for sh...]
    concatenate x4 -> x5, other arithmetic: 22.7 us -> 0.2 us  [rows(): return jnp.concatenate([shard] + others, axis=0)]
  transfers between devices with their start and end apart: 6 -> 73, of which waited for: 4 -> 31; matrix products, arithmetic and copies ran while one was open for 13% -> 1% of each run, Pallas kernels for 0% -> 14%
where the time goes in v2:
time: 250 us; the launch traced here: 249 us
  waiting for transfers between devices  120 us (48%)
  starting transfers between devices  69.3 us (28%)
  Pallas kernels  53.5 us (21%)
  other arithmetic  2.92 us (1%)
    ppermute x73, waiting for transfers between devices, swap(): lax.ppermute(array, ('rep', 'fsdp'), [(i, i ^ mask) for i in range(32)])  120 us
    ppermute x73, starting transfers between devices, swap(): lax.ppermute(array, ('rep', 'fsdp'), [(i, i ^ mask) for i in range(32)])  69.3 us
    pallas_call x30, Pallas kernels, call(): pl.pallas_call(body, out_shape=[jax.ShapeDtypeStruct(shape, dtype) for sh...  53.5 us
  transfers between devices with their start and end apart: 73, of which 31 were waited for; matrix products, arithmetic and copies ran while one was open for 1% of the time, Pallas kernels for 14%

profile of v2, /device:TPU:0, one launch (start us, length us, event | category | flops | bytes accessed | tf_op | source)
XLA Modules:
  0.0 249.4 jit_solution(12546550104218552932)
XLA Ops:
  3.8 5.1 %collective-permute-start.2 = (bf16[48,1152]{1,0:T(8,128)(2,1)S(1)}, bf16[48,1152]{1,0:T(8,128)(2,1)S(1)}, u32[]{:S(2)}, u32[]{:S(2)}) collective-permute-start(bf16[48,1152]{1,0:T(8,128)(2,1)S(1)} %get-tuple-element.211), channel_id=1, source_target_pairs={{0,12},{1,13},{2,14},{3,15},{4,8},{5,9},{6,10},{7,11},{8,4},{9,5},... | collective-permute-start | bytes 331784 | tf_op jit(solution)/shard_map/ppermute | solution.py:727
  11.0 1.7 collective-permute-start.4
  12.8 2.4 collective-permute-done.4
  15.2 3.0 %collective-permute-done.1 = bf16[48,1152]{1,0:T(8,128)(2,1)S(1)} collective-permute-done((bf16[48,1152]{1,0:T(8,128)(2,1)S(1)}, bf16[48,1152]{1,0:T(8,128)(2,1)S(1)}, u32[]{:S(2)}, u32[]{:S(2)}) %collective-permute-start.1) | collective-permute-done | bytes 110624 | tf_op jit(solution)/shard_map/ppermute | solution.py:727
  18.3 1.6 collective-permute-start.9
  21.6 2.2 collective-permute-start.7
  24.8 1.7 collective-permute-done.10
  26.5 2.9 %collective-permute-done.7 = bf16[48,1152]{1,0:T(8,128)(2,1)S(1)} collective-permute-done((bf16[48,1152]{1,0:T(8,128)(2,1)S(1)}, bf16[48,1152]{1,0:T(8,128)(2,1)S(1)}, u32[]{:S(2)}, u32[]{:S(2)}) %collective-permute-start.7) | collective-permute-done | bytes 110624 | tf_op jit(solution)/shard_map/ppermute | solution.py:727
  29.4 3.8 %collective-permute-done.6 = bf16[48,1152]{1,0:T(8,128)(2,1)S(1)} collective-permute-done((bf16[48,1152]{1,0:T(8,128)(2,1)S(1)}, bf16[48,1152]{1,0:T(8,128)(2,1)S(1)}, u32[]{:S(2)}, u32[]{:S(2)}) %collective-permute-start.6) | collective-permute-done | bytes 110624 | tf_op jit(solution)/shard_map/ppermute | solution.py:727
  33.3 2.5 %collective-permute-start.13 = (bf16[48,1536]{1,0:T(8,128)(2,1)S(1)}, bf16[48,1536]{1,0:T(8,128)(2,1)S(1)}, u32[]{:S(2)}, u32[]{:S(2)}) collective-permute-start(bf16[48,1536]{1,0:T(8,128)(2,1)S(1)} %get-tuple-element.217), channel_id=1, source_target_pairs={{0,12},{1,13},{2,14},{3,15},{4,8},{5,9},{6,10},{7,11},{8,4},{9,5},... | collective-permute-start | bytes 442376 | tf_op jit(solution)/shard_map/ppermute | solution.py:727
  35.8 2.9 %collective-permute-start.16 = (f32[16,768]{1,0:T(8,128)S(1)}, f32[16,768]{1,0:T(8,128)S(1)}, u32[]{:S(2)}, u32[]{:S(2)}) collective-permute-start(f32[16,768]{1,0:T(8,128)S(1)} %add.79), channel_id=1, source_target_pairs={{0,8},{1,9},{2,10},{3,11},{4,12},{5,13},{6,14},{7,15},{8,0},{9,1},... | collective-permute-start | bytes 147464 | tf_op jit(solution)/shard_map/ppermute | solution.py:727
  39.8 9.4 %collective-permute-done.16 = f32[16,768]{1,0:T(8,128)S(1)} collective-permute-done((f32[16,768]{1,0:T(8,128)S(1)}, f32[16,768]{1,0:T(8,128)S(1)}, u32[]{:S(2)}, u32[]{:S(2)}) %collective-permute-start.16) | collective-permute-done | bytes 49184 | tf_op jit(solution)/shard_map/ppermute | solution.py:727
  49.7 4.6 %collective-permute-done.11 = bf16[48,1536]{1,0:T(8,128)(2,1)S(1)} collective-permute-done((bf16[48,1536]{1,0:T(8,128)(2,1)S(1)}, bf16[48,1536]{1,0:T(8,128)(2,1)S(1)}, u32[]{:S(2)}, u32[]{:S(2)}) %collective-permute-start.11) | collective-permute-done | bytes 147488 | tf_op jit(solution)/shard_map/ppermute | solution.py:727
  54.4 2.1 collective-permute-start.19
  57.0 2.4 collective-permute-start.17
  59.3 3.7 %collective-permute-done.19 = bf16[48,1536]{1,0:T(8,128)(2,1)S(1)} collective-permute-done((bf16[48,1536]{1,0:T(8,128)(2,1)S(1)}, bf16[48,1536]{1,0:T(8,128)(2,1)S(1)}, u32[]{:S(2)}, u32[]{:S(2)}) %collective-permute-start.19) | collective-permute-done | bytes 147488 | tf_op jit(solution)/shard_map/ppermute | solution.py:727
  63.6 6.0 %collective-permute-done.18 = bf16[48,1536]{1,0:T(8,128)(2,1)S(1)} collective-permute-done((bf16[48,1536]{1,0:T(8,128)(2,1)S(1)}, bf16[48,1536]{1,0:T(8,128)(2,1)S(1)}, u32[]{:S(2)}, u32[]{:S(2)}) %collective-permute-start.18) | collective-permute-done | bytes 147488 | tf_op jit(solution)/shard_map/ppermute | solution.py:727
  71.4 2.9 %collective-permute-done.20.refs_2_ = bf16[192,1152]{1,0:T(8,128)(2,1)S(1)} collective-permute-done((bf16[192,1152]{1,0:T(8,128)(2,1)S(1)}, bf16[192,1152]{1,0:T(8,128)(2,1)S(1)}, u32[]{:S(2)}, u32[]{:S(2)}) %collective-permute-start.20) | collective-permute-done | bytes 442400 | tf_op jit(solution)/shard_map/ppermute | solution.py:727
  74.3 2.0 collective-permute-start.28
  76.4 3.8 %collective-permute-start.27 = (bf16[48,1536]{1,0:T(8,128)(2,1)S(1)}, bf16[48,1536]{1,0:T(8,128)(2,1)S(1)}, u32[]{:S(2)}, u32[]{:S(2)}) collective-permute-start(bf16[48,1536]{1,0:T(8,128)(2,1)S(1)} %get-tuple-element.232), channel_id=1, source_target_pairs={{0,8},{1,9},{2,10},{3,11},{4,12},{5,13},{6,14},{7,15},{8,0},{9,1},... | collective-permute-start | bytes 442376 | tf_op jit(solution)/shard_map/ppermute | solution.py:727
  81.9 8.2 %collective-permute-done.27 = bf16[48,1536]{1,0:T(8,128)(2,1)S(1)} collective-permute-done((bf16[48,1536]{1,0:T(8,128)(2,1)S(1)}, bf16[48,1536]{1,0:T(8,128)(2,1)S(1)}, u32[]{:S(2)}, u32[]{:S(2)}) %collective-permute-start.27) | collective-permute-done | bytes 147488 | tf_op jit(solution)/shard_map/ppermute | solution.py:727
  91.5 3.5 %attention.1 = (bf16[256,2304]{1,0:T(8,128)(2,1)S(1)}, bf16[256,768]{1,0:T(8,128)(2,1)S(1)}, f32[16,256]{1,0:T(8,128)S(1)}) custom-call(s32[4]{0:T(128)S(1)} %pad_add_fusion.co_ref, bf16[256,768]{1,0:T(8,128)(2,1)S(1)} %get-tuple-element.237.refs_0_, f32[16,768]{1,0:T(8,128)S(1)} %add.80.refs_2_.refs_1_.refs_3_, ...), custom_call_target="tpu_custom_call" | custom-call | flops 1048576 | bytes 1048576 | tf_op jit(solution)/shard_map/attention/pallas_call | solution.py:352
  95.1 6.1 %collective-permute-done.29.refs_3_ = bf16[192,1152]{1,0:T(8,128)(2,1)S(1)} collective-permute-done((bf16[192,1152]{1,0:T(8,128)(2,1)S(1)}, bf16[192,1152]{1,0:T(8,128)(2,1)S(1)}, u32[]{:S(2)}, u32[]{:S(2)}) %collective-permute-start.29) | collective-permute-done | bytes 442400 | tf_op jit(solution)/shard_map/ppermute | solution.py:727
  105.3 6.3 %hidden.1 = (bf16[256,1536]{1,0:T(8,128)(2,1)S(1)}, bf16[256,1536]{1,0:T(8,128)(2,1)S(1)}, f32[256,1536]{1,0:T(8,128)S(1)}, f32[256,1536]{1,0:T(8,128)S(1)}, bf1...) custom-call(s32[4]{0:T(128)S(1)} %pad_add_fusion.co_ref, ...), custom_call_target="tpu_custom_call" | custom-call | flops 1048576 | bytes 1048576 | tf_op jit(solution)/shard_map/hidden/pallas_call | solution.py:352
  113.1 14.4 %collective-permute-done.40.refs_1_ = bf16[192,1536]{1,0:T(8,128)(2,1)S(1)} collective-permute-done((bf16[192,1536]{1,0:T(8,128)(2,1)S(1)}, bf16[192,1536]{1,0:T(8,128)(2,1)S(1)}, u32[]{:S(2)}, u32[]{:S(2)}) %collective-permute-start.40) | collective-permute-done | bytes 589856 | tf_op jit(solution)/shard_map/ppermute | solution.py:727
  130.1 5.3 %hidden_grad.1 = (bf16[256,1536]{1,0:T(8,128)(2,1)S(1)}, bf16[256,1536]{1,0:T(8,128)(2,1)S(1)}, f32[8,768]{1,0:T(8,128)S(1)}, bf16[4,2,48,3072]{3,2,1,0:T(8,128)(2,1)S(1)}, f32[4,2,48,3072]{3,2,1,0:T(8,128)S(1)}) custom-call(s32[4]{0:T(128)S(1)} %pad_add_fusion.co_ref, bf16[256,768]{1,0:T(8,128)(2,1)S(1)} %copy-done.2, ...), custom_call_target="tpu_custom_call" | custom-call | flops 1048576 | bytes 1048576 | tf_op jit(solution)/shard_map/hidden_grad/pallas_call | solution.py:352
  137.8 3.3 %norm2_back.1 = (f32[256,768]{1,0:T(8,128)S(1)}, bf16[256,768]{1,0:T(8,128)(2,1)S(1)}, bf16[768,256]{1,0:T(8,128)(2,1)S(1)}, f32[8,768]{1,0:T(8,128)S(1)}) custom-call(s32[4]{0:T(128)S(1)} %pad_add_fusion.co_ref, bf16[256,768]{1,0:T(8,128)(2,1)S(1)} %copy-done.2, f32[256,768]{1,0:T(8,128)S(1)} %get-tuple-element.336.refs_1_.refs_0_, ...), custom_call_target="tpu_custom_call" | custom-call | flops 1048576 | bytes 1048576 | tf_op jit(solution)/shard_map/norm2_back/pallas_call | solution.py:352
  141.0 5.8 %attention_back.1 = (bf16[256,2304]{1,0:T(8,128)(2,1)S(1)}, f32[8,768]{1,0:T(8,128)S(1)}) custom-call(s32[4]{0:T(128)S(1)} %pad_add_fusion.co_ref, f32[8,256]{1,0:T(8,128)S(1)} %scatter.4.refs_1_.refs_2_.refs_0_, f32[256,128]{1,0:T(8,128)S(1)} %get-tuple-element.223.refs_3_.refs_1_.refs_2_, f32[16,256]{1,0:T(8,128)S(1)} %get-tuple-element.280.refs_2_, ...), custom_call_target="tpu_custom_call" | custom-call | flops 1048576 | bytes 1048576 | tf_op jit(solution)/shard_map/attention_back/pallas_call | solution.py:352
  146.8 2.9 %attention_grad.1 = (bf16[4,2,48,3072]{3,2,1,0:T(8,128)(2,1)S(1)}, f32[4,2,48,3072]{3,2,1,0:T(8,128)S(1)}) custom-call(s32[4]{0:T(128)S(1)} %pad_add_fusion.co_ref, bf16[768,256]{1,0:T(8,128)(2,1)S(1)} %get-tuple-element.279.refs_0_, bf16[256,2304]{1,0:T(8,128)(2,1)S(1)} %get-tuple-element.307.refs_1_.refs_0_, ...), custom_call_target="tpu_custom_call" | custom-call | flops 1048576 | bytes 1048576 | tf_op jit(solution)/shard_map/attention_grad/pallas_call | solution.py:352
  149.7 2.5 collective-permute-done.43.refs_1_
  156.3 3.0 %collective-permute-start.47 = (bf16[48,1536]{1,0:T(8,128)(2,1)S(1)}, bf16[48,1536]{1,0:T(8,128)(2,1)S(1)}, u32[]{:S(2)}, u32[]{:S(2)}) collective-permute-start(bf16[48,1536]{1,0:T(8,128)(2,1)S(1)} %get-tuple-element.302), channel_id=1, source_target_pairs={{0,8},{1,9},{2,10},{3,11},{4,12},{5,13},{6,14},{7,15},{8,0},{9,1},... | collective-permute-start | bytes 442376 | tf_op jit(solution)/shard_map/ppermute | solution.py:727
  159.3 5.6 %collective-permute-done.46.refs_1_ = bf16[48,1536]{1,0:T(8,128)(2,1)S(1)} collective-permute-done((bf16[48,1536]{1,0:T(8,128)(2,1)S(1)}, bf16[48,1536]{1,0:T(8,128)(2,1)S(1)}, u32[]{:S(2)}, u32[]{:S(2)}) %collective-permute-start.46) | collective-permute-done | bytes 147488 | tf_op jit(solution)/shard_map/ppermute | solution.py:727
  166.3 2.8 %norm1_back.1 = (bf16[256,768]{1,0:T(8,128)(2,1)}, f32[16,768]{1,0:T(8,128)S(1)}) custom-call(s32[4]{0:T(128)S(1)} %pad_add_fusion.co_ref, bf16[256,2304]{1,0:T(8,128)(2,1)S(1)} %get-tuple-element.307.refs_1_.refs_0_, bf16[256,768]{1,0:T(8,128)(2,1)S(1)} %copy-done.3, f32[256,128]{1,0:T(8,128)S(1)} %get-tuple-element.223.refs_3_.refs_1_.refs_2_, ...), custom_call_target="tpu_custom_call" | custom-call | flops 1048576 | bytes 1048576 | tf_op jit(solution)/shard_map/norm1_back/pallas_call | solution.py:352
  169.1 2.7 %collective-permute-done.48.refs_3_ = bf16[48,1536]{1,0:T(8,128)(2,1)S(1)} collective-permute-done((bf16[48,1536]{1,0:T(8,128)(2,1)S(1)}, bf16[48,1536]{1,0:T(8,128)(2,1)S(1)}, u32[]{:S(2)}, u32[]{:S(2)}) %collective-permute-start.48) | collective-permute-done | bytes 147488 | tf_op jit(solution)/shard_map/ppermute | solution.py:727
  174.8 1.5 collective-permute-start.56
  181.1 8.1 %collective-permute-done.59 = f32[16,768]{1,0:T(8,128)S(1)} collective-permute-done((f32[16,768]{1,0:T(8,128)S(1)}, f32[16,768]{1,0:T(8,128)S(1)}, u32[]{:S(2)}, u32[]{:S(2)}) %collective-permute-start.59) | collective-permute-done | bytes 49184 | tf_op jit(solution)/shard_map/ppermute | solution.py:727
  189.2 2.4 collective-permute-start.54
  192.2 2.7 %output.1 = bf16[256,768]{1,0:T(8,128)(2,1)} custom-call(s32[4]{0:T(128)S(1)} %pad_add_fusion.co_ref, f32[256,768]{1,0:T(8,128)S(1)} %get-tuple-element.336.refs_1_.refs_0_, f32[16,768]{1,0:T(8,128)S(1)} %add.80.refs_2_.refs_1_.refs_3_, bf16[256,1536]{1,0:T(8,128)(2,1)S(1)} %get-tuple-element.337.refs_2_, bf16[256,1536]{1,0:T(8,128)(2,1)S(1)} %get-tuple-element.338.refs_3_, ...), custom_call_target="tpu_custom_call" | custom-call | flops 1048576 | bytes 1048576 | tf_op jit(solution)/shard_map/output/pallas_call | solution.py:352
  202.6 1.9 collective-permute-start.62
  205.9 2.0 collective-permute-done.60.refs_1_
  207.9 4.4 %collective-permute-done.61.refs_2_ = bf16[48,1536]{1,0:T(8,128)(2,1)S(1)} collective-permute-done((bf16[48,1536]{1,0:T(8,128)(2,1)S(1)}, bf16[48,1536]{1,0:T(8,128)(2,1)S(1)}, u32[]{:S(2)}, u32[]{:S(2)}) %collective-permute-start.61) | collective-permute-done | bytes 147488 | tf_op jit(solution)/shard_map/ppermute | solution.py:727
  212.3 5.1 %collective-permute-done.63.refs_1_ = bf16[4,48,2304]{2,1,0:T(8,128)(2,1)S(1)} collective-permute-done((bf16[4,48,2304]{2,1,0:T(8,128)(2,1)S(1)}, bf16[4,48,2304]{2,1,0:T(8,128)(2,1)S(1)}, u32[]{:S(2)}, u32[]{:S(2)}) %collective-permute-start.63) | collective-permute-done | bytes 884768 | tf_op jit(solution)/shard_map/ppermute | solution.py:727
  221.6 1.6 collective-permute-start.68
  224.4 7.7 %collective-permute-done.70 = f32[16,768]{1,0:T(8,128)S(1)} collective-permute-done((f32[16,768]{1,0:T(8,128)S(1)}, f32[16,768]{1,0:T(8,128)S(1)}, u32[]{:S(2)}, u32[]{:S(2)}) %collective-permute-start.70) | collective-permute-done | bytes 49184 | tf_op jit(solution)/shard_map/ppermute | solution.py:727
  232.2 4.2 %collective-permute-done.67.refs_2_ = bf16[48,2304]{1,0:T(8,128)(2,1)S(1)} collective-permute-done((bf16[48,2304]{1,0:T(8,128)(2,1)S(1)}, bf16[48,2304]{1,0:T(8,128)(2,1)S(1)}, u32[]{:S(2)}, u32[]{:S(2)}) %collective-permute-start.67) | collective-permute-done | bytes 221216 | tf_op jit(solution)/shard_map/ppermute | solution.py:727
  236.4 4.1 %collective-permute-start.72 = (f32[16,768]{1,0:T(8,128)S(1)}, f32[16,768]{1,0:T(8,128)S(1)}, u32[]{:S(2)}, u32[]{:S(2)}) collective-permute-start(f32[16,768]{1,0:T(8,128)S(1)} %add.84), channel_id=1, source_target_pairs={{0,8},{1,9},{2,10},{3,11},{4,12},{5,13},{6,14},{7,15},{8,0},{9,1},... | collective-permute-start | bytes 147464 | tf_op jit(solution)/shard_map/ppermute | solution.py:727
  241.4 3.0 %update_mlp.1 = (f32[48,6144]{1,0:T(8,128)}, f32[48,6144]{1,0:T(8,128)}, f32[48,6144]{1,0:T(8,128)}, bf16[48,6144]{1,0:T(8,128)(2,1)}) custom-call(s32[4]{0:T(128)S(1)} %pad_add_fusion.co_ref, f32[48,6144]{1,0:T(8,128)S(1)} %copy-done.1, f32[48,6144]{1,0:T(8,128)S(1)} %copy-done.6, f32[48,6144]{1,0:T(8,128)S(1)} %copy-done.7, ...), custom_call_target="tpu_custom_call" | custom-call | flops 1048576 | bytes 1048576 | tf_op jit(solution)/shard_map/update_mlp/pallas_call | solution.py:352
  247.3 2.1 update_attn.1
  (196 shorter events, 58.0 us)
Async XLA Ops:
  3.8 11.4 %collective-permute-start.2 = (bf16[48,1152]{1,0:T(8,128)(2,1)S(1)}, bf16[48,1152]{1,0:T(8,128)(2,1)S(1)}, u32[]{:S(2)}, u32[]{:S(2)}) collective-permute-start(bf16[48,1152]{1,0:T(8,128)(2,1)S(1)} %get-tuple-element.211), channel_id=1, source_target_pairs={{0,12},{1,13},{2,14},{3,15},{4,8},{5,9},{6,10},{7,11},{8,4},{9,5},... | collective-permute-start | bytes 331784 | tf_op jit(solution)/shard_map/ppermute | solution.py:727
  8.9 9.3 %collective-permute-start.1 = (bf16[48,1152]{1,0:T(8,128)(2,1)S(1)}, bf16[48,1152]{1,0:T(8,128)(2,1)S(1)}, u32[]{:S(2)}, u32[]{:S(2)}) collective-permute-start(bf16[48,1152]{1,0:T(8,128)(2,1)S(1)} %get-tuple-element.211), channel_id=1, source_target_pairs={{0,8},{1,9},{2,10},{3,11},{4,12},{5,13},{6,14},{7,15},{8,0},{9,1},... | collective-permute-start | bytes 331784 | tf_op jit(solution)/shard_map/ppermute | solution.py:727
  8.9 9.3 %collective-permute-start = (bf16[48,1152]{1,0:T(8,128)(2,1)S(1)}, bf16[48,1152]{1,0:T(8,128)(2,1)S(1)}, u32[]{:S(2)}, u32[]{:S(2)}) collective-permute-start(bf16[48,1152]{1,0:T(8,128)(2,1)S(1)} %get-tuple-element.211), channel_id=1, source_target_pairs={{0,4},{1,5},{2,6},{3,7},{4,0},{5,1},{6,2},{7,3},{8,12},{9,13},{10,... | collective-permute-start | bytes 331784 | tf_op jit(solution)/shard_map/ppermute | solution.py:727
  18.3 15.0 %collective-permute-start.9 = (bf16[192,1152]{1,0:T(8,128)(2,1)S(1)}, bf16[192,1152]{1,0:T(8,128)(2,1)S(1)}, u32[]{:S(2)}, u32[]{:S(2)}) collective-permute-start(bf16[192,1152]{1,0:T(8,128)(2,1)S(1)} %pad_maximum_fusion.3.refs_0_), channel_id=1, source_target_pairs={{0,16},{1,17},{2,18},{3,19},{4,20},{5,21},{6,22},{7,23},{8,24},{9,... | collective-permute-start | bytes 1327112 | tf_op jit(solution)/shard_map/ppermute | solution.py:727
  19.8 13.4 %collective-permute-start.8 = (bf16[192,1152]{1,0:T(8,128)(2,1)S(1)}, bf16[192,1152]{1,0:T(8,128)(2,1)S(1)}, u32[]{:S(2)}, u32[]{:S(2)}) collective-permute-start(bf16[192,1152]{1,0:T(8,128)(2,1)S(1)} %pad_maximum_fusion.3.refs_0_), channel_id=1, source_target_pairs={{0,2},{1,3},{2,0},{3,1},{4,6},{5,7},{6,4},{7,5},{8,10},{9,11},{10,... | collective-permute-start | bytes 1327112 | tf_op jit(solution)/shard_map/ppermute | solution.py:727
  23.8 9.4 %collective-permute-start.6 = (bf16[48,1152]{1,0:T(8,128)(2,1)S(1)}, bf16[48,1152]{1,0:T(8,128)(2,1)S(1)}, u32[]{:S(2)}, u32[]{:S(2)}) collective-permute-start(bf16[48,1152]{1,0:T(8,128)(2,1)S(1)} %get-tuple-element.213), channel_id=1, source_target_pairs={{0,8},{1,9},{2,10},{3,11},{4,12},{5,13},{6,14},{7,15},{8,0},{9,1},... | collective-permute-start | bytes 331784 | tf_op jit(solution)/shard_map/ppermute | solution.py:727
  33.3 15.9 %collective-permute-start.13 = (bf16[48,1536]{1,0:T(8,128)(2,1)S(1)}, bf16[48,1536]{1,0:T(8,128)(2,1)S(1)}, u32[]{:S(2)}, u32[]{:S(2)}) collective-permute-start(bf16[48,1536]{1,0:T(8,128)(2,1)S(1)} %get-tuple-element.217), channel_id=1, source_target_pairs={{0,12},{1,13},{2,14},{3,15},{4,8},{5,9},{6,10},{7,11},{8,4},{9,5},... | collective-permute-start | bytes 442376 | tf_op jit(solution)/shard_map/ppermute | solution.py:727
  35.8 13.4 %collective-permute-start.12 = (bf16[48,1536]{1,0:T(8,128)(2,1)S(1)}, bf16[48,1536]{1,0:T(8,128)(2,1)S(1)}, u32[]{:S(2)}, u32[]{:S(2)}) collective-permute-start(bf16[48,1536]{1,0:T(8,128)(2,1)S(1)} %get-tuple-element.217), channel_id=1, source_target_pairs={{0,8},{1,9},{2,10},{3,11},{4,12},{5,13},{6,14},{7,15},{8,0},{9,1},... | collective-permute-start | bytes 442376 | tf_op jit(solution)/shard_map/ppermute | solution.py:727
  35.8 13.3 %collective-permute-start.16 = (f32[16,768]{1,0:T(8,128)S(1)}, f32[16,768]{1,0:T(8,128)S(1)}, u32[]{:S(2)}, u32[]{:S(2)}) collective-permute-start(f32[16,768]{1,0:T(8,128)S(1)} %add.79), channel_id=1, source_target_pairs={{0,8},{1,9},{2,10},{3,11},{4,12},{5,13},{6,14},{7,15},{8,0},{9,1},... | collective-permute-start | bytes 147464 | tf_op jit(solution)/shard_map/ppermute | solution.py:727
  38.7 15.6 %collective-permute-start.14 = (bf16[192,1152]{1,0:T(8,128)(2,1)S(1)}, bf16[192,1152]{1,0:T(8,128)(2,1)S(1)}, u32[]{:S(2)}, u32[]{:S(2)}) collective-permute-start(bf16[192,1152]{1,0:T(8,128)(2,1)S(1)} %pad_maximum_fusion.4.refs_0_), channel_id=1, source_target_pairs={{0,2},{1,3},{2,0},{3,1},{4,6},{5,7},{6,4},{7,5},{8,10},{9,11},{10,... | collective-permute-start | bytes 1327112 | tf_op jit(solution)/shard_map/ppermute | solution.py:727
  39.2 15.1 %collective-permute-start.15 = (bf16[192,1152]{1,0:T(8,128)(2,1)S(1)}, bf16[192,1152]{1,0:T(8,128)(2,1)S(1)}, u32[]{:S(2)}, u32[]{:S(2)}) collective-permute-start(bf16[192,1152]{1,0:T(8,128)(2,1)S(1)} %collective-permute-done.8.refs_1_), channel_id=1, source_target_pairs={{0,16},{1,17},{2,18},{3,19},{4,20},{5,21},{6,22},{7,23},{8,24},{9,... | collective-permute-start | bytes 1327112 | tf_op jit(solution)/shard_map/ppermute | solution.py:727
  56.5 17.9 %collective-permute-start.21 = (bf16[192,1536]{1,0:T(8,128)(2,1)S(1)}, bf16[192,1536]{1,0:T(8,128)(2,1)S(1)}, u32[]{:S(2)}, u32[]{:S(2)}) collective-permute-start(bf16[192,1536]{1,0:T(8,128)(2,1)S(1)} %pad_maximum_fusion.refs_0_), channel_id=1, source_target_pairs={{0,2},{1,3},{2,0},{3,1},{4,6},{5,7},{6,4},{7,5},{8,10},{9,11},{10,... | collective-permute-start | bytes 1769480 | tf_op jit(solution)/shard_map/ppermute | solution.py:727
  57.0 12.6 %collective-permute-start.18 = (bf16[48,1536]{1,0:T(8,128)(2,1)S(1)}, bf16[48,1536]{1,0:T(8,128)(2,1)S(1)}, u32[]{:S(2)}, u32[]{:S(2)}) collective-permute-start(bf16[48,1536]{1,0:T(8,128)(2,1)S(1)} %get-tuple-element.224), channel_id=1, source_target_pairs={{0,8},{1,9},{2,10},{3,11},{4,12},{5,13},{6,14},{7,15},{8,0},{9,1},... | collective-permute-start | bytes 442376 | tf_op jit(solution)/shard_map/ppermute | solution.py:727
  57.0 12.6 %collective-permute-start.17 = (bf16[48,1536]{1,0:T(8,128)(2,1)S(1)}, bf16[48,1536]{1,0:T(8,128)(2,1)S(1)}, u32[]{:S(2)}, u32[]{:S(2)}) collective-permute-start(bf16[48,1536]{1,0:T(8,128)(2,1)S(1)} %get-tuple-element.224), channel_id=1, source_target_pairs={{0,4},{1,5},{2,6},{3,7},{4,0},{5,1},{6,2},{7,3},{8,12},{9,13},{10,... | collective-permute-start | bytes 442376 | tf_op jit(solution)/shard_map/ppermute | solution.py:727
  59.3 12.0 %collective-permute-start.25 = (bf16[192,1152]{1,0:T(8,128)(2,1)S(1)}, bf16[192,1152]{1,0:T(8,128)(2,1)S(1)}, u32[]{:S(2)}, u32[]{:S(2)}) collective-permute-start(bf16[192,1152]{1,0:T(8,128)(2,1)S(1)} %collective-permute-done.15.refs_3_), channel_id=1, source_target_pairs={{0,1},{1,0},{2,3},{3,2},{4,5},{5,4},{6,7},{7,6},{8,9},{9,8},{10,11... | collective-permute-start | bytes 1327112 | tf_op jit(solution)/shard_map/ppermute | solution.py:727
  63.0 11.3 %collective-permute-start.20 = (bf16[192,1152]{1,0:T(8,128)(2,1)S(1)}, bf16[192,1152]{1,0:T(8,128)(2,1)S(1)}, u32[]{:S(2)}, u32[]{:S(2)}) collective-permute-start(bf16[192,1152]{1,0:T(8,128)(2,1)S(1)} %pad_maximum_fusion.4.refs_0_), channel_id=1, source_target_pairs={{0,16},{1,17},{2,18},{3,19},{4,20},{5,21},{6,22},{7,23},{8,24},{9,... | collective-permute-start | bytes 1327112 | tf_op jit(solution)/shard_map/ppermute | solution.py:727
  69.6 10.6 %collective-permute-start.31 = (bf16[192,1152]{1,0:T(8,128)(2,1)S(1)}, bf16[192,1152]{1,0:T(8,128)(2,1)S(1)}, u32[]{:S(2)}, u32[]{:S(2)}) collective-permute-start(bf16[192,1152]{1,0:T(8,128)(2,1)S(1)} %pad_maximum_fusion.4.refs_0_), channel_id=1, source_target_pairs={{0,1},{1,0},{2,3},{3,2},{4,5},{5,4},{6,7},{7,6},{8,9},{9,8},{10,11... | collective-permute-start | bytes 1327112 | tf_op jit(solution)/shard_map/ppermute | solution.py:727
  69.6 10.6 %collective-permute-start.32 = (bf16[192,1152]{1,0:T(8,128)(2,1)S(1)}, bf16[192,1152]{1,0:T(8,128)(2,1)S(1)}, u32[]{:S(2)}, u32[]{:S(2)}) collective-permute-start(bf16[192,1152]{1,0:T(8,128)(2,1)S(1)} %collective-permute-done.14.refs_1_), channel_id=1, source_target_pairs={{0,1},{1,0},{2,3},{3,2},{4,5},{5,4},{6,7},{7,6},{8,9},{9,8},{10,11... | collective-permute-start | bytes 1327112 | tf_op jit(solution)/shard_map/ppermute | solution.py:727
  76.4 18.7 %collective-permute-start.34 = (bf16[192,1536]{1,0:T(8,128)(2,1)S(1)}, bf16[192,1536]{1,0:T(8,128)(2,1)S(1)}, u32[]{:S(2)}, u32[]{:S(2)}) collective-permute-start(bf16[192,1536]{1,0:T(8,128)(2,1)S(1)} %pad_maximum_fusion.refs_0_), channel_id=1, source_target_pairs={{0,1},{1,0},{2,3},{3,2},{4,5},{5,4},{6,7},{7,6},{8,9},{9,8},{10,11... | collective-permute-start | bytes 1769480 | tf_op jit(solution)/shard_map/ppermute | solution.py:727
  76.4 13.8 %collective-permute-start.27 = (bf16[48,1536]{1,0:T(8,128)(2,1)S(1)}, bf16[48,1536]{1,0:T(8,128)(2,1)S(1)}, u32[]{:S(2)}, u32[]{:S(2)}) collective-permute-start(bf16[48,1536]{1,0:T(8,128)(2,1)S(1)} %get-tuple-element.232), channel_id=1, source_target_pairs={{0,8},{1,9},{2,10},{3,11},{4,12},{5,13},{6,14},{7,15},{8,0},{9,1},... | collective-permute-start | bytes 442376 | tf_op jit(solution)/shard_map/ppermute | solution.py:727
  80.2 10.5 %collective-permute-start.26 = (bf16[48,1536]{1,0:T(8,128)(2,1)S(1)}, bf16[48,1536]{1,0:T(8,128)(2,1)S(1)}, u32[]{:S(2)}, u32[]{:S(2)}) collective-permute-start(bf16[48,1536]{1,0:T(8,128)(2,1)S(1)} %get-tuple-element.232), channel_id=1, source_target_pairs={{0,4},{1,5},{2,6},{3,7},{4,0},{5,1},{6,2},{7,3},{8,12},{9,13},{10,... | collective-permute-start | bytes 442376 | tf_op jit(solution)/shard_map/ppermute | solution.py:727
  80.2 21.0 %collective-permute-start.35 = (bf16[192,1536]{1,0:T(8,128)(2,1)S(1)}, bf16[192,1536]{1,0:T(8,128)(2,1)S(1)}, u32[]{:S(2)}, u32[]{:S(2)}) collective-permute-start(bf16[192,1536]{1,0:T(8,128)(2,1)S(1)} %collective-permute-done.21.refs_1_), channel_id=1, source_target_pairs={{0,1},{1,0},{2,3},{3,2},{4,5},{5,4},{6,7},{7,6},{8,9},{9,8},{10,11... | collective-permute-start | bytes 1769480 | tf_op jit(solution)/shard_map/ppermute | solution.py:727
  81.4 19.8 %collective-permute-start.30 = (bf16[192,1536]{1,0:T(8,128)(2,1)S(1)}, bf16[192,1536]{1,0:T(8,128)(2,1)S(1)}, u32[]{:S(2)}, u32[]{:S(2)}) collective-permute-start(bf16[192,1536]{1,0:T(8,128)(2,1)S(1)} %pad_maximum_fusion.1.refs_0_), channel_id=1, source_target_pairs={{0,2},{1,3},{2,0},{3,1},{4,6},{5,7},{6,4},{7,5},{8,10},{9,11},{10,... | collective-permute-start | bytes 1769480 | tf_op jit(solution)/shard_map/ppermute | solution.py:727
  90.1 11.0 %collective-permute-start.29 = (bf16[192,1152]{1,0:T(8,128)(2,1)S(1)}, bf16[192,1152]{1,0:T(8,128)(2,1)S(1)}, u32[]{:S(2)}, u32[]{:S(2)}) collective-permute-start(bf16[192,1152]{1,0:T(8,128)(2,1)S(1)} %collective-permute-done.14.refs_1_), channel_id=1, source_target_pairs={{0,16},{1,17},{2,18},{3,19},{4,20},{5,21},{6,22},{7,23},{8,24},{9,... | collective-permute-start | bytes 1327112 | tf_op jit(solution)/shard_map/ppermute | solution.py:727
  90.7 10.5 %collective-permute-start.33 = (bf16[192,1152]{1,0:T(8,128)(2,1)S(1)}, bf16[192,1152]{1,0:T(8,128)(2,1)S(1)}, u32[]{:S(2)}, u32[]{:S(2)}) collective-permute-start(bf16[192,1152]{1,0:T(8,128)(2,1)S(1)} %collective-permute-done.20.refs_2_), channel_id=1, source_target_pairs={{0,1},{1,0},{2,3},{3,2},{4,5},{5,4},{6,7},{7,6},{8,9},{9,8},{10,11... | collective-permute-start | bytes 1327112 | tf_op jit(solution)/shard_map/ppermute | solution.py:727
  111.6 23.8 %collective-permute-start.37 = (bf16[4,2,48,3072]{3,2,1,0:T(8,128)(2,1)S(1)}, bf16[4,2,48,3072]{3,2,1,0:T(8,128)(2,1)S(1)}, u32[]{:S(2)}, u32[]{:S(2)}) collective-permute-start(bf16[4,2,48,3072]{3,2,1,0:T(8,128)(2,1)S(1)} %get-tuple-element.263), channel_id=1, source_target_pairs={{0,1},{1,0},{2,3},{3,2},{4,5},{5,4},{6,7},{7,6},{8,9},{9,8},{10,11... | collective-permute-start | bytes 7077896 | tf_op jit(solution)/shard_map/ppermute | solution.py:727
  111.8 15.6 %collective-permute-start.40 = (bf16[192,1536]{1,0:T(8,128)(2,1)S(1)}, bf16[192,1536]{1,0:T(8,128)(2,1)S(1)}, u32[]{:S(2)}, u32[]{:S(2)}) collective-permute-start(bf16[192,1536]{1,0:T(8,128)(2,1)S(1)} %pad_maximum_fusion.2.refs_0_), channel_id=1, source_target_pairs={{0,2},{1,3},{2,0},{3,1},{4,6},{5,7},{6,4},{7,5},{8,10},{9,11},{10,... | collective-permute-start | bytes 1769480 | tf_op jit(solution)/shard_map/ppermute | solution.py:727
  112.5 15.0 %collective-permute-start.38 = (bf16[192,1536]{1,0:T(8,128)(2,1)S(1)}, bf16[192,1536]{1,0:T(8,128)(2,1)S(1)}, u32[]{:S(2)}, u32[]{:S(2)}) collective-permute-start(bf16[192,1536]{1,0:T(8,128)(2,1)S(1)} %pad_maximum_fusion.1.refs_0_), channel_id=1, source_target_pairs={{0,1},{1,0},{2,3},{3,2},{4,5},{5,4},{6,7},{7,6},{8,9},{9,8},{10,11... | collective-permute-start | bytes 1769480 | tf_op jit(solution)/shard_map/ppermute | solution.py:727
  112.6 14.9 %collective-permute-start.39 = (bf16[192,1536]{1,0:T(8,128)(2,1)S(1)}, bf16[192,1536]{1,0:T(8,128)(2,1)S(1)}, u32[]{:S(2)}, u32[]{:S(2)}) collective-permute-start(bf16[192,1536]{1,0:T(8,128)(2,1)S(1)} %collective-permute-done.30.refs_1_), channel_id=1, source_target_pairs={{0,1},{1,0},{2,3},{3,2},{4,5},{5,4},{6,7},{7,6},{8,9},{9,8},{10,11... | collective-permute-start | bytes 1769480 | tf_op jit(solution)/shard_map/ppermute | solution.py:727
  113.0 15.2 %collective-permute-start.41 = (bf16[192,1536]{1,0:T(8,128)(2,1)S(1)}, bf16[192,1536]{1,0:T(8,128)(2,1)S(1)}, u32[]{:S(2)}, u32[]{:S(2)}) collective-permute-start(bf16[192,1536]{1,0:T(8,128)(2,1)S(1)} %pad_maximum_fusion.2.refs_0_), channel_id=1, source_target_pairs={{0,1},{1,0},{2,3},{3,2},{4,5},{5,4},{6,7},{7,6},{8,9},{9,8},{10,11... | collective-permute-start | bytes 1769480 | tf_op jit(solution)/shard_map/ppermute | solution.py:727
  136.4 16.2 %collective-permute-start.45 = (bf16[4,2,48,3072]{3,2,1,0:T(8,128)(2,1)S(1)}, bf16[4,2,48,3072]{3,2,1,0:T(8,128)(2,1)S(1)}, u32[]{:S(2)}, u32[]{:S(2)}) collective-permute-start(bf16[4,2,48,3072]{3,2,1,0:T(8,128)(2,1)S(1)} %get-tuple-element.278), channel_id=1, source_target_pairs={{0,1},{1,0},{2,3},{3,2},{4,5},{5,4},{6,7},{7,6},{8,9},{9,8},{10,11... | collective-permute-start | bytes 7077896 | tf_op jit(solution)/shard_map/ppermute | solution.py:727
  136.6 15.6 %collective-permute-start.43 = (bf16[4,48,1536]{2,1,0:T(8,128)(2,1)S(1)}, bf16[4,48,1536]{2,1,0:T(8,128)(2,1)S(1)}, u32[]{:S(2)}, u32[]{:S(2)}) collective-permute-start(bf16[4,48,1536]{2,1,0:T(8,128)(2,1)S(1)} %get-tuple-element.276), channel_id=1, source_target_pairs={{0,2},{1,3},{2,0},{3,1},{4,6},{5,7},{6,4},{7,5},{8,10},{9,11},{10,... | collective-permute-start | bytes 1769480 | tf_op jit(solution)/shard_map/ppermute | solution.py:727
  137.2 15.3 %collective-permute-start.44 = (bf16[4,2,48,768]{3,2,1,0:T(8,128)(2,1)S(1)}, bf16[4,2,48,768]{3,2,1,0:T(8,128)(2,1)S(1)}, u32[]{:S(2)}, u32[]{:S(2)}) collective-permute-start(bf16[4,2,48,768]{3,2,1,0:T(8,128)(2,1)S(1)} %get-tuple-element.277), channel_id=1, source_target_pairs={{0,16},{1,17},{2,18},{3,19},{4,20},{5,21},{6,22},{7,23},{8,24},{9,... | collective-permute-start | bytes 1769480 | tf_op jit(solution)/shard_map/ppermute | solution.py:727
  154.2 17.6 %collective-permute-start.51 = (bf16[4,2,48,3072]{3,2,1,0:T(8,128)(2,1)S(1)}, bf16[4,2,48,3072]{3,2,1,0:T(8,128)(2,1)S(1)}, u32[]{:S(2)}, u32[]{:S(2)}) collective-permute-start(bf16[4,2,48,3072]{3,2,1,0:T(8,128)(2,1)S(1)} %get-tuple-element.306), channel_id=1, source_target_pairs={{0,1},{1,0},{2,3},{3,2},{4,5},{5,4},{6,7},{7,6},{8,9},{9,8},{10,11... | collective-permute-start | bytes 7077896 | tf_op jit(solution)/shard_map/ppermute | solution.py:727
  154.3 17.6 %collective-permute-start.49 = (bf16[4,48,1536]{2,1,0:T(8,128)(2,1)S(1)}, bf16[4,48,1536]{2,1,0:T(8,128)(2,1)S(1)}, u32[]{:S(2)}, u32[]{:S(2)}) collective-permute-start(bf16[4,48,1536]{2,1,0:T(8,128)(2,1)S(1)} %get-tuple-element.304), channel_id=1, source_target_pairs={{0,2},{1,3},{2,0},{3,1},{4,6},{5,7},{6,4},{7,5},{8,10},{9,11},{10,... | collective-permute-start | bytes 1769480 | tf_op jit(solution)/shard_map/ppermute | solution.py:727
  155.7 16.1 %collective-permute-start.50 = (bf16[4,2,48,768]{3,2,1,0:T(8,128)(2,1)S(1)}, bf16[4,2,48,768]{3,2,1,0:T(8,128)(2,1)S(1)}, u32[]{:S(2)}, u32[]{:S(2)}) collective-permute-start(bf16[4,2,48,768]{3,2,1,0:T(8,128)(2,1)S(1)} %get-tuple-element.305), channel_id=1, source_target_pairs={{0,16},{1,17},{2,18},{3,19},{4,20},{5,21},{6,22},{7,23},{8,24},{9,... | collective-permute-start | bytes 1769480 | tf_op jit(solution)/shard_map/ppermute | solution.py:727
  156.3 12.8 %collective-permute-start.47 = (bf16[48,1536]{1,0:T(8,128)(2,1)S(1)}, bf16[48,1536]{1,0:T(8,128)(2,1)S(1)}, u32[]{:S(2)}, u32[]{:S(2)}) collective-permute-start(bf16[48,1536]{1,0:T(8,128)(2,1)S(1)} %get-tuple-element.302), channel_id=1, source_target_pairs={{0,8},{1,9},{2,10},{3,11},{4,12},{5,13},{6,14},{7,15},{8,0},{9,1},... | collective-permute-start | bytes 442376 | tf_op jit(solution)/shard_map/ppermute | solution.py:727
  174.2 22.5 %collective-permute-start.55 = (bf16[4,48,1536]{2,1,0:T(8,128)(2,1)S(1)}, bf16[4,48,1536]{2,1,0:T(8,128)(2,1)S(1)}, u32[]{:S(2)}, u32[]{:S(2)}) collective-permute-start(bf16[4,48,1536]{2,1,0:T(8,128)(2,1)S(1)} %get-tuple-element.332), channel_id=1, source_target_pairs={{0,2},{1,3},{2,0},{3,1},{4,6},{5,7},{6,4},{7,5},{8,10},{9,11},{10,... | collective-permute-start | bytes 1769480 | tf_op jit(solution)/shard_map/ppermute | solution.py:727
  174.8 21.9 %collective-permute-start.56 = (bf16[4,2,48,768]{3,2,1,0:T(8,128)(2,1)S(1)}, bf16[4,2,48,768]{3,2,1,0:T(8,128)(2,1)S(1)}, u32[]{:S(2)}, u32[]{:S(2)}) collective-permute-start(bf16[4,2,48,768]{3,2,1,0:T(8,128)(2,1)S(1)} %get-tuple-element.333), channel_id=1, source_target_pairs={{0,16},{1,17},{2,18},{3,19},{4,20},{5,21},{6,22},{7,23},{8,24},{9,... | collective-permute-start | bytes 1769480 | tf_op jit(solution)/shard_map/ppermute | solution.py:727
  176.4 15.2 %collective-permute-start.52 = (bf16[48,1536]{1,0:T(8,128)(2,1)S(1)}, bf16[48,1536]{1,0:T(8,128)(2,1)S(1)}, u32[]{:S(2)}, u32[]{:S(2)}) collective-permute-start(bf16[48,1536]{1,0:T(8,128)(2,1)S(1)} %get-tuple-element.329), channel_id=1, source_target_pairs={{0,4},{1,5},{2,6},{3,7},{4,0},{5,1},{6,2},{7,3},{8,12},{9,13},{10,... | collective-permute-start | bytes 442376 | tf_op jit(solution)/shard_map/ppermute | solution.py:727
  178.8 10.5 %collective-permute-start.59 = (f32[16,768]{1,0:T(8,128)S(1)}, f32[16,768]{1,0:T(8,128)S(1)}, u32[]{:S(2)}, u32[]{:S(2)}) collective-permute-start(f32[16,768]{1,0:T(8,128)S(1)} %add.81), channel_id=1, source_target_pairs={{0,2},{1,3},{2,0},{3,1},{4,6},{5,7},{6,4},{7,5},{8,10},{9,11},{10,... | collective-permute-start | bytes 147464 | tf_op jit(solution)/shard_map/ppermute | solution.py:727
  180.2 14.7 %collective-permute-start.53 = (bf16[48,1536]{1,0:T(8,128)(2,1)S(1)}, bf16[48,1536]{1,0:T(8,128)(2,1)S(1)}, u32[]{:S(2)}, u32[]{:S(2)}) collective-permute-start(bf16[48,1536]{1,0:T(8,128)(2,1)S(1)} %get-tuple-element.330), channel_id=1, source_target_pairs={{0,8},{1,9},{2,10},{3,11},{4,12},{5,13},{6,14},{7,15},{8,0},{9,1},... | collective-permute-start | bytes 442376 | tf_op jit(solution)/shard_map/ppermute | solution.py:727
  198.8 18.6 %collective-permute-start.63 = (bf16[4,48,2304]{2,1,0:T(8,128)(2,1)S(1)}, bf16[4,48,2304]{2,1,0:T(8,128)(2,1)S(1)}, u32[]{:S(2)}, u32[]{:S(2)}) collective-permute-start(bf16[4,48,2304]{2,1,0:T(8,128)(2,1)S(1)} %get-tuple-element.359), channel_id=1, source_target_pairs={{0,2},{1,3},{2,0},{3,1},{4,6},{5,7},{6,4},{7,5},{8,10},{9,11},{10,... | collective-permute-start | bytes 2654216 | tf_op jit(solution)/shard_map/ppermute | solution.py:727
  201.5 10.8 %collective-permute-start.61 = (bf16[48,1536]{1,0:T(8,128)(2,1)S(1)}, bf16[48,1536]{1,0:T(8,128)(2,1)S(1)}, u32[]{:S(2)}, u32[]{:S(2)}) collective-permute-start(bf16[48,1536]{1,0:T(8,128)(2,1)S(1)} %get-tuple-element.357), channel_id=1, source_target_pairs={{0,8},{1,9},{2,10},{3,11},{4,12},{5,13},{6,14},{7,15},{8,0},{9,1},... | collective-permute-start | bytes 442376 | tf_op jit(solution)/shard_map/ppermute | solution.py:727
  202.6 9.7 %collective-permute-start.62 = (bf16[48,1536]{1,0:T(8,128)(2,1)S(1)}, bf16[48,1536]{1,0:T(8,128)(2,1)S(1)}, u32[]{:S(2)}, u32[]{:S(2)}) collective-permute-start(bf16[48,1536]{1,0:T(8,128)(2,1)S(1)} %get-tuple-element.358), channel_id=1, source_target_pairs={{0,12},{1,13},{2,14},{3,15},{4,8},{5,9},{6,10},{7,11},{8,4},{9,5},... | collective-permute-start | bytes 442376 | tf_op jit(solution)/shard_map/ppermute | solution.py:727
  218.8 13.4 %collective-permute-start.66 = (bf16[48,2304]{1,0:T(8,128)(2,1)S(1)}, bf16[48,2304]{1,0:T(8,128)(2,1)S(1)}, u32[]{:S(2)}, u32[]{:S(2)}) collective-permute-start(bf16[48,2304]{1,0:T(8,128)(2,1)S(1)} %get-tuple-element.372), channel_id=1, source_target_pairs={{0,4},{1,5},{2,6},{3,7},{4,0},{5,1},{6,2},{7,3},{8,12},{9,13},{10,... | collective-permute-start | bytes 663560 | tf_op jit(solution)/shard_map/ppermute | solution.py:727
  220.2 16.2 %collective-permute-start.67 = (bf16[48,2304]{1,0:T(8,128)(2,1)S(1)}, bf16[48,2304]{1,0:T(8,128)(2,1)S(1)}, u32[]{:S(2)}, u32[]{:S(2)}) collective-permute-start(bf16[48,2304]{1,0:T(8,128)(2,1)S(1)} %get-tuple-element.373), channel_id=1, source_target_pairs={{0,8},{1,9},{2,10},{3,11},{4,12},{5,13},{6,14},{7,15},{8,0},{9,1},... | collective-permute-start | bytes 663560 | tf_op jit(solution)/shard_map/ppermute | solution.py:727
  221.6 14.8 %collective-permute-start.68 = (bf16[48,2304]{1,0:T(8,128)(2,1)S(1)}, bf16[48,2304]{1,0:T(8,128)(2,1)S(1)}, u32[]{:S(2)}, u32[]{:S(2)}) collective-permute-start(bf16[48,2304]{1,0:T(8,128)(2,1)S(1)} %get-tuple-element.374), channel_id=1, source_target_pairs={{0,12},{1,13},{2,14},{3,15},{4,8},{5,9},{6,10},{7,11},{8,4},{9,5},... | collective-permute-start | bytes 663560 | tf_op jit(solution)/shard_map/ppermute | solution.py:727
  (46 other events, 493.8 us)

commit v3 on v2

--- a/solution.py
+++ b/solution.py
@@ -368,8 +368,7 @@
         a, i = (number // 4, number % 2) if count == 8 else (number // 2, number % 2)
         b = (number // 2) % 2 if count == 8 else 0
         for k in range(4):
-            row = lax.bitwise_xor(co[1], k) * 192
-            row = row + lax.bitwise_xor(co[2], i) * 96 + lax.bitwise_xor(co[3], a) * 48
+            row = k * 192 + lax.bitwise_xor(co[2], i) * 96 + lax.bitwise_xor(co[3], a) * 48
             rows = pl.ds(pl.multiple_of(row, 16), 48)
             for (start, size), out in zip(ranges, refs[count:]):
                 out[rows, b * size : b * size + size] = refs[number][
@@ -411,17 +410,19 @@
     return centred * rstd, rstd
 
 
-def prep_kernel(co, attn, mlp, s0, s1, s2, s3, s4):
+def prep_kernel(co, attn, mlp, s0, s1, s2):
     r = co[0]
     for part in range(3):
         cols = lanes(part * D + 384 * r, 384)
         s0[:, part * 384 : part * 384 + 384] = attn[:, cols].astype(BF)
-    s1[:, :384] = attn[:, lanes(3 * D + 384 * r, 384)].astype(BF)
-    s1[:, 384:] = mlp[:, lanes(1536 * r, 768)].astype(BF)
-    for b, out in ((0, s3), (1, s4)):
+    s0[:, 1152:1536] = attn[:, lanes(3 * D + 384 * r, 384)].astype(BF)
+    s0[:, 1536:] = mlp[:, lanes(1536 * r, 768)].astype(BF)
+    for b in range(2):
         half = lax.bitwise_xor(r, b)
-        s2[:, b * 768 : b * 768 + 768] = mlp[:, lanes(1536 * half + 768, 768)].astype(BF)
-        out[...] = mlp[:, lanes(FF + 1536 * half, 1536)].astype(BF)
+        s1[:, b * D : b * D + D] = mlp[:, lanes(1536 * half + D, D)].astype(BF)
+    s1[:, 2 * D :] = mlp[:, lanes(FF + 1536 * r, D)].astype(BF)
+    s2[:, :D] = mlp[:, lanes(FF + 1536 * r + D, D)].astype(BF)
+    s2[:, D:] = mlp[:, lanes(FF + 1536 * (1 - r), 2 * D)].astype(BF)
 
 
 def first_norm_kernel(co, tokens, info, vec, h1, h1t, cols):
@@ -498,14 +499,15 @@
 
 
 def hidden_grad_kernel(
-    co, dz, slope0, slope1, w0, w1, left, du0, du1, db1, send, keep, scratch
+    co, dz, slope0, slope1, w00, w01, w1, left, du0, du1, db1, send, keep, scratch
 ):
     for part, slope, du in ((0, slope0, du0), (1, slope1, du1)):
-        for b, weight in ((0, w0), (1, w1)):
+        for b in range(2):
+            weight, start = (w1, part * D) if b else ((w00, w01)[part], 0)
             half = lax.bitwise_xor(co[0], b)
             for sub in range(0, D, 384):
                 at = slice(b * D + sub, b * D + sub + 384)
-                da = nn(dz[...], weight[:, part * D + sub : part * D + sub + 384])
+                da = nn(dz[...], weight[:, start + sub : start + sub + 384])
                 d = (da * slope[:, at]).astype(BF)
                 du[:, at] = d
                 db1[pl.ds(2 * half + part, 1), sub : sub + 384] = jnp.sum(
@@ -516,12 +518,11 @@
                 share_rows(co[3], scratch, send, keep, dst)
 
 
-def output_kernel(co, y1, vec, g0, g1, w0, w1, act):
+def output_kernel(co, y1, vec, g0, g1, w00, w01, w1, act):
     acc = y1[...] + vec[7:8, :]
     for part, g in ((0, g0), (1, g1)):
-        for b, weight in ((0, w0), (1, w1)):
-            w = weight[:, part * D : part * D + D]
-            acc = acc + nt(g[:, b * D : b * D + D], w)
+        acc = acc + nt(g[:, :D], (w00, w01)[part][...])
+        acc = acc + nt(g[:, D:], w1[:, part * D : part * D + D])
     act[...] = acc.astype(BF)
 
 
@@ -630,65 +631,79 @@
     every = slice(None)
     for k in range(4):
         for out, i in ((y_send, 1 - y), (y_keep, y)):
-            out[k] = both(keep, got, k, i, every, slice(0, 2 * D)).astype(out.dtype)
+            out[k * 48 : k * 48 + 48, :] = both(keep, got, k, i, every, slice(0, 2 * D)).astype(
+                out.dtype
+            )
     x_keep[...] = both(keep, got, every, every, every, slice(2 * D, 3 * D))
     x_send[...] = both(keep, got, every, every, every, slice(3 * D, 4 * D)).astype(BF)
 
 
-def split_second_kernel(co, x_keep, x_got, keep, got, y_send, y_keep, x_send, x_next, rest):
+def split_second_kernel(co, x_keep, x_got, keep, got, y_send, y_keep, x_send, x_next):
     y = co[2]
     every = slice(None)
     for k in range(4):
+        rows = slice(k * 48, k * 48 + 48)
         for out, i in ((y_send, 1 - y), (y_keep, y)):
-            out[k, :, :D] = both(x_keep, x_got, k, i).astype(out.dtype)
-            out[k, :, D:] = both(keep, got, k, i, every, slice(0, D)).astype(out.dtype)
-    rest[...] = both(keep, got, every, every, every, slice(D, 2 * D))
+            out[rows, :D] = both(x_keep, x_got, k, i).astype(out.dtype)
+            out[rows, D:] = both(keep, got, k, i, every, slice(0, 2 * D)).astype(out.dtype)
     x_next[...] = both(keep, got, every, every, every, slice(2 * D, 3 * D))
     x_send[...] = both(keep, got, every, every, every, slice(3 * D, 4 * D)).astype(BF)
 
 
-def split_third_kernel(co, x_keep, x_got, rest, keep, got, y_send, y_keep, x_send, x_next, last):
+def split_third_kernel(co, x_keep, x_got, keep, got, y_send, y_keep, x_send, x_next, last):
     y = co[2]
     every = slice(None)
     for k in range(4):
+        rows = slice(k * 48, k * 48 + 48)
         for out, i in ((y_send, 1 - y), (y_keep, y)):
-            out[k, :, :D] = both(x_keep, x_got, k, i).astype(out.dtype)
-            out[k, :, D:] = rest[k, i].astype(out.dtype)
+            out[rows, :D] = both(x_keep, x_got, k, i).astype(out.dtype)
+            out[rows, D:] = both(keep, got, k, i, every, slice(2 * D, 3 * D)).astype(out.dtype)
     x_next[...] = both(keep, got, every, every, every, slice(0, D))
     x_send[...] = both(keep, got, every, every, every, slice(D, 2 * D)).astype(BF)
-    last[...] = both(keep, got, every, every, every, slice(2 * D, 4 * D))
-
-
-def split_fourth_kernel(co, x_keep, x_got, rest, y_send, y_keep):
+    last[...] = both(keep, got, every, every, every, slice(3 * D, 4 * D))
+
+
+def split_fourth_kernel(co, x_keep, x_got, last, vec, y_send, y_keep):
     y = co[2]
-    for k in range(4):
-        for out, i in ((y_send, 1 - y), (y_keep, y)):
-            out[k, :, :D] = both(x_keep, x_got, k, i).astype(out.dtype)
-            out[k, :, D:] = rest[k, i].astype(out.dtype)
-
-
-def split_z_kernel(co, keep, got, z1, z2, z3, z_keep):
-    z = co[1]
-    for k, out in ((1, z1), (2, z2), (3, z3)):
-        out[...] = both(keep, got, lax.bitwise_xor(z, k)).astype(BF)
-    z_keep[...] = both(keep, got, z)
-
-
-def sum_z_kernel(co, keep, g1, g2, g3, out):
-    out[...] = (
-        keep[...] + g1[...].astype(F32) + g2[...].astype(F32) + g3[...].astype(F32)
-    ).astype(BF)
+    for out, i in ((y_send, 1 - y), (y_keep, y)):
+        for k in range(4):
+            rows = slice(k * 48, k * 48 + 48)
+            out[rows, :D] = both(x_keep, x_got, k, i).astype(out.dtype)
+            out[rows, D:] = last[k, i].astype(out.dtype)
+        out[192:208, :D] = vec[...].astype(out.dtype)
+        out[192:208, D:] = jnp.zeros((16, D), out.dtype)
+
+
+def split_near_kernel(co, keep, got, send, rest, *small):
+    side = co[1] % 2
+    for out, at in ((send, 1 - side), (rest, side)):
+        for far in range(2):
+            row = pl.multiple_of((2 * far + at) * 48, 16)
+            out[far * 48 : far * 48 + 48, :] = both(keep, got, pl.ds(row, 48)).astype(out.dtype)
+    if small:
+        small[0][...] = both(keep, got, slice(192, 208), slice(0, D))
+
+
+def split_far_kernel(co, keep, got, send, rest):
+    side = co[1] // 2
+    for out, at in ((send, 1 - side), (rest, side)):
+        row = pl.multiple_of(at * 48, 16)
+        out[...] = both(keep, got, pl.ds(row, 48)).astype(out.dtype)
+
+
+def sum_far_kernel(co, keep, got, out):
+    out[...] = (keep[...] + got[...].astype(F32)).astype(BF)
 
 
 def update_kernel(rate, moves, co, *refs):
     state, grads, new = refs[:3], refs[3:-4], refs[-4:]
-    for numbers, src, size, b, col, stride in moves:
-        grad = grads[numbers[0]][:, src : src + size].astype(F32)
-        if len(numbers) == 2:
-            grad = grad + grads[numbers[1]][:, src : src + size].astype(F32)
+    for numbers, row, src, size, b, col, stride in moves:
+        grad = 0.0
+        for number in numbers:
+            grad = grad + grads[number][row : row + 48, src : src + size].astype(F32)
         place = col if b is None else col + stride * lax.bitwise_xor(co[0], b)
         at = lanes(place, size)
-        w, m, a = (ref.ref[:, at] for ref in state)
+        w, m, a = (ref[:, at] for ref in state)
         m_new = momentum_decay * m + grad
         w_new = w - rate * (grad + momentum_decay * m_new)
         new[0][:, at] = w_new
@@ -728,9 +743,9 @@
 
     CORE, Y, Z, X = 1, 2, 4, 16
 
-    s0, s1, s2, s3, s4 = call(
+    s0, s1, s2 = call(
         prep_kernel,
-        [((48, 1152), BF)] * 2 + [((48, 1536), BF)] * 3,
+        [((48, 3 * D), BF)] * 3,
         [co, attn_weight, mlp_weight],
         name="prep",
     )
@@ -742,36 +757,33 @@
     flat = lax.dynamic_update_slice(flat, offset_vector.astype(BF).astype(F32), (2 * D + 528 * f,))
     vec = flat.reshape(16, D)
 
+    groups = [[4 * z + at for z in range(4)] for at in range(4)]
+
     def along_z(shard):
-        return [swap(shard, Z * k) for k in (1, 2, 3)]
-
-    def rows(shard, others):
-        return jnp.concatenate([shard] + others, axis=0)
+        return lax.all_gather(shard, "fsdp", axis=0, tiled=True, axis_index_groups=groups)
 
     def core_pair(pieces):
         return pieces + [swap(piece, CORE) for piece in pieces]
 
-    z0 = along_z(s0)
     vec = vec + swap(vec, CORE)
+    s0, vec = hold((s0, vec))
+    stack0 = along_z(s0)
     vec = vec + swap(vec, Y)
-    stack0, s1, vec = hold((rows(s0, z0), s1, vec))
+    stack0, s1, vec = hold((stack0, s1, vec))
     across0 = swap(stack0, Y)
     far0 = swap(stack0, X)
-    z1 = along_z(s1)
+    near0 = [swap(stack0, CORE)]
+    stack1 = along_z(s1)
     vec = vec + swap(vec, Z)
-    stack1, across0, far0, s2, vec = hold((rows(s1, z1), across0, far0, s2, vec))
+    stack1, across0, far0, near0, s2, vec = hold((stack1, across0, far0, near0, s2, vec))
     far_across0 = swap(across0, X)
     across1 = swap(stack1, Y)
-    z2 = along_z(s2)
+    near0 += [swap(across0, CORE), swap(far0, CORE)]
+    stack2 = along_z(s2)
     vec = vec + swap(vec, 2 * Z)
-    pieces0 = core_pair([stack0, across0, far0])
-    stack2, stack1, across1, far_across0, vec, s3 = hold(
-        (rows(s2, z2), stack1, across1, far_across0, vec, s3)
-    )
-    far1 = swap(stack1, X)
+    stack2, across1, far_across0, near0, vec = hold((stack2, across1, far_across0, near0, vec))
+    pieces0 = [stack0, across0, far0, far_across0, *near0, swap(far_across0, CORE)]
     across2 = swap(stack2, Y)
-    z3 = along_z(s3)
-    pieces0 = pieces0[:3] + [far_across0] + pieces0[3:] + [swap(far_across0, CORE)]
     pieces1 = core_pair([stack1, across1])
     h1, h1t, cols = call(
         first_norm_kernel,
@@ -779,14 +791,6 @@
         [co, tokens, info, vec],
         name="norm1",
     )
-    stack3, far1, across1, across2, pieces0, h1, s4 = hold(
-        (rows(s3, z3), far1, across1, across2, pieces0, h1, s4)
-    )
-    far_across1 = swap(across1, X)
-    across3 = swap(stack3, Y)
-    z4 = along_z(s4)
-    pieces1 = [*pieces1[:2], far1, *pieces1[2:], swap(far1, CORE)]
-    pieces2 = core_pair([stack2, across2])
     (w_qkv,) = assemble(co, pieces0, (0, 1152))
     qkv, att, lse = call(
         attention_kernel,
@@ -794,14 +798,8 @@
         [co, h1, vec, info, cols, w_qkv],
         name="attention",
     )
-    stack4, far_across1, across3, pieces1, pieces2, att = hold(
-        (rows(s4, z4), far_across1, across3, pieces1, pieces2, att)
-    )
-    across4 = swap(stack4, Y)
-    pieces1 = [*pieces1[:3], far_across1, *pieces1[3:], swap(far_across1, CORE)]
-    pieces3 = core_pair([stack3, across3])
-    (w_up1,) = assemble(co, pieces2, (0, 1536))
-    w_out, w_up0 = assemble(co, pieces1, (0, 384), (384, 768))
+    w_out, w_up0 = assemble(co, pieces0, (1152, 384), (1536, 768))
+    w_up1, w_down00 = assemble(co, pieces1, (0, 1536), (1536, 768))
 
     y1, h2, h2t = call(
         second_norm_kernel,
@@ -817,20 +815,21 @@
         scratch=[pltpu.VMEM((D, 256), BF), pltpu.VMEM((D, 384), F32)],
         name="hidden",
     )
-    pieces4 = core_pair([stack4, across4])
-
+
+    across2, down_send = hold((across2, down_send))
+    pieces2 = core_pair([stack2, across2])
+    pieces2, down_send = hold((pieces2, down_send))
     down_got = swap(down_send, CORE)
-    (w_down0,) = assemble(co, pieces3, (0, 1536))
-    (w_down1,) = assemble(co, pieces4, (0, 1536))
+    w_down01, w_down1 = assemble(co, pieces2, (0, 768), (768, 1536))
     du0, du1, db1, up_send, up_keep = call(
         hidden_grad_kernel,
         [((256, 2 * D), BF), ((256, 2 * D), BF), ((8, D), F32)] + shares,
-        [co, cotangent, slope0, slope1, w_down0, w_down1, h2t],
+        [co, cotangent, slope0, slope1, w_down00, w_down01, w_down1, h2t],
         scratch=[pltpu.VMEM((D, 384), F32)],
         name="hidden_grad",
     )
     down_got, up_send = hold((down_got, up_send))
-    y_shares = [((4, 48, 2 * D), BF), ((4, 48, 2 * D), F32)]
+    y_shares = [((192, 2 * D), BF), ((192, 2 * D), F32)]
     x_shares = [((4, 2, 48, D), BF), ((4, 2, 48, D), F32)]
     y_send0, y_keep0, x_send1, x_keep1 = call(
         split_first_kernel, y_shares + x_shares, [co, down_keep, down_got], name="split_first"
@@ -859,34 +858,41 @@
         name="attention_grad",
     )
 
-    def split_z(keep, got):
-        width = keep.shape[2]
-        *sends, z_keep = call(
-            split_z_kernel,
-            [((48, width), BF)] * 3 + [((48, width), F32)],
+    def split_near(keep, got, small=()):
+        width = keep.shape[1]
+        return call(
+            split_near_kernel,
+            [((96, width), BF), ((96, width), F32), *small],
             [co, keep, got],
-            name="split_z",
+            name="split_near",
         )
-        return sends, z_keep
-
-    def swap_z(sends):
-        return [swap(send, Z * k) for send, k in zip(sends, (1, 2, 3))]
-
-    def sum_z(z_keep, z_got):
-        return call(sum_z_kernel, [(z_keep.shape, BF)], [co, z_keep, *z_got], name="sum_z")[0]
+
+    def split_far(keep, got):
+        width = keep.shape[1]
+        return call(
+            split_far_kernel,
+            [((48, width), BF), ((48, width), F32)],
+            [co, keep, got],
+            name="split_far",
+        )
+
+    def sum_far(keep, got):
+        return call(sum_far_kernel, [(keep.shape, BF)], [co, keep, got], name="sum_far")[0]
 
     y_got0, x_got1, up_got, attn_send = hold((y_got0, x_got1, up_got, attn_send))
-    z_send0, z_keep0 = split_z(y_keep0, y_got0)
-    y_send1, y_keep1, x_send2, x_keep2, rest2 = call(
+    y_send1, y_keep1, x_send2, x_keep2 = call(
         split_second_kernel,
-        y_shares + x_shares + x_shares[1:],
+        [((192, 3 * D), BF), ((192, 3 * D), F32)] + x_shares,
         [co, x_keep1, x_got1, up_keep, up_got],
         name="split_second",
     )
-    z_send0, y_send1, x_send2, attn_send, dqkv = hold((z_send0, y_send1, x_send2, attn_send, dqkv))
+    near_send0, near_keep0 = split_near(y_keep0, y_got0)
+    near_send0, y_send1, x_send2, attn_send, dqkv = hold(
+        (near_send0, y_send1, x_send2, attn_send, dqkv)
+    )
+    y_got1 = swap(y_send1, Y)
     x_got2 = swap(x_send2, X)
-    y_got1 = swap(y_send1, Y)
-    z_got0 = swap_z(z_send0)
+    near_got0 = swap(near_send0, Z)
     attn_got = swap(attn_send, CORE)
     input_grad, total = call(
         first_back_kernel,
@@ -894,54 +900,68 @@
         [co, dqkv, tokens, cols, vec, dy1, db1, small2, small_a, w_qkv],
         name="norm1_back",
     )
-    z_got0, y_got1, x_got2, attn_got, total = hold((z_got0, y_got1, x_got2, attn_got, total))
-    z_send1, z_keep1 = split_z(y_keep1, y_got1)
-    y_send2, y_keep2, x_send3, x_keep3, rest3 = call(
+    near_got0, y_got1, x_got2, attn_got, total = hold(
+        (near_got0, y_got1, x_got2, attn_got, total)
+    )
+    y_send2, y_keep2, x_send3, x_keep3, last = call(
         split_third_kernel,
-        y_shares + x_shares + [((4, 2, 48, 2 * D), F32)],
-        [co, x_keep2, x_got2, rest2, attn_keep, attn_got],
+        y_shares + x_shares + x_shares[1:],
+        [co, x_keep2, x_got2, attn_keep, attn_got],
         name="split_third",
     )
-    mine0 = sum_z(z_keep0, z_got0)
-    z_send1, y_send2, x_send3, mine0, total, y1 = hold(
-        (z_send1, y_send2, x_send3, mine0, total, y1)
+    near_send1, near_keep1 = split_near(y_keep1, y_got1)
+    far_send0, far_keep0 = split_far(near_keep0, near_got0)
+    far_send0, near_send1, y_send2, x_send3, total, y1 = hold(
+        (far_send0, near_send1, y_send2, x_send3, total, y1)
     )
     x_got3 = swap(x_send3, X)
     y_got2 = swap(y_send2, Y)
-    z_got1 = swap_z(z_send1)
-    got0 = swap(mine0, X)
+    near_got1 = swap(near_send1, Z)
+    far_got0 = swap(far_send0, 2 * Z)
     total = total + swap(total, CORE)
-    total = total + swap(total, Y)
     (activations,) = call(
-        output_kernel, [((256, D), BF)], [co, y1, vec, g0, g1, w_down0, w_down1], name="output"
-    )
-    z_got1, y_got2, x_got3, got0, total, activations = hold(
-        (z_got1, y_got2, x_got3, got0, total, activations)
-    )
-    z_send2, z_keep2 = split_z(y_keep2, y_got2)
+        output_kernel,
+        [((256, D), BF)],
+        [co, y1, vec, g0, g1, w_down00, w_down01, w_down1],
+        name="output",
+    )
+    far_got0, near_got1, y_got2, x_got3, total, activations = hold(
+        (far_got0, near_got1, y_got2, x_got3, total, activations)
+    )
     y_send3, y_keep3 = call(
         split_fourth_kernel,
-        [((4, 48, 3 * D), BF), ((4, 48, 3 * D), F32)],
-        [co, x_keep3, x_got3, rest3],
+        [((208, 2 * D), BF), ((208, 2 * D), F32)],
+        [co, x_keep3, x_got3, last, total],
         name="split_fourth",
     )
-    mine1 = sum_z(z_keep1, z_got1)
-    z_send2, y_send3, mine1, total = hold((z_send2, y_send3, mine1, total))
+    near_send2, near_keep2 = split_near(y_keep2, y_got2)
+    far_send1, far_keep1 = split_far(near_keep1, near_got1)
+    mine0 = sum_far(far_keep0, far_got0)
+    mine0, far_send1, near_send2, y_send3 = hold((mine0, far_send1, near_send2, y_send3))
     y_got3 = swap(y_send3, Y)
-    z_got2 = swap_z(z_send2)
+    near_got2 = swap(near_send2, Z)
+    far_got1 = swap(far_send1, 2 * Z)
+    got0 = swap(mine0, X)
+    got0, far_got1, near_got2, y_got3 = hold((got0, far_got1, near_got2, y_got3))
+    near_send3, near_keep3, total = split_near(y_keep3, y_got3, [((16, D), F32)])
+    far_send2, far_keep2 = split_far(near_keep2, near_got2)
+    mine1 = sum_far(far_keep1, far_got1)
+    mine1, far_send2, near_send3, total = hold((mine1, far_send2, near_send3, total))
+    near_got3 = swap(near_send3, Z)
+    far_got2 = swap(far_send2, 2 * Z)
     got1 = swap(mine1, X)
+    total = total + swap(total, Z)
+    got1, far_got2, near_got3, total = hold((got1, far_got2, near_got3, total))
+    far_send3, far_keep3 = split_far(near_keep3, near_got3)
+    mine2 = sum_far(far_keep2, far_got2)
+    mine2, far_send3, total = hold((mine2, far_send3, total))
+    far_got3 = swap(far_send3, 2 * Z)
+    got2 = swap(mine2, X)
+    total = total + swap(total, 2 * Z)
+    got2, far_got3, total = hold((got2, far_got3, total))
+    mine3 = sum_far(far_keep3, far_got3)
+    got3 = swap(mine3, X)
     total = total + swap(total, X)
-    z_got2, y_got3, got1, total = hold((z_got2, y_got3, got1, total))
-    z_send3, z_keep3 = split_z(y_keep3, y_got3)
-    mine2 = sum_z(z_keep2, z_got2)
-    z_send3, mine2, total = hold((z_send3, mine2, total))
-    z_got3 = swap_z(z_send3)
-    got2 = swap(mine2, X)
-    total = total + swap(total, Z)
-    z_got3, got2, total = hold((z_got3, got2, total))
-    mine3 = sum_z(z_keep3, z_got3)
-    got3 = swap(mine3, X)
-    total = total + swap(total, 2 * Z)
     flat = total.reshape(-1)
     gain_g = lax.dynamic_slice(flat, (96 * f,), (96,))
     offset_g = lax.dynamic_slice(flat, (2 * D + 528 * f,), (528,))
@@ -956,10 +976,10 @@
             name=name,
         )
 
-    mlp_moves = [((0, 1), h * D, D, None, FF + h * 2 * D, 0) for h in range(2)]
-    mlp_moves += [((2 + b,), 0, D, b, FF + D, 2 * D) for b in range(2)]
-    mlp_moves += [((2, 3), D, D, None, 0, 0), ((4, 5), D, D, None, 2 * D, 0)]
-    mlp_moves += [((4 + b,), 0, D, b, D, 2 * D) for b in range(2)]
+    mlp_moves = [((0, 1), 0, h * D, D, None, FF + h * 2 * D, 0) for h in range(2)]
+    mlp_moves += [((2 + b,), 0, 0, D, b, FF + D, 2 * D) for b in range(2)]
+    mlp_moves += [((2, 3), 0, D + h * D, D, None, h * 2 * D, 0) for h in range(2)]
+    mlp_moves += [((4 + b,), 0, 0, D, b, D, 2 * D) for b in range(2)]
     mlp = update(
         mlp_moves,
         [mlp_weight, mlp_moment, mlp_average],
@@ -967,14 +987,14 @@
         2 * FF,
         "update_mlp",
     )
-    attn_moves = [((0, 1), D, D, None, 0, 0)]
-    attn_moves += [((b,), 0, 384, b, D, 384) for b in range(2)]
-    attn_moves += [((b,), 384, 384, b, 2 * D, 384) for b in range(2)]
-    attn_moves += [((0, 1), 2 * D, D, None, 3 * D, 0)]
+    attn_moves = [((0, 1), 0, D, D, None, 0, 0)]
+    attn_moves += [((2 + b,), 0, 0, 384, b, D, 384) for b in range(2)]
+    attn_moves += [((2 + b,), 0, 384, 384, b, 2 * D, 384) for b in range(2)]
+    attn_moves += [((2, 3), 0, D, D, None, 3 * D, 0)]
     attn = update(
         attn_moves,
         [attn_weight, attn_moment, attn_average],
-        [mine3, got3],
+        [mine2, got2, mine3, got3],
         4 * D,
         "update_attn",
     )

time: 250 us -> 219 us (0.88)
  blocking collectives: 0 us -> 59.7 us
  waiting for transfers between devices: 120 us -> 61.5 us
  starting transfers between devices: 69.3 us -> 34.6 us
    all_gather x0 -> x3, blocking collectives: none -> 59.7 us  [along_z(): lax.all_gather(shard, 'fsdp', axis=0, tiled=True, axis_index_groups=groups)]
    ppermute x73 -> x43, waiting for transfers between devices: 120 us -> 61.5 us  [swap(): lax.ppermute(array, ('rep', 'fsdp'), [(i, i ^ mask) for i in range(32)])]
    ppermute x73 -> x43, starting transfers between devices: 69.3 us -> 34.6 us  [swap(): lax.ppermute(array, ('rep', 'fsdp'), [(i, i ^ mask) for i in range(32)])]
    pallas_call x30 -> x33, Pallas kernels: 53.5 us -> 55.3 us  [call(): pl.pallas_call(body, out_shape=[jax.ShapeDtypeStruct(shape, dtype) for sh...]
  transfers between devices with their start and end apart: 73 -> 43, of which waited for: 31 -> 18; matrix products, arithmetic and copies ran while one was open for 1% -> 1% of each run, Pallas kernels for 14% -> 19%
where the time goes in v3:
time: 219 us
  waiting for transfers between devices  61.5 us (28%)
  blocking collectives  59.7 us (27%)
  Pallas kernels  55.3 us (25%)
  starting transfers between devices  34.6 us (16%)
  other arithmetic  4.08 us (2%)
  local copies, waits for them, and re-layouts  2.66 us (1%)
    ppermute x43, waiting for transfers between devices, swap(): lax.ppermute(array, ('rep', 'fsdp'), [(i, i ^ mask) for i in range(32)])  61.5 us
    all_gather x3, blocking collectives, along_z(): lax.all_gather(shard, 'fsdp', axis=0, tiled=True, axis_index_groups=groups)  59.7 us
    pallas_call x33, Pallas kernels, call(): pl.pallas_call(body, out_shape=[jax.ShapeDtypeStruct(shape, dtype) for sh...  55.3 us
    ppermute x43, starting transfers between devices, swap(): lax.ppermute(array, ('rep', 'fsdp'), [(i, i ^ mask) for i in range(32)])  34.6 us
  transfers between devices with their start and end apart: 43, of which 18 were waited for; matrix products, arithmetic and copies ran while one was open for 1% of the time, Pallas kernels for 19%

profile of v3, /device:TPU:0, one launch (start us, length us, event | category | flops | bytes accessed | tf_op | source)
XLA Modules:
  0.0 219.1 jit_solution(18228701806692375774)
XLA Ops:
  2.8 1.3 copy-done
  4.1 1.1 copy-done.4
  5.8 2.6 %collective-permute-start.1 = (f32[16,768]{1,0:T(8,128)S(1)}, f32[16,768]{1,0:T(8,128)S(1)}, u32[]{:S(2)}, u32[]{:S(2)}) collective-permute-start(f32[16,768]{1,0:T(8,128)S(1)} %add.74), channel_id=1, source_target_pairs={{0,2},{1,3},{2,0},{3,1},{4,6},{5,7},{6,4},{7,5},{8,10},{9,11},{10,... | collective-permute-start | bytes 147464 | tf_op jit(solution)/shard_map/ppermute | solution.py:742
  8.5 20.9 %all_gather.9.refs_0_ = bf16[192,2304]{1,0:T(8,128)(2,1)S(1)} all-gather(bf16[48,2304]{1,0:T(8,128)(2,1)S(1)} %get-tuple-element.189), channel_id=1, replica_groups={{0,4,8,12},{1,5,9,13},{2,6,10,14},{3,7,11,15},{16,20,24,28},{17,21,25,2..., dimensions={0}, use_global_device_ids=true | all-gather | bytes 1105920 | tf_op jit(solution)/shard_map/all_gather | solution.py:763
  29.5 1.6 collective-permute-start.3
  31.6 19.6 %all_gather.10.refs_0_ = bf16[192,2304]{1,0:T(8,128)(2,1)S(1)} all-gather(bf16[48,2304]{1,0:T(8,128)(2,1)S(1)} %get-tuple-element.192), channel_id=1, replica_groups={{0,4,8,12},{1,5,9,13},{2,6,10,14},{3,7,11,15},{16,20,24,28},{17,21,25,2..., dimensions={0}, use_global_device_ids=true | all-gather | bytes 1105920 | tf_op jit(solution)/shard_map/all_gather | solution.py:763
  51.5 1.2 collective-permute-done.2.refs_1_
  55.2 19.2 %all_gather.11.refs_0_ = bf16[192,2304]{1,0:T(8,128)(2,1)S(1)} all-gather(bf16[48,2304]{1,0:T(8,128)(2,1)S(1)} %get-tuple-element.196), channel_id=1, replica_groups={{0,4,8,12},{1,5,9,13},{2,6,10,14},{3,7,11,15},{16,20,24,28},{17,21,25,2..., dimensions={0}, use_global_device_ids=true | all-gather | bytes 1105920 | tf_op jit(solution)/shard_map/all_gather | solution.py:763
  75.8 1.5 collective-permute-start.14
  77.7 1.1 norm1.1
  79.7 3.5 %attention.1 = (bf16[256,2304]{1,0:T(8,128)(2,1)S(1)}, bf16[256,768]{1,0:T(8,128)(2,1)S(1)}, f32[16,256]{1,0:T(8,128)S(1)}) custom-call(s32[4]{0:T(128)S(1)} %pad_add_fusion.co_ref, bf16[256,768]{1,0:T(8,128)(2,1)S(1)} %get-tuple-element.204.refs_0_, f32[16,768]{1,0:T(8,128)S(1)} %add.77.refs_2_.refs_1_.refs_3_, ...), custom_call_target="tpu_custom_call" | custom-call | flops 1048576 | bytes 1048576 | tf_op jit(solution)/shard_map/attention/pallas_call | solution.py:352
  84.0 1.4 norm2.1
  86.5 6.1 %hidden.1 = (bf16[256,1536]{1,0:T(8,128)(2,1)S(1)}, bf16[256,1536]{1,0:T(8,128)(2,1)S(1)}, f32[256,1536]{1,0:T(8,128)S(1)}, f32[256,1536]{1,0:T(8,128)S(1)}, bf1...) custom-call(s32[4]{0:T(128)S(1)} %pad_add_fusion.co_ref, ...), custom_call_target="tpu_custom_call" | custom-call | flops 1048576 | bytes 1048576 | tf_op jit(solution)/shard_map/hidden/pallas_call | solution.py:352
  92.6 5.3 %collective-permute-done.14.refs_1_ = bf16[192,2304]{1,0:T(8,128)(2,1)S(1)} collective-permute-done((bf16[192,2304]{1,0:T(8,128)(2,1)S(1)}, bf16[192,2304]{1,0:T(8,128)(2,1)S(1)}, u32[]{:S(2)}, u32[]{:S(2)}) %collective-permute-start.14) | collective-permute-done | bytes 884768 | tf_op jit(solution)/shard_map/ppermute | solution.py:742
  97.9 2.4 %collective-permute-done.16.refs_3_ = bf16[192,2304]{1,0:T(8,128)(2,1)S(1)} collective-permute-done((bf16[192,2304]{1,0:T(8,128)(2,1)S(1)}, bf16[192,2304]{1,0:T(8,128)(2,1)S(1)}, u32[]{:S(2)}, u32[]{:S(2)}) %collective-permute-start.16) | collective-permute-done | bytes 884768 | tf_op jit(solution)/shard_map/ppermute | solution.py:742
  101.3 5.5 %hidden_grad.1 = (bf16[256,1536]{1,0:T(8,128)(2,1)S(1)}, bf16[256,1536]{1,0:T(8,128)(2,1)S(1)}, f32[8,768]{1,0:T(8,128)S(1)}, bf16[4,2,48,3072]{3,2,1,0:T(8,128)(2,1)S(1)}, f32[4,2,48,3072]{3,2,1,0:T(8,128)S(1)}) custom-call(s32[4]{0:T(128)S(1)} %pad_add_fusion.co_ref, bf16[256,768]{1,0:T(8,128)(2,1)S(1)} %copy-done.2, ...), custom_call_target="tpu_custom_call" | custom-call | flops 1048576 | bytes 1048576 | tf_op jit(solution)/shard_map/hidden_grad/pallas_call | solution.py:352
  108.1 1.5 collective-permute-start.18
  110.3 3.3 %norm2_back.1 = (f32[256,768]{1,0:T(8,128)S(1)}, bf16[256,768]{1,0:T(8,128)(2,1)S(1)}, bf16[768,256]{1,0:T(8,128)(2,1)S(1)}, f32[8,768]{1,0:T(8,128)S(1)}) custom-call(s32[4]{0:T(128)S(1)} %pad_add_fusion.co_ref, bf16[256,768]{1,0:T(8,128)(2,1)S(1)} %copy-done.2, f32[256,768]{1,0:T(8,128)S(1)} %get-tuple-element.288.refs_1_.refs_0_, ...), custom_call_target="tpu_custom_call" | custom-call | flops 1048576 | bytes 1048576 | tf_op jit(solution)/shard_map/norm2_back/pallas_call | solution.py:352
  113.6 5.6 %attention_back.1 = (bf16[256,2304]{1,0:T(8,128)(2,1)S(1)}, f32[8,768]{1,0:T(8,128)S(1)}) custom-call(s32[4]{0:T(128)S(1)} %pad_add_fusion.co_ref, f32[8,256]{1,0:T(8,128)S(1)} %scatter.4.refs_1_.refs_2_.refs_0_, f32[256,128]{1,0:T(8,128)S(1)} %get-tuple-element.203.refs_3_.refs_1_.refs_2_, f32[16,256]{1,0:T(8,128)S(1)} %get-tuple-element.242.refs_2_, ...), custom_call_target="tpu_custom_call" | custom-call | flops 1048576 | bytes 1048576 | tf_op jit(solution)/shard_map/attention_back/pallas_call | solution.py:352
  119.2 3.1 %attention_grad.1 = (bf16[4,2,48,3072]{3,2,1,0:T(8,128)(2,1)S(1)}, f32[4,2,48,3072]{3,2,1,0:T(8,128)S(1)}) custom-call(s32[4]{0:T(128)S(1)} %pad_add_fusion.co_ref, bf16[768,256]{1,0:T(8,128)(2,1)S(1)} %get-tuple-element.241.refs_0_, bf16[256,2304]{1,0:T(8,128)(2,1)S(1)} %get-tuple-element.265.refs_1_.refs_0_, ...), custom_call_target="tpu_custom_call" | custom-call | flops 1048576 | bytes 1048576 | tf_op jit(solution)/shard_map/attention_grad/pallas_call | solution.py:352
  122.3 1.2 collective-permute-done.18.refs_1_
  123.5 1.2 collective-permute-done.19.refs_1_
  125.4 1.0 split_second.1
  127.8 2.8 %norm1_back.1 = (bf16[256,768]{1,0:T(8,128)(2,1)}, f32[16,768]{1,0:T(8,128)S(1)}) custom-call(s32[4]{0:T(128)S(1)} %pad_add_fusion.co_ref, bf16[256,2304]{1,0:T(8,128)(2,1)S(1)} %get-tuple-element.265.refs_1_.refs_0_, bf16[256,768]{1,0:T(8,128)(2,1)S(1)} %copy-done.3, f32[256,128]{1,0:T(8,128)S(1)} %get-tuple-element.203.refs_3_.refs_1_.refs_2_, ...), custom_call_target="tpu_custom_call" | custom-call | flops 1048576 | bytes 1048576 | tf_op jit(solution)/shard_map/norm1_back/pallas_call | solution.py:352
  130.6 6.0 %collective-permute-done.21.refs_1_ = bf16[96,1536]{1,0:T(8,128)(2,1)S(1)} collective-permute-done((bf16[96,1536]{1,0:T(8,128)(2,1)S(1)}, bf16[96,1536]{1,0:T(8,128)(2,1)S(1)}, u32[]{:S(2)}, u32[]{:S(2)}) %collective-permute-start.21) | collective-permute-done | bytes 294944 | tf_op jit(solution)/shard_map/ppermute | solution.py:742
  136.6 5.9 %collective-permute-done.23.refs_1_ = bf16[4,2,48,768]{3,2,1,0:T(8,128)(2,1)S(1)} collective-permute-done((bf16[4,2,48,768]{3,2,1,0:T(8,128)(2,1)S(1)}, bf16[4,2,48,768]{3,2,1,0:T(8,128)(2,1)S(1)}, u32[]{:S(2)}, u32[]{:S(2)}) %collective-permute-start.23) | collective-permute-done | bytes 589856 | tf_op jit(solution)/shard_map/ppermute | solution.py:742
  142.4 6.1 %collective-permute-done.22.refs_1_ = bf16[192,2304]{1,0:T(8,128)(2,1)S(1)} collective-permute-done((bf16[192,2304]{1,0:T(8,128)(2,1)S(1)}, bf16[192,2304]{1,0:T(8,128)(2,1)S(1)}, u32[]{:S(2)}, u32[]{:S(2)}) %collective-permute-start.22) | collective-permute-done | bytes 884768 | tf_op jit(solution)/shard_map/ppermute | solution.py:742
  149.9 1.0 split_third.1
  152.2 2.5 %collective-permute-start.25 = (bf16[48,1536]{1,0:T(8,128)(2,1)S(1)}, bf16[48,1536]{1,0:T(8,128)(2,1)S(1)}, u32[]{:S(2)}, u32[]{:S(2)}) collective-permute-start(bf16[48,1536]{1,0:T(8,128)(2,1)S(1)} %get-tuple-element.283), channel_id=1, source_target_pairs={{0,8},{1,9},{2,10},{3,11},{4,12},{5,13},{6,14},{7,15},{8,0},{9,1},... | collective-permute-start | bytes 442376 | tf_op jit(solution)/shard_map/ppermute | solution.py:742
  154.7 2.7 %output.1 = bf16[256,768]{1,0:T(8,128)(2,1)} custom-call(s32[4]{0:T(128)S(1)} %pad_add_fusion.co_ref, f32[256,768]{1,0:T(8,128)S(1)} %get-tuple-element.288.refs_1_.refs_0_, f32[16,768]{1,0:T(8,128)S(1)} %add.77.refs_2_.refs_1_.refs_3_, bf16[256,1536]{1,0:T(8,128)(2,1)S(1)} %get-tuple-element.289.refs_2_, bf16[256,1536]{1,0:T(8,128)(2,1)S(1)} %get-tuple-element.290.refs_3_, ...), custom_call_target="tpu_custom_call" | custom-call | flops 1048576 | bytes 1048576 | tf_op jit(solution)/shard_map/output/pallas_call | solution.py:352
  157.5 6.9 %collective-permute-done.25.refs_1_ = bf16[48,1536]{1,0:T(8,128)(2,1)S(1)} collective-permute-done((bf16[48,1536]{1,0:T(8,128)(2,1)S(1)}, bf16[48,1536]{1,0:T(8,128)(2,1)S(1)}, u32[]{:S(2)}, u32[]{:S(2)}) %collective-permute-start.25) | collective-permute-done | bytes 147488 | tf_op jit(solution)/shard_map/ppermute | solution.py:742
  164.3 2.2 %collective-permute-done.26.refs_1_ = bf16[96,2304]{1,0:T(8,128)(2,1)S(1)} collective-permute-done((bf16[96,2304]{1,0:T(8,128)(2,1)S(1)}, bf16[96,2304]{1,0:T(8,128)(2,1)S(1)}, u32[]{:S(2)}, u32[]{:S(2)}) %collective-permute-start.26) | collective-permute-done | bytes 442400 | tf_op jit(solution)/shard_map/ppermute | solution.py:742
  169.2 1.6 collective-permute-start.33
  171.6 1.6 collective-permute-start.31
  173.3 1.5 collective-permute-start.30
  174.8 3.6 %collective-permute-done.30.refs_4_ = bf16[48,1536]{1,0:T(8,128)(2,1)S(1)} collective-permute-done((bf16[48,1536]{1,0:T(8,128)(2,1)S(1)}, bf16[48,1536]{1,0:T(8,128)(2,1)S(1)}, u32[]{:S(2)}, u32[]{:S(2)}) %collective-permute-start.30) | collective-permute-done | bytes 147488 | tf_op jit(solution)/shard_map/ppermute | solution.py:742
  178.4 2.6 %collective-permute-done.31.refs_1_ = bf16[48,2304]{1,0:T(8,128)(2,1)S(1)} collective-permute-done((bf16[48,2304]{1,0:T(8,128)(2,1)S(1)}, bf16[48,2304]{1,0:T(8,128)(2,1)S(1)}, u32[]{:S(2)}, u32[]{:S(2)}) %collective-permute-start.31) | collective-permute-done | bytes 221216 | tf_op jit(solution)/shard_map/ppermute | solution.py:742
  181.0 2.2 %collective-permute-done.32.refs_1_ = bf16[96,1536]{1,0:T(8,128)(2,1)S(1)} collective-permute-done((bf16[96,1536]{1,0:T(8,128)(2,1)S(1)}, bf16[96,1536]{1,0:T(8,128)(2,1)S(1)}, u32[]{:S(2)}, u32[]{:S(2)}) %collective-permute-start.32) | collective-permute-done | bytes 294944 | tf_op jit(solution)/shard_map/ppermute | solution.py:742
  183.2 1.4 collective-permute-done.33.refs_1_
  186.5 1.4 collective-permute-start.34
  187.9 2.6 %collective-permute-start.35 = (bf16[48,1536]{1,0:T(8,128)(2,1)S(1)}, bf16[48,1536]{1,0:T(8,128)(2,1)S(1)}, u32[]{:S(2)}, u32[]{:S(2)}) collective-permute-start(bf16[48,1536]{1,0:T(8,128)(2,1)S(1)} %get-tuple-element.321), channel_id=1, source_target_pairs={{0,8},{1,9},{2,10},{3,11},{4,12},{5,13},{6,14},{7,15},{8,0},{9,1},... | collective-permute-start | bytes 442376 | tf_op jit(solution)/shard_map/ppermute | solution.py:742
  190.6 7.2 %collective-permute-done.37 = f32[16,768]{1,0:T(8,128)S(1)} collective-permute-done((f32[16,768]{1,0:T(8,128)S(1)}, f32[16,768]{1,0:T(8,128)S(1)}, u32[]{:S(2)}, u32[]{:S(2)}) %collective-permute-start.37) | collective-permute-done | bytes 49184 | tf_op jit(solution)/shard_map/ppermute | solution.py:742
  199.7 1.6 collective-permute-start.38
  201.3 2.0 collective-permute-start.40
  203.3 4.9 %collective-permute-done.40 = f32[16,768]{1,0:T(8,128)S(1)} collective-permute-done((f32[16,768]{1,0:T(8,128)S(1)}, f32[16,768]{1,0:T(8,128)S(1)}, u32[]{:S(2)}, u32[]{:S(2)}) %collective-permute-start.40) | collective-permute-done | bytes 49184 | tf_op jit(solution)/shard_map/ppermute | solution.py:742
  208.2 2.4 %collective-permute-start.42 = (f32[16,768]{1,0:T(8,128)S(1)}, f32[16,768]{1,0:T(8,128)S(1)}, u32[]{:S(2)}, u32[]{:S(2)}) collective-permute-start(f32[16,768]{1,0:T(8,128)S(1)} %add.80), channel_id=1, source_target_pairs={{0,16},{1,17},{2,18},{3,19},{4,20},{5,21},{6,22},{7,23},{8,24},{9,... | collective-permute-start | bytes 147464 | tf_op jit(solution)/shard_map/ppermute | solution.py:742
  211.5 3.0 %update_mlp.1 = (f32[48,6144]{1,0:T(8,128)}, f32[48,6144]{1,0:T(8,128)}, f32[48,6144]{1,0:T(8,128)}, bf16[48,6144]{1,0:T(8,128)(2,1)}) custom-call(s32[4]{0:T(128)S(1)} %pad_add_fusion.co_ref, f32[48,6144]{1,0:T(8,128)S(1)} %copy-done.1, f32[48,6144]{1,0:T(8,128)S(1)} %copy-done.6, f32[48,6144]{1,0:T(8,128)S(1)} %copy-done.7, ...), custom_call_target="tpu_custom_call" | custom-call | flops 1048576 | bytes 1048576 | tf_op jit(solution)/shard_map/update_mlp/pallas_call | solution.py:352
  217.0 2.1 update_attn.1
  (136 shorter events, 28.6 us)
Async XLA Ops:
  2.2 3.6 %collective-permute-start = (f32[16,768]{1,0:T(8,128)S(1)}, f32[16,768]{1,0:T(8,128)S(1)}, u32[]{:S(2)}, u32[]{:S(2)}) collective-permute-start(f32[16,768]{1,0:T(8,128)S(1)} %reshape.68), channel_id=1, source_target_pairs={{0,1},{1,0},{2,3},{3,2},{4,5},{5,4},{6,7},{7,6},{8,9},{9,8},{10,11... | collective-permute-start | bytes 147464 | tf_op jit(solution)/shard_map/ppermute | solution.py:742
  5.8 23.5 %collective-permute-start.1 = (f32[16,768]{1,0:T(8,128)S(1)}, f32[16,768]{1,0:T(8,128)S(1)}, u32[]{:S(2)}, u32[]{:S(2)}) collective-permute-start(f32[16,768]{1,0:T(8,128)S(1)} %add.74), channel_id=1, source_target_pairs={{0,2},{1,3},{2,0},{3,1},{4,6},{5,7},{6,4},{7,5},{8,10},{9,11},{10,... | collective-permute-start | bytes 147464 | tf_op jit(solution)/shard_map/ppermute | solution.py:742
  29.4 48.0 %copy-start.14 = (s32[256]{0:T(256)S(1)}, s32[256]{0:T(256)}, u32[]{:S(2)}) copy-start(s32[256]{0:T(256)} %param.23) | copy-start | bytes 3076
  29.4 48.0 %copy-start.15 = (s32[256]{0:T(256)S(1)}, s32[256]{0:T(256)}, u32[]{:S(2)}) copy-start(s32[256]{0:T(256)} %param.22) | copy-start | bytes 3076
  29.4 48.0 %copy-start.16 = (s32[256]{0:T(256)S(1)}, s32[256]{0:T(256)}, u32[]{:S(2)}) copy-start(s32[256]{0:T(256)} %param.21) | copy-start | bytes 3076
  29.4 48.3 %copy-start.3 = (bf16[256,768]{1,0:T(8,128)(2,1)S(1)}, bf16[256,768]{1,0:T(8,128)(2,1)}, u32[]{:S(2)}) copy-start(bf16[256,768]{1,0:T(8,128)(2,1)} %refs_1_.5) | copy-start | bytes 1179652
  29.4 21.8 %collective-permute-start.4 = (bf16[192,2304]{1,0:T(8,128)(2,1)S(1)}, bf16[192,2304]{1,0:T(8,128)(2,1)S(1)}, u32[]{:S(2)}, u32[]{:S(2)}) collective-permute-start(bf16[192,2304]{1,0:T(8,128)(2,1)S(1)} %all_gather.9.refs_0_), channel_id=1, source_target_pairs={{0,1},{1,0},{2,3},{3,2},{4,5},{5,4},{6,7},{7,6},{8,9},{9,8},{10,11... | collective-permute-start | bytes 2654216 | tf_op jit(solution)/shard_map/ppermute | solution.py:742
  29.5 22.1 %collective-permute-start.3 = (bf16[192,2304]{1,0:T(8,128)(2,1)S(1)}, bf16[192,2304]{1,0:T(8,128)(2,1)S(1)}, u32[]{:S(2)}, u32[]{:S(2)}) collective-permute-start(bf16[192,2304]{1,0:T(8,128)(2,1)S(1)} %all_gather.9.refs_0_), channel_id=1, source_target_pairs={{0,16},{1,17},{2,18},{3,19},{4,20},{5,21},{6,22},{7,23},{8,24},{9,... | collective-permute-start | bytes 2654216 | tf_op jit(solution)/shard_map/ppermute | solution.py:742
  31.0 21.7 %collective-permute-start.2 = (bf16[192,2304]{1,0:T(8,128)(2,1)S(1)}, bf16[192,2304]{1,0:T(8,128)(2,1)S(1)}, u32[]{:S(2)}, u32[]{:S(2)}) collective-permute-start(bf16[192,2304]{1,0:T(8,128)(2,1)S(1)} %all_gather.9.refs_0_), channel_id=1, source_target_pairs={{0,2},{1,3},{2,0},{3,1},{4,6},{5,7},{6,4},{7,5},{8,10},{9,11},{10,... | collective-permute-start | bytes 2654216 | tf_op jit(solution)/shard_map/ppermute | solution.py:742
  31.5 19.7 %collective-permute-start.5 = (f32[16,768]{1,0:T(8,128)S(1)}, f32[16,768]{1,0:T(8,128)S(1)}, u32[]{:S(2)}, u32[]{:S(2)}) collective-permute-start(f32[16,768]{1,0:T(8,128)S(1)} %add.75), channel_id=1, source_target_pairs={{0,4},{1,5},{2,6},{3,7},{4,0},{5,1},{6,2},{7,3},{8,12},{9,13},{10,... | collective-permute-start | bytes 147464 | tf_op jit(solution)/shard_map/ppermute | solution.py:742
  52.8 21.7 %collective-permute-start.6 = (bf16[192,2304]{1,0:T(8,128)(2,1)S(1)}, bf16[192,2304]{1,0:T(8,128)(2,1)S(1)}, u32[]{:S(2)}, u32[]{:S(2)}) collective-permute-start(bf16[192,2304]{1,0:T(8,128)(2,1)S(1)} %all_gather.10.refs_0_), channel_id=1, source_target_pairs={{0,2},{1,3},{2,0},{3,1},{4,6},{5,7},{6,4},{7,5},{8,10},{9,11},{10,... | collective-permute-start | bytes 2654216 | tf_op jit(solution)/shard_map/ppermute | solution.py:742
  53.3 21.2 %collective-permute-start.9 = (bf16[192,2304]{1,0:T(8,128)(2,1)S(1)}, bf16[192,2304]{1,0:T(8,128)(2,1)S(1)}, u32[]{:S(2)}, u32[]{:S(2)}) collective-permute-start(bf16[192,2304]{1,0:T(8,128)(2,1)S(1)} %collective-permute-done.3.refs_2_), channel_id=1, source_target_pairs={{0,1},{1,0},{2,3},{3,2},{4,5},{5,4},{6,7},{7,6},{8,9},{9,8},{10,11... | collective-permute-start | bytes 2654216 | tf_op jit(solution)/shard_map/ppermute | solution.py:742
  53.3 21.2 %collective-permute-start.8 = (bf16[192,2304]{1,0:T(8,128)(2,1)S(1)}, bf16[192,2304]{1,0:T(8,128)(2,1)S(1)}, u32[]{:S(2)}, u32[]{:S(2)}) collective-permute-start(bf16[192,2304]{1,0:T(8,128)(2,1)S(1)} %collective-permute-done.2.refs_1_), channel_id=1, source_target_pairs={{0,1},{1,0},{2,3},{3,2},{4,5},{5,4},{6,7},{7,6},{8,9},{9,8},{10,11... | collective-permute-start | bytes 2654216 | tf_op jit(solution)/shard_map/ppermute | solution.py:742
  53.8 21.6 %collective-permute-start.7 = (bf16[192,2304]{1,0:T(8,128)(2,1)S(1)}, bf16[192,2304]{1,0:T(8,128)(2,1)S(1)}, u32[]{:S(2)}, u32[]{:S(2)}) collective-permute-start(bf16[192,2304]{1,0:T(8,128)(2,1)S(1)} %collective-permute-done.2.refs_1_), channel_id=1, source_target_pairs={{0,16},{1,17},{2,18},{3,19},{4,20},{5,21},{6,22},{7,23},{8,24},{9,... | collective-permute-start | bytes 2654216 | tf_op jit(solution)/shard_map/ppermute | solution.py:742
  54.3 20.1 %collective-permute-start.10 = (f32[16,768]{1,0:T(8,128)S(1)}, f32[16,768]{1,0:T(8,128)S(1)}, u32[]{:S(2)}, u32[]{:S(2)}) collective-permute-start(f32[16,768]{1,0:T(8,128)S(1)} %add.76), channel_id=1, source_target_pairs={{0,8},{1,9},{2,10},{3,11},{4,12},{5,13},{6,14},{7,15},{8,0},{9,1},... | collective-permute-start | bytes 147464 | tf_op jit(solution)/shard_map/ppermute | solution.py:742
  75.3 3.5 %collective-permute-start.11 = (bf16[192,2304]{1,0:T(8,128)(2,1)S(1)}, bf16[192,2304]{1,0:T(8,128)(2,1)S(1)}, u32[]{:S(2)}, u32[]{:S(2)}) collective-permute-start(bf16[192,2304]{1,0:T(8,128)(2,1)S(1)} %collective-permute-done.7.refs_3_), channel_id=1, source_target_pairs={{0,1},{1,0},{2,3},{3,2},{4,5},{5,4},{6,7},{7,6},{8,9},{9,8},{10,11... | collective-permute-start | bytes 2654216 | tf_op jit(solution)/shard_map/ppermute | solution.py:742
  75.3 10.2 %collective-permute-start.12 = (bf16[192,2304]{1,0:T(8,128)(2,1)S(1)}, bf16[192,2304]{1,0:T(8,128)(2,1)S(1)}, u32[]{:S(2)}, u32[]{:S(2)}) collective-permute-start(bf16[192,2304]{1,0:T(8,128)(2,1)S(1)} %all_gather.10.refs_0_), channel_id=1, source_target_pairs={{0,1},{1,0},{2,3},{3,2},{4,5},{5,4},{6,7},{7,6},{8,9},{9,8},{10,11... | collective-permute-start | bytes 2654216 | tf_op jit(solution)/shard_map/ppermute | solution.py:742
  75.8 9.7 %collective-permute-start.13 = (bf16[192,2304]{1,0:T(8,128)(2,1)S(1)}, bf16[192,2304]{1,0:T(8,128)(2,1)S(1)}, u32[]{:S(2)}, u32[]{:S(2)}) collective-permute-start(bf16[192,2304]{1,0:T(8,128)(2,1)S(1)} %collective-permute-done.6.refs_1_), channel_id=1, source_target_pairs={{0,1},{1,0},{2,3},{3,2},{4,5},{5,4},{6,7},{7,6},{8,9},{9,8},{10,11... | collective-permute-start | bytes 2654216 | tf_op jit(solution)/shard_map/ppermute | solution.py:742
  75.8 22.1 %collective-permute-start.14 = (bf16[192,2304]{1,0:T(8,128)(2,1)S(1)}, bf16[192,2304]{1,0:T(8,128)(2,1)S(1)}, u32[]{:S(2)}, u32[]{:S(2)}) collective-permute-start(bf16[192,2304]{1,0:T(8,128)(2,1)S(1)} %all_gather.11.refs_0_), channel_id=1, source_target_pairs={{0,2},{1,3},{2,0},{3,1},{4,6},{5,7},{6,4},{7,5},{8,10},{9,11},{10,... | collective-permute-start | bytes 2654216 | tf_op jit(solution)/shard_map/ppermute | solution.py:742
  77.4 20.5 %collective-permute-start.15 = (bf16[192,2304]{1,0:T(8,128)(2,1)S(1)}, bf16[192,2304]{1,0:T(8,128)(2,1)S(1)}, u32[]{:S(2)}, u32[]{:S(2)}) collective-permute-start(bf16[192,2304]{1,0:T(8,128)(2,1)S(1)} %all_gather.11.refs_0_), channel_id=1, source_target_pairs={{0,1},{1,0},{2,3},{3,2},{4,5},{5,4},{6,7},{7,6},{8,9},{9,8},{10,11... | collective-permute-start | bytes 2654216 | tf_op jit(solution)/shard_map/ppermute | solution.py:742
  97.9 2.4 %collective-permute-start.16 = (bf16[192,2304]{1,0:T(8,128)(2,1)S(1)}, bf16[192,2304]{1,0:T(8,128)(2,1)S(1)}, u32[]{:S(2)}, u32[]{:S(2)}) collective-permute-start(bf16[192,2304]{1,0:T(8,128)(2,1)S(1)} %collective-permute-done.14.refs_1_), channel_id=1, source_target_pairs={{0,1},{1,0},{2,3},{3,2},{4,5},{5,4},{6,7},{7,6},{8,9},{9,8},{10,11... | collective-permute-start | bytes 2654216 | tf_op jit(solution)/shard_map/ppermute | solution.py:742
  100.3 6.4 %collective-permute-start.17 = (bf16[4,2,48,3072]{3,2,1,0:T(8,128)(2,1)S(1)}, bf16[4,2,48,3072]{3,2,1,0:T(8,128)(2,1)S(1)}, u32[]{:S(2)}, u32[]{:S(2)}) collective-permute-start(bf16[4,2,48,3072]{3,2,1,0:T(8,128)(2,1)S(1)} %get-tuple-element.220), channel_id=1, source_target_pairs={{0,1},{1,0},{2,3},{3,2},{4,5},{5,4},{6,7},{7,6},{8,9},{9,8},{10,11... | collective-permute-start | bytes 7077896 | tf_op jit(solution)/shard_map/ppermute | solution.py:742
  107.7 17.1 %collective-permute-start.20 = (bf16[4,2,48,3072]{3,2,1,0:T(8,128)(2,1)S(1)}, bf16[4,2,48,3072]{3,2,1,0:T(8,128)(2,1)S(1)}, u32[]{:S(2)}, u32[]{:S(2)}) collective-permute-start(bf16[4,2,48,3072]{3,2,1,0:T(8,128)(2,1)S(1)} %get-tuple-element.240), channel_id=1, source_target_pairs={{0,1},{1,0},{2,3},{3,2},{4,5},{5,4},{6,7},{7,6},{8,9},{9,8},{10,11... | collective-permute-start | bytes 7077896 | tf_op jit(solution)/shard_map/ppermute | solution.py:742
  108.1 15.3 %collective-permute-start.18 = (bf16[192,1536]{1,0:T(8,128)(2,1)S(1)}, bf16[192,1536]{1,0:T(8,128)(2,1)S(1)}, u32[]{:S(2)}, u32[]{:S(2)}) collective-permute-start(bf16[192,1536]{1,0:T(8,128)(2,1)S(1)} %get-tuple-element.238), channel_id=1, source_target_pairs={{0,2},{1,3},{2,0},{3,1},{4,6},{5,7},{6,4},{7,5},{8,10},{9,11},{10,... | collective-permute-start | bytes 1769480 | tf_op jit(solution)/shard_map/ppermute | solution.py:742
  109.6 15.1 %collective-permute-start.19 = (bf16[4,2,48,768]{3,2,1,0:T(8,128)(2,1)S(1)}, bf16[4,2,48,768]{3,2,1,0:T(8,128)(2,1)S(1)}, u32[]{:S(2)}, u32[]{:S(2)}) collective-permute-start(bf16[4,2,48,768]{3,2,1,0:T(8,128)(2,1)S(1)} %get-tuple-element.239), channel_id=1, source_target_pairs={{0,16},{1,17},{2,18},{3,19},{4,20},{5,21},{6,22},{7,23},{8,24},{9,... | collective-permute-start | bytes 1769480 | tf_op jit(solution)/shard_map/ppermute | solution.py:742
  126.4 22.1 %collective-permute-start.24 = (bf16[4,2,48,3072]{3,2,1,0:T(8,128)(2,1)S(1)}, bf16[4,2,48,3072]{3,2,1,0:T(8,128)(2,1)S(1)}, u32[]{:S(2)}, u32[]{:S(2)}) collective-permute-start(bf16[4,2,48,3072]{3,2,1,0:T(8,128)(2,1)S(1)} %get-tuple-element.264), channel_id=1, source_target_pairs={{0,1},{1,0},{2,3},{3,2},{4,5},{5,4},{6,7},{7,6},{8,9},{9,8},{10,11... | collective-permute-start | bytes 7077896 | tf_op jit(solution)/shard_map/ppermute | solution.py:742
  126.5 22.1 %collective-permute-start.22 = (bf16[192,2304]{1,0:T(8,128)(2,1)S(1)}, bf16[192,2304]{1,0:T(8,128)(2,1)S(1)}, u32[]{:S(2)}, u32[]{:S(2)}) collective-permute-start(bf16[192,2304]{1,0:T(8,128)(2,1)S(1)} %get-tuple-element.262), channel_id=1, source_target_pairs={{0,2},{1,3},{2,0},{3,1},{4,6},{5,7},{6,4},{7,5},{8,10},{9,11},{10,... | collective-permute-start | bytes 2654216 | tf_op jit(solution)/shard_map/ppermute | solution.py:742
  127.0 15.4 %collective-permute-start.23 = (bf16[4,2,48,768]{3,2,1,0:T(8,128)(2,1)S(1)}, bf16[4,2,48,768]{3,2,1,0:T(8,128)(2,1)S(1)}, u32[]{:S(2)}, u32[]{:S(2)}) collective-permute-start(bf16[4,2,48,768]{3,2,1,0:T(8,128)(2,1)S(1)} %get-tuple-element.263), channel_id=1, source_target_pairs={{0,16},{1,17},{2,18},{3,19},{4,20},{5,21},{6,22},{7,23},{8,24},{9,... | collective-permute-start | bytes 1769480 | tf_op jit(solution)/shard_map/ppermute | solution.py:742
  127.8 8.8 %collective-permute-start.21 = (bf16[96,1536]{1,0:T(8,128)(2,1)S(1)}, bf16[96,1536]{1,0:T(8,128)(2,1)S(1)}, u32[]{:S(2)}, u32[]{:S(2)}) collective-permute-start(bf16[96,1536]{1,0:T(8,128)(2,1)S(1)} %get-tuple-element.261), channel_id=1, source_target_pairs={{0,4},{1,5},{2,6},{3,7},{4,0},{5,1},{6,2},{7,3},{8,12},{9,13},{10,... | collective-permute-start | bytes 884744 | tf_op jit(solution)/shard_map/ppermute | solution.py:742
  150.9 15.6 %collective-permute-start.27 = (bf16[192,1536]{1,0:T(8,128)(2,1)S(1)}, bf16[192,1536]{1,0:T(8,128)(2,1)S(1)}, u32[]{:S(2)}, u32[]{:S(2)}) collective-permute-start(bf16[192,1536]{1,0:T(8,128)(2,1)S(1)} %get-tuple-element.285), channel_id=1, source_target_pairs={{0,2},{1,3},{2,0},{3,1},{4,6},{5,7},{6,4},{7,5},{8,10},{9,11},{10,... | collective-permute-start | bytes 1769480 | tf_op jit(solution)/shard_map/ppermute | solution.py:742
  151.5 15.0 %collective-permute-start.28 = (bf16[4,2,48,768]{3,2,1,0:T(8,128)(2,1)S(1)}, bf16[4,2,48,768]{3,2,1,0:T(8,128)(2,1)S(1)}, u32[]{:S(2)}, u32[]{:S(2)}) collective-permute-start(bf16[4,2,48,768]{3,2,1,0:T(8,128)(2,1)S(1)} %get-tuple-element.286), channel_id=1, source_target_pairs={{0,16},{1,17},{2,18},{3,19},{4,20},{5,21},{6,22},{7,23},{8,24},{9,... | collective-permute-start | bytes 1769480 | tf_op jit(solution)/shard_map/ppermute | solution.py:742
  152.2 14.3 %collective-permute-start.26 = (bf16[96,2304]{1,0:T(8,128)(2,1)S(1)}, bf16[96,2304]{1,0:T(8,128)(2,1)S(1)}, u32[]{:S(2)}, u32[]{:S(2)}) collective-permute-start(bf16[96,2304]{1,0:T(8,128)(2,1)S(1)} %get-tuple-element.284), channel_id=1, source_target_pairs={{0,4},{1,5},{2,6},{3,7},{4,0},{5,1},{6,2},{7,3},{8,12},{9,13},{10,... | collective-permute-start | bytes 1327112 | tf_op jit(solution)/shard_map/ppermute | solution.py:742
  152.2 12.1 %collective-permute-start.25 = (bf16[48,1536]{1,0:T(8,128)(2,1)S(1)}, bf16[48,1536]{1,0:T(8,128)(2,1)S(1)}, u32[]{:S(2)}, u32[]{:S(2)}) collective-permute-start(bf16[48,1536]{1,0:T(8,128)(2,1)S(1)} %get-tuple-element.283), channel_id=1, source_target_pairs={{0,8},{1,9},{2,10},{3,11},{4,12},{5,13},{6,14},{7,15},{8,0},{9,1},... | collective-permute-start | bytes 442376 | tf_op jit(solution)/shard_map/ppermute | solution.py:742
  154.7 2.7 %collective-permute-start.29 = (f32[16,768]{1,0:T(8,128)S(1)}, f32[16,768]{1,0:T(8,128)S(1)}, u32[]{:S(2)}, u32[]{:S(2)}) collective-permute-start(f32[16,768]{1,0:T(8,128)S(1)} %get-tuple-element.287), channel_id=1, source_target_pairs={{0,1},{1,0},{2,3},{3,2},{4,5},{5,4},{6,7},{7,6},{8,9},{9,8},{10,11... | collective-permute-start | bytes 147464 | tf_op jit(solution)/shard_map/ppermute | solution.py:742
  169.2 15.4 %collective-permute-start.33 = (bf16[208,1536]{1,0:T(8,128)(2,1)S(1)}, bf16[208,1536]{1,0:T(8,128)(2,1)S(1)}, u32[]{:S(2)}, u32[]{:S(2)}) collective-permute-start(bf16[208,1536]{1,0:T(8,128)(2,1)S(1)} %get-tuple-element.310), channel_id=1, source_target_pairs={{0,2},{1,3},{2,0},{3,1},{4,6},{5,7},{6,4},{7,5},{8,10},{9,11},{10,... | collective-permute-start | bytes 1916936 | tf_op jit(solution)/shard_map/ppermute | solution.py:742
  170.7 12.4 %collective-permute-start.32 = (bf16[96,1536]{1,0:T(8,128)(2,1)S(1)}, bf16[96,1536]{1,0:T(8,128)(2,1)S(1)}, u32[]{:S(2)}, u32[]{:S(2)}) collective-permute-start(bf16[96,1536]{1,0:T(8,128)(2,1)S(1)} %get-tuple-element.309), channel_id=1, source_target_pairs={{0,4},{1,5},{2,6},{3,7},{4,0},{5,1},{6,2},{7,3},{8,12},{9,13},{10,... | collective-permute-start | bytes 884744 | tf_op jit(solution)/shard_map/ppermute | solution.py:742
  171.6 9.4 %collective-permute-start.31 = (bf16[48,2304]{1,0:T(8,128)(2,1)S(1)}, bf16[48,2304]{1,0:T(8,128)(2,1)S(1)}, u32[]{:S(2)}, u32[]{:S(2)}) collective-permute-start(bf16[48,2304]{1,0:T(8,128)(2,1)S(1)} %get-tuple-element.308), channel_id=1, source_target_pairs={{0,8},{1,9},{2,10},{3,11},{4,12},{5,13},{6,14},{7,15},{8,0},{9,1},... | collective-permute-start | bytes 663560 | tf_op jit(solution)/shard_map/ppermute | solution.py:742
  173.3 5.1 %collective-permute-start.30 = (bf16[48,1536]{1,0:T(8,128)(2,1)S(1)}, bf16[48,1536]{1,0:T(8,128)(2,1)S(1)}, u32[]{:S(2)}, u32[]{:S(2)}) collective-permute-start(bf16[48,1536]{1,0:T(8,128)(2,1)S(1)} %sum_far.4.refs_3_), channel_id=1, source_target_pairs={{0,16},{1,17},{2,18},{3,19},{4,20},{5,21},{6,22},{7,23},{8,24},{9,... | collective-permute-start | bytes 442376 | tf_op jit(solution)/shard_map/ppermute | solution.py:742
  185.2 26.2 %copy-start.7 = (f32[48,6144]{1,0:T(8,128)S(1)}, f32[48,6144]{1,0:T(8,128)}, u32[]{:S(2)}) copy-start(f32[48,6144]{1,0:T(8,128)} %refs_2_.5) | copy-start | bytes 3538948
  186.5 11.3 %collective-permute-start.36 = (bf16[96,1536]{1,0:T(8,128)(2,1)S(1)}, bf16[96,1536]{1,0:T(8,128)(2,1)S(1)}, u32[]{:S(2)}, u32[]{:S(2)}) collective-permute-start(bf16[96,1536]{1,0:T(8,128)(2,1)S(1)} %get-tuple-element.322), channel_id=1, source_target_pairs={{0,4},{1,5},{2,6},{3,7},{4,0},{5,1},{6,2},{7,3},{8,12},{9,13},{10,... | collective-permute-start | bytes 884744 | tf_op jit(solution)/shard_map/ppermute | solution.py:742
  186.5 11.3 %collective-permute-start.34 = (bf16[48,2304]{1,0:T(8,128)(2,1)S(1)}, bf16[48,2304]{1,0:T(8,128)(2,1)S(1)}, u32[]{:S(2)}, u32[]{:S(2)}) collective-permute-start(bf16[48,2304]{1,0:T(8,128)(2,1)S(1)} %sum_far.5.refs_5_), channel_id=1, source_target_pairs={{0,16},{1,17},{2,18},{3,19},{4,20},{5,21},{6,22},{7,23},{8,24},{9,... | collective-permute-start | bytes 663560 | tf_op jit(solution)/shard_map/ppermute | solution.py:742
  187.9 9.9 %collective-permute-start.35 = (bf16[48,1536]{1,0:T(8,128)(2,1)S(1)}, bf16[48,1536]{1,0:T(8,128)(2,1)S(1)}, u32[]{:S(2)}, u32[]{:S(2)}) collective-permute-start(bf16[48,1536]{1,0:T(8,128)(2,1)S(1)} %get-tuple-element.321), channel_id=1, source_target_pairs={{0,8},{1,9},{2,10},{3,11},{4,12},{5,13},{6,14},{7,15},{8,0},{9,1},... | collective-permute-start | bytes 442376 | tf_op jit(solution)/shard_map/ppermute | solution.py:742
  190.5 7.2 %collective-permute-start.37 = (f32[16,768]{1,0:T(8,128)S(1)}, f32[16,768]{1,0:T(8,128)S(1)}, u32[]{:S(2)}, u32[]{:S(2)}) collective-permute-start(f32[16,768]{1,0:T(8,128)S(1)} %get-tuple-element.323), channel_id=1, source_target_pairs={{0,4},{1,5},{2,6},{3,7},{4,0},{5,1},{6,2},{7,3},{8,12},{9,13},{10,... | collective-permute-start | bytes 147464 | tf_op jit(solution)/shard_map/ppermute | solution.py:742
  199.0 9.2 %collective-permute-start.39 = (bf16[48,1536]{1,0:T(8,128)(2,1)S(1)}, bf16[48,1536]{1,0:T(8,128)(2,1)S(1)}, u32[]{:S(2)}, u32[]{:S(2)}) collective-permute-start(bf16[48,1536]{1,0:T(8,128)(2,1)S(1)} %get-tuple-element.330), channel_id=1, source_target_pairs={{0,8},{1,9},{2,10},{3,11},{4,12},{5,13},{6,14},{7,15},{8,0},{9,1},... | collective-permute-start | bytes 442376 | tf_op jit(solution)/shard_map/ppermute | solution.py:742
  199.7 8.5 %collective-permute-start.38 = (bf16[48,1536]{1,0:T(8,128)(2,1)S(1)}, bf16[48,1536]{1,0:T(8,128)(2,1)S(1)}, u32[]{:S(2)}, u32[]{:S(2)}) collective-permute-start(bf16[48,1536]{1,0:T(8,128)(2,1)S(1)} %sum_far.6.refs_3_.refs_7_), channel_id=1, source_target_pairs={{0,16},{1,17},{2,18},{3,19},{4,20},{5,21},{6,22},{7,23},{8,24},{9,... | collective-permute-start | bytes 442376 | tf_op jit(solution)/shard_map/ppermute | solution.py:742
  201.3 6.9 %collective-permute-start.40 = (f32[16,768]{1,0:T(8,128)S(1)}, f32[16,768]{1,0:T(8,128)S(1)}, u32[]{:S(2)}, u32[]{:S(2)}) collective-permute-start(f32[16,768]{1,0:T(8,128)S(1)} %add.79), channel_id=1, source_target_pairs={{0,8},{1,9},{2,10},{3,11},{4,12},{5,13},{6,14},{7,15},{8,0},{9,1},... | collective-permute-start | bytes 147464 | tf_op jit(solution)/shard_map/ppermute | solution.py:742
  208.2 6.3 %collective-permute-start.42 = (f32[16,768]{1,0:T(8,128)S(1)}, f32[16,768]{1,0:T(8,128)S(1)}, u32[]{:S(2)}, u32[]{:S(2)}) collective-permute-start(f32[16,768]{1,0:T(8,128)S(1)} %add.80), channel_id=1, source_target_pairs={{0,16},{1,17},{2,18},{3,19},{4,20},{5,21},{6,22},{7,23},{8,24},{9,... | collective-permute-start | bytes 147464 | tf_op jit(solution)/shard_map/ppermute | solution.py:742
  211.4 5.6 %collective-permute-start.41 = (bf16[48,1536]{1,0:T(8,128)(2,1)S(1)}, bf16[48,1536]{1,0:T(8,128)(2,1)S(1)}, u32[]{:S(2)}, u32[]{:S(2)}) collective-permute-start(bf16[48,1536]{1,0:T(8,128)(2,1)S(1)} %sum_far.7.refs_5_), channel_id=1, source_target_pairs={{0,16},{1,17},{2,18},{3,19},{4,20},{5,21},{6,22},{7,23},{8,24},{9,... | collective-permute-start | bytes 442376 | tf_op jit(solution)/shard_map/ppermute | solution.py:742
  (16 other events, 101.2 us)

commit v4 on v3

--- a/solution.py
+++ b/solution.py
@@ -338,13 +338,13 @@
 
 class Operand:
     def __init__(self, ref):
-        self.ref = ref
+        self.ref, self.shape = ref, ref.shape
 
     def __getitem__(self, index):
         return self.ref[index]
 
 
-def call(kernel, outs, args, scratch=(), name=None, limit=8):
+def call(kernel, outs, args, scratch=(), name=None, limit=8, space=pltpu.VMEM):
     def body(co_ref, *refs):
         operands = [Operand(ref) for ref in refs[: len(args) - 1]]
         kernel(co_ref, *operands, *refs[len(args) - 1 :])
@@ -353,7 +353,7 @@
         body,
         out_shape=[jax.ShapeDtypeStruct(shape, dtype) for shape, dtype in outs],
         in_specs=[pl.BlockSpec(memory_space=pltpu.SMEM)]
-        + [pl.BlockSpec(memory_space=pltpu.VMEM)] * (len(args) - 1),
+        + [pl.BlockSpec(memory_space=space)] * (len(args) - 1),
         out_specs=[pl.BlockSpec(memory_space=pltpu.VMEM)] * len(outs),
         scratch_shapes=list(scratch),
         compiler_params=pltpu.CompilerParams(vmem_limit_bytes=limit * 2**20),
@@ -364,15 +364,18 @@
 
 def assemble_kernel(ranges, co, *refs):
     count = len(refs) - len(ranges)
+    each = count // 2
     for number in range(count):
-        a, i = (number // 4, number % 2) if count == 8 else (number // 2, number % 2)
-        b = (number // 2) % 2 if count == 8 else 0
-        for k in range(4):
-            row = k * 192 + lax.bitwise_xor(co[2], i) * 96 + lax.bitwise_xor(co[3], a) * 48
+        blocks = refs[number].shape[0] // 48
+        for block in range(blocks):
+            i, k = (number % 2, block) if blocks == 4 else (block // 4, block % 4)
+            b = (number // 2) % 2 if each == 4 else 0
+            row = k * 192 + lax.bitwise_xor(co[2], i) * 96
+            row = row + lax.bitwise_xor(co[3], number // each) * 48
             rows = pl.ds(pl.multiple_of(row, 16), 48)
             for (start, size), out in zip(ranges, refs[count:]):
                 out[rows, b * size : b * size + size] = refs[number][
-                    k * 48 : k * 48 + 48, start : start + size
+                    block * 48 : block * 48 + 48, start : start + size
                 ]
 
 
@@ -410,19 +413,27 @@
     return centred * rstd, rstd
 
 
-def prep_kernel(co, attn, mlp, s0, s1, s2):
+def prep_first_kernel(co, attn, mlp, s0, wide, sems):
     r = co[0]
-    for part in range(3):
-        cols = lanes(part * D + 384 * r, 384)
-        s0[:, part * 384 : part * 384 + 384] = attn[:, cols].astype(BF)
-    s0[:, 1152:1536] = attn[:, lanes(3 * D + 384 * r, 384)].astype(BF)
-    s0[:, 1536:] = mlp[:, lanes(1536 * r, 768)].astype(BF)
+    sources = [attn.ref.at[:, lanes(part * D + 384 * r, 384)] for part in range(4)]
+    sources += [mlp.ref.at[:, lanes(1536 * r + n * 384, 384)] for n in range(2)]
+    copies = [
+        pltpu.make_async_copy(source, wide.at[n], sems.at[n]) for n, source in enumerate(sources)
+    ]
+    for copy in copies:
+        copy.start()
+    for n, copy in enumerate(copies):
+        copy.wait()
+        s0[:, n * 384 : n * 384 + 384] = wide[n].astype(BF)
+
+
+def prep_second_kernel(co, mlp, s1, s2):
+    r = co[0]
     for b in range(2):
         half = lax.bitwise_xor(r, b)
         s1[:, b * D : b * D + D] = mlp[:, lanes(1536 * half + D, D)].astype(BF)
+        s2[:, b * D : b * D + D] = mlp[:, lanes(FF + 1536 * half + D, D)].astype(BF)
     s1[:, 2 * D :] = mlp[:, lanes(FF + 1536 * r, D)].astype(BF)
-    s2[:, :D] = mlp[:, lanes(FF + 1536 * r + D, D)].astype(BF)
-    s2[:, D:] = mlp[:, lanes(FF + 1536 * (1 - r), 2 * D)].astype(BF)
 
 
 def first_norm_kernel(co, tokens, info, vec, h1, h1t, cols):
@@ -499,15 +510,15 @@
 
 
 def hidden_grad_kernel(
-    co, dz, slope0, slope1, w00, w01, w1, left, du0, du1, db1, send, keep, scratch
+    co, dz, slope0, slope1, w00, w01, w10, w11, left, du0, du1, db1, send, keep, scratch
 ):
     for part, slope, du in ((0, slope0, du0), (1, slope1, du1)):
         for b in range(2):
-            weight, start = (w1, part * D) if b else ((w00, w01)[part], 0)
+            weight = ((w00, w01), (w10, w11))[b][part]
             half = lax.bitwise_xor(co[0], b)
             for sub in range(0, D, 384):
                 at = slice(b * D + sub, b * D + sub + 384)
-                da = nn(dz[...], weight[:, start + sub : start + sub + 384])
+                da = nn(dz[...], weight[:, sub : sub + 384])
                 d = (da * slope[:, at]).astype(BF)
                 du[:, at] = d
                 db1[pl.ds(2 * half + part, 1), sub : sub + 384] = jnp.sum(
@@ -518,11 +529,11 @@
                 share_rows(co[3], scratch, send, keep, dst)
 
 
-def output_kernel(co, y1, vec, g0, g1, w00, w01, w1, act):
+def output_kernel(co, y1, vec, g0, g1, w00, w01, w10, w11, act):
     acc = y1[...] + vec[7:8, :]
     for part, g in ((0, g0), (1, g1)):
         acc = acc + nt(g[:, :D], (w00, w01)[part][...])
-        acc = acc + nt(g[:, D:], w1[:, part * D : part * D + D])
+        acc = acc + nt(g[:, D:], (w10, w11)[part][...])
     act[...] = acc.astype(BF)
 
 
@@ -645,7 +656,7 @@
         rows = slice(k * 48, k * 48 + 48)
         for out, i in ((y_send, 1 - y), (y_keep, y)):
             out[rows, :D] = both(x_keep, x_got, k, i).astype(out.dtype)
-            out[rows, D:] = both(keep, got, k, i, every, slice(0, 2 * D)).astype(out.dtype)
+            out[rows, D:] = both(keep, got, k, i, every, slice(0, D)).astype(out.dtype)
     x_next[...] = both(keep, got, every, every, every, slice(2 * D, 3 * D))
     x_send[...] = both(keep, got, every, every, every, slice(3 * D, 4 * D)).astype(BF)
 
@@ -663,15 +674,53 @@
     last[...] = both(keep, got, every, every, every, slice(3 * D, 4 * D))
 
 
-def split_fourth_kernel(co, x_keep, x_got, last, vec, y_send, y_keep):
+def split_fourth_kernel(co, x_keep, x_got, last, vec, far_keep, far_got, y_send, y_keep):
     y = co[2]
     for out, i in ((y_send, 1 - y), (y_keep, y)):
         for k in range(4):
             rows = slice(k * 48, k * 48 + 48)
             out[rows, :D] = both(x_keep, x_got, k, i).astype(out.dtype)
             out[rows, D:] = last[k, i].astype(out.dtype)
-        out[192:208, :D] = vec[...].astype(out.dtype)
-        out[192:208, D:] = jnp.zeros((16, D), out.dtype)
+        row = pl.multiple_of(96 + i * 48, 16)
+        out[192:240, :D] = both(far_keep, far_got, pl.ds(row, 48)).astype(out.dtype)
+        out[192:208, D:] = vec[...].astype(out.dtype)
+        out[208:240, D:] = jnp.zeros((32, D), out.dtype)
+
+
+def split_near_first_kernel(co, keep, got, up_keep, up_got, send, rest):
+    side = co[1] % 2
+    for out, at in ((send, 1 - side), (rest, side)):
+        for far in range(2):
+            row = pl.multiple_of((2 * far + at) * 48, 16)
+            for half in range(2):
+                to = half * 96 + far * 48
+                cols = slice(half * D, half * D + D)
+                out[to : to + 48, :] = both(keep, got, pl.ds(row, 48), cols).astype(out.dtype)
+                to = 192 + far * 96 + half * 48
+                total = both(up_keep, up_got, 2 * far + at, half, slice(None), slice(D, 2 * D))
+                out[to : to + 48, :] = total.astype(out.dtype)
+
+
+def split_far_first_kernel(co, keep, got, send, rest):
+    side = co[1] // 2
+    for out, at in ((send, 1 - side), (rest, side)):
+        for half in range(2):
+            row = pl.multiple_of(half * 96 + at * 48, 16)
+            to = half * 48
+            out[to : to + 48, :] = both(keep, got, pl.ds(row, 48)).astype(out.dtype)
+        row = pl.multiple_of(192 + at * 96, 16)
+        out[96:192, :] = both(keep, got, pl.ds(row, 96)).astype(out.dtype)
+
+
+def sum_far_first_kernel(co, keep, got, out):
+    for half in range(2):
+        rows = slice(half * 48, half * 48 + 48)
+        out[:, half * D : half * D + D] = both(keep, got, rows).astype(BF)
+
+
+def sum_far_second_kernel(co, keep, got, other, out):
+    out[:, : 2 * D] = both(keep, got, slice(None)).astype(BF)
+    out[:, 2 * D :] = other[...].astype(BF)
 
 
 def split_near_kernel(co, keep, got, send, rest, *small):
@@ -681,7 +730,8 @@
             row = pl.multiple_of((2 * far + at) * 48, 16)
             out[far * 48 : far * 48 + 48, :] = both(keep, got, pl.ds(row, 48)).astype(out.dtype)
     if small:
-        small[0][...] = both(keep, got, slice(192, 208), slice(0, D))
+        small[0][...] = both(keep, got, slice(192, 208), slice(D, 2 * D))
+        small[1][...] = both(keep, got, slice(192, 240), slice(0, D))
 
 
 def split_far_kernel(co, keep, got, send, rest):
@@ -695,9 +745,13 @@
     out[...] = (keep[...] + got[...].astype(F32)).astype(BF)
 
 
-def update_kernel(rate, moves, co, *refs):
-    state, grads, new = refs[:3], refs[3:-4], refs[-4:]
-    for numbers, row, src, size, b, col, stride in moves:
+def update_kernel(rate, moves, n_states, n_grads, n_before, co, *refs):
+    grads = refs[3 * n_states :][:n_grads]
+    first = 3 * n_states + n_grads + n_before
+    parts, sems = refs[first + 4 * n_states : -1], refs[-1]
+    copies = []
+    for n, (which, numbers, row, src, size, b, col, stride) in enumerate(moves):
+        state, new = refs[3 * which :][:3], refs[first + 4 * which :][:4]
         grad = 0.0
         for number in numbers:
             grad = grad + grads[number][row : row + 48, src : src + size].astype(F32)
@@ -706,10 +760,18 @@
         w, m, a = (ref[:, at] for ref in state)
         m_new = momentum_decay * m + grad
         w_new = w - rate * (grad + momentum_decay * m_new)
-        new[0][:, at] = w_new
-        new[1][:, at] = m_new
-        new[2][:, at] = average_decay * a + (1.0 - average_decay) * w_new
-        new[3][:, at] = w_new.astype(BF)
+        full, low = parts[2 * n], parts[2 * n + 1]
+        full[0] = w_new
+        full[1] = m_new
+        full[2] = average_decay * a + (1.0 - average_decay) * w_new
+        low[...] = w_new.astype(BF)
+        for k in range(4):
+            source = full.at[k] if k < 3 else low
+            copy = pltpu.make_async_copy(source, new[k].at[:, at], sems.at[4 * n + k])
+            copy.start()
+            copies.append(copy)
+    for copy in copies:
+        copy.wait()
 
 
 def hold(arrays):
@@ -743,11 +805,14 @@
 
     CORE, Y, Z, X = 1, 2, 4, 16
 
-    s0, s1, s2 = call(
-        prep_kernel,
-        [((48, 3 * D), BF)] * 3,
+    (s0,) = call(
+        prep_first_kernel,
+        [((48, 3 * D), BF)],
         [co, attn_weight, mlp_weight],
+        scratch=[pltpu.VMEM((6, 48, 384), F32), pltpu.SemaphoreType.DMA((6,))],
         name="prep",
+        limit=60,
+        space=pltpu.HBM,
     )
     info = jnp.zeros((8, 256), F32).at[0:3].set(
         jnp.stack([clip_index, key_valid, patch_masked]).astype(F32)
@@ -765,25 +830,33 @@
     def core_pair(pieces):
         return pieces + [swap(piece, CORE) for piece in pieces]
 
-    vec = vec + swap(vec, CORE)
-    s0, vec = hold((s0, vec))
     stack0 = along_z(s0)
-    vec = vec + swap(vec, Y)
-    stack0, s1, vec = hold((stack0, s1, vec))
+    stack0, vec, mlp_late = hold((stack0, vec, mlp_weight))
+    s1, s2 = call(
+        prep_second_kernel,
+        [((48, 3 * D), BF), ((48, 2 * D), BF)],
+        [co, mlp_late],
+        name="prep",
+    )
     across0 = swap(stack0, Y)
     far0 = swap(stack0, X)
+    vec = vec + swap(vec, CORE)
+    s1, vec = hold((s1, vec))
     near0 = [swap(stack0, CORE)]
     stack1 = along_z(s1)
-    vec = vec + swap(vec, Z)
+    vec = vec + swap(vec, Y)
     stack1, across0, far0, near0, s2, vec = hold((stack1, across0, far0, near0, s2, vec))
     far_across0 = swap(across0, X)
     across1 = swap(stack1, Y)
     near0 += [swap(across0, CORE), swap(far0, CORE)]
+    vec = vec + swap(vec, Z)
+    s2, vec = hold((s2, vec))
     stack2 = along_z(s2)
     vec = vec + swap(vec, 2 * Z)
     stack2, across1, far_across0, near0, vec = hold((stack2, across1, far_across0, near0, vec))
     pieces0 = [stack0, across0, far0, far_across0, *near0, swap(far_across0, CORE)]
     across2 = swap(stack2, Y)
+    far1 = swap(jnp.concatenate([stack1[:, 2 * D :], across1[:, 2 * D :]], axis=0), X)
     pieces1 = core_pair([stack1, across1])
     h1, h1t, cols = call(
         first_norm_kernel,
@@ -816,15 +889,46 @@
         name="hidden",
     )
 
-    across2, down_send = hold((across2, down_send))
+    rate = base_rate / math.sqrt(tokens.shape[0] * 32)
+
+    def update(moves, states, grads, name, before=()):
+        parts, outs = [], []
+        for move in moves:
+            parts += [pltpu.VMEM((3, 48, move[4]), F32), pltpu.VMEM((48, move[4]), BF)]
+        for state in states:
+            outs += [jax.ShapeDtypeStruct(state[0].shape, F32)] * 3
+            outs += [jax.ShapeDtypeStruct(state[0].shape, BF)]
+        whole = pl.BlockSpec(memory_space=pltpu.VMEM)
+        far = pl.BlockSpec(memory_space=pltpu.HBM)
+        first = 1 + 3 * len(states) + len(grads)
+        return pl.pallas_call(
+            functools.partial(update_kernel, rate, moves, len(states), len(grads), len(before)),
+            out_shape=outs,
+            in_specs=[pl.BlockSpec(memory_space=pltpu.SMEM)]
+            + [whole] * (first - 1)
+            + [far] * len(before),
+            out_specs=[far] * len(outs),
+            input_output_aliases={first + k: k for k in range(len(before))},
+            scratch_shapes=[*parts, pltpu.SemaphoreType.DMA((4 * len(moves),))],
+            compiler_params=pltpu.CompilerParams(vmem_limit_bytes=8 * 2**20),
+            cost_estimate=pl.CostEstimate(flops=2**20, bytes_accessed=2**20, transcendentals=0),
+            name=name,
+        )(co, *(array for state in states for array in state), *grads, *before)
+
+    mlp_state = [mlp_weight, mlp_moment, mlp_average]
+    attn_state = [attn_weight, attn_moment, attn_average]
+
+    across2, far1, down_send = hold((across2, far1, down_send))
     pieces2 = core_pair([stack2, across2])
-    pieces2, down_send = hold((pieces2, down_send))
+    far1 = core_pair([far1])
+    pieces2, far1, down_send = hold((pieces2, far1, down_send))
     down_got = swap(down_send, CORE)
-    w_down01, w_down1 = assemble(co, pieces2, (0, 768), (768, 1536))
+    w_down01, w_down11 = assemble(co, pieces2, (0, D), (D, D))
+    (w_down10,) = assemble(co, far1, (0, D))
     du0, du1, db1, up_send, up_keep = call(
         hidden_grad_kernel,
         [((256, 2 * D), BF), ((256, 2 * D), BF), ((8, D), F32)] + shares,
-        [co, cotangent, slope0, slope1, w_down00, w_down01, w_down1, h2t],
+        [co, cotangent, slope0, slope1, w_down00, w_down01, w_down10, w_down11, h2t],
         scratch=[pltpu.VMEM((D, 384), F32)],
         name="hidden_grad",
     )
@@ -882,14 +986,18 @@
     y_got0, x_got1, up_got, attn_send = hold((y_got0, x_got1, up_got, attn_send))
     y_send1, y_keep1, x_send2, x_keep2 = call(
         split_second_kernel,
-        [((192, 3 * D), BF), ((192, 3 * D), F32)] + x_shares,
+        y_shares + x_shares,
         [co, x_keep1, x_got1, up_keep, up_got],
         name="split_second",
     )
-    near_send0, near_keep0 = split_near(y_keep0, y_got0)
-    near_send0, y_send1, x_send2, attn_send, dqkv = hold(
-        (near_send0, y_send1, x_send2, attn_send, dqkv)
-    )
+    y_got0 = hold((y_got0, y_send1))[0]
+    near_send0, near_keep0 = call(
+        split_near_first_kernel,
+        [((384, D), BF), ((384, D), F32)],
+        [co, y_keep0, y_got0, up_keep, up_got],
+        name="split_near",
+    )
+    dqkv = hold((dqkv, near_send0))[0]
     y_got1 = swap(y_send1, Y)
     x_got2 = swap(x_send2, X)
     near_got0 = swap(near_send0, Z)
@@ -903,17 +1011,22 @@
     near_got0, y_got1, x_got2, attn_got, total = hold(
         (near_got0, y_got1, x_got2, attn_got, total)
     )
+    far_send0, far_keep0 = call(
+        split_far_first_kernel,
+        [((192, D), BF), ((192, D), F32)],
+        [co, near_keep0, near_got0],
+        name="split_far",
+    )
+    x_got2 = hold((x_got2, far_send0))[0]
     y_send2, y_keep2, x_send3, x_keep3, last = call(
         split_third_kernel,
         y_shares + x_shares + x_shares[1:],
         [co, x_keep2, x_got2, attn_keep, attn_got],
         name="split_third",
     )
+    y_got1 = hold((y_got1, y_send2))[0]
     near_send1, near_keep1 = split_near(y_keep1, y_got1)
-    far_send0, far_keep0 = split_far(near_keep0, near_got0)
-    far_send0, near_send1, y_send2, x_send3, total, y1 = hold(
-        (far_send0, near_send1, y_send2, x_send3, total, y1)
-    )
+    y1 = hold((y1, near_send1))[0]
     x_got3 = swap(x_send3, X)
     y_got2 = swap(y_send2, Y)
     near_got1 = swap(near_send1, Z)
@@ -922,7 +1035,7 @@
     (activations,) = call(
         output_kernel,
         [((256, D), BF)],
-        [co, y1, vec, g0, g1, w_down00, w_down01, w_down1],
+        [co, y1, vec, g0, g1, w_down00, w_down01, w_down10, w_down11],
         name="output",
     )
     far_got0, near_got1, y_got2, x_got3, total, activations = hold(
@@ -930,74 +1043,74 @@
     )
     y_send3, y_keep3 = call(
         split_fourth_kernel,
-        [((208, 2 * D), BF), ((208, 2 * D), F32)],
-        [co, x_keep3, x_got3, last, total],
+        [((240, 2 * D), BF), ((240, 2 * D), F32)],
+        [co, x_keep3, x_got3, last, total, far_keep0, far_got0],
         name="split_fourth",
     )
+    y_got2 = hold((y_got2, y_send3))[0]
     near_send2, near_keep2 = split_near(y_keep2, y_got2)
+    near_got1 = hold((near_got1, near_send2))[0]
     far_send1, far_keep1 = split_far(near_keep1, near_got1)
-    mine0 = sum_far(far_keep0, far_got0)
-    mine0, far_send1, near_send2, y_send3 = hold((mine0, far_send1, near_send2, y_send3))
+    far_got0 = hold((far_got0, far_send1))[0]
+    (mine0,) = call(
+        sum_far_first_kernel, [((48, 2 * D), BF)], [co, far_keep0, far_got0], name="sum_far"
+    )
     y_got3 = swap(y_send3, Y)
     near_got2 = swap(near_send2, Z)
     far_got1 = swap(far_send1, 2 * Z)
     got0 = swap(mine0, X)
     got0, far_got1, near_got2, y_got3 = hold((got0, far_got1, near_got2, y_got3))
-    near_send3, near_keep3, total = split_near(y_keep3, y_got3, [((16, D), F32)])
+    near_send3, near_keep3, total, other = split_near(
+        y_keep3, y_got3, [((16, D), F32), ((48, D), F32)]
+    )
+    near_got2 = hold((near_got2, near_send3))[0]
     far_send2, far_keep2 = split_far(near_keep2, near_got2)
-    mine1 = sum_far(far_keep1, far_got1)
-    mine1, far_send2, near_send3, total = hold((mine1, far_send2, near_send3, total))
+    far_got1 = hold((far_got1, far_send2))[0]
+    (mine1,) = call(
+        sum_far_second_kernel,
+        [((48, 3 * D), BF)],
+        [co, far_keep1, far_got1, other],
+        name="sum_far",
+    )
     near_got3 = swap(near_send3, Z)
     far_got2 = swap(far_send2, 2 * Z)
     got1 = swap(mine1, X)
     total = total + swap(total, Z)
     got1, far_got2, near_got3, total = hold((got1, far_got2, near_got3, total))
     far_send3, far_keep3 = split_far(near_keep3, near_got3)
+    far_got2 = hold((far_got2, far_send3))[0]
     mine2 = sum_far(far_keep2, far_got2)
-    mine2, far_send3, total = hold((mine2, far_send3, total))
     far_got3 = swap(far_send3, 2 * Z)
     got2 = swap(mine2, X)
     total = total + swap(total, 2 * Z)
-    got2, far_got3, total = hold((got2, far_got3, total))
+    moves = [(0, (0, 1), 0, h * D, D, None, FF + h * 2 * D, 0) for h in range(2)]
+    moves += [(0, (2 + b,), 0, 0, D, b, FF + D, 2 * D) for b in range(2)]
+    moves += [(0, (2, 3), 0, D + h * D, D, None, h * 2 * D, 0) for h in range(2)]
+    got1 = hold((got1, mine2))[0]
+    mlp = update(moves, [mlp_state], [mine0, got0, mine1, got1], "update_mlp")
+    got2, far_got3, total, mlp = hold((got2, far_got3, total, mlp))
     mine3 = sum_far(far_keep3, far_got3)
     got3 = swap(mine3, X)
     total = total + swap(total, X)
+    got2 = hold((got2, mine3))[0]
+    moves = [(0, (b,), 0, 0, D, b, D, 2 * D) for b in range(2)]
+    moves += [(1, (0, 1), 0, D, D, None, 0, 0)]
+    both_new = update(
+        moves,
+        [mlp_state, attn_state],
+        [mine2, got2],
+        "update_both",
+        mlp,
+    )
+    mlp, attn = both_new[:4], both_new[4:]
+    moves = [(0, (b,), 0, 0, 384, b, D, 384) for b in range(2)]
+    moves += [(0, (b,), 0, 384, 384, b, 2 * D, 384) for b in range(2)]
+    moves += [(0, (0, 1), 0, D, D, None, 3 * D, 0)]
+    attn = update(moves, [attn_state], [mine3, got3], "update_attn", attn)
     flat = total.reshape(-1)
     gain_g = lax.dynamic_slice(flat, (96 * f,), (96,))
     offset_g = lax.dynamic_slice(flat, (2 * D + 528 * f,), (528,))
 
-    rate = base_rate / math.sqrt(tokens.shape[0] * 32)
-
-    def update(moves, state, grads, width, name):
-        return call(
-            functools.partial(update_kernel, rate, moves),
-            [((48, width), F32)] * 3 + [((48, width), BF)],
-            [co, *state, *grads],
-            name=name,
-        )
-
-    mlp_moves = [((0, 1), 0, h * D, D, None, FF + h * 2 * D, 0) for h in range(2)]
-    mlp_moves += [((2 + b,), 0, 0, D, b, FF + D, 2 * D) for b in range(2)]
-    mlp_moves += [((2, 3), 0, D + h * D, D, None, h * 2 * D, 0) for h in range(2)]
-    mlp_moves += [((4 + b,), 0, 0, D, b, D, 2 * D) for b in range(2)]
-    mlp = update(
-        mlp_moves,
-        [mlp_weight, mlp_moment, mlp_average],
-        [mine0, got0, mine1, got1, mine2, got2],
-        2 * FF,
-        "update_mlp",
-    )
-    attn_moves = [((0, 1), 0, D, D, None, 0, 0)]
-    attn_moves += [((2 + b,), 0, 0, 384, b, D, 384) for b in range(2)]
-    attn_moves += [((2 + b,), 0, 384, 384, b, 2 * D, 384) for b in range(2)]
-    attn_moves += [((2, 3), 0, D, D, None, 3 * D, 0)]
-    attn = update(
-        attn_moves,
-        [attn_weight, attn_moment, attn_average],
-        [mine2, got2, mine3, got3],
-        4 * D,
-        "update_attn",
-    )
     gains = advance(gain_g, gain_vector, gain_moment, gain_average, rate)
     offsets = advance(offset_g, offset_vector, offset_moment, offset_average, rate)
     return (activations, input_grad, *attn, *mlp, *gains, *offsets)

time: 219 us -> 208 us (0.950)
  waiting for transfers between devices: 61.5 us -> 47.8 us
  Pallas kernels: 55.3 us -> 59.4 us
  local copies, waits for them, and re-layouts: 2.66 us -> 0.37 us
    ppermute x43 -> x45, waiting for transfers between devices: 61.5 us -> 47.8 us  [swap(): lax.ppermute(array, ('rep', 'fsdp'), [(i, i ^ mask) for i in range(32)])]
    pallas_call x0 -> x3, Pallas kernels: none -> 6.15 us  [update(): pl.pallas_call(functools.partial(update_kernel, rate, moves, len(states),...]
    unnamed x42 -> x40, local copies, waits for them, and re-layouts: 2.63 us -> 0.29 us
    ppermute x43 -> x45, starting transfers between devices: 34.6 us -> 35.6 us  [swap(): lax.ppermute(array, ('rep', 'fsdp'), [(i, i ^ mask) for i in range(32)])]
  transfers between devices with their start and end apart: 43 -> 45, of which waited for: 18 -> 17; matrix products, arithmetic and copies ran while one was open for 1% -> 1% of each run, Pallas kernels for 19% -> 24%
where the time goes in v4:
time: 208 us
  Pallas kernels  59.4 us (29%)
  blocking collectives  58.2 us (28%)
  waiting for transfers between devices  47.8 us (23%)
  starting transfers between devices  35.6 us (17%)
  other arithmetic  4.64 us (2%)
    all_gather x3, blocking collectives, along_z(): lax.all_gather(shard, 'fsdp', axis=0, tiled=True, axis_index_groups=groups)  58.2 us
    pallas_call x33, Pallas kernels, call(): pl.pallas_call(body, out_shape=[jax.ShapeDtypeStruct(shape, dtype) for sh...  53.3 us
    ppermute x45, waiting for transfers between devices, swap(): lax.ppermute(array, ('rep', 'fsdp'), [(i, i ^ mask) for i in range(32)])  47.8 us
    ppermute x45, starting transfers between devices, swap(): lax.ppermute(array, ('rep', 'fsdp'), [(i, i ^ mask) for i in range(32)])  35.6 us
    pallas_call x3, Pallas kernels, update(): pl.pallas_call(functools.partial(update_kernel, rate, moves, len(states),...  6.15 us
  transfers between devices with their start and end apart: 45, of which 17 were waited for; matrix products, arithmetic and copies ran while one was open for 1% of the time, Pallas kernels for 24%

profile of v4, /device:TPU:0, one launch (start us, length us, event | category | flops | bytes accessed | tf_op | source)
XLA Modules:
  0.0 207.6 jit_solution(10109394160950713707)
XLA Ops:
  2.9 2.6 %prep.2 = bf16[48,2304]{1,0:T(8,128)(2,1)} custom-call(s32[4]{0:T(128)} %pad_add_fusion.co_ref.co, f32[48,3072]{1,0:T(8,128)} %refs_0_.16, f32[48,6144]{1,0:T(8,128)} %refs_0_.15), custom_call_target="tpu_custom_call" | custom-call | flops 1048576 | bytes 1048576 | tf_op jit(solution)/shard_map/prep/pallas_call | solution.py:352
  5.5 22.6 %all_gather.9.refs_0_ = bf16[192,2304]{1,0:T(8,128)(2,1)S(1)} all-gather(bf16[48,2304]{1,0:T(8,128)(2,1)} %prep.2), channel_id=1, replica_groups={{0,4,8,12},{1,5,9,13},{2,6,10,14},{3,7,11,15},{16,20,24,28},{17,21,25,2..., dimensions={0}, use_global_device_ids=true | all-gather | bytes 1105920 | tf_op jit(solution)/shard_map/all_gather | solution.py:828
  28.1 1.5 collective-permute-start.2
  29.6 1.5 collective-permute-start.1
  32.9 19.2 %all_gather.10.refs_0_ = bf16[192,2304]{1,0:T(8,128)(2,1)S(1)} all-gather(bf16[48,2304]{1,0:T(8,128)(2,1)S(1)} %get-tuple-element.199), channel_id=1, replica_groups={{0,4,8,12},{1,5,9,13},{2,6,10,14},{3,7,11,15},{16,20,24,28},{17,21,25,2..., dimensions={0}, use_global_device_ids=true | all-gather | bytes 1105920 | tf_op jit(solution)/shard_map/all_gather | solution.py:828
  52.5 1.6 collective-permute-start.6
  54.8 4.1 %collective-permute-done.5 = f32[16,768]{1,0:T(8,128)S(1)} collective-permute-done((f32[16,768]{1,0:T(8,128)S(1)}, f32[16,768]{1,0:T(8,128)S(1)}, u32[]{:S(2)}, u32[]{:S(2)}) %collective-permute-start.5) | collective-permute-done | bytes 49184 | tf_op jit(solution)/shard_map/ppermute | solution.py:804
  58.9 0.9 collective-permute-start.10
  59.8 16.4 %all_gather.11.refs_0_ = bf16[192,1536]{1,0:T(8,128)(2,1)S(1)} all-gather(bf16[48,1536]{1,0:T(8,128)(2,1)S(1)} %get-tuple-element.205), channel_id=1, replica_groups={{0,4,8,12},{1,5,9,13},{2,6,10,14},{3,7,11,15},{16,20,24,28},{17,21,25,2..., dimensions={0}, use_global_device_ids=true | all-gather | bytes 737280 | tf_op jit(solution)/shard_map/all_gather | solution.py:828
  77.1 1.6 collective-permute-start.15
  79.2 1.1 norm1.1
  81.3 3.5 %attention.1 = (bf16[256,2304]{1,0:T(8,128)(2,1)S(1)}, bf16[256,768]{1,0:T(8,128)(2,1)S(1)}, f32[16,256]{1,0:T(8,128)S(1)}) custom-call(s32[4]{0:T(128)S(1)} %copy-done.8, bf16[256,768]{1,0:T(8,128)(2,1)S(1)} %get-tuple-element.213.refs_0_, f32[16,768]{1,0:T(8,128)S(1)} %add.77.refs_2_.refs_1_.refs_3_, f32[8,256]{1,0:T(8,128)S(1)} %scatter.4.refs_1_.refs_2_.refs_0_, ...), custom_call_target="tpu_custom_call" | custom-call | flops 1048576 | bytes 1048576 | tf_op jit(solution)/shard_map/attention/pallas_call | solution.py:352
  85.6 1.4 norm2.1
  88.1 6.1 %hidden.1 = (bf16[256,1536]{1,0:T(8,128)(2,1)S(1)}, bf16[256,1536]{1,0:T(8,128)(2,1)S(1)}, f32[256,1536]{1,0:T(8,128)S(1)}, f32[256,1536]{1,0:T(8,128)S(1)}, bf1...) custom-call(s32[4]{0:T(128)S(1)} %copy-done.8, bf16[256,768]{1,0:T(8,128)(2,1)S(1)} %get-tuple-element.220.refs_0_, ...), custom_call_target="tpu_custom_call" | custom-call | flops 1048576 | bytes 1048576 | tf_op jit(solution)/shard_map/hidden/pallas_call | solution.py:352
  94.9 1.5 collective-permute-done.17.refs_3_
  99.0 5.5 %hidden_grad.1 = (bf16[256,1536]{1,0:T(8,128)(2,1)S(1)}, bf16[256,1536]{1,0:T(8,128)(2,1)S(1)}, f32[8,768]{1,0:T(8,128)S(1)}, bf16[4,2,48,3072]{3,2,1,0:T(8,128)(2,1)S(1)}, f32[4,2,48,3072]{3,2,1,0:T(8,128)S(1)}) custom-call(s32[4]{0:T(128)S(1)} %copy-done.8, bf16[256,768]{1,0:T(8,128)(2,1)S(1)} %copy-done.4, f32[256,1536]{1,0:T(8,128)S(1)} %get-tuple-element.231.refs_1_, ...), custom_call_target="tpu_custom_call" | custom-call | flops 1048576 | bytes 1048576 | tf_op jit(solution)/shard_map/hidden_grad/pallas_call | solution.py:352
  104.5 0.9 split_first.1
  105.6 1.5 collective-permute-start.20
  107.7 3.3 %norm2_back.1 = (f32[256,768]{1,0:T(8,128)S(1)}, bf16[256,768]{1,0:T(8,128)(2,1)S(1)}, bf16[768,256]{1,0:T(8,128)(2,1)S(1)}, f32[8,768]{1,0:T(8,128)S(1)}) custom-call(s32[4]{0:T(128)S(1)} %copy-done.8, bf16[256,768]{1,0:T(8,128)(2,1)S(1)} %copy-done.4, f32[256,768]{1,0:T(8,128)S(1)} %get-tuple-element.294.refs_1_.refs_0_, ...), custom_call_target="tpu_custom_call" | custom-call | flops 1048576 | bytes 1048576 | tf_op jit(solution)/shard_map/norm2_back/pallas_call | solution.py:352
  110.9 5.6 %attention_back.1 = (bf16[256,2304]{1,0:T(8,128)(2,1)S(1)}, f32[8,768]{1,0:T(8,128)S(1)}) custom-call(s32[4]{0:T(128)S(1)} %copy-done.8, f32[8,256]{1,0:T(8,128)S(1)} %scatter.4.refs_1_.refs_2_.refs_0_, f32[256,128]{1,0:T(8,128)S(1)} %get-tuple-element.212.refs_3_.refs_1_.refs_2_, f32[16,256]{1,0:T(8,128)S(1)} %get-tuple-element.254.refs_2_, ...), custom_call_target="tpu_custom_call" | custom-call | flops 1048576 | bytes 1048576 | tf_op jit(solution)/shard_map/attention_back/pallas_call | solution.py:352
  116.5 3.1 %attention_grad.1 = (bf16[4,2,48,3072]{3,2,1,0:T(8,128)(2,1)S(1)}, f32[4,2,48,3072]{3,2,1,0:T(8,128)S(1)}) custom-call(s32[4]{0:T(128)S(1)} %copy-done.8, bf16[768,256]{1,0:T(8,128)(2,1)S(1)} %get-tuple-element.253.refs_0_, bf16[256,2304]{1,0:T(8,128)(2,1)S(1)} %get-tuple-element.274.refs_1_.refs_0_, bf16[768,256]{1,0:T(8,128)(2,1)S(1)} %get-tuple-element.261.refs_2_, ...), custom_call_target="tpu_custom_call" | custom-call | flops 1048576 | bytes 1048576 | tf_op jit(solution)/shard_map/attention_grad/pallas_call | solution.py:352
  119.6 1.6 collective-permute-done.20.refs_1_
  121.2 1.2 collective-permute-done.21.refs_1_
  122.5 0.9 split_second.1
  125.3 2.8 %norm1_back.1 = (bf16[256,768]{1,0:T(8,128)(2,1)}, f32[16,768]{1,0:T(8,128)S(1)}) custom-call(s32[4]{0:T(128)S(1)} %copy-done.8, bf16[256,2304]{1,0:T(8,128)(2,1)S(1)} %get-tuple-element.274.refs_1_.refs_0_, bf16[256,768]{1,0:T(8,128)(2,1)S(1)} %copy-done.5, f32[256,128]{1,0:T(8,128)S(1)} %get-tuple-element.212.refs_3_.refs_1_.refs_2_, ...), custom_call_target="tpu_custom_call" | custom-call | flops 1048576 | bytes 1048576 | tf_op jit(solution)/shard_map/norm1_back/pallas_call | solution.py:352
  128.1 11.8 %collective-permute-done.23.refs_1_ = bf16[384,768]{1,0:T(8,128)(2,1)S(1)} collective-permute-done((bf16[384,768]{1,0:T(8,128)(2,1)S(1)}, bf16[384,768]{1,0:T(8,128)(2,1)S(1)}, u32[]{:S(2)}, u32[]{:S(2)}) %collective-permute-start.23) | collective-permute-done | bytes 589856 | tf_op jit(solution)/shard_map/ppermute | solution.py:804
  141.0 1.1 split_third.1
  142.1 1.6 collective-permute-start.30
  144.8 1.7 collective-permute-start.28
  147.3 2.7 %output.1 = bf16[256,768]{1,0:T(8,128)(2,1)} custom-call(s32[4]{0:T(128)S(1)} %copy-done.8, f32[256,768]{1,0:T(8,128)S(1)} %get-tuple-element.294.refs_1_.refs_0_, f32[16,768]{1,0:T(8,128)S(1)} %add.77.refs_2_.refs_1_.refs_3_, bf16[256,1536]{1,0:T(8,128)(2,1)S(1)} %get-tuple-element.295.refs_2_, bf16[256,1536]{1,0:T(8,128)(2,1)S(1)} %get-tuple-element.296.refs_3_, ...), custom_call_target="tpu_custom_call" | custom-call | flops 1048576 | bytes 1048576 | tf_op jit(solution)/shard_map/output/pallas_call | solution.py:352
  150.0 7.6 %collective-permute-done.28.refs_1_ = bf16[96,1536]{1,0:T(8,128)(2,1)S(1)} collective-permute-done((bf16[96,1536]{1,0:T(8,128)(2,1)S(1)}, bf16[96,1536]{1,0:T(8,128)(2,1)S(1)}, u32[]{:S(2)}, u32[]{:S(2)}) %collective-permute-start.28) | collective-permute-done | bytes 294944 | tf_op jit(solution)/shard_map/ppermute | solution.py:804
  157.6 3.4 %collective-permute-done.27.refs_5_.refs_1_ = bf16[192,768]{1,0:T(8,128)(2,1)S(1)} collective-permute-done((bf16[192,768]{1,0:T(8,128)(2,1)S(1)}, bf16[192,768]{1,0:T(8,128)(2,1)S(1)}, u32[]{:S(2)}, u32[]{:S(2)}) %collective-permute-start.27) | collective-permute-done | bytes 294944 | tf_op jit(solution)/shard_map/ppermute | solution.py:804
  161.7 1.6 collective-permute-start.35
  165.9 1.9 collective-permute-start.33
  167.8 2.7 %collective-permute-done.32.refs_4_ = bf16[48,1536]{1,0:T(8,128)(2,1)S(1)} collective-permute-done((bf16[48,1536]{1,0:T(8,128)(2,1)S(1)}, bf16[48,1536]{1,0:T(8,128)(2,1)S(1)}, u32[]{:S(2)}, u32[]{:S(2)}) %collective-permute-start.32) | collective-permute-done | bytes 147488 | tf_op jit(solution)/shard_map/ppermute | solution.py:804
  170.5 3.1 %collective-permute-done.33.refs_1_ = bf16[48,1536]{1,0:T(8,128)(2,1)S(1)} collective-permute-done((bf16[48,1536]{1,0:T(8,128)(2,1)S(1)}, bf16[48,1536]{1,0:T(8,128)(2,1)S(1)}, u32[]{:S(2)}, u32[]{:S(2)}) %collective-permute-start.33) | collective-permute-done | bytes 147488 | tf_op jit(solution)/shard_map/ppermute | solution.py:804
  173.6 1.8 collective-permute-done.35.refs_1_
  176.1 1.6 collective-permute-start.38
  179.7 1.3 collective-permute-start.37
  181.0 1.8 collective-permute-start.39
  182.8 3.8 %collective-permute-done.39 = f32[16,768]{1,0:T(8,128)S(1)} collective-permute-done((f32[16,768]{1,0:T(8,128)S(1)}, f32[16,768]{1,0:T(8,128)S(1)}, u32[]{:S(2)}, u32[]{:S(2)}) %collective-permute-start.39) | collective-permute-done | bytes 49184 | tf_op jit(solution)/shard_map/ppermute | solution.py:804
  187.9 2.1 %collective-permute-start.40 = (bf16[48,1536]{1,0:T(8,128)(2,1)S(1)}, bf16[48,1536]{1,0:T(8,128)(2,1)S(1)}, u32[]{:S(2)}, u32[]{:S(2)}) collective-permute-start(bf16[48,1536]{1,0:T(8,128)(2,1)S(1)} %sum_far.6.refs_6_), channel_id=1, source_target_pairs={{0,16},{1,17},{2,18},{3,19},{4,20},{5,21},{6,22},{7,23},{8,24},{9,... | collective-permute-start | bytes 442376 | tf_op jit(solution)/shard_map/ppermute | solution.py:804
  190.7 2.3 %collective-permute-start.42 = (f32[16,768]{1,0:T(8,128)S(1)}, f32[16,768]{1,0:T(8,128)S(1)}, u32[]{:S(2)}, u32[]{:S(2)}) collective-permute-start(f32[16,768]{1,0:T(8,128)S(1)} %add.79), channel_id=1, source_target_pairs={{0,8},{1,9},{2,10},{3,11},{4,12},{5,13},{6,14},{7,15},{8,0},{9,1},... | collective-permute-start | bytes 147464 | tf_op jit(solution)/shard_map/ppermute | solution.py:804
  193.0 2.4 %update_mlp.1 = (f32[48,6144]{1,0:T(8,128)}, f32[48,6144]{1,0:T(8,128)}, f32[48,6144]{1,0:T(8,128)}, bf16[48,6144]{1,0:T(8,128)(2,1)}) custom-call(s32[4]{0:T(128)S(1)} %copy-done.8, f32[48,6144]{1,0:T(8,128)S(1)} %copy-done, f32[48,6144]{1,0:T(8,128)S(1)} %copy-done.2, f32[48,6144]{1,0:T(8,128)S(1)} %copy-done.3, bf16[48,1536]{1,0:T(8,128)(2,1)S(1)} %sum_far.4.refs_3_, ...), custom_call_target="tpu_custom_call" | custom-call | flops 1048576 | bytes 1048576 | tf_op jit(solution)/shard_map/update_mlp/pallas_call | solution.py:904
  195.5 2.9 %collective-permute-done.42 = f32[16,768]{1,0:T(8,128)S(1)} collective-permute-done((f32[16,768]{1,0:T(8,128)S(1)}, f32[16,768]{1,0:T(8,128)S(1)}, u32[]{:S(2)}, u32[]{:S(2)}) %collective-permute-start.42) | collective-permute-done | bytes 49184 | tf_op jit(solution)/shard_map/ppermute | solution.py:804
  199.6 1.6 collective-permute-start.43
  201.2 1.8 update_both.1
  205.5 1.9 update_attn.1
  (144 shorter events, 29.2 us)
Async XLA Ops:
  2.9 28.2 %copy-start = (f32[48,6144]{1,0:T(8,128)S(1)}, f32[48,6144]{1,0:T(8,128)}, u32[]{:S(2)}) copy-start(f32[48,6144]{1,0:T(8,128)} %refs_0_.15) | copy-start | bytes 3538948
  2.9 28.2 %copy-start.8 = (s32[4]{0:T(128)S(1)}, s32[4]{0:T(128)}, u32[]{:S(2)}) copy-start(s32[4]{0:T(128)} %pad_add_fusion.co_ref.co) | copy-start | bytes 52
  28.1 24.3 %collective-permute-start.3 = (bf16[192,2304]{1,0:T(8,128)(2,1)S(1)}, bf16[192,2304]{1,0:T(8,128)(2,1)S(1)}, u32[]{:S(2)}, u32[]{:S(2)}) collective-permute-start(bf16[192,2304]{1,0:T(8,128)(2,1)S(1)} %all_gather.9.refs_0_), channel_id=1, source_target_pairs={{0,1},{1,0},{2,3},{3,2},{4,5},{5,4},{6,7},{7,6},{8,9},{9,8},{10,11... | collective-permute-start | bytes 2654216 | tf_op jit(solution)/shard_map/ppermute | solution.py:804
  28.1 24.3 %collective-permute-start.2 = (bf16[192,2304]{1,0:T(8,128)(2,1)S(1)}, bf16[192,2304]{1,0:T(8,128)(2,1)S(1)}, u32[]{:S(2)}, u32[]{:S(2)}) collective-permute-start(bf16[192,2304]{1,0:T(8,128)(2,1)S(1)} %all_gather.9.refs_0_), channel_id=1, source_target_pairs={{0,16},{1,17},{2,18},{3,19},{4,20},{5,21},{6,22},{7,23},{8,24},{9,... | collective-permute-start | bytes 2654216 | tf_op jit(solution)/shard_map/ppermute | solution.py:804
  29.6 22.9 %collective-permute-start.1 = (bf16[192,2304]{1,0:T(8,128)(2,1)S(1)}, bf16[192,2304]{1,0:T(8,128)(2,1)S(1)}, u32[]{:S(2)}, u32[]{:S(2)}) collective-permute-start(bf16[192,2304]{1,0:T(8,128)(2,1)S(1)} %all_gather.9.refs_0_), channel_id=1, source_target_pairs={{0,2},{1,3},{2,0},{3,1},{4,6},{5,7},{6,4},{7,5},{8,10},{9,11},{10,... | collective-permute-start | bytes 2654216 | tf_op jit(solution)/shard_map/ppermute | solution.py:804
  31.1 1.2 collective-permute-start
  32.4 20.1 %collective-permute-start.4 = (f32[16,768]{1,0:T(8,128)S(1)}, f32[16,768]{1,0:T(8,128)S(1)}, u32[]{:S(2)}, u32[]{:S(2)}) collective-permute-start(f32[16,768]{1,0:T(8,128)S(1)} %add.74), channel_id=1, source_target_pairs={{0,2},{1,3},{2,0},{3,1},{4,6},{5,7},{6,4},{7,5},{8,10},{9,11},{10,... | collective-permute-start | bytes 147464 | tf_op jit(solution)/shard_map/ppermute | solution.py:804
  52.5 23.9 %collective-permute-start.9 = (bf16[192,2304]{1,0:T(8,128)(2,1)S(1)}, bf16[192,2304]{1,0:T(8,128)(2,1)S(1)}, u32[]{:S(2)}, u32[]{:S(2)}) collective-permute-start(bf16[192,2304]{1,0:T(8,128)(2,1)S(1)} %collective-permute-done.2.refs_2_), channel_id=1, source_target_pairs={{0,1},{1,0},{2,3},{3,2},{4,5},{5,4},{6,7},{7,6},{8,9},{9,8},{10,11... | collective-permute-start | bytes 2654216 | tf_op jit(solution)/shard_map/ppermute | solution.py:804
  52.5 23.8 %collective-permute-start.6 = (bf16[192,2304]{1,0:T(8,128)(2,1)S(1)}, bf16[192,2304]{1,0:T(8,128)(2,1)S(1)}, u32[]{:S(2)}, u32[]{:S(2)}) collective-permute-start(bf16[192,2304]{1,0:T(8,128)(2,1)S(1)} %all_gather.10.refs_0_), channel_id=1, source_target_pairs={{0,2},{1,3},{2,0},{3,1},{4,6},{5,7},{6,4},{7,5},{8,10},{9,11},{10,... | collective-permute-start | bytes 2654216 | tf_op jit(solution)/shard_map/ppermute | solution.py:804
  54.1 22.2 %collective-permute-start.8 = (bf16[192,2304]{1,0:T(8,128)(2,1)S(1)}, bf16[192,2304]{1,0:T(8,128)(2,1)S(1)}, u32[]{:S(2)}, u32[]{:S(2)}) collective-permute-start(bf16[192,2304]{1,0:T(8,128)(2,1)S(1)} %collective-permute-done.1.refs_1_), channel_id=1, source_target_pairs={{0,1},{1,0},{2,3},{3,2},{4,5},{5,4},{6,7},{7,6},{8,9},{9,8},{10,11... | collective-permute-start | bytes 2654216 | tf_op jit(solution)/shard_map/ppermute | solution.py:804
  54.3 22.1 %collective-permute-start.7 = (bf16[192,2304]{1,0:T(8,128)(2,1)S(1)}, bf16[192,2304]{1,0:T(8,128)(2,1)S(1)}, u32[]{:S(2)}, u32[]{:S(2)}) collective-permute-start(bf16[192,2304]{1,0:T(8,128)(2,1)S(1)} %collective-permute-done.1.refs_1_), channel_id=1, source_target_pairs={{0,16},{1,17},{2,18},{3,19},{4,20},{5,21},{6,22},{7,23},{8,24},{9,... | collective-permute-start | bytes 2654216 | tf_op jit(solution)/shard_map/ppermute | solution.py:804
  54.8 4.1 %collective-permute-start.5 = (f32[16,768]{1,0:T(8,128)S(1)}, f32[16,768]{1,0:T(8,128)S(1)}, u32[]{:S(2)}, u32[]{:S(2)}) collective-permute-start(f32[16,768]{1,0:T(8,128)S(1)} %add.75), channel_id=1, source_target_pairs={{0,4},{1,5},{2,6},{3,7},{4,0},{5,1},{6,2},{7,3},{8,12},{9,13},{10,... | collective-permute-start | bytes 147464 | tf_op jit(solution)/shard_map/ppermute | solution.py:804
  58.9 17.4 %collective-permute-start.10 = (f32[16,768]{1,0:T(8,128)S(1)}, f32[16,768]{1,0:T(8,128)S(1)}, u32[]{:S(2)}, u32[]{:S(2)}) collective-permute-start(f32[16,768]{1,0:T(8,128)S(1)} %add.76), channel_id=1, source_target_pairs={{0,8},{1,9},{2,10},{3,11},{4,12},{5,13},{6,14},{7,15},{8,0},{9,1},... | collective-permute-start | bytes 147464 | tf_op jit(solution)/shard_map/ppermute | solution.py:804
  76.4 4.0 %collective-permute-start.11 = (bf16[192,2304]{1,0:T(8,128)(2,1)S(1)}, bf16[192,2304]{1,0:T(8,128)(2,1)S(1)}, u32[]{:S(2)}, u32[]{:S(2)}) collective-permute-start(bf16[192,2304]{1,0:T(8,128)(2,1)S(1)} %collective-permute-done.7.refs_3_), channel_id=1, source_target_pairs={{0,1},{1,0},{2,3},{3,2},{4,5},{5,4},{6,7},{7,6},{8,9},{9,8},{10,11... | collective-permute-start | bytes 2654216 | tf_op jit(solution)/shard_map/ppermute | solution.py:804
  76.5 10.6 %collective-permute-start.12 = (bf16[192,2304]{1,0:T(8,128)(2,1)S(1)}, bf16[192,2304]{1,0:T(8,128)(2,1)S(1)}, u32[]{:S(2)}, u32[]{:S(2)}) collective-permute-start(bf16[192,2304]{1,0:T(8,128)(2,1)S(1)} %all_gather.10.refs_0_), channel_id=1, source_target_pairs={{0,1},{1,0},{2,3},{3,2},{4,5},{5,4},{6,7},{7,6},{8,9},{9,8},{10,11... | collective-permute-start | bytes 2654216 | tf_op jit(solution)/shard_map/ppermute | solution.py:804
  77.0 10.1 %collective-permute-start.13 = (bf16[192,2304]{1,0:T(8,128)(2,1)S(1)}, bf16[192,2304]{1,0:T(8,128)(2,1)S(1)}, u32[]{:S(2)}, u32[]{:S(2)}) collective-permute-start(bf16[192,2304]{1,0:T(8,128)(2,1)S(1)} %collective-permute-done.6.refs_1_), channel_id=1, source_target_pairs={{0,1},{1,0},{2,3},{3,2},{4,5},{5,4},{6,7},{7,6},{8,9},{9,8},{10,11... | collective-permute-start | bytes 2654216 | tf_op jit(solution)/shard_map/ppermute | solution.py:804
  77.1 17.1 %collective-permute-start.15 = (bf16[384,768]{1,0:T(8,128)(2,1)S(1)}, bf16[384,768]{1,0:T(8,128)(2,1)S(1)}, u32[]{:S(2)}, u32[]{:S(2)}) collective-permute-start(bf16[384,768]{1,0:T(8,128)(2,1)S(1)} %pad_maximum_fusion), channel_id=1, source_target_pairs={{0,16},{1,17},{2,18},{3,19},{4,20},{5,21},{6,22},{7,23},{8,24},{9,... | collective-permute-start | bytes 1769480 | tf_op jit(solution)/shard_map/ppermute | solution.py:804
  78.7 15.5 %collective-permute-start.14 = (bf16[192,1536]{1,0:T(8,128)(2,1)S(1)}, bf16[192,1536]{1,0:T(8,128)(2,1)S(1)}, u32[]{:S(2)}, u32[]{:S(2)}) collective-permute-start(bf16[192,1536]{1,0:T(8,128)(2,1)S(1)} %all_gather.11.refs_0_), channel_id=1, source_target_pairs={{0,2},{1,3},{2,0},{3,1},{4,6},{5,7},{6,4},{7,5},{8,10},{9,11},{10,... | collective-permute-start | bytes 1769480 | tf_op jit(solution)/shard_map/ppermute | solution.py:804
  80.4 14.5 %collective-permute-start.16 = (bf16[192,1536]{1,0:T(8,128)(2,1)S(1)}, bf16[192,1536]{1,0:T(8,128)(2,1)S(1)}, u32[]{:S(2)}, u32[]{:S(2)}) collective-permute-start(bf16[192,1536]{1,0:T(8,128)(2,1)S(1)} %all_gather.11.refs_0_), channel_id=1, source_target_pairs={{0,1},{1,0},{2,3},{3,2},{4,5},{5,4},{6,7},{7,6},{8,9},{9,8},{10,11... | collective-permute-start | bytes 1769480 | tf_op jit(solution)/shard_map/ppermute | solution.py:804
  94.2 2.2 %collective-permute-start.17 = (bf16[192,1536]{1,0:T(8,128)(2,1)S(1)}, bf16[192,1536]{1,0:T(8,128)(2,1)S(1)}, u32[]{:S(2)}, u32[]{:S(2)}) collective-permute-start(bf16[192,1536]{1,0:T(8,128)(2,1)S(1)} %collective-permute-done.14.refs_1_), channel_id=1, source_target_pairs={{0,1},{1,0},{2,3},{3,2},{4,5},{5,4},{6,7},{7,6},{8,9},{9,8},{10,11... | collective-permute-start | bytes 1769480 | tf_op jit(solution)/shard_map/ppermute | solution.py:804
  94.8 2.5 %collective-permute-start.18 = (bf16[384,768]{1,0:T(8,128)(2,1)S(1)}, bf16[384,768]{1,0:T(8,128)(2,1)S(1)}, u32[]{:S(2)}, u32[]{:S(2)}) collective-permute-start(bf16[384,768]{1,0:T(8,128)(2,1)S(1)} %collective-permute-done.15.refs_0_), channel_id=1, source_target_pairs={{0,1},{1,0},{2,3},{3,2},{4,5},{5,4},{6,7},{7,6},{8,9},{9,8},{10,11... | collective-permute-start | bytes 1769480 | tf_op jit(solution)/shard_map/ppermute | solution.py:804
  97.3 7.2 %collective-permute-start.19 = (bf16[4,2,48,3072]{3,2,1,0:T(8,128)(2,1)S(1)}, bf16[4,2,48,3072]{3,2,1,0:T(8,128)(2,1)S(1)}, u32[]{:S(2)}, u32[]{:S(2)}) collective-permute-start(bf16[4,2,48,3072]{3,2,1,0:T(8,128)(2,1)S(1)} %get-tuple-element.230), channel_id=1, source_target_pairs={{0,1},{1,0},{2,3},{3,2},{4,5},{5,4},{6,7},{7,6},{8,9},{9,8},{10,11... | collective-permute-start | bytes 7077896 | tf_op jit(solution)/shard_map/ppermute | solution.py:804
  105.4 17.1 %collective-permute-start.22 = (bf16[4,2,48,3072]{3,2,1,0:T(8,128)(2,1)S(1)}, bf16[4,2,48,3072]{3,2,1,0:T(8,128)(2,1)S(1)}, u32[]{:S(2)}, u32[]{:S(2)}) collective-permute-start(bf16[4,2,48,3072]{3,2,1,0:T(8,128)(2,1)S(1)} %get-tuple-element.252), channel_id=1, source_target_pairs={{0,1},{1,0},{2,3},{3,2},{4,5},{5,4},{6,7},{7,6},{8,9},{9,8},{10,11... | collective-permute-start | bytes 7077896 | tf_op jit(solution)/shard_map/ppermute | solution.py:804
  105.6 15.6 %collective-permute-start.20 = (bf16[192,1536]{1,0:T(8,128)(2,1)S(1)}, bf16[192,1536]{1,0:T(8,128)(2,1)S(1)}, u32[]{:S(2)}, u32[]{:S(2)}) collective-permute-start(bf16[192,1536]{1,0:T(8,128)(2,1)S(1)} %get-tuple-element.250), channel_id=1, source_target_pairs={{0,2},{1,3},{2,0},{3,1},{4,6},{5,7},{6,4},{7,5},{8,10},{9,11},{10,... | collective-permute-start | bytes 1769480 | tf_op jit(solution)/shard_map/ppermute | solution.py:804
  107.1 15.3 %collective-permute-start.21 = (bf16[4,2,48,768]{3,2,1,0:T(8,128)(2,1)S(1)}, bf16[4,2,48,768]{3,2,1,0:T(8,128)(2,1)S(1)}, u32[]{:S(2)}, u32[]{:S(2)}) collective-permute-start(bf16[4,2,48,768]{3,2,1,0:T(8,128)(2,1)S(1)} %get-tuple-element.251), channel_id=1, source_target_pairs={{0,16},{1,17},{2,18},{3,19},{4,20},{5,21},{6,22},{7,23},{8,24},{9,... | collective-permute-start | bytes 1769480 | tf_op jit(solution)/shard_map/ppermute | solution.py:804
  122.5 17.8 %collective-permute-start.26 = (bf16[4,2,48,3072]{3,2,1,0:T(8,128)(2,1)S(1)}, bf16[4,2,48,3072]{3,2,1,0:T(8,128)(2,1)S(1)}, u32[]{:S(2)}, u32[]{:S(2)}) collective-permute-start(bf16[4,2,48,3072]{3,2,1,0:T(8,128)(2,1)S(1)} %get-tuple-element.273), channel_id=1, source_target_pairs={{0,1},{1,0},{2,3},{3,2},{4,5},{5,4},{6,7},{7,6},{8,9},{9,8},{10,11... | collective-permute-start | bytes 7077896 | tf_op jit(solution)/shard_map/ppermute | solution.py:804
  124.1 15.8 %collective-permute-start.23 = (bf16[384,768]{1,0:T(8,128)(2,1)S(1)}, bf16[384,768]{1,0:T(8,128)(2,1)S(1)}, u32[]{:S(2)}, u32[]{:S(2)}) collective-permute-start(bf16[384,768]{1,0:T(8,128)(2,1)S(1)} %get-tuple-element.271), channel_id=1, source_target_pairs={{0,4},{1,5},{2,6},{3,7},{4,0},{5,1},{6,2},{7,3},{8,12},{9,13},{10,... | collective-permute-start | bytes 1769480 | tf_op jit(solution)/shard_map/ppermute | solution.py:804
  124.2 15.8 %collective-permute-start.25 = (bf16[4,2,48,768]{3,2,1,0:T(8,128)(2,1)S(1)}, bf16[4,2,48,768]{3,2,1,0:T(8,128)(2,1)S(1)}, u32[]{:S(2)}, u32[]{:S(2)}) collective-permute-start(bf16[4,2,48,768]{3,2,1,0:T(8,128)(2,1)S(1)} %get-tuple-element.272), channel_id=1, source_target_pairs={{0,16},{1,17},{2,18},{3,19},{4,20},{5,21},{6,22},{7,23},{8,24},{9,... | collective-permute-start | bytes 1769480 | tf_op jit(solution)/shard_map/ppermute | solution.py:804
  124.8 15.5 %collective-permute-start.24 = (bf16[192,1536]{1,0:T(8,128)(2,1)S(1)}, bf16[192,1536]{1,0:T(8,128)(2,1)S(1)}, u32[]{:S(2)}, u32[]{:S(2)}) collective-permute-start(bf16[192,1536]{1,0:T(8,128)(2,1)S(1)} %get-tuple-element.268), channel_id=1, source_target_pairs={{0,2},{1,3},{2,0},{3,1},{4,6},{5,7},{6,4},{7,5},{8,10},{9,11},{10,... | collective-permute-start | bytes 1769480 | tf_op jit(solution)/shard_map/ppermute | solution.py:804
  142.1 18.9 %collective-permute-start.30 = (bf16[4,2,48,768]{3,2,1,0:T(8,128)(2,1)S(1)}, bf16[4,2,48,768]{3,2,1,0:T(8,128)(2,1)S(1)}, u32[]{:S(2)}, u32[]{:S(2)}) collective-permute-start(bf16[4,2,48,768]{3,2,1,0:T(8,128)(2,1)S(1)} %get-tuple-element.292), channel_id=1, source_target_pairs={{0,16},{1,17},{2,18},{3,19},{4,20},{5,21},{6,22},{7,23},{8,24},{9,... | collective-permute-start | bytes 1769480 | tf_op jit(solution)/shard_map/ppermute | solution.py:804
  143.7 17.3 %collective-permute-start.29 = (bf16[192,1536]{1,0:T(8,128)(2,1)S(1)}, bf16[192,1536]{1,0:T(8,128)(2,1)S(1)}, u32[]{:S(2)}, u32[]{:S(2)}) collective-permute-start(bf16[192,1536]{1,0:T(8,128)(2,1)S(1)} %get-tuple-element.289), channel_id=1, source_target_pairs={{0,2},{1,3},{2,0},{3,1},{4,6},{5,7},{6,4},{7,5},{8,10},{9,11},{10,... | collective-permute-start | bytes 1769480 | tf_op jit(solution)/shard_map/ppermute | solution.py:804
  144.8 12.8 %collective-permute-start.28 = (bf16[96,1536]{1,0:T(8,128)(2,1)S(1)}, bf16[96,1536]{1,0:T(8,128)(2,1)S(1)}, u32[]{:S(2)}, u32[]{:S(2)}) collective-permute-start(bf16[96,1536]{1,0:T(8,128)(2,1)S(1)} %get-tuple-element.291), channel_id=1, source_target_pairs={{0,4},{1,5},{2,6},{3,7},{4,0},{5,1},{6,2},{7,3},{8,12},{9,13},{10,... | collective-permute-start | bytes 884744 | tf_op jit(solution)/shard_map/ppermute | solution.py:804
  146.5 14.4 %collective-permute-start.27 = (bf16[192,768]{1,0:T(8,128)(2,1)S(1)}, bf16[192,768]{1,0:T(8,128)(2,1)S(1)}, u32[]{:S(2)}, u32[]{:S(2)}) collective-permute-start(bf16[192,768]{1,0:T(8,128)(2,1)S(1)} %get-tuple-element.281), channel_id=1, source_target_pairs={{0,8},{1,9},{2,10},{3,11},{4,12},{5,13},{6,14},{7,15},{8,0},{9,1},... | collective-permute-start | bytes 884744 | tf_op jit(solution)/shard_map/ppermute | solution.py:804
  147.3 2.7 %collective-permute-start.31 = (f32[16,768]{1,0:T(8,128)S(1)}, f32[16,768]{1,0:T(8,128)S(1)}, u32[]{:S(2)}, u32[]{:S(2)}) collective-permute-start(f32[16,768]{1,0:T(8,128)S(1)} %get-tuple-element.293), channel_id=1, source_target_pairs={{0,1},{1,0},{2,3},{3,2},{4,5},{5,4},{6,7},{7,6},{8,9},{9,8},{10,11... | collective-permute-start | bytes 147464 | tf_op jit(solution)/shard_map/ppermute | solution.py:804
  161.7 13.7 %collective-permute-start.35 = (bf16[240,1536]{1,0:T(8,128)(2,1)S(1)}, bf16[240,1536]{1,0:T(8,128)(2,1)S(1)}, u32[]{:S(2)}, u32[]{:S(2)}) collective-permute-start(bf16[240,1536]{1,0:T(8,128)(2,1)S(1)} %get-tuple-element.310), channel_id=1, source_target_pairs={{0,2},{1,3},{2,0},{3,1},{4,6},{5,7},{6,4},{7,5},{8,10},{9,11},{10,... | collective-permute-start | bytes 2211848 | tf_op jit(solution)/shard_map/ppermute | solution.py:804
  164.0 9.6 %collective-permute-start.34 = (bf16[96,1536]{1,0:T(8,128)(2,1)S(1)}, bf16[96,1536]{1,0:T(8,128)(2,1)S(1)}, u32[]{:S(2)}, u32[]{:S(2)}) collective-permute-start(bf16[96,1536]{1,0:T(8,128)(2,1)S(1)} %get-tuple-element.312), channel_id=1, source_target_pairs={{0,4},{1,5},{2,6},{3,7},{4,0},{5,1},{6,2},{7,3},{8,12},{9,13},{10,... | collective-permute-start | bytes 884744 | tf_op jit(solution)/shard_map/ppermute | solution.py:804
  165.3 5.2 %collective-permute-start.32 = (bf16[48,1536]{1,0:T(8,128)(2,1)S(1)}, bf16[48,1536]{1,0:T(8,128)(2,1)S(1)}, u32[]{:S(2)}, u32[]{:S(2)}) collective-permute-start(bf16[48,1536]{1,0:T(8,128)(2,1)S(1)} %sum_far.4.refs_3_), channel_id=1, source_target_pairs={{0,16},{1,17},{2,18},{3,19},{4,20},{5,21},{6,22},{7,23},{8,24},{9,... | collective-permute-start | bytes 442376 | tf_op jit(solution)/shard_map/ppermute | solution.py:804
  165.9 7.7 %collective-permute-start.33 = (bf16[48,1536]{1,0:T(8,128)(2,1)S(1)}, bf16[48,1536]{1,0:T(8,128)(2,1)S(1)}, u32[]{:S(2)}, u32[]{:S(2)}) collective-permute-start(bf16[48,1536]{1,0:T(8,128)(2,1)S(1)} %get-tuple-element.314), channel_id=1, source_target_pairs={{0,8},{1,9},{2,10},{3,11},{4,12},{5,13},{6,14},{7,15},{8,0},{9,1},... | collective-permute-start | bytes 442376 | tf_op jit(solution)/shard_map/ppermute | solution.py:804
  176.1 10.6 %collective-permute-start.38 = (bf16[96,1536]{1,0:T(8,128)(2,1)S(1)}, bf16[96,1536]{1,0:T(8,128)(2,1)S(1)}, u32[]{:S(2)}, u32[]{:S(2)}) collective-permute-start(bf16[96,1536]{1,0:T(8,128)(2,1)S(1)} %get-tuple-element.322), channel_id=1, source_target_pairs={{0,4},{1,5},{2,6},{3,7},{4,0},{5,1},{6,2},{7,3},{8,12},{9,13},{10,... | collective-permute-start | bytes 884744 | tf_op jit(solution)/shard_map/ppermute | solution.py:804
  178.4 14.6 %copy-start.2 = (f32[48,6144]{1,0:T(8,128)S(1)}, f32[48,6144]{1,0:T(8,128)}, u32[]{:S(2)}) copy-start(f32[48,6144]{1,0:T(8,128)} %refs_1_.8) | copy-start | bytes 3538948
  179.0 7.7 %collective-permute-start.36 = (bf16[48,2304]{1,0:T(8,128)(2,1)S(1)}, bf16[48,2304]{1,0:T(8,128)(2,1)S(1)}, u32[]{:S(2)}, u32[]{:S(2)}) collective-permute-start(bf16[48,2304]{1,0:T(8,128)(2,1)S(1)} %sum_far.5.refs_5_), channel_id=1, source_target_pairs={{0,16},{1,17},{2,18},{3,19},{4,20},{5,21},{6,22},{7,23},{8,24},{9,... | collective-permute-start | bytes 663560 | tf_op jit(solution)/shard_map/ppermute | solution.py:804
  179.7 6.9 %collective-permute-start.37 = (bf16[48,1536]{1,0:T(8,128)(2,1)S(1)}, bf16[48,1536]{1,0:T(8,128)(2,1)S(1)}, u32[]{:S(2)}, u32[]{:S(2)}) collective-permute-start(bf16[48,1536]{1,0:T(8,128)(2,1)S(1)} %get-tuple-element.324), channel_id=1, source_target_pairs={{0,8},{1,9},{2,10},{3,11},{4,12},{5,13},{6,14},{7,15},{8,0},{9,1},... | collective-permute-start | bytes 442376 | tf_op jit(solution)/shard_map/ppermute | solution.py:804
  181.0 5.7 %collective-permute-start.39 = (f32[16,768]{1,0:T(8,128)S(1)}, f32[16,768]{1,0:T(8,128)S(1)}, u32[]{:S(2)}, u32[]{:S(2)}) collective-permute-start(f32[16,768]{1,0:T(8,128)S(1)} %get-tuple-element.327), channel_id=1, source_target_pairs={{0,4},{1,5},{2,6},{3,7},{4,0},{5,1},{6,2},{7,3},{8,12},{9,13},{10,... | collective-permute-start | bytes 147464 | tf_op jit(solution)/shard_map/ppermute | solution.py:804
  187.9 10.4 %collective-permute-start.40 = (bf16[48,1536]{1,0:T(8,128)(2,1)S(1)}, bf16[48,1536]{1,0:T(8,128)(2,1)S(1)}, u32[]{:S(2)}, u32[]{:S(2)}) collective-permute-start(bf16[48,1536]{1,0:T(8,128)(2,1)S(1)} %sum_far.6.refs_6_), channel_id=1, source_target_pairs={{0,16},{1,17},{2,18},{3,19},{4,20},{5,21},{6,22},{7,23},{8,24},{9,... | collective-permute-start | bytes 442376 | tf_op jit(solution)/shard_map/ppermute | solution.py:804
  190.1 8.3 %collective-permute-start.41 = (bf16[48,1536]{1,0:T(8,128)(2,1)S(1)}, bf16[48,1536]{1,0:T(8,128)(2,1)S(1)}, u32[]{:S(2)}, u32[]{:S(2)}) collective-permute-start(bf16[48,1536]{1,0:T(8,128)(2,1)S(1)} %get-tuple-element.332), channel_id=1, source_target_pairs={{0,8},{1,9},{2,10},{3,11},{4,12},{5,13},{6,14},{7,15},{8,0},{9,1},... | collective-permute-start | bytes 442376 | tf_op jit(solution)/shard_map/ppermute | solution.py:804
  190.7 7.6 %collective-permute-start.42 = (f32[16,768]{1,0:T(8,128)S(1)}, f32[16,768]{1,0:T(8,128)S(1)}, u32[]{:S(2)}, u32[]{:S(2)}) collective-permute-start(f32[16,768]{1,0:T(8,128)S(1)} %add.79), channel_id=1, source_target_pairs={{0,8},{1,9},{2,10},{3,11},{4,12},{5,13},{6,14},{7,15},{8,0},{9,1},... | collective-permute-start | bytes 147464 | tf_op jit(solution)/shard_map/ppermute | solution.py:804
  198.4 4.7 %collective-permute-start.44 = (f32[16,768]{1,0:T(8,128)S(1)}, f32[16,768]{1,0:T(8,128)S(1)}, u32[]{:S(2)}, u32[]{:S(2)}) collective-permute-start(f32[16,768]{1,0:T(8,128)S(1)} %add.80), channel_id=1, source_target_pairs={{0,16},{1,17},{2,18},{3,19},{4,20},{5,21},{6,22},{7,23},{8,24},{9,... | collective-permute-start | bytes 147464 | tf_op jit(solution)/shard_map/ppermute | solution.py:804
  199.6 5.9 %collective-permute-start.43 = (bf16[48,1536]{1,0:T(8,128)(2,1)S(1)}, bf16[48,1536]{1,0:T(8,128)(2,1)S(1)}, u32[]{:S(2)}, u32[]{:S(2)}) collective-permute-start(bf16[48,1536]{1,0:T(8,128)(2,1)S(1)} %sum_far.7.refs_3_), channel_id=1, source_target_pairs={{0,16},{1,17},{2,18},{3,19},{4,20},{5,21},{6,22},{7,23},{8,24},{9,... | collective-permute-start | bytes 442376 | tf_op jit(solution)/shard_map/ppermute | solution.py:804
  (17 other events, 99.6 us)

commit v5 on v4

--- a/solution.py
+++ b/solution.py
@@ -362,6 +362,22 @@
     )(*args)
 
 
+def call_all(co, jobs, name):
+    args = [arg for job in jobs for arg in job[2]]
+    outs = [out for job in jobs for out in job[1]]
+
+    def body(co_ref, *refs):
+        first, last = 0, len(args)
+        for kernel, job_outs, job_args in jobs:
+            ins = refs[first : first + len(job_args)]
+            results = refs[last : last + len(job_outs)]
+            kernel(co_ref, *ins, *results)
+            first += len(job_args)
+            last += len(job_outs)
+
+    return call(body, outs, [co, *args], name=name)
+
+
 def assemble_kernel(ranges, co, *refs):
     count = len(refs) - len(ranges)
     each = count // 2
@@ -436,14 +452,22 @@
     s1[:, 2 * D :] = mlp[:, lanes(FF + 1536 * r, D)].astype(BF)
 
 
-def first_norm_kernel(co, tokens, info, vec, h1, h1t, cols):
+def turn(co, values, scratch, send, keep):
+    scratch[...] = values.T
+    for out, core in ((send, 1 - co[3]), (keep, co[3])):
+        for block in range(8):
+            row = pl.multiple_of(block * 96 + 48 * core, 16)
+            out[block * 48 : block * 48 + 48, :] = scratch[pl.ds(row, 48), :].astype(BF)
+
+
+def first_norm_kernel(co, tokens, info, vec, h1, h1t_send, h1t_keep, cols, scratch):
     turned = jnp.transpose(info[...])
     cols[:, 0:8] = turned
     x0 = jnp.where(turned[:, 2:3] == 1.0, vec[8:9, :], tokens[...].astype(F32))
     xh, rstd = row_norm(x0)
     h = xh * vec[0:1, :] + vec[2:3, :]
     h1[...] = h.astype(BF)
-    h1t[...] = h.T.astype(BF)
+    turn(co, h, scratch, h1t_send, h1t_keep)
 
 
 def allowed_pairs(info, cols):
@@ -479,18 +503,22 @@
         att[:, pair * 128 : pair * 128 + 128] = jnp.where(low, mixed[0], mixed[1]).astype(BF)
 
 
-def second_norm_kernel(co, tokens, cols, vec, att, weight, y1, h2, h2t):
+def second_norm_kernel(
+    co, tokens, cols, vec, att, weight, dz, y1, h2, h2t_send, h2t_keep, dzt_send, dzt_keep, scratch
+):
     x0 = jnp.where(cols[:, 2:3] == 1.0, vec[8:9, :], tokens[...].astype(F32))
     y = x0 + nt(att[...], whole(weight, 0, D)) + vec[5:6, :]
     y1[...] = y
     xh, rstd = row_norm(y)
     h = xh * vec[1:2, :] + vec[6:7, :]
     h2[...] = h.astype(BF)
-    h2t[...] = h.T.astype(BF)
-
-
-def hidden_kernel(co, h2, vec, dz, w0, w1, g0, g1, slope0, slope1, send, keep, dzt, scratch):
-    dzt[...] = dz[...].astype(F32).T.astype(BF)
+    turn(co, h, scratch, h2t_send, h2t_keep)
+    turn(co, dz[...].astype(F32), scratch, dzt_send, dzt_keep)
+
+
+def hidden_kernel(
+    co, h2, vec, dzt_send, dzt_keep, w0, w1, g0, g1, slope0, slope1, send, keep
+):
     for part, weight, g, slope in ((0, w0, g0, slope0), (1, w1, g1, slope1)):
         for b in range(2):
             half = lax.bitwise_xor(co[0], b)
@@ -504,13 +532,26 @@
                 slope[:, at] = phi + u * (
                     jnp.exp(-0.5 * u * u) * (1.0 / math.sqrt(2.0 * math.pi))
                 )
-                scratch[...] = nn(dzt[...], act)
                 dst = lanes(half * D + sub, 384) if part == 0 else lanes((2 + b) * D + sub, 384)
-                share_rows(co[3], scratch, send, keep, dst)
+                share_rows(dzt_send, dzt_keep, act, send, keep, dst)
 
 
 def hidden_grad_kernel(
-    co, dz, slope0, slope1, w00, w01, w10, w11, left, du0, du1, db1, send, keep, scratch
+    co,
+    dz,
+    slope0,
+    slope1,
+    w00,
+    w01,
+    w10,
+    w11,
+    left_send,
+    left_keep,
+    du0,
+    du1,
+    db1,
+    send,
+    keep,
 ):
     for part, slope, du in ((0, slope0, du0), (1, slope1, du1)):
         for b in range(2):
@@ -524,9 +565,8 @@
                 db1[pl.ds(2 * half + part, 1), sub : sub + 384] = jnp.sum(
                     d.astype(F32), axis=0, keepdims=True
                 )
-                scratch[...] = nn(left[...], d)
                 dst = lanes(half * D + sub, 384) if part == 0 else lanes((2 + b) * D + sub, 384)
-                share_rows(co[3], scratch, send, keep, dst)
+                share_rows(left_send, left_keep, d, send, keep, dst)
 
 
 def output_kernel(co, y1, vec, g0, g1, w00, w01, w10, w11, act):
@@ -537,28 +577,27 @@
     act[...] = acc.astype(BF)
 
 
-def share_rows(c, scratch, send, keep, dst):
-    for k in range(4):
-        for i in range(2):
-            row = k * 192 + i * 96
-            theirs = scratch[pl.ds(pl.multiple_of(row + 48 * (1 - c), 16), 48), :]
-            mine = scratch[pl.ds(pl.multiple_of(row + 48 * c, 16), 48), :]
-            send[k, i, :, dst] = theirs.astype(BF)
-            keep[k, i, :, dst] = mine
-
-
-def attention_grad_kernel(co, h1t, dqkv, dpt, att, send, keep, scratch):
-    moves = [(h1t, dqkv, b * 1152 + 384 + n * 384, b * D + n * 384) for b in (0, 1) for n in (0, 1)]
+def share_rows(left_send, left_keep, right, send, keep, dst):
+    send[:, dst] = nn(left_send[...], right).astype(BF)
+    keep[:, dst] = nn(left_keep[...], right)
+
+
+def attention_grad_kernel(
+    co, h1t_send, h1t_keep, dqkv, dpt_send, dpt_keep, att, send, keep
+):
+    first, second = (h1t_send, h1t_keep), (dpt_send, dpt_keep)
+    moves = [(first, dqkv, b * 1152 + 384 + n * 384, b * D + n * 384) for b in (0, 1) for n in (0, 1)]
     for b in range(2):
         place = 384 * lax.bitwise_xor(co[0], b)
-        moves.append((h1t, dqkv, b * 1152, 2 * D + place))
-        moves.append((dpt, att, b * 384, 3 * D + place))
+        moves.append((first, dqkv, b * 1152, 2 * D + place))
+        moves.append((second, att, b * 384, 3 * D + place))
     for left, right, src, dst in moves:
-        scratch[...] = nn(left[...], right[:, src : src + 384])
-        share_rows(co[3], scratch, send, keep, lanes(dst, 384))
-
-
-def second_back_kernel(co, dz, y1, vec, du0, du1, w0, w1, weight_o, dy1, datt, dpt, small):
+        share_rows(*left, right[:, src : src + 384], send, keep, lanes(dst, 384))
+
+
+def second_back_kernel(
+    co, dz, y1, vec, du0, du1, w0, w1, weight_o, dy1, datt, dpt_send, dpt_keep, small, scratch
+):
     yh, rstd = row_norm(y1[...])
     dy = dz[...].astype(F32)
     dh = nt(du0[...], whole(w0, 0, 2 * D)) + nt(du1[...], whole(w1, 0, 2 * D))
@@ -571,7 +610,7 @@
     )
     dy1[...] = d
     small[2:3, :] = jnp.sum(d, axis=0, keepdims=True)
-    dpt[...] = d.T.astype(BF)
+    turn(co, d, scratch, dpt_send, dpt_keep)
     datt[...] = nn(d.astype(BF), whole(weight_o, 0, D)).astype(BF)
 
 
@@ -674,7 +713,7 @@
     last[...] = both(keep, got, every, every, every, slice(3 * D, 4 * D))
 
 
-def split_fourth_kernel(co, x_keep, x_got, last, vec, far_keep, far_got, y_send, y_keep):
+def split_fourth_kernel(co, x_keep, x_got, last, far_keep, far_got, y_send, y_keep):
     y = co[2]
     for out, i in ((y_send, 1 - y), (y_keep, y)):
         for k in range(4):
@@ -682,9 +721,10 @@
             out[rows, :D] = both(x_keep, x_got, k, i).astype(out.dtype)
             out[rows, D:] = last[k, i].astype(out.dtype)
         row = pl.multiple_of(96 + i * 48, 16)
-        out[192:240, :D] = both(far_keep, far_got, pl.ds(row, 48)).astype(out.dtype)
-        out[192:208, D:] = vec[...].astype(out.dtype)
-        out[208:240, D:] = jnp.zeros((32, D), out.dtype)
+        block = both(far_keep, far_got, pl.ds(row, 48)).astype(out.dtype)
+        out[192:224, :D] = block[:32]
+        out[192:208, D:] = block[32:]
+        out[208:224, D:] = jnp.zeros((16, D), out.dtype)
 
 
 def split_near_first_kernel(co, keep, got, up_keep, up_got, send, rest):
@@ -730,8 +770,8 @@
             row = pl.multiple_of((2 * far + at) * 48, 16)
             out[far * 48 : far * 48 + 48, :] = both(keep, got, pl.ds(row, 48)).astype(out.dtype)
     if small:
-        small[0][...] = both(keep, got, slice(192, 208), slice(D, 2 * D))
-        small[1][...] = both(keep, got, slice(192, 240), slice(0, D))
+        small[0][0:32, :] = both(keep, got, slice(192, 224), slice(0, D))
+        small[0][32:48, :] = both(keep, got, slice(192, 208), slice(D, 2 * D))
 
 
 def split_far_kernel(co, keep, got, send, rest):
@@ -858,10 +898,12 @@
     across2 = swap(stack2, Y)
     far1 = swap(jnp.concatenate([stack1[:, 2 * D :], across1[:, 2 * D :]], axis=0), X)
     pieces1 = core_pair([stack1, across1])
-    h1, h1t, cols = call(
+    halves_t = [((384, 256), BF)] * 2
+    h1, h1t_send, h1t_keep, cols = call(
         first_norm_kernel,
-        [((256, D), BF), ((D, 256), BF), ((256, 128), F32)],
+        [((256, D), BF), *halves_t, ((256, 128), F32)],
         [co, tokens, info, vec],
+        scratch=[pltpu.VMEM((D, 256), F32)],
         name="norm1",
     )
     (w_qkv,) = assemble(co, pieces0, (0, 1152))
@@ -874,20 +916,23 @@
     w_out, w_up0 = assemble(co, pieces0, (1152, 384), (1536, 768))
     w_up1, w_down00 = assemble(co, pieces1, (0, 1536), (1536, 768))
 
-    y1, h2, h2t = call(
+    y1, h2, h2t_send, h2t_keep, dzt_send, dzt_keep = call(
         second_norm_kernel,
-        [((256, D), F32), ((256, D), BF), ((D, 256), BF)],
-        [co, tokens, cols, vec, att, w_out],
+        [((256, D), F32), ((256, D), BF), *halves_t, *halves_t],
+        [co, tokens, cols, vec, att, w_out, cotangent],
+        scratch=[pltpu.VMEM((D, 256), F32)],
         name="norm2",
     )
-    shares = [((4, 2, 48, 4 * D), BF), ((4, 2, 48, 4 * D), F32)]
+    shares = [((384, 4 * D), BF), ((384, 4 * D), F32)]
     g0, g1, slope0, slope1, down_send, down_keep = call(
         hidden_kernel,
         [((256, 2 * D), BF)] * 2 + [((256, 2 * D), F32)] * 2 + shares,
-        [co, h2, vec, cotangent, w_up0, w_up1],
-        scratch=[pltpu.VMEM((D, 256), BF), pltpu.VMEM((D, 384), F32)],
+        [co, h2, vec, dzt_send, dzt_keep, w_up0, w_up1],
         name="hidden",
     )
+
+    def blocks(array):
+        return array.reshape(4, 2, 48, -1)
 
     rate = base_rate / math.sqrt(tokens.shape[0] * 32)
 
@@ -922,14 +967,14 @@
     pieces2 = core_pair([stack2, across2])
     far1 = core_pair([far1])
     pieces2, far1, down_send = hold((pieces2, far1, down_send))
-    down_got = swap(down_send, CORE)
+    down_got = blocks(swap(down_send, CORE))
+    down_keep = blocks(down_keep)
     w_down01, w_down11 = assemble(co, pieces2, (0, D), (D, D))
     (w_down10,) = assemble(co, far1, (0, D))
     du0, du1, db1, up_send, up_keep = call(
         hidden_grad_kernel,
         [((256, 2 * D), BF), ((256, 2 * D), BF), ((8, D), F32)] + shares,
-        [co, cotangent, slope0, slope1, w_down00, w_down01, w_down10, w_down11, h2t],
-        scratch=[pltpu.VMEM((D, 384), F32)],
+        [co, cotangent, slope0, slope1, w_down00, w_down01, w_down10, w_down11, h2t_send, h2t_keep],
         name="hidden_grad",
     )
     down_got, up_send = hold((down_got, up_send))
@@ -941,11 +986,13 @@
     y_send0, x_send1, up_send, du0 = hold((y_send0, x_send1, up_send, du0))
     y_got0 = swap(y_send0, Y)
     x_got1 = swap(x_send1, X)
-    up_got = swap(up_send, CORE)
-    dy1, datt, dpt, small2 = call(
+    up_got = blocks(swap(up_send, CORE))
+    up_keep = blocks(up_keep)
+    dy1, datt, dpt_send, dpt_keep, small2 = call(
         second_back_kernel,
-        [((256, D), F32), ((256, D), BF), ((D, 256), BF), ((8, D), F32)],
+        [((256, D), F32), ((256, D), BF), *halves_t, ((8, D), F32)],
         [co, cotangent, y1, vec, du0, du1, w_up0, w_up1, w_out],
+        scratch=[pltpu.VMEM((D, 256), F32)],
         name="norm2_back",
     )
     dqkv, small_a = call(
@@ -957,8 +1004,7 @@
     attn_send, attn_keep = call(
         attention_grad_kernel,
         shares,
-        [co, h1t, dqkv, dpt, att],
-        scratch=[pltpu.VMEM((D, 384), F32)],
+        [co, h1t_send, h1t_keep, dqkv, dpt_send, dpt_keep, att],
         name="attention_grad",
     )
 
@@ -983,25 +1029,36 @@
     def sum_far(keep, got):
         return call(sum_far_kernel, [(keep.shape, BF)], [co, keep, got], name="sum_far")[0]
 
+    def near_job(keep, got, small=()):
+        width = keep.shape[1]
+        return split_near_kernel, [((96, width), BF), ((96, width), F32), *small], [keep, got]
+
+    def far_job(keep, got):
+        width = keep.shape[1]
+        return split_far_kernel, [((48, width), BF), ((48, width), F32)], [keep, got]
+
+    def sum_job(keep, got):
+        return sum_far_kernel, [(keep.shape, BF)], [keep, got]
+
     y_got0, x_got1, up_got, attn_send = hold((y_got0, x_got1, up_got, attn_send))
-    y_send1, y_keep1, x_send2, x_keep2 = call(
-        split_second_kernel,
-        y_shares + x_shares,
-        [co, x_keep1, x_got1, up_keep, up_got],
-        name="split_second",
-    )
-    y_got0 = hold((y_got0, y_send1))[0]
-    near_send0, near_keep0 = call(
-        split_near_first_kernel,
-        [((384, D), BF), ((384, D), F32)],
-        [co, y_keep0, y_got0, up_keep, up_got],
-        name="split_near",
+    y_send1, y_keep1, x_send2, x_keep2, near_send0, near_keep0 = call_all(
+        co,
+        [
+            (split_second_kernel, y_shares + x_shares, [x_keep1, x_got1, up_keep, up_got]),
+            (
+                split_near_first_kernel,
+                [((384, D), BF), ((384, D), F32)],
+                [y_keep0, y_got0, up_keep, up_got],
+            ),
+        ],
+        "split_third_round",
     )
     dqkv = hold((dqkv, near_send0))[0]
     y_got1 = swap(y_send1, Y)
     x_got2 = swap(x_send2, X)
     near_got0 = swap(near_send0, Z)
-    attn_got = swap(attn_send, CORE)
+    attn_got = blocks(swap(attn_send, CORE))
+    attn_keep = blocks(attn_keep)
     input_grad, total = call(
         first_back_kernel,
         [((256, D), BF), ((16, D), F32)],
@@ -1043,8 +1100,8 @@
     )
     y_send3, y_keep3 = call(
         split_fourth_kernel,
-        [((240, 2 * D), BF), ((240, 2 * D), F32)],
-        [co, x_keep3, x_got3, last, total, far_keep0, far_got0],
+        [((224, 2 * D), BF), ((224, 2 * D), F32)],
+        [co, x_keep3, x_got3, last, far_keep0, far_got0],
         name="split_fourth",
     )
     y_got2 = hold((y_got2, y_send3))[0]
@@ -1059,13 +1116,15 @@
     near_got2 = swap(near_send2, Z)
     far_got1 = swap(far_send1, 2 * Z)
     got0 = swap(mine0, X)
-    got0, far_got1, near_got2, y_got3 = hold((got0, far_got1, near_got2, y_got3))
-    near_send3, near_keep3, total, other = split_near(
-        y_keep3, y_got3, [((16, D), F32), ((48, D), F32)]
-    )
-    near_got2 = hold((near_got2, near_send3))[0]
-    far_send2, far_keep2 = split_far(near_keep2, near_got2)
-    far_got1 = hold((far_got1, far_send2))[0]
+    total = total + swap(total, 2 * Z)
+    got0, far_got1, near_got2, y_got3, total = hold(
+        (got0, far_got1, near_got2, y_got3, total)
+    )
+    near_send3, near_keep3, other, far_send2, far_keep2 = call_all(
+        co,
+        [near_job(y_keep3, y_got3, [((48, D), F32)]), far_job(near_keep2, near_got2)],
+        "split_sixth_round",
+    )
     (mine1,) = call(
         sum_far_second_kernel,
         [((48, 3 * D), BF)],
@@ -1082,7 +1141,7 @@
     mine2 = sum_far(far_keep2, far_got2)
     far_got3 = swap(far_send3, 2 * Z)
     got2 = swap(mine2, X)
-    total = total + swap(total, 2 * Z)
+    total = total + swap(total, Y)
     moves = [(0, (0, 1), 0, h * D, D, None, FF + h * 2 * D, 0) for h in range(2)]
     moves += [(0, (2 + b,), 0, 0, D, b, FF + D, 2 * D) for b in range(2)]
     moves += [(0, (2, 3), 0, D + h * D, D, None, h * 2 * D, 0) for h in range(2)]

time: 208 us -> 204 us (0.981)
    pallas_call x33 -> x31, Pallas kernels: 53.3 us -> 51.2 us  [call(): pl.pallas_call(body, out_shape=[jax.ShapeDtypeStruct(shape, dtype) for sh...]
    ppermute x45 -> x46, starting transfers between devices: 35.6 us -> 33.6 us  [swap(): lax.ppermute(array, ('rep', 'fsdp'), [(i, i ^ mask) for i in range(32)])]
    ppermute x45 -> x46, waiting for transfers between devices: 47.8 us -> 48.3 us  [swap(): lax.ppermute(array, ('rep', 'fsdp'), [(i, i ^ mask) for i in range(32)])]
  transfers between devices with their start and end apart: 45 -> 46, of which waited for: 17 -> 17; matrix products, arithmetic and copies ran while one was open for 1% -> 1% of each run, Pallas kernels for 24% -> 23%
where the time goes in v5:
time: 204 us
  blocking collectives  58.2 us (29%)
  Pallas kernels  57.4 us (28%)
  waiting for transfers between devices  48.3 us (24%)
  starting transfers between devices  33.6 us (16%)
  other arithmetic  4.64 us (2%)
    all_gather x3, blocking collectives, along_z(): lax.all_gather(shard, 'fsdp', axis=0, tiled=True, axis_index_groups=groups)  58.2 us
    pallas_call x31, Pallas kernels, call(): pl.pallas_call(body, out_shape=[jax.ShapeDtypeStruct(shape, dtype) for sh...  51.2 us
    ppermute x46, waiting for transfers between devices, swap(): lax.ppermute(array, ('rep', 'fsdp'), [(i, i ^ mask) for i in range(32)])  48.3 us
    ppermute x46, starting transfers between devices, swap(): lax.ppermute(array, ('rep', 'fsdp'), [(i, i ^ mask) for i in range(32)])  33.6 us
    pallas_call x3, Pallas kernels, update(): pl.pallas_call(functools.partial(update_kernel, rate, moves, len(states),...  6.15 us
  transfers between devices with their start and end apart: 46, of which 17 were waited for; matrix products, arithmetic and copies ran while one was open for 1% of the time, Pallas kernels for 23%

profile of v5, /device:TPU:0, one launch (start us, length us, event | category | flops | bytes accessed | tf_op | source)
XLA Modules:
  0.0 204.0 jit_solution(16245822936351426370)
XLA Ops:
  2.9 2.6 %prep.2 = bf16[48,2304]{1,0:T(8,128)(2,1)} custom-call(s32[4]{0:T(128)} %pad_add_fusion.co_ref.co, f32[48,3072]{1,0:T(8,128)} %refs_0_.16, f32[48,6144]{1,0:T(8,128)} %refs_0_.15), custom_call_target="tpu_custom_call" | custom-call | flops 1048576 | bytes 1048576 | tf_op jit(solution)/shard_map/prep/pallas_call | solution.py:352
  5.5 22.6 %all_gather.9.refs_0_ = bf16[192,2304]{1,0:T(8,128)(2,1)S(1)} all-gather(bf16[48,2304]{1,0:T(8,128)(2,1)} %prep.2), channel_id=1, replica_groups={{0,4,8,12},{1,5,9,13},{2,6,10,14},{3,7,11,15},{16,20,24,28},{17,21,25,2..., dimensions={0}, use_global_device_ids=true | all-gather | bytes 1105920 | tf_op jit(solution)/shard_map/all_gather | solution.py:868
  28.1 1.5 collective-permute-start.2
  29.6 1.5 collective-permute-start.1
  32.9 19.2 %all_gather.10.refs_0_ = bf16[192,2304]{1,0:T(8,128)(2,1)S(1)} all-gather(bf16[48,2304]{1,0:T(8,128)(2,1)S(1)} %get-tuple-element.201), channel_id=1, replica_groups={{0,4,8,12},{1,5,9,13},{2,6,10,14},{3,7,11,15},{16,20,24,28},{17,21,25,2..., dimensions={0}, use_global_device_ids=true | all-gather | bytes 1105920 | tf_op jit(solution)/shard_map/all_gather | solution.py:868
  52.5 1.6 collective-permute-start.6
  54.8 4.1 %collective-permute-done.5 = f32[16,768]{1,0:T(8,128)S(1)} collective-permute-done((f32[16,768]{1,0:T(8,128)S(1)}, f32[16,768]{1,0:T(8,128)S(1)}, u32[]{:S(2)}, u32[]{:S(2)}) %collective-permute-start.5) | collective-permute-done | bytes 49184 | tf_op jit(solution)/shard_map/ppermute | solution.py:844
  58.9 0.9 collective-permute-start.10
  59.8 16.4 %all_gather.11.refs_0_ = bf16[192,1536]{1,0:T(8,128)(2,1)S(1)} all-gather(bf16[48,1536]{1,0:T(8,128)(2,1)S(1)} %get-tuple-element.207), channel_id=1, replica_groups={{0,4,8,12},{1,5,9,13},{2,6,10,14},{3,7,11,15},{16,20,24,28},{17,21,25,2..., dimensions={0}, use_global_device_ids=true | all-gather | bytes 737280 | tf_op jit(solution)/shard_map/all_gather | solution.py:868
  77.1 1.6 collective-permute-start.15
  79.2 1.3 norm1.1
  81.4 3.5 %attention.1 = (bf16[256,2304]{1,0:T(8,128)(2,1)S(1)}, bf16[256,768]{1,0:T(8,128)(2,1)S(1)}, f32[16,256]{1,0:T(8,128)S(1)}) custom-call(s32[4]{0:T(128)S(1)} %copy-done.8, bf16[256,768]{1,0:T(8,128)(2,1)S(1)} %get-tuple-element.215.refs_0_, f32[16,768]{1,0:T(8,128)S(1)} %add.80.refs_2_.refs_1_.refs_3_, f32[8,256]{1,0:T(8,128)S(1)} %scatter.4.refs_1_.refs_2_.refs_0_, ...), custom_call_target="tpu_custom_call" | custom-call | flops 1048576 | bytes 1048576 | tf_op jit(solution)/shard_map/attention/pallas_call | solution.py:352
  85.9 1.7 norm2.1
  88.4 5.9 %hidden.1 = (bf16[256,1536]{1,0:T(8,128)(2,1)S(1)}, bf16[256,1536]{1,0:T(8,128)(2,1)S(1)}, f32[256,1536]{1,0:T(8,128)S(1)}, f32[256,1536]{1,0:T(8,128)S(1)}, bf1...) custom-call(s32[4]{0:T(128)S(1)} %copy-done.8, bf16[256,768]{1,0:T(8,128)(2,1)S(1)} %get-tuple-element.222.refs_0_, ...), custom_call_target="tpu_custom_call" | custom-call | flops 1048576 | bytes 1048576 | tf_op jit(solution)/shard_map/hidden/pallas_call | solution.py:352
  94.9 1.5 collective-permute-done.17.refs_3_
  96.5 0.8 collective-permute-done.18.refs_1_
  99.0 5.3 %hidden_grad.1 = (bf16[256,1536]{1,0:T(8,128)(2,1)S(1)}, bf16[256,1536]{1,0:T(8,128)(2,1)S(1)}, f32[8,768]{1,0:T(8,128)S(1)}, bf16[384,3072]{1,0:T(8,128)(2,1)S(1)}, f32[384,3072]{1,0:T(8,128)S(1)}) custom-call(s32[4]{0:T(128)S(1)} %copy-done.8, bf16[256,768]{1,0:T(8,128)(2,1)S(1)} %copy-done.4, f32[256,1536]{1,0:T(8,128)S(1)} %get-tuple-element.235.refs_1_, ...), custom_call_target="tpu_custom_call" | custom-call | flops 1048576 | bytes 1048576 | tf_op jit(solution)/shard_map/hidden_grad/pallas_call | solution.py:352
  104.3 0.9 split_first.1
  105.4 1.5 collective-permute-start.20
  107.5 3.2 %norm2_back.1 = (f32[256,768]{1,0:T(8,128)S(1)}, bf16[256,768]{1,0:T(8,128)(2,1)S(1)}, bf16[384,256]{1,0:T(8,128)(2,1)S(1)}, bf16[384,256]{1,0:T(8,128)(2,1)S(1)}, f32[8,768]{1,0:T(8,128)S(1)}) custom-call(s32[4]{0:T(128)S(1)} %copy-done.8, bf16[256,768]{1,0:T(8,128)(2,1)S(1)} %copy-done.4, f32[256,768]{1,0:T(8,128)S(1)} %get-tuple-element.300.refs_1_.refs_0_, ...), custom_call_target="tpu_custom_call" | custom-call | flops 1048576 | bytes 1048576 | tf_op jit(solution)/shard_map/norm2_back/pallas_call | solution.py:352
  110.7 5.6 %attention_back.1 = (bf16[256,2304]{1,0:T(8,128)(2,1)S(1)}, f32[8,768]{1,0:T(8,128)S(1)}) custom-call(s32[4]{0:T(128)S(1)} %copy-done.8, f32[8,256]{1,0:T(8,128)S(1)} %scatter.4.refs_1_.refs_2_.refs_0_, f32[256,128]{1,0:T(8,128)S(1)} %get-tuple-element.214.refs_3_.refs_1_.refs_2_, f32[16,256]{1,0:T(8,128)S(1)} %get-tuple-element.260.refs_2_, ...), custom_call_target="tpu_custom_call" | custom-call | flops 1048576 | bytes 1048576 | tf_op jit(solution)/shard_map/attention_back/pallas_call | solution.py:352
  116.2 2.6 %attention_grad.1 = (bf16[384,3072]{1,0:T(8,128)(2,1)S(1)}, f32[384,3072]{1,0:T(8,128)S(1)}) custom-call(s32[4]{0:T(128)S(1)} %copy-done.8, bf16[384,256]{1,0:T(8,128)(2,1)S(1)} %get-tuple-element.258.refs_0_, bf16[384,256]{1,0:T(8,128)(2,1)S(1)} %get-tuple-element.259.refs_1_, bf16[256,2304]{1,0:T(8,128)(2,1)S(1)} %get-tuple-element.280.refs_2_.refs_0_, ...), custom_call_target="tpu_custom_call" | custom-call | flops 1048576 | bytes 1048576 | tf_op jit(solution)/shard_map/attention_grad/pallas_call | solution.py:352
  118.8 2.2 %collective-permute-done.20.refs_5_ = bf16[192,1536]{1,0:T(8,128)(2,1)S(1)} collective-permute-done((bf16[192,1536]{1,0:T(8,128)(2,1)S(1)}, bf16[192,1536]{1,0:T(8,128)(2,1)S(1)}, u32[]{:S(2)}, u32[]{:S(2)}) %collective-permute-start.20) | collective-permute-done | bytes 589856 | tf_op jit(solution)/shard_map/ppermute | solution.py:844
  121.0 1.2 collective-permute-done.21.refs_1_
  122.3 1.1 split_third_round.1
  124.5 2.7 %norm1_back.1 = (bf16[256,768]{1,0:T(8,128)(2,1)}, f32[16,768]{1,0:T(8,128)S(1)}) custom-call(s32[4]{0:T(128)S(1)} %copy-done.8, bf16[256,2304]{1,0:T(8,128)(2,1)S(1)} %get-tuple-element.280.refs_2_.refs_0_, bf16[256,768]{1,0:T(8,128)(2,1)S(1)} %copy-done.5, f32[256,128]{1,0:T(8,128)S(1)} %get-tuple-element.214.refs_3_.refs_1_.refs_2_, ...), custom_call_target="tpu_custom_call" | custom-call | flops 1048576 | bytes 1048576 | tf_op jit(solution)/shard_map/norm1_back/pallas_call | solution.py:352
  127.3 12.0 %collective-permute-done.24.refs_1_ = bf16[192,1536]{1,0:T(8,128)(2,1)S(1)} collective-permute-done((bf16[192,1536]{1,0:T(8,128)(2,1)S(1)}, bf16[192,1536]{1,0:T(8,128)(2,1)S(1)}, u32[]{:S(2)}, u32[]{:S(2)}) %collective-permute-start.24) | collective-permute-done | bytes 589856 | tf_op jit(solution)/shard_map/ppermute | solution.py:844
  140.4 1.0 split_third.1
  141.4 1.6 collective-permute-start.30
  142.9 1.5 collective-permute-start.29
  145.5 1.5 collective-permute-start.27
  147.0 2.7 %output.1 = bf16[256,768]{1,0:T(8,128)(2,1)} custom-call(s32[4]{0:T(128)S(1)} %copy-done.8, f32[256,768]{1,0:T(8,128)S(1)} %get-tuple-element.300.refs_1_.refs_0_, f32[16,768]{1,0:T(8,128)S(1)} %add.80.refs_2_.refs_1_.refs_3_, bf16[256,1536]{1,0:T(8,128)(2,1)S(1)} %get-tuple-element.301.refs_2_, bf16[256,1536]{1,0:T(8,128)(2,1)S(1)} %get-tuple-element.302.refs_3_, ...), custom_call_target="tpu_custom_call" | custom-call | flops 1048576 | bytes 1048576 | tf_op jit(solution)/shard_map/output/pallas_call | solution.py:352
  149.7 8.2 %collective-permute-done.28.refs_1_ = bf16[96,1536]{1,0:T(8,128)(2,1)S(1)} collective-permute-done((bf16[96,1536]{1,0:T(8,128)(2,1)S(1)}, bf16[96,1536]{1,0:T(8,128)(2,1)S(1)}, u32[]{:S(2)}, u32[]{:S(2)}) %collective-permute-start.28) | collective-permute-done | bytes 294944 | tf_op jit(solution)/shard_map/ppermute | solution.py:844
  158.0 2.2 %collective-permute-done.27.refs_4_.refs_1_ = bf16[192,768]{1,0:T(8,128)(2,1)S(1)} collective-permute-done((bf16[192,768]{1,0:T(8,128)(2,1)S(1)}, bf16[192,768]{1,0:T(8,128)(2,1)S(1)}, u32[]{:S(2)}, u32[]{:S(2)}) %collective-permute-start.27) | collective-permute-done | bytes 294944 | tf_op jit(solution)/shard_map/ppermute | solution.py:844
  164.1 2.3 %collective-permute-start.33 = (bf16[48,1536]{1,0:T(8,128)(2,1)S(1)}, bf16[48,1536]{1,0:T(8,128)(2,1)S(1)}, u32[]{:S(2)}, u32[]{:S(2)}) collective-permute-start(bf16[48,1536]{1,0:T(8,128)(2,1)S(1)} %get-tuple-element.319), channel_id=1, source_target_pairs={{0,8},{1,9},{2,10},{3,11},{4,12},{5,13},{6,14},{7,15},{8,0},{9,1},... | collective-permute-start | bytes 442376 | tf_op jit(solution)/shard_map/ppermute | solution.py:844
  167.0 6.3 %collective-permute-done.36 = f32[16,768]{1,0:T(8,128)S(1)} collective-permute-done((f32[16,768]{1,0:T(8,128)S(1)}, f32[16,768]{1,0:T(8,128)S(1)}, u32[]{:S(2)}, u32[]{:S(2)}) %collective-permute-start.36) | collective-permute-done | bytes 49184 | tf_op jit(solution)/shard_map/ppermute | solution.py:844
  173.3 1.6 collective-permute-done.35.refs_1_
  177.7 1.5 collective-permute-start.38
  179.1 1.5 collective-permute-start.40
  180.6 4.0 %collective-permute-done.40 = f32[16,768]{1,0:T(8,128)S(1)} collective-permute-done((f32[16,768]{1,0:T(8,128)S(1)}, f32[16,768]{1,0:T(8,128)S(1)}, u32[]{:S(2)}, u32[]{:S(2)}) %collective-permute-start.40) | collective-permute-done | bytes 49184 | tf_op jit(solution)/shard_map/ppermute | solution.py:844
  185.9 1.4 collective-permute-start.41
  187.3 2.1 %collective-permute-start.42 = (bf16[48,1536]{1,0:T(8,128)(2,1)S(1)}, bf16[48,1536]{1,0:T(8,128)(2,1)S(1)}, u32[]{:S(2)}, u32[]{:S(2)}) collective-permute-start(bf16[48,1536]{1,0:T(8,128)(2,1)S(1)} %get-tuple-element.336), channel_id=1, source_target_pairs={{0,8},{1,9},{2,10},{3,11},{4,12},{5,13},{6,14},{7,15},{8,0},{9,1},... | collective-permute-start | bytes 442376 | tf_op jit(solution)/shard_map/ppermute | solution.py:844
  189.9 2.4 %update_mlp.1 = (f32[48,6144]{1,0:T(8,128)}, f32[48,6144]{1,0:T(8,128)}, f32[48,6144]{1,0:T(8,128)}, bf16[48,6144]{1,0:T(8,128)(2,1)}) custom-call(s32[4]{0:T(128)S(1)} %copy-done.8, f32[48,6144]{1,0:T(8,128)S(1)} %copy-done, f32[48,6144]{1,0:T(8,128)S(1)} %copy-done.2, f32[48,6144]{1,0:T(8,128)S(1)} %copy-done.3, bf16[48,1536]{1,0:T(8,128)(2,1)S(1)} %sum_far.4.refs_3_, ...), custom_call_target="tpu_custom_call" | custom-call | flops 1048576 | bytes 1048576 | tf_op jit(solution)/shard_map/update_mlp/pallas_call | solution.py:949
  192.3 1.1 collective-permute-done.43
  193.5 1.5 collective-permute-done.42.refs_1_
  195.9 1.8 collective-permute-start.44
  197.7 1.8 update_both.1
  202.0 1.9 update_attn.1
  (145 shorter events, 27.6 us)
Async XLA Ops:
  2.9 28.2 %copy-start = (f32[48,6144]{1,0:T(8,128)S(1)}, f32[48,6144]{1,0:T(8,128)}, u32[]{:S(2)}) copy-start(f32[48,6144]{1,0:T(8,128)} %refs_0_.15) | copy-start | bytes 3538948
  2.9 28.2 %copy-start.8 = (s32[4]{0:T(128)S(1)}, s32[4]{0:T(128)}, u32[]{:S(2)}) copy-start(s32[4]{0:T(128)} %pad_add_fusion.co_ref.co) | copy-start | bytes 52
  28.1 24.3 %collective-permute-start.3 = (bf16[192,2304]{1,0:T(8,128)(2,1)S(1)}, bf16[192,2304]{1,0:T(8,128)(2,1)S(1)}, u32[]{:S(2)}, u32[]{:S(2)}) collective-permute-start(bf16[192,2304]{1,0:T(8,128)(2,1)S(1)} %all_gather.9.refs_0_), channel_id=1, source_target_pairs={{0,1},{1,0},{2,3},{3,2},{4,5},{5,4},{6,7},{7,6},{8,9},{9,8},{10,11... | collective-permute-start | bytes 2654216 | tf_op jit(solution)/shard_map/ppermute | solution.py:844
  28.1 24.3 %collective-permute-start.2 = (bf16[192,2304]{1,0:T(8,128)(2,1)S(1)}, bf16[192,2304]{1,0:T(8,128)(2,1)S(1)}, u32[]{:S(2)}, u32[]{:S(2)}) collective-permute-start(bf16[192,2304]{1,0:T(8,128)(2,1)S(1)} %all_gather.9.refs_0_), channel_id=1, source_target_pairs={{0,16},{1,17},{2,18},{3,19},{4,20},{5,21},{6,22},{7,23},{8,24},{9,... | collective-permute-start | bytes 2654216 | tf_op jit(solution)/shard_map/ppermute | solution.py:844
  29.6 22.9 %collective-permute-start.1 = (bf16[192,2304]{1,0:T(8,128)(2,1)S(1)}, bf16[192,2304]{1,0:T(8,128)(2,1)S(1)}, u32[]{:S(2)}, u32[]{:S(2)}) collective-permute-start(bf16[192,2304]{1,0:T(8,128)(2,1)S(1)} %all_gather.9.refs_0_), channel_id=1, source_target_pairs={{0,2},{1,3},{2,0},{3,1},{4,6},{5,7},{6,4},{7,5},{8,10},{9,11},{10,... | collective-permute-start | bytes 2654216 | tf_op jit(solution)/shard_map/ppermute | solution.py:844
  31.1 1.2 collective-permute-start
  32.4 20.1 %collective-permute-start.4 = (f32[16,768]{1,0:T(8,128)S(1)}, f32[16,768]{1,0:T(8,128)S(1)}, u32[]{:S(2)}, u32[]{:S(2)}) collective-permute-start(f32[16,768]{1,0:T(8,128)S(1)} %add.77), channel_id=1, source_target_pairs={{0,2},{1,3},{2,0},{3,1},{4,6},{5,7},{6,4},{7,5},{8,10},{9,11},{10,... | collective-permute-start | bytes 147464 | tf_op jit(solution)/shard_map/ppermute | solution.py:844
  52.5 23.9 %collective-permute-start.9 = (bf16[192,2304]{1,0:T(8,128)(2,1)S(1)}, bf16[192,2304]{1,0:T(8,128)(2,1)S(1)}, u32[]{:S(2)}, u32[]{:S(2)}) collective-permute-start(bf16[192,2304]{1,0:T(8,128)(2,1)S(1)} %collective-permute-done.2.refs_2_), channel_id=1, source_target_pairs={{0,1},{1,0},{2,3},{3,2},{4,5},{5,4},{6,7},{7,6},{8,9},{9,8},{10,11... | collective-permute-start | bytes 2654216 | tf_op jit(solution)/shard_map/ppermute | solution.py:844
  52.5 23.8 %collective-permute-start.6 = (bf16[192,2304]{1,0:T(8,128)(2,1)S(1)}, bf16[192,2304]{1,0:T(8,128)(2,1)S(1)}, u32[]{:S(2)}, u32[]{:S(2)}) collective-permute-start(bf16[192,2304]{1,0:T(8,128)(2,1)S(1)} %all_gather.10.refs_0_), channel_id=1, source_target_pairs={{0,2},{1,3},{2,0},{3,1},{4,6},{5,7},{6,4},{7,5},{8,10},{9,11},{10,... | collective-permute-start | bytes 2654216 | tf_op jit(solution)/shard_map/ppermute | solution.py:844
  54.1 22.2 %collective-permute-start.8 = (bf16[192,2304]{1,0:T(8,128)(2,1)S(1)}, bf16[192,2304]{1,0:T(8,128)(2,1)S(1)}, u32[]{:S(2)}, u32[]{:S(2)}) collective-permute-start(bf16[192,2304]{1,0:T(8,128)(2,1)S(1)} %collective-permute-done.1.refs_1_), channel_id=1, source_target_pairs={{0,1},{1,0},{2,3},{3,2},{4,5},{5,4},{6,7},{7,6},{8,9},{9,8},{10,11... | collective-permute-start | bytes 2654216 | tf_op jit(solution)/shard_map/ppermute | solution.py:844
  54.3 22.1 %collective-permute-start.7 = (bf16[192,2304]{1,0:T(8,128)(2,1)S(1)}, bf16[192,2304]{1,0:T(8,128)(2,1)S(1)}, u32[]{:S(2)}, u32[]{:S(2)}) collective-permute-start(bf16[192,2304]{1,0:T(8,128)(2,1)S(1)} %collective-permute-done.1.refs_1_), channel_id=1, source_target_pairs={{0,16},{1,17},{2,18},{3,19},{4,20},{5,21},{6,22},{7,23},{8,24},{9,... | collective-permute-start | bytes 2654216 | tf_op jit(solution)/shard_map/ppermute | solution.py:844
  54.8 4.1 %collective-permute-start.5 = (f32[16,768]{1,0:T(8,128)S(1)}, f32[16,768]{1,0:T(8,128)S(1)}, u32[]{:S(2)}, u32[]{:S(2)}) collective-permute-start(f32[16,768]{1,0:T(8,128)S(1)} %add.78), channel_id=1, source_target_pairs={{0,4},{1,5},{2,6},{3,7},{4,0},{5,1},{6,2},{7,3},{8,12},{9,13},{10,... | collective-permute-start | bytes 147464 | tf_op jit(solution)/shard_map/ppermute | solution.py:844
  58.9 17.4 %collective-permute-start.10 = (f32[16,768]{1,0:T(8,128)S(1)}, f32[16,768]{1,0:T(8,128)S(1)}, u32[]{:S(2)}, u32[]{:S(2)}) collective-permute-start(f32[16,768]{1,0:T(8,128)S(1)} %add.79), channel_id=1, source_target_pairs={{0,8},{1,9},{2,10},{3,11},{4,12},{5,13},{6,14},{7,15},{8,0},{9,1},... | collective-permute-start | bytes 147464 | tf_op jit(solution)/shard_map/ppermute | solution.py:844
  76.4 4.2 %collective-permute-start.11 = (bf16[192,2304]{1,0:T(8,128)(2,1)S(1)}, bf16[192,2304]{1,0:T(8,128)(2,1)S(1)}, u32[]{:S(2)}, u32[]{:S(2)}) collective-permute-start(bf16[192,2304]{1,0:T(8,128)(2,1)S(1)} %collective-permute-done.7.refs_3_), channel_id=1, source_target_pairs={{0,1},{1,0},{2,3},{3,2},{4,5},{5,4},{6,7},{7,6},{8,9},{9,8},{10,11... | collective-permute-start | bytes 2654216 | tf_op jit(solution)/shard_map/ppermute | solution.py:844
  76.5 11.1 %collective-permute-start.12 = (bf16[192,2304]{1,0:T(8,128)(2,1)S(1)}, bf16[192,2304]{1,0:T(8,128)(2,1)S(1)}, u32[]{:S(2)}, u32[]{:S(2)}) collective-permute-start(bf16[192,2304]{1,0:T(8,128)(2,1)S(1)} %all_gather.10.refs_0_), channel_id=1, source_target_pairs={{0,1},{1,0},{2,3},{3,2},{4,5},{5,4},{6,7},{7,6},{8,9},{9,8},{10,11... | collective-permute-start | bytes 2654216 | tf_op jit(solution)/shard_map/ppermute | solution.py:844
  77.0 10.6 %collective-permute-start.13 = (bf16[192,2304]{1,0:T(8,128)(2,1)S(1)}, bf16[192,2304]{1,0:T(8,128)(2,1)S(1)}, u32[]{:S(2)}, u32[]{:S(2)}) collective-permute-start(bf16[192,2304]{1,0:T(8,128)(2,1)S(1)} %collective-permute-done.6.refs_1_), channel_id=1, source_target_pairs={{0,1},{1,0},{2,3},{3,2},{4,5},{5,4},{6,7},{7,6},{8,9},{9,8},{10,11... | collective-permute-start | bytes 2654216 | tf_op jit(solution)/shard_map/ppermute | solution.py:844
  77.1 17.1 %collective-permute-start.15 = (bf16[384,768]{1,0:T(8,128)(2,1)S(1)}, bf16[384,768]{1,0:T(8,128)(2,1)S(1)}, u32[]{:S(2)}, u32[]{:S(2)}) collective-permute-start(bf16[384,768]{1,0:T(8,128)(2,1)S(1)} %pad_maximum_fusion), channel_id=1, source_target_pairs={{0,16},{1,17},{2,18},{3,19},{4,20},{5,21},{6,22},{7,23},{8,24},{9,... | collective-permute-start | bytes 1769480 | tf_op jit(solution)/shard_map/ppermute | solution.py:844
  78.7 15.6 %collective-permute-start.14 = (bf16[192,1536]{1,0:T(8,128)(2,1)S(1)}, bf16[192,1536]{1,0:T(8,128)(2,1)S(1)}, u32[]{:S(2)}, u32[]{:S(2)}) collective-permute-start(bf16[192,1536]{1,0:T(8,128)(2,1)S(1)} %all_gather.11.refs_0_), channel_id=1, source_target_pairs={{0,2},{1,3},{2,0},{3,1},{4,6},{5,7},{6,4},{7,5},{8,10},{9,11},{10,... | collective-permute-start | bytes 1769480 | tf_op jit(solution)/shard_map/ppermute | solution.py:844
  80.5 14.4 %collective-permute-start.16 = (bf16[192,1536]{1,0:T(8,128)(2,1)S(1)}, bf16[192,1536]{1,0:T(8,128)(2,1)S(1)}, u32[]{:S(2)}, u32[]{:S(2)}) collective-permute-start(bf16[192,1536]{1,0:T(8,128)(2,1)S(1)} %all_gather.11.refs_0_), channel_id=1, source_target_pairs={{0,1},{1,0},{2,3},{3,2},{4,5},{5,4},{6,7},{7,6},{8,9},{9,8},{10,11... | collective-permute-start | bytes 1769480 | tf_op jit(solution)/shard_map/ppermute | solution.py:844
  94.3 2.2 %collective-permute-start.17 = (bf16[192,1536]{1,0:T(8,128)(2,1)S(1)}, bf16[192,1536]{1,0:T(8,128)(2,1)S(1)}, u32[]{:S(2)}, u32[]{:S(2)}) collective-permute-start(bf16[192,1536]{1,0:T(8,128)(2,1)S(1)} %collective-permute-done.14.refs_1_), channel_id=1, source_target_pairs={{0,1},{1,0},{2,3},{3,2},{4,5},{5,4},{6,7},{7,6},{8,9},{9,8},{10,11... | collective-permute-start | bytes 1769480 | tf_op jit(solution)/shard_map/ppermute | solution.py:844
  94.8 2.5 %collective-permute-start.18 = (bf16[384,768]{1,0:T(8,128)(2,1)S(1)}, bf16[384,768]{1,0:T(8,128)(2,1)S(1)}, u32[]{:S(2)}, u32[]{:S(2)}) collective-permute-start(bf16[384,768]{1,0:T(8,128)(2,1)S(1)} %collective-permute-done.15.refs_0_), channel_id=1, source_target_pairs={{0,1},{1,0},{2,3},{3,2},{4,5},{5,4},{6,7},{7,6},{8,9},{9,8},{10,11... | collective-permute-start | bytes 1769480 | tf_op jit(solution)/shard_map/ppermute | solution.py:844
  97.3 7.0 %collective-permute-start.19 = (bf16[384,3072]{1,0:T(8,128)(2,1)S(1)}, bf16[384,3072]{1,0:T(8,128)(2,1)S(1)}, u32[]{:S(2)}, u32[]{:S(2)}) collective-permute-start(bf16[384,3072]{1,0:T(8,128)(2,1)S(1)} %get-tuple-element.234), channel_id=1, source_target_pairs={{0,1},{1,0},{2,3},{3,2},{4,5},{5,4},{6,7},{7,6},{8,9},{9,8},{10,11... | collective-permute-start | bytes 7077896 | tf_op jit(solution)/shard_map/ppermute | solution.py:844
  105.2 17.1 %collective-permute-start.22 = (bf16[384,3072]{1,0:T(8,128)(2,1)S(1)}, bf16[384,3072]{1,0:T(8,128)(2,1)S(1)}, u32[]{:S(2)}, u32[]{:S(2)}) collective-permute-start(bf16[384,3072]{1,0:T(8,128)(2,1)S(1)} %get-tuple-element.257), channel_id=1, source_target_pairs={{0,1},{1,0},{2,3},{3,2},{4,5},{5,4},{6,7},{7,6},{8,9},{9,8},{10,11... | collective-permute-start | bytes 7077896 | tf_op jit(solution)/shard_map/ppermute | solution.py:844
  105.4 15.6 %collective-permute-start.20 = (bf16[192,1536]{1,0:T(8,128)(2,1)S(1)}, bf16[192,1536]{1,0:T(8,128)(2,1)S(1)}, u32[]{:S(2)}, u32[]{:S(2)}) collective-permute-start(bf16[192,1536]{1,0:T(8,128)(2,1)S(1)} %get-tuple-element.255), channel_id=1, source_target_pairs={{0,2},{1,3},{2,0},{3,1},{4,6},{5,7},{6,4},{7,5},{8,10},{9,11},{10,... | collective-permute-start | bytes 1769480 | tf_op jit(solution)/shard_map/ppermute | solution.py:844
  107.0 15.3 %collective-permute-start.21 = (bf16[4,2,48,768]{3,2,1,0:T(8,128)(2,1)S(1)}, bf16[4,2,48,768]{3,2,1,0:T(8,128)(2,1)S(1)}, u32[]{:S(2)}, u32[]{:S(2)}) collective-permute-start(bf16[4,2,48,768]{3,2,1,0:T(8,128)(2,1)S(1)} %get-tuple-element.256), channel_id=1, source_target_pairs={{0,16},{1,17},{2,18},{3,19},{4,20},{5,21},{6,22},{7,23},{8,24},{9,... | collective-permute-start | bytes 1769480 | tf_op jit(solution)/shard_map/ppermute | solution.py:844
  122.3 17.4 %collective-permute-start.26 = (bf16[384,3072]{1,0:T(8,128)(2,1)S(1)}, bf16[384,3072]{1,0:T(8,128)(2,1)S(1)}, u32[]{:S(2)}, u32[]{:S(2)}) collective-permute-start(bf16[384,3072]{1,0:T(8,128)(2,1)S(1)} %get-tuple-element.279), channel_id=1, source_target_pairs={{0,1},{1,0},{2,3},{3,2},{4,5},{5,4},{6,7},{7,6},{8,9},{9,8},{10,11... | collective-permute-start | bytes 7077896 | tf_op jit(solution)/shard_map/ppermute | solution.py:844
  123.4 15.8 %collective-permute-start.24 = (bf16[192,1536]{1,0:T(8,128)(2,1)S(1)}, bf16[192,1536]{1,0:T(8,128)(2,1)S(1)}, u32[]{:S(2)}, u32[]{:S(2)}) collective-permute-start(bf16[192,1536]{1,0:T(8,128)(2,1)S(1)} %get-tuple-element.277), channel_id=1, source_target_pairs={{0,2},{1,3},{2,0},{3,1},{4,6},{5,7},{6,4},{7,5},{8,10},{9,11},{10,... | collective-permute-start | bytes 1769480 | tf_op jit(solution)/shard_map/ppermute | solution.py:844
  124.0 15.5 %collective-permute-start.25 = (bf16[4,2,48,768]{3,2,1,0:T(8,128)(2,1)S(1)}, bf16[4,2,48,768]{3,2,1,0:T(8,128)(2,1)S(1)}, u32[]{:S(2)}, u32[]{:S(2)}) collective-permute-start(bf16[4,2,48,768]{3,2,1,0:T(8,128)(2,1)S(1)} %get-tuple-element.278), channel_id=1, source_target_pairs={{0,16},{1,17},{2,18},{3,19},{4,20},{5,21},{6,22},{7,23},{8,24},{9,... | collective-permute-start | bytes 1769480 | tf_op jit(solution)/shard_map/ppermute | solution.py:844
  124.5 15.2 %collective-permute-start.23 = (bf16[384,768]{1,0:T(8,128)(2,1)S(1)}, bf16[384,768]{1,0:T(8,128)(2,1)S(1)}, u32[]{:S(2)}, u32[]{:S(2)}) collective-permute-start(bf16[384,768]{1,0:T(8,128)(2,1)S(1)} %get-tuple-element.276), channel_id=1, source_target_pairs={{0,4},{1,5},{2,6},{3,7},{4,0},{5,1},{6,2},{7,3},{8,12},{9,13},{10,... | collective-permute-start | bytes 1769480 | tf_op jit(solution)/shard_map/ppermute | solution.py:844
  141.4 18.8 %collective-permute-start.30 = (bf16[4,2,48,768]{3,2,1,0:T(8,128)(2,1)S(1)}, bf16[4,2,48,768]{3,2,1,0:T(8,128)(2,1)S(1)}, u32[]{:S(2)}, u32[]{:S(2)}) collective-permute-start(bf16[4,2,48,768]{3,2,1,0:T(8,128)(2,1)S(1)} %get-tuple-element.298), channel_id=1, source_target_pairs={{0,16},{1,17},{2,18},{3,19},{4,20},{5,21},{6,22},{7,23},{8,24},{9,... | collective-permute-start | bytes 1769480 | tf_op jit(solution)/shard_map/ppermute | solution.py:844
  142.9 17.3 %collective-permute-start.29 = (bf16[192,1536]{1,0:T(8,128)(2,1)S(1)}, bf16[192,1536]{1,0:T(8,128)(2,1)S(1)}, u32[]{:S(2)}, u32[]{:S(2)}) collective-permute-start(bf16[192,1536]{1,0:T(8,128)(2,1)S(1)} %get-tuple-element.295), channel_id=1, source_target_pairs={{0,2},{1,3},{2,0},{3,1},{4,6},{5,7},{6,4},{7,5},{8,10},{9,11},{10,... | collective-permute-start | bytes 1769480 | tf_op jit(solution)/shard_map/ppermute | solution.py:844
  145.1 12.8 %collective-permute-start.28 = (bf16[96,1536]{1,0:T(8,128)(2,1)S(1)}, bf16[96,1536]{1,0:T(8,128)(2,1)S(1)}, u32[]{:S(2)}, u32[]{:S(2)}) collective-permute-start(bf16[96,1536]{1,0:T(8,128)(2,1)S(1)} %get-tuple-element.297), channel_id=1, source_target_pairs={{0,4},{1,5},{2,6},{3,7},{4,0},{5,1},{6,2},{7,3},{8,12},{9,13},{10,... | collective-permute-start | bytes 884744 | tf_op jit(solution)/shard_map/ppermute | solution.py:844
  145.5 14.7 %collective-permute-start.27 = (bf16[192,768]{1,0:T(8,128)(2,1)S(1)}, bf16[192,768]{1,0:T(8,128)(2,1)S(1)}, u32[]{:S(2)}, u32[]{:S(2)}) collective-permute-start(bf16[192,768]{1,0:T(8,128)(2,1)S(1)} %get-tuple-element.287), channel_id=1, source_target_pairs={{0,8},{1,9},{2,10},{3,11},{4,12},{5,13},{6,14},{7,15},{8,0},{9,1},... | collective-permute-start | bytes 884744 | tf_op jit(solution)/shard_map/ppermute | solution.py:844
  147.0 2.7 %collective-permute-start.31 = (f32[16,768]{1,0:T(8,128)S(1)}, f32[16,768]{1,0:T(8,128)S(1)}, u32[]{:S(2)}, u32[]{:S(2)}) collective-permute-start(f32[16,768]{1,0:T(8,128)S(1)} %get-tuple-element.299), channel_id=1, source_target_pairs={{0,1},{1,0},{2,3},{3,2},{4,5},{5,4},{6,7},{7,6},{8,9},{9,8},{10,11... | collective-permute-start | bytes 147464 | tf_op jit(solution)/shard_map/ppermute | solution.py:844
  161.0 13.9 %collective-permute-start.35 = (bf16[224,1536]{1,0:T(8,128)(2,1)S(1)}, bf16[224,1536]{1,0:T(8,128)(2,1)S(1)}, u32[]{:S(2)}, u32[]{:S(2)}) collective-permute-start(bf16[224,1536]{1,0:T(8,128)(2,1)S(1)} %get-tuple-element.315), channel_id=1, source_target_pairs={{0,2},{1,3},{2,0},{3,1},{4,6},{5,7},{6,4},{7,5},{8,10},{9,11},{10,... | collective-permute-start | bytes 2064392 | tf_op jit(solution)/shard_map/ppermute | solution.py:844
  162.2 11.1 %collective-permute-start.34 = (bf16[96,1536]{1,0:T(8,128)(2,1)S(1)}, bf16[96,1536]{1,0:T(8,128)(2,1)S(1)}, u32[]{:S(2)}, u32[]{:S(2)}) collective-permute-start(bf16[96,1536]{1,0:T(8,128)(2,1)S(1)} %get-tuple-element.317), channel_id=1, source_target_pairs={{0,4},{1,5},{2,6},{3,7},{4,0},{5,1},{6,2},{7,3},{8,12},{9,13},{10,... | collective-permute-start | bytes 884744 | tf_op jit(solution)/shard_map/ppermute | solution.py:844
  163.5 9.8 %collective-permute-start.32 = (bf16[48,1536]{1,0:T(8,128)(2,1)S(1)}, bf16[48,1536]{1,0:T(8,128)(2,1)S(1)}, u32[]{:S(2)}, u32[]{:S(2)}) collective-permute-start(bf16[48,1536]{1,0:T(8,128)(2,1)S(1)} %sum_far.4.refs_3_), channel_id=1, source_target_pairs={{0,16},{1,17},{2,18},{3,19},{4,20},{5,21},{6,22},{7,23},{8,24},{9,... | collective-permute-start | bytes 442376 | tf_op jit(solution)/shard_map/ppermute | solution.py:844
  164.1 9.2 %collective-permute-start.33 = (bf16[48,1536]{1,0:T(8,128)(2,1)S(1)}, bf16[48,1536]{1,0:T(8,128)(2,1)S(1)}, u32[]{:S(2)}, u32[]{:S(2)}) collective-permute-start(bf16[48,1536]{1,0:T(8,128)(2,1)S(1)} %get-tuple-element.319), channel_id=1, source_target_pairs={{0,8},{1,9},{2,10},{3,11},{4,12},{5,13},{6,14},{7,15},{8,0},{9,1},... | collective-permute-start | bytes 442376 | tf_op jit(solution)/shard_map/ppermute | solution.py:844
  166.4 6.9 %collective-permute-start.36 = (f32[16,768]{1,0:T(8,128)S(1)}, f32[16,768]{1,0:T(8,128)S(1)}, u32[]{:S(2)}, u32[]{:S(2)}) collective-permute-start(f32[16,768]{1,0:T(8,128)S(1)} %add.81), channel_id=1, source_target_pairs={{0,8},{1,9},{2,10},{3,11},{4,12},{5,13},{6,14},{7,15},{8,0},{9,1},... | collective-permute-start | bytes 147464 | tf_op jit(solution)/shard_map/ppermute | solution.py:844
  175.6 9.1 %collective-permute-start.39 = (bf16[96,1536]{1,0:T(8,128)(2,1)S(1)}, bf16[96,1536]{1,0:T(8,128)(2,1)S(1)}, u32[]{:S(2)}, u32[]{:S(2)}) collective-permute-start(bf16[96,1536]{1,0:T(8,128)(2,1)S(1)} %get-tuple-element.330), channel_id=1, source_target_pairs={{0,4},{1,5},{2,6},{3,7},{4,0},{5,1},{6,2},{7,3},{8,12},{9,13},{10,... | collective-permute-start | bytes 884744 | tf_op jit(solution)/shard_map/ppermute | solution.py:844
  177.0 7.7 %collective-permute-start.37 = (bf16[48,2304]{1,0:T(8,128)(2,1)S(1)}, bf16[48,2304]{1,0:T(8,128)(2,1)S(1)}, u32[]{:S(2)}, u32[]{:S(2)}) collective-permute-start(bf16[48,2304]{1,0:T(8,128)(2,1)S(1)} %sum_far.5.refs_5_), channel_id=1, source_target_pairs={{0,16},{1,17},{2,18},{3,19},{4,20},{5,21},{6,22},{7,23},{8,24},{9,... | collective-permute-start | bytes 663560 | tf_op jit(solution)/shard_map/ppermute | solution.py:844
  177.7 7.0 %collective-permute-start.38 = (bf16[48,1536]{1,0:T(8,128)(2,1)S(1)}, bf16[48,1536]{1,0:T(8,128)(2,1)S(1)}, u32[]{:S(2)}, u32[]{:S(2)}) collective-permute-start(bf16[48,1536]{1,0:T(8,128)(2,1)S(1)} %get-tuple-element.329), channel_id=1, source_target_pairs={{0,8},{1,9},{2,10},{3,11},{4,12},{5,13},{6,14},{7,15},{8,0},{9,1},... | collective-permute-start | bytes 442376 | tf_op jit(solution)/shard_map/ppermute | solution.py:844
  179.1 5.5 %collective-permute-start.40 = (f32[16,768]{1,0:T(8,128)S(1)}, f32[16,768]{1,0:T(8,128)S(1)}, u32[]{:S(2)}, u32[]{:S(2)}) collective-permute-start(f32[16,768]{1,0:T(8,128)S(1)} %add.82), channel_id=1, source_target_pairs={{0,4},{1,5},{2,6},{3,7},{4,0},{5,1},{6,2},{7,3},{8,12},{9,13},{10,... | collective-permute-start | bytes 147464 | tf_op jit(solution)/shard_map/ppermute | solution.py:844
  185.9 7.5 %collective-permute-start.41 = (bf16[48,1536]{1,0:T(8,128)(2,1)S(1)}, bf16[48,1536]{1,0:T(8,128)(2,1)S(1)}, u32[]{:S(2)}, u32[]{:S(2)}) collective-permute-start(bf16[48,1536]{1,0:T(8,128)(2,1)S(1)} %sum_far.6.refs_6_), channel_id=1, source_target_pairs={{0,16},{1,17},{2,18},{3,19},{4,20},{5,21},{6,22},{7,23},{8,24},{9,... | collective-permute-start | bytes 442376 | tf_op jit(solution)/shard_map/ppermute | solution.py:844
  187.3 7.6 %collective-permute-start.42 = (bf16[48,1536]{1,0:T(8,128)(2,1)S(1)}, bf16[48,1536]{1,0:T(8,128)(2,1)S(1)}, u32[]{:S(2)}, u32[]{:S(2)}) collective-permute-start(bf16[48,1536]{1,0:T(8,128)(2,1)S(1)} %get-tuple-element.336), channel_id=1, source_target_pairs={{0,8},{1,9},{2,10},{3,11},{4,12},{5,13},{6,14},{7,15},{8,0},{9,1},... | collective-permute-start | bytes 442376 | tf_op jit(solution)/shard_map/ppermute | solution.py:844
  189.4 4.1 %collective-permute-start.43 = (f32[16,768]{1,0:T(8,128)S(1)}, f32[16,768]{1,0:T(8,128)S(1)}, u32[]{:S(2)}, u32[]{:S(2)}) collective-permute-start(f32[16,768]{1,0:T(8,128)S(1)} %add.83), channel_id=1, source_target_pairs={{0,2},{1,3},{2,0},{3,1},{4,6},{5,7},{6,4},{7,5},{8,10},{9,11},{10,... | collective-permute-start | bytes 147464 | tf_op jit(solution)/shard_map/ppermute | solution.py:844
  194.9 4.6 %collective-permute-start.45 = (f32[16,768]{1,0:T(8,128)S(1)}, f32[16,768]{1,0:T(8,128)S(1)}, u32[]{:S(2)}, u32[]{:S(2)}) collective-permute-start(f32[16,768]{1,0:T(8,128)S(1)} %add.84), channel_id=1, source_target_pairs={{0,16},{1,17},{2,18},{3,19},{4,20},{5,21},{6,22},{7,23},{8,24},{9,... | collective-permute-start | bytes 147464 | tf_op jit(solution)/shard_map/ppermute | solution.py:844
  195.9 6.1 %collective-permute-start.44 = (bf16[48,1536]{1,0:T(8,128)(2,1)S(1)}, bf16[48,1536]{1,0:T(8,128)(2,1)S(1)}, u32[]{:S(2)}, u32[]{:S(2)}) collective-permute-start(bf16[48,1536]{1,0:T(8,128)(2,1)S(1)} %sum_far.7.refs_3_), channel_id=1, source_target_pairs={{0,16},{1,17},{2,18},{3,19},{4,20},{5,21},{6,22},{7,23},{8,24},{9,... | collective-permute-start | bytes 442376 | tf_op jit(solution)/shard_map/ppermute | solution.py:844
  (18 other events, 108.2 us)

commit v6 on v5

--- a/solution.py
+++ b/solution.py
@@ -516,9 +516,7 @@
     turn(co, dz[...].astype(F32), scratch, dzt_send, dzt_keep)
 
 
-def hidden_kernel(
-    co, h2, vec, dzt_send, dzt_keep, w0, w1, g0, g1, slope0, slope1, send, keep
-):
+def hidden_kernel(co, h2, vec, w0, w1, g0, g1, slope0, slope1):
     for part, weight, g, slope in ((0, w0, g0, slope0), (1, w1, g1, slope1)):
         for b in range(2):
             half = lax.bitwise_xor(co[0], b)
@@ -527,13 +525,18 @@
                 u = nn(h2[...], weight[:, at])
                 u = u + vec[pl.ds(9 + 2 * half + part, 1), sub : sub + 384]
                 phi = 0.5 * (1.0 + lax.erf(u * math.sqrt(0.5)))
-                act = (u * phi).astype(BF)
-                g[:, at] = act
+                g[:, at] = (u * phi).astype(BF)
                 slope[:, at] = phi + u * (
                     jnp.exp(-0.5 * u * u) * (1.0 / math.sqrt(2.0 * math.pi))
                 )
-                dst = lanes(half * D + sub, 384) if part == 0 else lanes((2 + b) * D + sub, 384)
-                share_rows(dzt_send, dzt_keep, act, send, keep, dst)
+
+
+def down_grad_kernel(co, dzt_send, dzt_keep, g0, g1, send, keep):
+    for part, g in ((0, g0), (1, g1)):
+        for b in range(2):
+            half = lax.bitwise_xor(co[0], b)
+            dst = lanes(half * D, D) if part == 0 else lanes((2 + b) * D, D)
+            share_rows(dzt_send, dzt_keep, g[:, b * D : b * D + D], send, keep, dst)
 
 
 def hidden_grad_kernel(
@@ -924,10 +927,10 @@
         name="norm2",
     )
     shares = [((384, 4 * D), BF), ((384, 4 * D), F32)]
-    g0, g1, slope0, slope1, down_send, down_keep = call(
+    g0, g1, slope0, slope1 = call(
         hidden_kernel,
-        [((256, 2 * D), BF)] * 2 + [((256, 2 * D), F32)] * 2 + shares,
-        [co, h2, vec, dzt_send, dzt_keep, w_up0, w_up1],
+        [((256, 2 * D), BF)] * 2 + [((256, 2 * D), F32)] * 2,
+        [co, h2, vec, w_up0, w_up1],
         name="hidden",
     )
 
@@ -963,9 +966,12 @@
     mlp_state = [mlp_weight, mlp_moment, mlp_average]
     attn_state = [attn_weight, attn_moment, attn_average]
 
-    across2, far1, down_send = hold((across2, far1, down_send))
+    across2, far1, g0, g1 = hold((across2, far1, g0, g1))
     pieces2 = core_pair([stack2, across2])
     far1 = core_pair([far1])
+    down_send, down_keep = call(
+        down_grad_kernel, shares, [co, dzt_send, dzt_keep, g0, g1], name="down_grad"
+    )
     pieces2, far1, down_send = hold((pieces2, far1, down_send))
     down_got = blocks(swap(down_send, CORE))
     down_keep = blocks(down_keep)

time: 204 us -> 203 us (level)
    pallas_call x31 -> x32, Pallas kernels: 51.2 us -> 50.3 us  [call(): pl.pallas_call(body, out_shape=[jax.ShapeDtypeStruct(shape, dtype) for sh...]
  transfers between devices with their start and end apart: 46 -> 46, of which waited for: 17 -> 18; matrix products, arithmetic and copies ran while one was open for 1% -> 1% of each run, Pallas kernels for 23% -> 23%
where the time goes in v6:
time: 203 us
  blocking collectives  58.2 us (29%)
  Pallas kernels  56.4 us (28%)
  waiting for transfers between devices  47.3 us (23%)
  starting transfers between devices  34.1 us (17%)
  other arithmetic  4.64 us (2%)
    all_gather x3, blocking collectives, along_z(): lax.all_gather(shard, 'fsdp', axis=0, tiled=True, axis_index_groups=groups)  58.2 us
    pallas_call x32, Pallas kernels, call(): pl.pallas_call(body, out_shape=[jax.ShapeDtypeStruct(shape, dtype) for sh...  50.3 us
    ppermute x46, waiting for transfers between devices, swap(): lax.ppermute(array, ('rep', 'fsdp'), [(i, i ^ mask) for i in range(32)])  47.3 us
    ppermute x46, starting transfers between devices, swap(): lax.ppermute(array, ('rep', 'fsdp'), [(i, i ^ mask) for i in range(32)])  34.1 us
    pallas_call x3, Pallas kernels, update(): pl.pallas_call(functools.partial(update_kernel, rate, moves, len(states),...  6.15 us
  transfers between devices with their start and end apart: 46, of which 18 were waited for; matrix products, arithmetic and copies ran while one was open for 1% of the time, Pallas kernels for 23%

profile of v6, /device:TPU:0, one launch (start us, length us, event | category | flops | bytes accessed | tf_op | source)
XLA Modules:
  0.0 202.6 jit_solution(11307648883910679493)
XLA Ops:
  2.9 2.6 %prep.2 = bf16[48,2304]{1,0:T(8,128)(2,1)} custom-call(s32[4]{0:T(128)} %pad_add_fusion.co_ref.co, f32[48,3072]{1,0:T(8,128)} %refs_0_.16, f32[48,6144]{1,0:T(8,128)} %refs_0_.15), custom_call_target="tpu_custom_call" | custom-call | flops 1048576 | bytes 1048576 | tf_op jit(solution)/shard_map/prep/pallas_call | solution.py:352
  5.5 22.6 %all_gather.9.refs_0_ = bf16[192,2304]{1,0:T(8,128)(2,1)S(1)} all-gather(bf16[48,2304]{1,0:T(8,128)(2,1)} %prep.2), channel_id=1, replica_groups={{0,4,8,12},{1,5,9,13},{2,6,10,14},{3,7,11,15},{16,20,24,28},{17,21,25,2..., dimensions={0}, use_global_device_ids=true | all-gather | bytes 1105920 | tf_op jit(solution)/shard_map/all_gather | solution.py:871
  28.1 1.5 collective-permute-start.2
  29.6 1.5 collective-permute-start.1
  32.9 19.2 %all_gather.10.refs_0_ = bf16[192,2304]{1,0:T(8,128)(2,1)S(1)} all-gather(bf16[48,2304]{1,0:T(8,128)(2,1)S(1)} %get-tuple-element.202), channel_id=1, replica_groups={{0,4,8,12},{1,5,9,13},{2,6,10,14},{3,7,11,15},{16,20,24,28},{17,21,25,2..., dimensions={0}, use_global_device_ids=true | all-gather | bytes 1105920 | tf_op jit(solution)/shard_map/all_gather | solution.py:871
  52.5 1.6 collective-permute-start.6
  54.8 4.1 %collective-permute-done.5 = f32[16,768]{1,0:T(8,128)S(1)} collective-permute-done((f32[16,768]{1,0:T(8,128)S(1)}, f32[16,768]{1,0:T(8,128)S(1)}, u32[]{:S(2)}, u32[]{:S(2)}) %collective-permute-start.5) | collective-permute-done | bytes 49184 | tf_op jit(solution)/shard_map/ppermute | solution.py:847
  58.9 0.9 collective-permute-start.10
  59.8 16.4 %all_gather.11.refs_0_ = bf16[192,1536]{1,0:T(8,128)(2,1)S(1)} all-gather(bf16[48,1536]{1,0:T(8,128)(2,1)S(1)} %get-tuple-element.208), channel_id=1, replica_groups={{0,4,8,12},{1,5,9,13},{2,6,10,14},{3,7,11,15},{16,20,24,28},{17,21,25,2..., dimensions={0}, use_global_device_ids=true | all-gather | bytes 737280 | tf_op jit(solution)/shard_map/all_gather | solution.py:871
  77.1 1.6 collective-permute-start.13
  79.2 1.3 norm1.1
  81.4 3.5 %attention.1 = (bf16[256,2304]{1,0:T(8,128)(2,1)S(1)}, bf16[256,768]{1,0:T(8,128)(2,1)S(1)}, f32[16,256]{1,0:T(8,128)S(1)}) custom-call(s32[4]{0:T(128)S(1)} %copy-done.8, bf16[256,768]{1,0:T(8,128)(2,1)S(1)} %get-tuple-element.216.refs_0_, f32[16,768]{1,0:T(8,128)S(1)} %add.80.refs_2_.refs_1_.refs_3_, f32[8,256]{1,0:T(8,128)S(1)} %scatter.4.refs_1_.refs_2_.refs_0_, ...), custom_call_target="tpu_custom_call" | custom-call | flops 1048576 | bytes 1048576 | tf_op jit(solution)/shard_map/attention/pallas_call | solution.py:352
  85.9 1.7 norm2.1
  88.4 2.7 %hidden.1 = (bf16[256,1536]{1,0:T(8,128)(2,1)S(1)}, bf16[256,1536]{1,0:T(8,128)(2,1)S(1)}, f32[256,1536]{1,0:T(8,128)S(1)}, f32[256,1536]{1,0:T(8,128)S(1)}) custom-call(s32[4]{0:T(128)S(1)} %copy-done.8, bf16[256,768]{1,0:T(8,128)(2,1)S(1)} %get-tuple-element.227.refs_0_, f32[16,768]{1,0:T(8,128)S(1)} %add.80.refs_2_.refs_1_.refs_3_, ...), custom_call_target="tpu_custom_call" | custom-call | flops 1048576 | bytes 1048576 | tf_op jit(solution)/shard_map/hidden/pallas_call | solution.py:352
  91.1 1.8 collective-permute-done.13.refs_0_
  92.9 1.2 collective-permute-done.12.refs_1_
  94.6 1.9 down_grad.1
  98.4 5.3 %hidden_grad.1 = (bf16[256,1536]{1,0:T(8,128)(2,1)S(1)}, bf16[256,1536]{1,0:T(8,128)(2,1)S(1)}, f32[8,768]{1,0:T(8,128)S(1)}, bf16[384,3072]{1,0:T(8,128)(2,1)S(1)}, f32[384,3072]{1,0:T(8,128)S(1)}) custom-call(s32[4]{0:T(128)S(1)} %copy-done.8, bf16[256,768]{1,0:T(8,128)(2,1)S(1)} %copy-done.4, f32[256,1536]{1,0:T(8,128)S(1)} %get-tuple-element.239.refs_1_, ...), custom_call_target="tpu_custom_call" | custom-call | flops 1048576 | bytes 1048576 | tf_op jit(solution)/shard_map/hidden_grad/pallas_call | solution.py:352
  106.1 3.2 %norm2_back.1 = (f32[256,768]{1,0:T(8,128)S(1)}, bf16[256,768]{1,0:T(8,128)(2,1)S(1)}, bf16[384,256]{1,0:T(8,128)(2,1)S(1)}, bf16[384,256]{1,0:T(8,128)(2,1)S(1)}, f32[8,768]{1,0:T(8,128)S(1)}) custom-call(s32[4]{0:T(128)S(1)} %copy-done.8, bf16[256,768]{1,0:T(8,128)(2,1)S(1)} %copy-done.4, f32[256,768]{1,0:T(8,128)S(1)} %get-tuple-element.304.refs_1_.refs_0_, ...), custom_call_target="tpu_custom_call" | custom-call | flops 1048576 | bytes 1048576 | tf_op jit(solution)/shard_map/norm2_back/pallas_call | solution.py:352
  109.3 5.6 %attention_back.1 = (bf16[256,2304]{1,0:T(8,128)(2,1)S(1)}, f32[8,768]{1,0:T(8,128)S(1)}) custom-call(s32[4]{0:T(128)S(1)} %copy-done.8, f32[8,256]{1,0:T(8,128)S(1)} %scatter.4.refs_1_.refs_2_.refs_0_, f32[256,128]{1,0:T(8,128)S(1)} %get-tuple-element.215.refs_3_.refs_1_.refs_2_, f32[16,256]{1,0:T(8,128)S(1)} %get-tuple-element.264.refs_2_, ...), custom_call_target="tpu_custom_call" | custom-call | flops 1048576 | bytes 1048576 | tf_op jit(solution)/shard_map/attention_back/pallas_call | solution.py:352
  114.9 2.3 %attention_grad.1 = (bf16[384,3072]{1,0:T(8,128)(2,1)S(1)}, f32[384,3072]{1,0:T(8,128)S(1)}) custom-call(s32[4]{0:T(128)S(1)} %copy-done.8, bf16[384,256]{1,0:T(8,128)(2,1)S(1)} %get-tuple-element.262.refs_0_, bf16[384,256]{1,0:T(8,128)(2,1)S(1)} %get-tuple-element.263.refs_1_, bf16[256,2304]{1,0:T(8,128)(2,1)S(1)} %get-tuple-element.284.refs_2_.refs_0_, ...), custom_call_target="tpu_custom_call" | custom-call | flops 1048576 | bytes 1048576 | tf_op jit(solution)/shard_map/attention_grad/pallas_call | solution.py:352
  117.2 3.2 %collective-permute-done.20.refs_5_ = bf16[192,1536]{1,0:T(8,128)(2,1)S(1)} collective-permute-done((bf16[192,1536]{1,0:T(8,128)(2,1)S(1)}, bf16[192,1536]{1,0:T(8,128)(2,1)S(1)}, u32[]{:S(2)}, u32[]{:S(2)}) %collective-permute-start.20) | collective-permute-done | bytes 589856 | tf_op jit(solution)/shard_map/ppermute | solution.py:847
  120.7 1.1 split_third_round.1
  121.8 1.6 collective-permute-start.24
  123.9 3.0 %norm1_back.1 = (bf16[256,768]{1,0:T(8,128)(2,1)}, f32[16,768]{1,0:T(8,128)S(1)}) custom-call(s32[4]{0:T(128)S(1)} %copy-done.8, bf16[256,2304]{1,0:T(8,128)(2,1)S(1)} %get-tuple-element.284.refs_2_.refs_0_, bf16[256,768]{1,0:T(8,128)(2,1)S(1)} %copy-done.5, f32[256,128]{1,0:T(8,128)S(1)} %get-tuple-element.215.refs_3_.refs_1_.refs_2_, ...), custom_call_target="tpu_custom_call" | custom-call | flops 1048576 | bytes 1048576 | tf_op jit(solution)/shard_map/norm1_back/pallas_call | solution.py:352
  126.9 10.7 %collective-permute-done.24.refs_1_ = bf16[192,1536]{1,0:T(8,128)(2,1)S(1)} collective-permute-done((bf16[192,1536]{1,0:T(8,128)(2,1)S(1)}, bf16[192,1536]{1,0:T(8,128)(2,1)S(1)}, u32[]{:S(2)}, u32[]{:S(2)}) %collective-permute-start.24) | collective-permute-done | bytes 589856 | tf_op jit(solution)/shard_map/ppermute | solution.py:847
  137.6 1.2 collective-permute-done.25.refs_1_
  139.8 1.1 split_third.1
  140.9 1.6 collective-permute-start.30
  144.0 1.5 collective-permute-start.27
  145.5 2.7 %output.1 = bf16[256,768]{1,0:T(8,128)(2,1)} custom-call(s32[4]{0:T(128)S(1)} %copy-done.8, f32[256,768]{1,0:T(8,128)S(1)} %get-tuple-element.304.refs_1_.refs_0_, f32[16,768]{1,0:T(8,128)S(1)} %add.80.refs_2_.refs_1_.refs_3_, bf16[256,1536]{1,0:T(8,128)(2,1)S(1)} %get-tuple-element.232.refs_2_, bf16[256,1536]{1,0:T(8,128)(2,1)S(1)} %get-tuple-element.233.refs_3_, ...), custom_call_target="tpu_custom_call" | custom-call | flops 1048576 | bytes 1048576 | tf_op jit(solution)/shard_map/output/pallas_call | solution.py:352
  148.2 8.2 %collective-permute-done.28.refs_1_ = bf16[96,1536]{1,0:T(8,128)(2,1)S(1)} collective-permute-done((bf16[96,1536]{1,0:T(8,128)(2,1)S(1)}, bf16[96,1536]{1,0:T(8,128)(2,1)S(1)}, u32[]{:S(2)}, u32[]{:S(2)}) %collective-permute-start.28) | collective-permute-done | bytes 294944 | tf_op jit(solution)/shard_map/ppermute | solution.py:847
  156.5 2.3 %collective-permute-done.27.refs_4_.refs_1_ = bf16[192,768]{1,0:T(8,128)(2,1)S(1)} collective-permute-done((bf16[192,768]{1,0:T(8,128)(2,1)S(1)}, bf16[192,768]{1,0:T(8,128)(2,1)S(1)}, u32[]{:S(2)}, u32[]{:S(2)}) %collective-permute-start.27) | collective-permute-done | bytes 294944 | tf_op jit(solution)/shard_map/ppermute | solution.py:847
  159.5 1.6 collective-permute-start.35
  163.6 2.2 %collective-permute-start.33 = (bf16[48,1536]{1,0:T(8,128)(2,1)S(1)}, bf16[48,1536]{1,0:T(8,128)(2,1)S(1)}, u32[]{:S(2)}, u32[]{:S(2)}) collective-permute-start(bf16[48,1536]{1,0:T(8,128)(2,1)S(1)} %get-tuple-element.321), channel_id=1, source_target_pairs={{0,8},{1,9},{2,10},{3,11},{4,12},{5,13},{6,14},{7,15},{8,0},{9,1},... | collective-permute-start | bytes 442376 | tf_op jit(solution)/shard_map/ppermute | solution.py:847
  166.6 6.4 %collective-permute-done.36 = f32[16,768]{1,0:T(8,128)S(1)} collective-permute-done((f32[16,768]{1,0:T(8,128)S(1)}, f32[16,768]{1,0:T(8,128)S(1)}, u32[]{:S(2)}, u32[]{:S(2)}) %collective-permute-start.36) | collective-permute-done | bytes 49184 | tf_op jit(solution)/shard_map/ppermute | solution.py:847
  175.5 0.9 collective-permute-start.37
  176.4 1.4 collective-permute-start.38
  177.7 1.4 collective-permute-start.40
  179.2 4.3 %collective-permute-done.40 = f32[16,768]{1,0:T(8,128)S(1)} collective-permute-done((f32[16,768]{1,0:T(8,128)S(1)}, f32[16,768]{1,0:T(8,128)S(1)}, u32[]{:S(2)}, u32[]{:S(2)}) %collective-permute-start.40) | collective-permute-done | bytes 49184 | tf_op jit(solution)/shard_map/ppermute | solution.py:847
  184.7 1.1 collective-permute-start.41
  185.9 2.0 collective-permute-start.42
  187.9 1.5 collective-permute-start.43
  189.4 2.4 %update_mlp.1 = (f32[48,6144]{1,0:T(8,128)}, f32[48,6144]{1,0:T(8,128)}, f32[48,6144]{1,0:T(8,128)}, bf16[48,6144]{1,0:T(8,128)(2,1)}) custom-call(s32[4]{0:T(128)S(1)} %copy-done.8, f32[48,6144]{1,0:T(8,128)S(1)} %copy-done, f32[48,6144]{1,0:T(8,128)S(1)} %copy-done.2, f32[48,6144]{1,0:T(8,128)S(1)} %copy-done.3, bf16[48,1536]{1,0:T(8,128)(2,1)S(1)} %sum_far.4.refs_3_, ...), custom_call_target="tpu_custom_call" | custom-call | flops 1048576 | bytes 1048576 | tf_op jit(solution)/shard_map/update_mlp/pallas_call | solution.py:952
  192.0 1.5 collective-permute-done.42.refs_1_
  194.3 1.9 collective-permute-start.44
  196.3 1.8 update_both.1
  200.6 1.9 update_attn.1
  (146 shorter events, 28.0 us)
Async XLA Ops:
  2.9 28.2 %copy-start = (f32[48,6144]{1,0:T(8,128)S(1)}, f32[48,6144]{1,0:T(8,128)}, u32[]{:S(2)}) copy-start(f32[48,6144]{1,0:T(8,128)} %refs_0_.15) | copy-start | bytes 3538948
  2.9 28.2 %copy-start.8 = (s32[4]{0:T(128)S(1)}, s32[4]{0:T(128)}, u32[]{:S(2)}) copy-start(s32[4]{0:T(128)} %pad_add_fusion.co_ref.co) | copy-start | bytes 52
  28.1 24.3 %collective-permute-start.3 = (bf16[192,2304]{1,0:T(8,128)(2,1)S(1)}, bf16[192,2304]{1,0:T(8,128)(2,1)S(1)}, u32[]{:S(2)}, u32[]{:S(2)}) collective-permute-start(bf16[192,2304]{1,0:T(8,128)(2,1)S(1)} %all_gather.9.refs_0_), channel_id=1, source_target_pairs={{0,1},{1,0},{2,3},{3,2},{4,5},{5,4},{6,7},{7,6},{8,9},{9,8},{10,11... | collective-permute-start | bytes 2654216 | tf_op jit(solution)/shard_map/ppermute | solution.py:847
  28.1 24.3 %collective-permute-start.2 = (bf16[192,2304]{1,0:T(8,128)(2,1)S(1)}, bf16[192,2304]{1,0:T(8,128)(2,1)S(1)}, u32[]{:S(2)}, u32[]{:S(2)}) collective-permute-start(bf16[192,2304]{1,0:T(8,128)(2,1)S(1)} %all_gather.9.refs_0_), channel_id=1, source_target_pairs={{0,16},{1,17},{2,18},{3,19},{4,20},{5,21},{6,22},{7,23},{8,24},{9,... | collective-permute-start | bytes 2654216 | tf_op jit(solution)/shard_map/ppermute | solution.py:847
  29.6 22.9 %collective-permute-start.1 = (bf16[192,2304]{1,0:T(8,128)(2,1)S(1)}, bf16[192,2304]{1,0:T(8,128)(2,1)S(1)}, u32[]{:S(2)}, u32[]{:S(2)}) collective-permute-start(bf16[192,2304]{1,0:T(8,128)(2,1)S(1)} %all_gather.9.refs_0_), channel_id=1, source_target_pairs={{0,2},{1,3},{2,0},{3,1},{4,6},{5,7},{6,4},{7,5},{8,10},{9,11},{10,... | collective-permute-start | bytes 2654216 | tf_op jit(solution)/shard_map/ppermute | solution.py:847
  31.1 1.2 collective-permute-start
  32.4 20.1 %collective-permute-start.4 = (f32[16,768]{1,0:T(8,128)S(1)}, f32[16,768]{1,0:T(8,128)S(1)}, u32[]{:S(2)}, u32[]{:S(2)}) collective-permute-start(f32[16,768]{1,0:T(8,128)S(1)} %add.77), channel_id=1, source_target_pairs={{0,2},{1,3},{2,0},{3,1},{4,6},{5,7},{6,4},{7,5},{8,10},{9,11},{10,... | collective-permute-start | bytes 147464 | tf_op jit(solution)/shard_map/ppermute | solution.py:847
  52.5 23.9 %collective-permute-start.9 = (bf16[192,2304]{1,0:T(8,128)(2,1)S(1)}, bf16[192,2304]{1,0:T(8,128)(2,1)S(1)}, u32[]{:S(2)}, u32[]{:S(2)}) collective-permute-start(bf16[192,2304]{1,0:T(8,128)(2,1)S(1)} %collective-permute-done.2.refs_2_), channel_id=1, source_target_pairs={{0,1},{1,0},{2,3},{3,2},{4,5},{5,4},{6,7},{7,6},{8,9},{9,8},{10,11... | collective-permute-start | bytes 2654216 | tf_op jit(solution)/shard_map/ppermute | solution.py:847
  52.5 23.8 %collective-permute-start.6 = (bf16[192,2304]{1,0:T(8,128)(2,1)S(1)}, bf16[192,2304]{1,0:T(8,128)(2,1)S(1)}, u32[]{:S(2)}, u32[]{:S(2)}) collective-permute-start(bf16[192,2304]{1,0:T(8,128)(2,1)S(1)} %all_gather.10.refs_0_), channel_id=1, source_target_pairs={{0,2},{1,3},{2,0},{3,1},{4,6},{5,7},{6,4},{7,5},{8,10},{9,11},{10,... | collective-permute-start | bytes 2654216 | tf_op jit(solution)/shard_map/ppermute | solution.py:847
  54.1 22.2 %collective-permute-start.8 = (bf16[192,2304]{1,0:T(8,128)(2,1)S(1)}, bf16[192,2304]{1,0:T(8,128)(2,1)S(1)}, u32[]{:S(2)}, u32[]{:S(2)}) collective-permute-start(bf16[192,2304]{1,0:T(8,128)(2,1)S(1)} %collective-permute-done.1.refs_1_), channel_id=1, source_target_pairs={{0,1},{1,0},{2,3},{3,2},{4,5},{5,4},{6,7},{7,6},{8,9},{9,8},{10,11... | collective-permute-start | bytes 2654216 | tf_op jit(solution)/shard_map/ppermute | solution.py:847
  54.3 22.1 %collective-permute-start.7 = (bf16[192,2304]{1,0:T(8,128)(2,1)S(1)}, bf16[192,2304]{1,0:T(8,128)(2,1)S(1)}, u32[]{:S(2)}, u32[]{:S(2)}) collective-permute-start(bf16[192,2304]{1,0:T(8,128)(2,1)S(1)} %collective-permute-done.1.refs_1_), channel_id=1, source_target_pairs={{0,16},{1,17},{2,18},{3,19},{4,20},{5,21},{6,22},{7,23},{8,24},{9,... | collective-permute-start | bytes 2654216 | tf_op jit(solution)/shard_map/ppermute | solution.py:847
  54.8 4.1 %collective-permute-start.5 = (f32[16,768]{1,0:T(8,128)S(1)}, f32[16,768]{1,0:T(8,128)S(1)}, u32[]{:S(2)}, u32[]{:S(2)}) collective-permute-start(f32[16,768]{1,0:T(8,128)S(1)} %add.78), channel_id=1, source_target_pairs={{0,4},{1,5},{2,6},{3,7},{4,0},{5,1},{6,2},{7,3},{8,12},{9,13},{10,... | collective-permute-start | bytes 147464 | tf_op jit(solution)/shard_map/ppermute | solution.py:847
  58.9 17.4 %collective-permute-start.10 = (f32[16,768]{1,0:T(8,128)S(1)}, f32[16,768]{1,0:T(8,128)S(1)}, u32[]{:S(2)}, u32[]{:S(2)}) collective-permute-start(f32[16,768]{1,0:T(8,128)S(1)} %add.79), channel_id=1, source_target_pairs={{0,8},{1,9},{2,10},{3,11},{4,12},{5,13},{6,14},{7,15},{8,0},{9,1},... | collective-permute-start | bytes 147464 | tf_op jit(solution)/shard_map/ppermute | solution.py:847
  76.4 4.2 %collective-permute-start.11 = (bf16[192,2304]{1,0:T(8,128)(2,1)S(1)}, bf16[192,2304]{1,0:T(8,128)(2,1)S(1)}, u32[]{:S(2)}, u32[]{:S(2)}) collective-permute-start(bf16[192,2304]{1,0:T(8,128)(2,1)S(1)} %collective-permute-done.7.refs_3_), channel_id=1, source_target_pairs={{0,1},{1,0},{2,3},{3,2},{4,5},{5,4},{6,7},{7,6},{8,9},{9,8},{10,11... | collective-permute-start | bytes 2654216 | tf_op jit(solution)/shard_map/ppermute | solution.py:847
  76.5 11.1 %collective-permute-start.14 = (bf16[192,2304]{1,0:T(8,128)(2,1)S(1)}, bf16[192,2304]{1,0:T(8,128)(2,1)S(1)}, u32[]{:S(2)}, u32[]{:S(2)}) collective-permute-start(bf16[192,2304]{1,0:T(8,128)(2,1)S(1)} %all_gather.10.refs_0_), channel_id=1, source_target_pairs={{0,1},{1,0},{2,3},{3,2},{4,5},{5,4},{6,7},{7,6},{8,9},{9,8},{10,11... | collective-permute-start | bytes 2654216 | tf_op jit(solution)/shard_map/ppermute | solution.py:847
  77.0 10.6 %collective-permute-start.15 = (bf16[192,2304]{1,0:T(8,128)(2,1)S(1)}, bf16[192,2304]{1,0:T(8,128)(2,1)S(1)}, u32[]{:S(2)}, u32[]{:S(2)}) collective-permute-start(bf16[192,2304]{1,0:T(8,128)(2,1)S(1)} %collective-permute-done.6.refs_1_), channel_id=1, source_target_pairs={{0,1},{1,0},{2,3},{3,2},{4,5},{5,4},{6,7},{7,6},{8,9},{9,8},{10,11... | collective-permute-start | bytes 2654216 | tf_op jit(solution)/shard_map/ppermute | solution.py:847
  77.1 15.7 %collective-permute-start.13 = (bf16[384,768]{1,0:T(8,128)(2,1)S(1)}, bf16[384,768]{1,0:T(8,128)(2,1)S(1)}, u32[]{:S(2)}, u32[]{:S(2)}) collective-permute-start(bf16[384,768]{1,0:T(8,128)(2,1)S(1)} %pad_maximum_fusion), channel_id=1, source_target_pairs={{0,16},{1,17},{2,18},{3,19},{4,20},{5,21},{6,22},{7,23},{8,24},{9,... | collective-permute-start | bytes 1769480 | tf_op jit(solution)/shard_map/ppermute | solution.py:847
  78.7 15.4 %collective-permute-start.12 = (bf16[192,1536]{1,0:T(8,128)(2,1)S(1)}, bf16[192,1536]{1,0:T(8,128)(2,1)S(1)}, u32[]{:S(2)}, u32[]{:S(2)}) collective-permute-start(bf16[192,1536]{1,0:T(8,128)(2,1)S(1)} %all_gather.11.refs_0_), channel_id=1, source_target_pairs={{0,2},{1,3},{2,0},{3,1},{4,6},{5,7},{6,4},{7,5},{8,10},{9,11},{10,... | collective-permute-start | bytes 1769480 | tf_op jit(solution)/shard_map/ppermute | solution.py:847
  80.5 16.0 %collective-permute-start.16 = (bf16[192,1536]{1,0:T(8,128)(2,1)S(1)}, bf16[192,1536]{1,0:T(8,128)(2,1)S(1)}, u32[]{:S(2)}, u32[]{:S(2)}) collective-permute-start(bf16[192,1536]{1,0:T(8,128)(2,1)S(1)} %all_gather.11.refs_0_), channel_id=1, source_target_pairs={{0,1},{1,0},{2,3},{3,2},{4,5},{5,4},{6,7},{7,6},{8,9},{9,8},{10,11... | collective-permute-start | bytes 1769480 | tf_op jit(solution)/shard_map/ppermute | solution.py:847
  94.1 2.5 %collective-permute-start.17 = (bf16[192,1536]{1,0:T(8,128)(2,1)S(1)}, bf16[192,1536]{1,0:T(8,128)(2,1)S(1)}, u32[]{:S(2)}, u32[]{:S(2)}) collective-permute-start(bf16[192,1536]{1,0:T(8,128)(2,1)S(1)} %collective-permute-done.12.refs_1_), channel_id=1, source_target_pairs={{0,1},{1,0},{2,3},{3,2},{4,5},{5,4},{6,7},{7,6},{8,9},{9,8},{10,11... | collective-permute-start | bytes 1769480 | tf_op jit(solution)/shard_map/ppermute | solution.py:847
  94.1 2.8 %collective-permute-start.18 = (bf16[384,768]{1,0:T(8,128)(2,1)S(1)}, bf16[384,768]{1,0:T(8,128)(2,1)S(1)}, u32[]{:S(2)}, u32[]{:S(2)}) collective-permute-start(bf16[384,768]{1,0:T(8,128)(2,1)S(1)} %collective-permute-done.13.refs_0_), channel_id=1, source_target_pairs={{0,1},{1,0},{2,3},{3,2},{4,5},{5,4},{6,7},{7,6},{8,9},{9,8},{10,11... | collective-permute-start | bytes 1769480 | tf_op jit(solution)/shard_map/ppermute | solution.py:847
  96.9 6.7 %collective-permute-start.19 = (bf16[384,3072]{1,0:T(8,128)(2,1)S(1)}, bf16[384,3072]{1,0:T(8,128)(2,1)S(1)}, u32[]{:S(2)}, u32[]{:S(2)}) collective-permute-start(bf16[384,3072]{1,0:T(8,128)(2,1)S(1)} %get-tuple-element.238), channel_id=1, source_target_pairs={{0,1},{1,0},{2,3},{3,2},{4,5},{5,4},{6,7},{7,6},{8,9},{9,8},{10,11... | collective-permute-start | bytes 7077896 | tf_op jit(solution)/shard_map/ppermute | solution.py:847
  104.6 16.1 %collective-permute-start.22 = (bf16[384,3072]{1,0:T(8,128)(2,1)S(1)}, bf16[384,3072]{1,0:T(8,128)(2,1)S(1)}, u32[]{:S(2)}, u32[]{:S(2)}) collective-permute-start(bf16[384,3072]{1,0:T(8,128)(2,1)S(1)} %get-tuple-element.261), channel_id=1, source_target_pairs={{0,1},{1,0},{2,3},{3,2},{4,5},{5,4},{6,7},{7,6},{8,9},{9,8},{10,11... | collective-permute-start | bytes 7077896 | tf_op jit(solution)/shard_map/ppermute | solution.py:847
  105.1 15.4 %collective-permute-start.20 = (bf16[192,1536]{1,0:T(8,128)(2,1)S(1)}, bf16[192,1536]{1,0:T(8,128)(2,1)S(1)}, u32[]{:S(2)}, u32[]{:S(2)}) collective-permute-start(bf16[192,1536]{1,0:T(8,128)(2,1)S(1)} %get-tuple-element.259), channel_id=1, source_target_pairs={{0,2},{1,3},{2,0},{3,1},{4,6},{5,7},{6,4},{7,5},{8,10},{9,11},{10,... | collective-permute-start | bytes 1769480 | tf_op jit(solution)/shard_map/ppermute | solution.py:847
  105.6 15.1 %collective-permute-start.21 = (bf16[4,2,48,768]{3,2,1,0:T(8,128)(2,1)S(1)}, bf16[4,2,48,768]{3,2,1,0:T(8,128)(2,1)S(1)}, u32[]{:S(2)}, u32[]{:S(2)}) collective-permute-start(bf16[4,2,48,768]{3,2,1,0:T(8,128)(2,1)S(1)} %get-tuple-element.260), channel_id=1, source_target_pairs={{0,16},{1,17},{2,18},{3,19},{4,20},{5,21},{6,22},{7,23},{8,24},{9,... | collective-permute-start | bytes 1769480 | tf_op jit(solution)/shard_map/ppermute | solution.py:847
  120.7 18.4 %collective-permute-start.26 = (bf16[384,3072]{1,0:T(8,128)(2,1)S(1)}, bf16[384,3072]{1,0:T(8,128)(2,1)S(1)}, u32[]{:S(2)}, u32[]{:S(2)}) collective-permute-start(bf16[384,3072]{1,0:T(8,128)(2,1)S(1)} %get-tuple-element.283), channel_id=1, source_target_pairs={{0,1},{1,0},{2,3},{3,2},{4,5},{5,4},{6,7},{7,6},{8,9},{9,8},{10,11... | collective-permute-start | bytes 7077896 | tf_op jit(solution)/shard_map/ppermute | solution.py:847
  121.8 15.8 %collective-permute-start.24 = (bf16[192,1536]{1,0:T(8,128)(2,1)S(1)}, bf16[192,1536]{1,0:T(8,128)(2,1)S(1)}, u32[]{:S(2)}, u32[]{:S(2)}) collective-permute-start(bf16[192,1536]{1,0:T(8,128)(2,1)S(1)} %get-tuple-element.281), channel_id=1, source_target_pairs={{0,2},{1,3},{2,0},{3,1},{4,6},{5,7},{6,4},{7,5},{8,10},{9,11},{10,... | collective-permute-start | bytes 1769480 | tf_op jit(solution)/shard_map/ppermute | solution.py:847
  123.4 15.5 %collective-permute-start.25 = (bf16[4,2,48,768]{3,2,1,0:T(8,128)(2,1)S(1)}, bf16[4,2,48,768]{3,2,1,0:T(8,128)(2,1)S(1)}, u32[]{:S(2)}, u32[]{:S(2)}) collective-permute-start(bf16[4,2,48,768]{3,2,1,0:T(8,128)(2,1)S(1)} %get-tuple-element.282), channel_id=1, source_target_pairs={{0,16},{1,17},{2,18},{3,19},{4,20},{5,21},{6,22},{7,23},{8,24},{9,... | collective-permute-start | bytes 1769480 | tf_op jit(solution)/shard_map/ppermute | solution.py:847
  123.9 15.2 %collective-permute-start.23 = (bf16[384,768]{1,0:T(8,128)(2,1)S(1)}, bf16[384,768]{1,0:T(8,128)(2,1)S(1)}, u32[]{:S(2)}, u32[]{:S(2)}) collective-permute-start(bf16[384,768]{1,0:T(8,128)(2,1)S(1)} %get-tuple-element.280), channel_id=1, source_target_pairs={{0,4},{1,5},{2,6},{3,7},{4,0},{5,1},{6,2},{7,3},{8,12},{9,13},{10,... | collective-permute-start | bytes 1769480 | tf_op jit(solution)/shard_map/ppermute | solution.py:847
  140.9 17.9 %collective-permute-start.30 = (bf16[4,2,48,768]{3,2,1,0:T(8,128)(2,1)S(1)}, bf16[4,2,48,768]{3,2,1,0:T(8,128)(2,1)S(1)}, u32[]{:S(2)}, u32[]{:S(2)}) collective-permute-start(bf16[4,2,48,768]{3,2,1,0:T(8,128)(2,1)S(1)} %get-tuple-element.302), channel_id=1, source_target_pairs={{0,16},{1,17},{2,18},{3,19},{4,20},{5,21},{6,22},{7,23},{8,24},{9,... | collective-permute-start | bytes 1769480 | tf_op jit(solution)/shard_map/ppermute | solution.py:847
  142.5 16.3 %collective-permute-start.29 = (bf16[192,1536]{1,0:T(8,128)(2,1)S(1)}, bf16[192,1536]{1,0:T(8,128)(2,1)S(1)}, u32[]{:S(2)}, u32[]{:S(2)}) collective-permute-start(bf16[192,1536]{1,0:T(8,128)(2,1)S(1)} %get-tuple-element.299), channel_id=1, source_target_pairs={{0,2},{1,3},{2,0},{3,1},{4,6},{5,7},{6,4},{7,5},{8,10},{9,11},{10,... | collective-permute-start | bytes 1769480 | tf_op jit(solution)/shard_map/ppermute | solution.py:847
  143.7 12.8 %collective-permute-start.28 = (bf16[96,1536]{1,0:T(8,128)(2,1)S(1)}, bf16[96,1536]{1,0:T(8,128)(2,1)S(1)}, u32[]{:S(2)}, u32[]{:S(2)}) collective-permute-start(bf16[96,1536]{1,0:T(8,128)(2,1)S(1)} %get-tuple-element.301), channel_id=1, source_target_pairs={{0,4},{1,5},{2,6},{3,7},{4,0},{5,1},{6,2},{7,3},{8,12},{9,13},{10,... | collective-permute-start | bytes 884744 | tf_op jit(solution)/shard_map/ppermute | solution.py:847
  144.0 14.7 %collective-permute-start.27 = (bf16[192,768]{1,0:T(8,128)(2,1)S(1)}, bf16[192,768]{1,0:T(8,128)(2,1)S(1)}, u32[]{:S(2)}, u32[]{:S(2)}) collective-permute-start(bf16[192,768]{1,0:T(8,128)(2,1)S(1)} %get-tuple-element.291), channel_id=1, source_target_pairs={{0,8},{1,9},{2,10},{3,11},{4,12},{5,13},{6,14},{7,15},{8,0},{9,1},... | collective-permute-start | bytes 884744 | tf_op jit(solution)/shard_map/ppermute | solution.py:847
  145.5 2.7 %collective-permute-start.31 = (f32[16,768]{1,0:T(8,128)S(1)}, f32[16,768]{1,0:T(8,128)S(1)}, u32[]{:S(2)}, u32[]{:S(2)}) collective-permute-start(f32[16,768]{1,0:T(8,128)S(1)} %get-tuple-element.303), channel_id=1, source_target_pairs={{0,1},{1,0},{2,3},{3,2},{4,5},{5,4},{6,7},{7,6},{8,9},{9,8},{10,11... | collective-permute-start | bytes 147464 | tf_op jit(solution)/shard_map/ppermute | solution.py:847
  159.5 13.9 %collective-permute-start.35 = (bf16[224,1536]{1,0:T(8,128)(2,1)S(1)}, bf16[224,1536]{1,0:T(8,128)(2,1)S(1)}, u32[]{:S(2)}, u32[]{:S(2)}) collective-permute-start(bf16[224,1536]{1,0:T(8,128)(2,1)S(1)} %get-tuple-element.317), channel_id=1, source_target_pairs={{0,2},{1,3},{2,0},{3,1},{4,6},{5,7},{6,4},{7,5},{8,10},{9,11},{10,... | collective-permute-start | bytes 2064392 | tf_op jit(solution)/shard_map/ppermute | solution.py:847
  161.8 11.2 %collective-permute-start.34 = (bf16[96,1536]{1,0:T(8,128)(2,1)S(1)}, bf16[96,1536]{1,0:T(8,128)(2,1)S(1)}, u32[]{:S(2)}, u32[]{:S(2)}) collective-permute-start(bf16[96,1536]{1,0:T(8,128)(2,1)S(1)} %get-tuple-element.319), channel_id=1, source_target_pairs={{0,4},{1,5},{2,6},{3,7},{4,0},{5,1},{6,2},{7,3},{8,12},{9,13},{10,... | collective-permute-start | bytes 884744 | tf_op jit(solution)/shard_map/ppermute | solution.py:847
  163.0 9.9 %collective-permute-start.32 = (bf16[48,1536]{1,0:T(8,128)(2,1)S(1)}, bf16[48,1536]{1,0:T(8,128)(2,1)S(1)}, u32[]{:S(2)}, u32[]{:S(2)}) collective-permute-start(bf16[48,1536]{1,0:T(8,128)(2,1)S(1)} %sum_far.4.refs_3_), channel_id=1, source_target_pairs={{0,16},{1,17},{2,18},{3,19},{4,20},{5,21},{6,22},{7,23},{8,24},{9,... | collective-permute-start | bytes 442376 | tf_op jit(solution)/shard_map/ppermute | solution.py:847
  163.6 9.3 %collective-permute-start.33 = (bf16[48,1536]{1,0:T(8,128)(2,1)S(1)}, bf16[48,1536]{1,0:T(8,128)(2,1)S(1)}, u32[]{:S(2)}, u32[]{:S(2)}) collective-permute-start(bf16[48,1536]{1,0:T(8,128)(2,1)S(1)} %get-tuple-element.321), channel_id=1, source_target_pairs={{0,8},{1,9},{2,10},{3,11},{4,12},{5,13},{6,14},{7,15},{8,0},{9,1},... | collective-permute-start | bytes 442376 | tf_op jit(solution)/shard_map/ppermute | solution.py:847
  165.8 7.1 %collective-permute-start.36 = (f32[16,768]{1,0:T(8,128)S(1)}, f32[16,768]{1,0:T(8,128)S(1)}, u32[]{:S(2)}, u32[]{:S(2)}) collective-permute-start(f32[16,768]{1,0:T(8,128)S(1)} %add.81), channel_id=1, source_target_pairs={{0,8},{1,9},{2,10},{3,11},{4,12},{5,13},{6,14},{7,15},{8,0},{9,1},... | collective-permute-start | bytes 147464 | tf_op jit(solution)/shard_map/ppermute | solution.py:847
  174.1 9.3 %collective-permute-start.39 = (bf16[96,1536]{1,0:T(8,128)(2,1)S(1)}, bf16[96,1536]{1,0:T(8,128)(2,1)S(1)}, u32[]{:S(2)}, u32[]{:S(2)}) collective-permute-start(bf16[96,1536]{1,0:T(8,128)(2,1)S(1)} %get-tuple-element.332), channel_id=1, source_target_pairs={{0,4},{1,5},{2,6},{3,7},{4,0},{5,1},{6,2},{7,3},{8,12},{9,13},{10,... | collective-permute-start | bytes 884744 | tf_op jit(solution)/shard_map/ppermute | solution.py:847
  175.5 8.0 %collective-permute-start.37 = (bf16[48,2304]{1,0:T(8,128)(2,1)S(1)}, bf16[48,2304]{1,0:T(8,128)(2,1)S(1)}, u32[]{:S(2)}, u32[]{:S(2)}) collective-permute-start(bf16[48,2304]{1,0:T(8,128)(2,1)S(1)} %sum_far.5.refs_5_), channel_id=1, source_target_pairs={{0,16},{1,17},{2,18},{3,19},{4,20},{5,21},{6,22},{7,23},{8,24},{9,... | collective-permute-start | bytes 663560 | tf_op jit(solution)/shard_map/ppermute | solution.py:847
  176.4 7.1 %collective-permute-start.38 = (bf16[48,1536]{1,0:T(8,128)(2,1)S(1)}, bf16[48,1536]{1,0:T(8,128)(2,1)S(1)}, u32[]{:S(2)}, u32[]{:S(2)}) collective-permute-start(bf16[48,1536]{1,0:T(8,128)(2,1)S(1)} %get-tuple-element.331), channel_id=1, source_target_pairs={{0,8},{1,9},{2,10},{3,11},{4,12},{5,13},{6,14},{7,15},{8,0},{9,1},... | collective-permute-start | bytes 442376 | tf_op jit(solution)/shard_map/ppermute | solution.py:847
  177.7 5.7 %collective-permute-start.40 = (f32[16,768]{1,0:T(8,128)S(1)}, f32[16,768]{1,0:T(8,128)S(1)}, u32[]{:S(2)}, u32[]{:S(2)}) collective-permute-start(f32[16,768]{1,0:T(8,128)S(1)} %add.82), channel_id=1, source_target_pairs={{0,4},{1,5},{2,6},{3,7},{4,0},{5,1},{6,2},{7,3},{8,12},{9,13},{10,... | collective-permute-start | bytes 147464 | tf_op jit(solution)/shard_map/ppermute | solution.py:847
  184.7 7.2 %collective-permute-start.41 = (bf16[48,1536]{1,0:T(8,128)(2,1)S(1)}, bf16[48,1536]{1,0:T(8,128)(2,1)S(1)}, u32[]{:S(2)}, u32[]{:S(2)}) collective-permute-start(bf16[48,1536]{1,0:T(8,128)(2,1)S(1)} %sum_far.6.refs_6_), channel_id=1, source_target_pairs={{0,16},{1,17},{2,18},{3,19},{4,20},{5,21},{6,22},{7,23},{8,24},{9,... | collective-permute-start | bytes 442376 | tf_op jit(solution)/shard_map/ppermute | solution.py:847
  185.9 7.6 %collective-permute-start.42 = (bf16[48,1536]{1,0:T(8,128)(2,1)S(1)}, bf16[48,1536]{1,0:T(8,128)(2,1)S(1)}, u32[]{:S(2)}, u32[]{:S(2)}) collective-permute-start(bf16[48,1536]{1,0:T(8,128)(2,1)S(1)} %get-tuple-element.338), channel_id=1, source_target_pairs={{0,8},{1,9},{2,10},{3,11},{4,12},{5,13},{6,14},{7,15},{8,0},{9,1},... | collective-permute-start | bytes 442376 | tf_op jit(solution)/shard_map/ppermute | solution.py:847
  187.9 4.1 %collective-permute-start.43 = (f32[16,768]{1,0:T(8,128)S(1)}, f32[16,768]{1,0:T(8,128)S(1)}, u32[]{:S(2)}, u32[]{:S(2)}) collective-permute-start(f32[16,768]{1,0:T(8,128)S(1)} %add.83), channel_id=1, source_target_pairs={{0,2},{1,3},{2,0},{3,1},{4,6},{5,7},{6,4},{7,5},{8,10},{9,11},{10,... | collective-permute-start | bytes 147464 | tf_op jit(solution)/shard_map/ppermute | solution.py:847
  193.5 4.6 %collective-permute-start.45 = (f32[16,768]{1,0:T(8,128)S(1)}, f32[16,768]{1,0:T(8,128)S(1)}, u32[]{:S(2)}, u32[]{:S(2)}) collective-permute-start(f32[16,768]{1,0:T(8,128)S(1)} %add.84), channel_id=1, source_target_pairs={{0,16},{1,17},{2,18},{3,19},{4,20},{5,21},{6,22},{7,23},{8,24},{9,... | collective-permute-start | bytes 147464 | tf_op jit(solution)/shard_map/ppermute | solution.py:847
  194.3 6.3 %collective-permute-start.44 = (bf16[48,1536]{1,0:T(8,128)(2,1)S(1)}, bf16[48,1536]{1,0:T(8,128)(2,1)S(1)}, u32[]{:S(2)}, u32[]{:S(2)}) collective-permute-start(bf16[48,1536]{1,0:T(8,128)(2,1)S(1)} %sum_far.7.refs_3_), channel_id=1, source_target_pairs={{0,16},{1,17},{2,18},{3,19},{4,20},{5,21},{6,22},{7,23},{8,24},{9,... | collective-permute-start | bytes 442376 | tf_op jit(solution)/shard_map/ppermute | solution.py:847
  (18 other events, 110.7 us)

commit v7 on v6

--- a/solution.py
+++ b/solution.py
@@ -362,20 +362,18 @@
     )(*args)
 
 
-def call_all(co, jobs, name):
+def call_all(co, jobs, name, dtype=None):
     args = [arg for job in jobs for arg in job[2]]
-    outs = [out for job in jobs for out in job[1]]
+    chosen = [out for job in jobs for out in job[1] if dtype in (None, out[1])]
 
     def body(co_ref, *refs):
-        first, last = 0, len(args)
+        first, results = 0, iter(refs[len(args) :])
         for kernel, job_outs, job_args in jobs:
-            ins = refs[first : first + len(job_args)]
-            results = refs[last : last + len(job_outs)]
-            kernel(co_ref, *ins, *results)
+            outs = [next(results) if dtype in (None, out[1]) else None for out in job_outs]
+            kernel(co_ref, *refs[first : first + len(job_args)], *outs)
             first += len(job_args)
-            last += len(job_outs)
-
-    return call(body, outs, [co, *args], name=name)
+
+    return call(body, chosen, [co, *args], name=name)
 
 
 def assemble_kernel(ranges, co, *refs):
@@ -684,11 +682,15 @@
     every = slice(None)
     for k in range(4):
         for out, i in ((y_send, 1 - y), (y_keep, y)):
+            if out is None:
+                continue
             out[k * 48 : k * 48 + 48, :] = both(keep, got, k, i, every, slice(0, 2 * D)).astype(
                 out.dtype
             )
-    x_keep[...] = both(keep, got, every, every, every, slice(2 * D, 3 * D))
-    x_send[...] = both(keep, got, every, every, every, slice(3 * D, 4 * D)).astype(BF)
+    if x_keep is not None:
+        x_keep[...] = both(keep, got, every, every, every, slice(2 * D, 3 * D))
+    if x_send is not None:
+        x_send[...] = both(keep, got, every, every, every, slice(3 * D, 4 * D)).astype(BF)
 
 
 def split_second_kernel(co, x_keep, x_got, keep, got, y_send, y_keep, x_send, x_next):
@@ -697,10 +699,14 @@
     for k in range(4):
         rows = slice(k * 48, k * 48 + 48)
         for out, i in ((y_send, 1 - y), (y_keep, y)):
+            if out is None:
+                continue
             out[rows, :D] = both(x_keep, x_got, k, i).astype(out.dtype)
             out[rows, D:] = both(keep, got, k, i, every, slice(0, D)).astype(out.dtype)
-    x_next[...] = both(keep, got, every, every, every, slice(2 * D, 3 * D))
-    x_send[...] = both(keep, got, every, every, every, slice(3 * D, 4 * D)).astype(BF)
+    if x_next is not None:
+        x_next[...] = both(keep, got, every, every, every, slice(2 * D, 3 * D))
+    if x_send is not None:
+        x_send[...] = both(keep, got, every, every, every, slice(3 * D, 4 * D)).astype(BF)
 
 
 def split_third_kernel(co, x_keep, x_got, keep, got, y_send, y_keep, x_send, x_next, last):
@@ -709,30 +715,32 @@
     for k in range(4):
         rows = slice(k * 48, k * 48 + 48)
         for out, i in ((y_send, 1 - y), (y_keep, y)):
+            if out is None:
+                continue
             out[rows, :D] = both(x_keep, x_got, k, i).astype(out.dtype)
             out[rows, D:] = both(keep, got, k, i, every, slice(2 * D, 3 * D)).astype(out.dtype)
-    x_next[...] = both(keep, got, every, every, every, slice(0, D))
-    x_send[...] = both(keep, got, every, every, every, slice(D, 2 * D)).astype(BF)
-    last[...] = both(keep, got, every, every, every, slice(3 * D, 4 * D))
-
-
-def split_fourth_kernel(co, x_keep, x_got, last, far_keep, far_got, y_send, y_keep):
+    if x_next is not None:
+        x_next[...] = both(keep, got, every, every, every, slice(0, D))
+    if x_send is not None:
+        x_send[...] = both(keep, got, every, every, every, slice(D, 2 * D)).astype(BF)
+    if last is not None:
+        last[...] = both(keep, got, every, every, every, slice(3 * D, 4 * D))
+
+
+def split_fourth_kernel(co, x_keep, x_got, last, y_send, y_keep):
     y = co[2]
     for out, i in ((y_send, 1 - y), (y_keep, y)):
         for k in range(4):
             rows = slice(k * 48, k * 48 + 48)
             out[rows, :D] = both(x_keep, x_got, k, i).astype(out.dtype)
             out[rows, D:] = last[k, i].astype(out.dtype)
-        row = pl.multiple_of(96 + i * 48, 16)
-        block = both(far_keep, far_got, pl.ds(row, 48)).astype(out.dtype)
-        out[192:224, :D] = block[:32]
-        out[192:208, D:] = block[32:]
-        out[208:224, D:] = jnp.zeros((16, D), out.dtype)
 
 
 def split_near_first_kernel(co, keep, got, up_keep, up_got, send, rest):
     side = co[1] % 2
     for out, at in ((send, 1 - side), (rest, side)):
+        if out is None:
+            continue
         for far in range(2):
             row = pl.multiple_of((2 * far + at) * 48, 16)
             for half in range(2):
@@ -747,6 +755,8 @@
 def split_far_first_kernel(co, keep, got, send, rest):
     side = co[1] // 2
     for out, at in ((send, 1 - side), (rest, side)):
+        if out is None:
+            continue
         for half in range(2):
             row = pl.multiple_of(half * 96 + at * 48, 16)
             to = half * 48
@@ -755,26 +765,34 @@
         out[96:192, :] = both(keep, got, pl.ds(row, 96)).astype(out.dtype)
 
 
-def sum_far_first_kernel(co, keep, got, out):
+def sum_far_first_kernel(co, keep, got, out, send, rest):
     for half in range(2):
         rows = slice(half * 48, half * 48 + 48)
         out[:, half * D : half * D + D] = both(keep, got, rows).astype(BF)
-
-
-def sum_far_second_kernel(co, keep, got, other, out):
+    for part, i in ((send, 1 - co[2]), (rest, co[2])):
+        row = pl.multiple_of(96 + i * 48, 16)
+        part[...] = both(keep, got, pl.ds(row, 48)).astype(part.dtype)
+
+
+def pack_kernel(co, early, vec, out):
+    out[0:48, :] = early[...]
+    out[48:64, :] = vec[...].astype(BF)
+
+
+def sum_third_kernel(co, keep, got, early_keep, packed, vec, out, vec_out):
     out[:, : 2 * D] = both(keep, got, slice(None)).astype(BF)
-    out[:, 2 * D :] = other[...].astype(BF)
-
-
-def split_near_kernel(co, keep, got, send, rest, *small):
+    out[:, 2 * D :] = both(early_keep, packed, slice(0, 48)).astype(BF)
+    vec_out[...] = vec[...] + packed[48:64, :].astype(F32)
+
+
+def split_near_kernel(co, keep, got, send, rest):
     side = co[1] % 2
     for out, at in ((send, 1 - side), (rest, side)):
+        if out is None:
+            continue
         for far in range(2):
             row = pl.multiple_of((2 * far + at) * 48, 16)
             out[far * 48 : far * 48 + 48, :] = both(keep, got, pl.ds(row, 48)).astype(out.dtype)
-    if small:
-        small[0][0:32, :] = both(keep, got, slice(192, 224), slice(0, D))
-        small[0][32:48, :] = both(keep, got, slice(192, 208), slice(D, 2 * D))
 
 
 def split_far_kernel(co, keep, got, send, rest):
@@ -986,10 +1004,11 @@
     down_got, up_send = hold((down_got, up_send))
     y_shares = [((192, 2 * D), BF), ((192, 2 * D), F32)]
     x_shares = [((4, 2, 48, D), BF), ((4, 2, 48, D), F32)]
-    y_send0, y_keep0, x_send1, x_keep1 = call(
-        split_first_kernel, y_shares + x_shares, [co, down_keep, down_got], name="split_first"
-    )
-    y_send0, x_send1, up_send, du0 = hold((y_send0, x_send1, up_send, du0))
+    first = (split_first_kernel, y_shares + x_shares)
+    y_send0, x_send1 = call_all(co, [(*first, [down_keep, down_got])], "split_first", BF)
+    y_send0, x_send1, up_send, down_got = hold((y_send0, x_send1, up_send, down_got))
+    y_keep0, x_keep1 = call_all(co, [(*first, [down_keep, down_got])], "keep_first", F32)
+    du0, y_keep0, x_keep1 = hold((du0, y_keep0, x_keep1))
     y_got0 = swap(y_send0, Y)
     x_got1 = swap(x_send1, X)
     up_got = blocks(swap(up_send, CORE))
@@ -1047,19 +1066,19 @@
         return sum_far_kernel, [(keep.shape, BF)], [keep, got]
 
     y_got0, x_got1, up_got, attn_send = hold((y_got0, x_got1, up_got, attn_send))
-    y_send1, y_keep1, x_send2, x_keep2, near_send0, near_keep0 = call_all(
-        co,
-        [
-            (split_second_kernel, y_shares + x_shares, [x_keep1, x_got1, up_keep, up_got]),
-            (
-                split_near_first_kernel,
-                [((384, D), BF), ((384, D), F32)],
-                [y_keep0, y_got0, up_keep, up_got],
-            ),
-        ],
-        "split_third_round",
-    )
-    dqkv = hold((dqkv, near_send0))[0]
+    near_shares = [((384, D), BF), ((384, D), F32)]
+
+    def second(y_got):
+        up = [up_keep, up_got]
+        return [
+            (split_second_kernel, y_shares + x_shares, [x_keep1, x_got1, *up]),
+            (split_near_first_kernel, near_shares, [y_keep0, y_got, *up]),
+        ]
+
+    y_send1, x_send2, near_send0 = call_all(co, second(y_got0), "split_second", BF)
+    y_got0, near_send0 = hold((y_got0, near_send0))
+    y_keep1, x_keep2, near_keep0 = call_all(co, second(y_got0), "keep_second", F32)
+    dqkv, y_keep1, x_keep2, near_keep0 = hold((dqkv, y_keep1, x_keep2, near_keep0))
     y_got1 = swap(y_send1, Y)
     x_got2 = swap(x_send2, X)
     near_got0 = swap(near_send0, Z)
@@ -1074,22 +1093,31 @@
     near_got0, y_got1, x_got2, attn_got, total = hold(
         (near_got0, y_got1, x_got2, attn_got, total)
     )
-    far_send0, far_keep0 = call(
-        split_far_first_kernel,
-        [((192, D), BF), ((192, D), F32)],
-        [co, near_keep0, near_got0],
-        name="split_far",
-    )
+    far_shares = [((192, D), BF), ((192, D), F32)]
+    third_shares = y_shares + x_shares + x_shares[1:]
+
+    def far_first(got):
+        return split_far_first_kernel, far_shares, [near_keep0, got]
+
+    def third(got):
+        return split_third_kernel, third_shares, [x_keep2, got, attn_keep, attn_got]
+
+    def near_second(got):
+        near = [((96, 2 * D), BF), ((96, 2 * D), F32)]
+        return split_near_kernel, near, [y_keep1, got]
+
+    (far_send0,) = call_all(co, [far_first(near_got0)], "split_far", BF)
     x_got2 = hold((x_got2, far_send0))[0]
-    y_send2, y_keep2, x_send3, x_keep3, last = call(
-        split_third_kernel,
-        y_shares + x_shares + x_shares[1:],
-        [co, x_keep2, x_got2, attn_keep, attn_got],
-        name="split_third",
-    )
+    y_send2, x_send3 = call_all(co, [third(x_got2)], "split_third", BF)
     y_got1 = hold((y_got1, y_send2))[0]
-    near_send1, near_keep1 = split_near(y_keep1, y_got1)
-    y1 = hold((y1, near_send1))[0]
+    (near_send1,) = call_all(co, [near_second(y_got1)], "split_near", BF)
+    near_got0, x_got2, y_got1, near_send1 = hold((near_got0, x_got2, y_got1, near_send1))
+    far_keep0, y_keep2, x_keep3, last, near_keep1 = call_all(
+        co, [far_first(near_got0), third(x_got2), near_second(y_got1)], "keep_third", F32
+    )
+    y1, far_keep0, y_keep2, x_keep3, last, near_keep1 = hold(
+        (y1, far_keep0, y_keep2, x_keep3, last, near_keep1)
+    )
     x_got3 = swap(x_send3, X)
     y_got2 = swap(y_send2, Y)
     near_got1 = swap(near_send1, Z)
@@ -1106,8 +1134,8 @@
     )
     y_send3, y_keep3 = call(
         split_fourth_kernel,
-        [((224, 2 * D), BF), ((224, 2 * D), F32)],
-        [co, x_keep3, x_got3, last, far_keep0, far_got0],
+        y_shares,
+        [co, x_keep3, x_got3, last],
         name="split_fourth",
     )
     y_got2 = hold((y_got2, y_send3))[0]
@@ -1115,8 +1143,11 @@
     near_got1 = hold((near_got1, near_send2))[0]
     far_send1, far_keep1 = split_far(near_keep1, near_got1)
     far_got0 = hold((far_got0, far_send1))[0]
-    (mine0,) = call(
-        sum_far_first_kernel, [((48, 2 * D), BF)], [co, far_keep0, far_got0], name="sum_far"
+    mine0, early_send, early_keep = call(
+        sum_far_first_kernel,
+        [((48, 2 * D), BF), ((48, D), BF), ((48, D), F32)],
+        [co, far_keep0, far_got0],
+        name="sum_far",
     )
     y_got3 = swap(y_send3, Y)
     near_got2 = swap(near_send2, Z)
@@ -1126,31 +1157,39 @@
     got0, far_got1, near_got2, y_got3, total = hold(
         (got0, far_got1, near_got2, y_got3, total)
     )
-    near_send3, near_keep3, other, far_send2, far_keep2 = call_all(
+    near_send3, near_keep3, far_send2, far_keep2, mine1, packed = call_all(
         co,
-        [near_job(y_keep3, y_got3, [((48, D), F32)]), far_job(near_keep2, near_got2)],
+        [
+            near_job(y_keep3, y_got3),
+            far_job(near_keep2, near_got2),
+            sum_job(far_keep1, far_got1),
+            (pack_kernel, [((64, D), BF)], [early_send, total]),
+        ],
         "split_sixth_round",
-    )
-    (mine1,) = call(
-        sum_far_second_kernel,
-        [((48, 3 * D), BF)],
-        [co, far_keep1, far_got1, other],
-        name="sum_far",
     )
     near_got3 = swap(near_send3, Z)
     far_got2 = swap(far_send2, 2 * Z)
     got1 = swap(mine1, X)
-    total = total + swap(total, Z)
-    got1, far_got2, near_got3, total = hold((got1, far_got2, near_got3, total))
-    far_send3, far_keep3 = split_far(near_keep3, near_got3)
-    far_got2 = hold((far_got2, far_send3))[0]
-    mine2 = sum_far(far_keep2, far_got2)
+    packed = swap(packed, Y)
+    got1, far_got2, near_got3, packed = hold((got1, far_got2, near_got3, packed))
+    far_send3, far_keep3, mine2, total = call_all(
+        co,
+        [
+            far_job(near_keep3, near_got3),
+            (
+                sum_third_kernel,
+                [((48, 3 * D), BF), ((16, D), F32)],
+                [far_keep2, far_got2, early_keep, packed, total],
+            ),
+        ],
+        "split_last_round",
+    )
     far_got3 = swap(far_send3, 2 * Z)
     got2 = swap(mine2, X)
-    total = total + swap(total, Y)
+    total = total + swap(total, Z)
     moves = [(0, (0, 1), 0, h * D, D, None, FF + h * 2 * D, 0) for h in range(2)]
     moves += [(0, (2 + b,), 0, 0, D, b, FF + D, 2 * D) for b in range(2)]
-    moves += [(0, (2, 3), 0, D + h * D, D, None, h * 2 * D, 0) for h in range(2)]
+    moves += [(0, (2, 3), 0, D, D, None, 0, 0)]
     got1 = hold((got1, mine2))[0]
     mlp = update(moves, [mlp_state], [mine0, got0, mine1, got1], "update_mlp")
     got2, far_got3, total, mlp = hold((got2, far_got3, total, mlp))
@@ -1159,7 +1198,7 @@
     total = total + swap(total, X)
     got2 = hold((got2, mine3))[0]
     moves = [(0, (b,), 0, 0, D, b, D, 2 * D) for b in range(2)]
-    moves += [(1, (0, 1), 0, D, D, None, 0, 0)]
+    moves += [(0, (0, 1), 0, 2 * D, D, None, 2 * D, 0), (1, (0, 1), 0, D, D, None, 0, 0)]
     both_new = update(
         moves,
         [mlp_state, attn_state],

time: 203 us -> 202 us (level)
    pallas_call x32 -> x33, Pallas kernels: 50.3 us -> 50.6 us  [call(): pl.pallas_call(body, out_shape=[jax.ShapeDtypeStruct(shape, dtype) for sh...]
  transfers between devices with their start and end apart: 46 -> 46, of which waited for: 18 -> 17; matrix products, arithmetic and copies ran while one was open for 1% -> 1% of each run, Pallas kernels for 23% -> 24%
where the time goes in v7:
time: 202 us; the launch traced here: 201 us
  blocking collectives  58.2 us (29%)
  Pallas kernels  56.8 us (28%)
  waiting for transfers between devices  46.5 us (23%)
  starting transfers between devices  33.4 us (17%)
  other arithmetic  4.64 us (2%)
    all_gather x3, blocking collectives, along_z(): lax.all_gather(shard, 'fsdp', axis=0, tiled=True, axis_index_groups=groups)  58.2 us
    pallas_call x33, Pallas kernels, call(): pl.pallas_call(body, out_shape=[jax.ShapeDtypeStruct(shape, dtype) for sh...  50.6 us
    ppermute x46, waiting for transfers between devices, swap(): lax.ppermute(array, ('rep', 'fsdp'), [(i, i ^ mask) for i in range(32)])  46.5 us
    ppermute x46, starting transfers between devices, swap(): lax.ppermute(array, ('rep', 'fsdp'), [(i, i ^ mask) for i in range(32)])  33.4 us
    pallas_call x3, Pallas kernels, update(): pl.pallas_call(functools.partial(update_kernel, rate, moves, len(states),...  6.15 us
  transfers between devices with their start and end apart: 46, of which 17 were waited for; matrix products, arithmetic and copies ran while one was open for 1% of the time, Pallas kernels for 24%

profile of v7, /device:TPU:0, one launch (start us, length us, event | category | flops | bytes accessed | tf_op | source)
XLA Modules:
  0.0 201.4 jit_solution(641951726814453329)
XLA Ops:
  2.9 2.6 %prep.2 = bf16[48,2304]{1,0:T(8,128)(2,1)} custom-call(s32[4]{0:T(128)} %pad_add_fusion.co_ref.co, f32[48,3072]{1,0:T(8,128)} %refs_0_.16, f32[48,6144]{1,0:T(8,128)} %refs_0_.15), custom_call_target="tpu_custom_call" | custom-call | flops 1048576 | bytes 1048576 | tf_op jit(solution)/shard_map/prep/pallas_call | solution.py:352
  5.5 22.6 %all_gather.9.refs_0_ = bf16[192,2304]{1,0:T(8,128)(2,1)S(1)} all-gather(bf16[48,2304]{1,0:T(8,128)(2,1)} %prep.2), channel_id=1, replica_groups={{0,4,8,12},{1,5,9,13},{2,6,10,14},{3,7,11,15},{16,20,24,28},{17,21,25,2..., dimensions={0}, use_global_device_ids=true | all-gather | bytes 1105920 | tf_op jit(solution)/shard_map/all_gather | solution.py:889
  28.1 1.5 collective-permute-start.2
  29.6 1.5 collective-permute-start.1
  32.9 19.2 %all_gather.10.refs_0_ = bf16[192,2304]{1,0:T(8,128)(2,1)S(1)} all-gather(bf16[48,2304]{1,0:T(8,128)(2,1)S(1)} %get-tuple-element.222), channel_id=1, replica_groups={{0,4,8,12},{1,5,9,13},{2,6,10,14},{3,7,11,15},{16,20,24,28},{17,21,25,2..., dimensions={0}, use_global_device_ids=true | all-gather | bytes 1105920 | tf_op jit(solution)/shard_map/all_gather | solution.py:889
  52.5 1.6 collective-permute-start.6
  54.8 4.1 %collective-permute-done.5 = f32[16,768]{1,0:T(8,128)S(1)} collective-permute-done((f32[16,768]{1,0:T(8,128)S(1)}, f32[16,768]{1,0:T(8,128)S(1)}, u32[]{:S(2)}, u32[]{:S(2)}) %collective-permute-start.5) | collective-permute-done | bytes 49184 | tf_op jit(solution)/shard_map/ppermute | solution.py:865
  58.9 0.9 collective-permute-start.10
  59.8 16.4 %all_gather.11.refs_0_ = bf16[192,1536]{1,0:T(8,128)(2,1)S(1)} all-gather(bf16[48,1536]{1,0:T(8,128)(2,1)S(1)} %get-tuple-element.228), channel_id=1, replica_groups={{0,4,8,12},{1,5,9,13},{2,6,10,14},{3,7,11,15},{16,20,24,28},{17,21,25,2..., dimensions={0}, use_global_device_ids=true | all-gather | bytes 737280 | tf_op jit(solution)/shard_map/all_gather | solution.py:889
  77.1 1.6 collective-permute-start.15
  79.2 1.3 norm1.1
  81.4 3.5 %attention.1 = (bf16[256,2304]{1,0:T(8,128)(2,1)S(1)}, bf16[256,768]{1,0:T(8,128)(2,1)S(1)}, f32[16,256]{1,0:T(8,128)S(1)}) custom-call(s32[4]{0:T(128)S(1)} %copy-done.8, bf16[256,768]{1,0:T(8,128)(2,1)S(1)} %get-tuple-element.236.refs_0_, f32[16,768]{1,0:T(8,128)S(1)} %add.77.refs_2_.refs_1_.refs_3_, f32[8,256]{1,0:T(8,128)S(1)} %scatter.4.refs_1_.refs_2_.refs_0_, ...), custom_call_target="tpu_custom_call" | custom-call | flops 1048576 | bytes 1048576 | tf_op jit(solution)/shard_map/attention/pallas_call | solution.py:352
  85.9 1.7 norm2.1
  88.4 2.7 %hidden.1 = (bf16[256,1536]{1,0:T(8,128)(2,1)S(1)}, bf16[256,1536]{1,0:T(8,128)(2,1)S(1)}, f32[256,1536]{1,0:T(8,128)S(1)}, f32[256,1536]{1,0:T(8,128)S(1)}) custom-call(s32[4]{0:T(128)S(1)} %copy-done.8, bf16[256,768]{1,0:T(8,128)(2,1)S(1)} %get-tuple-element.246.refs_0_, f32[16,768]{1,0:T(8,128)S(1)} %add.77.refs_2_.refs_1_.refs_3_, ...), custom_call_target="tpu_custom_call" | custom-call | flops 1048576 | bytes 1048576 | tf_op jit(solution)/shard_map/hidden/pallas_call | solution.py:352
  91.1 1.8 collective-permute-done.15.refs_0_
  92.9 1.2 collective-permute-done.14.refs_1_
  94.6 1.9 down_grad.1
  98.4 5.3 %hidden_grad.1 = (bf16[256,1536]{1,0:T(8,128)(2,1)S(1)}, bf16[256,1536]{1,0:T(8,128)(2,1)S(1)}, f32[8,768]{1,0:T(8,128)S(1)}, bf16[384,3072]{1,0:T(8,128)(2,1)S(1)}, f32[384,3072]{1,0:T(8,128)S(1)}) custom-call(s32[4]{0:T(128)S(1)} %copy-done.8, bf16[256,768]{1,0:T(8,128)(2,1)S(1)} %copy-done.4, f32[256,1536]{1,0:T(8,128)S(1)} %get-tuple-element.250.refs_1_, ...), custom_call_target="tpu_custom_call" | custom-call | flops 1048576 | bytes 1048576 | tf_op jit(solution)/shard_map/hidden_grad/pallas_call | solution.py:352
  106.7 3.2 %norm2_back.1 = (f32[256,768]{1,0:T(8,128)S(1)}, bf16[256,768]{1,0:T(8,128)(2,1)S(1)}, bf16[384,256]{1,0:T(8,128)(2,1)S(1)}, bf16[384,256]{1,0:T(8,128)(2,1)S(1)}, f32[8,768]{1,0:T(8,128)S(1)}) custom-call(s32[4]{0:T(128)S(1)} %copy-done.8, bf16[256,768]{1,0:T(8,128)(2,1)S(1)} %copy-done.4, f32[256,768]{1,0:T(8,128)S(1)} %get-tuple-element.339.refs_1_.refs_0_, ...), custom_call_target="tpu_custom_call" | custom-call | flops 1048576 | bytes 1048576 | tf_op jit(solution)/shard_map/norm2_back/pallas_call | solution.py:352
  109.9 5.6 %attention_back.1 = (bf16[256,2304]{1,0:T(8,128)(2,1)S(1)}, f32[8,768]{1,0:T(8,128)S(1)}) custom-call(s32[4]{0:T(128)S(1)} %copy-done.8, f32[8,256]{1,0:T(8,128)S(1)} %scatter.4.refs_1_.refs_2_.refs_0_, f32[256,128]{1,0:T(8,128)S(1)} %get-tuple-element.235.refs_3_.refs_1_.refs_2_, f32[16,256]{1,0:T(8,128)S(1)} %get-tuple-element.241.refs_2_, ...), custom_call_target="tpu_custom_call" | custom-call | flops 1048576 | bytes 1048576 | tf_op jit(solution)/shard_map/attention_back/pallas_call | solution.py:352
  115.4 2.3 %attention_grad.1 = (bf16[384,3072]{1,0:T(8,128)(2,1)S(1)}, f32[384,3072]{1,0:T(8,128)S(1)}) custom-call(s32[4]{0:T(128)S(1)} %copy-done.8, bf16[384,256]{1,0:T(8,128)(2,1)S(1)} %get-tuple-element.292.refs_0_, bf16[384,256]{1,0:T(8,128)(2,1)S(1)} %get-tuple-element.293.refs_1_, bf16[256,2304]{1,0:T(8,128)(2,1)S(1)} %get-tuple-element.312.refs_2_.refs_0_, ...), custom_call_target="tpu_custom_call" | custom-call | flops 1048576 | bytes 1048576 | tf_op jit(solution)/shard_map/attention_grad/pallas_call | solution.py:352
  117.8 2.5 %collective-permute-done.20.refs_5_ = bf16[192,1536]{1,0:T(8,128)(2,1)S(1)} collective-permute-done((bf16[192,1536]{1,0:T(8,128)(2,1)S(1)}, bf16[192,1536]{1,0:T(8,128)(2,1)S(1)}, u32[]{:S(2)}, u32[]{:S(2)}) %collective-permute-start.20) | collective-permute-done | bytes 589856 | tf_op jit(solution)/shard_map/ppermute | solution.py:865
  120.5 0.8 split_second.1
  121.4 1.6 collective-permute-start.24
  123.5 0.8 keep_second.1
  124.4 3.0 %norm1_back.1 = (bf16[256,768]{1,0:T(8,128)(2,1)}, f32[16,768]{1,0:T(8,128)S(1)}) custom-call(s32[4]{0:T(128)S(1)} %copy-done.8, bf16[256,2304]{1,0:T(8,128)(2,1)S(1)} %get-tuple-element.312.refs_2_.refs_0_, bf16[256,768]{1,0:T(8,128)(2,1)S(1)} %copy-done.5, f32[256,128]{1,0:T(8,128)S(1)} %get-tuple-element.235.refs_3_.refs_1_.refs_2_, ...), custom_call_target="tpu_custom_call" | custom-call | flops 1048576 | bytes 1048576 | tf_op jit(solution)/shard_map/norm1_back/pallas_call | solution.py:352
  127.4 9.8 %collective-permute-done.23.refs_1_ = bf16[384,768]{1,0:T(8,128)(2,1)S(1)} collective-permute-done((bf16[384,768]{1,0:T(8,128)(2,1)S(1)}, bf16[384,768]{1,0:T(8,128)(2,1)S(1)}, u32[]{:S(2)}, u32[]{:S(2)}) %collective-permute-start.23) | collective-permute-done | bytes 589856 | tf_op jit(solution)/shard_map/ppermute | solution.py:865
  137.2 1.2 collective-permute-done.25.refs_1_.refs_3_
  140.9 1.7 collective-permute-start.27
  144.0 0.9 keep_third.1
  145.0 2.7 %output.1 = bf16[256,768]{1,0:T(8,128)(2,1)} custom-call(s32[4]{0:T(128)S(1)} %copy-done.8, f32[256,768]{1,0:T(8,128)S(1)} %get-tuple-element.339.refs_1_.refs_0_, f32[16,768]{1,0:T(8,128)S(1)} %add.77.refs_2_.refs_1_.refs_3_, bf16[256,1536]{1,0:T(8,128)(2,1)S(1)} %get-tuple-element.260.refs_2_, bf16[256,1536]{1,0:T(8,128)(2,1)S(1)} %get-tuple-element.261.refs_3_, ...), custom_call_target="tpu_custom_call" | custom-call | flops 1048576 | bytes 1048576 | tf_op jit(solution)/shard_map/output/pallas_call | solution.py:352
  147.7 8.3 %collective-permute-done.27.refs_1_ = bf16[192,768]{1,0:T(8,128)(2,1)S(1)} collective-permute-done((bf16[192,768]{1,0:T(8,128)(2,1)S(1)}, bf16[192,768]{1,0:T(8,128)(2,1)S(1)}, u32[]{:S(2)}, u32[]{:S(2)}) %collective-permute-start.27) | collective-permute-done | bytes 294944 | tf_op jit(solution)/shard_map/ppermute | solution.py:865
  156.8 1.5 collective-permute-start.35
  160.7 1.3 collective-permute-start.32
  162.0 2.9 %collective-permute-start.33 = (bf16[48,1536]{1,0:T(8,128)(2,1)S(1)}, bf16[48,1536]{1,0:T(8,128)(2,1)S(1)}, u32[]{:S(2)}, u32[]{:S(2)}) collective-permute-start(bf16[48,1536]{1,0:T(8,128)(2,1)S(1)} %get-tuple-element.356), channel_id=1, source_target_pairs={{0,8},{1,9},{2,10},{3,11},{4,12},{5,13},{6,14},{7,15},{8,0},{9,1},... | collective-permute-start | bytes 442376 | tf_op jit(solution)/shard_map/ppermute | solution.py:865
  165.0 7.4 %collective-permute-done.36 = f32[16,768]{1,0:T(8,128)S(1)} collective-permute-done((f32[16,768]{1,0:T(8,128)S(1)}, f32[16,768]{1,0:T(8,128)S(1)}, u32[]{:S(2)}, u32[]{:S(2)}) %collective-permute-start.36) | collective-permute-done | bytes 49184 | tf_op jit(solution)/shard_map/ppermute | solution.py:865
  173.2 2.6 %collective-permute-start.38 = (bf16[48,1536]{1,0:T(8,128)(2,1)S(1)}, bf16[48,1536]{1,0:T(8,128)(2,1)S(1)}, u32[]{:S(2)}, u32[]{:S(2)}) collective-permute-start(bf16[48,1536]{1,0:T(8,128)(2,1)S(1)} %get-tuple-element.369), channel_id=1, source_target_pairs={{0,8},{1,9},{2,10},{3,11},{4,12},{5,13},{6,14},{7,15},{8,0},{9,1},... | collective-permute-start | bytes 442376 | tf_op jit(solution)/shard_map/ppermute | solution.py:865
  175.8 0.8 collective-permute-start.37
  177.4 3.9 %collective-permute-done.40.refs_5_ = bf16[64,768]{1,0:T(8,128)(2,1)S(1)} collective-permute-done((bf16[64,768]{1,0:T(8,128)(2,1)S(1)}, bf16[64,768]{1,0:T(8,128)(2,1)S(1)}, u32[]{:S(2)}, u32[]{:S(2)}) %collective-permute-start.40) | collective-permute-done | bytes 98336 | tf_op jit(solution)/shard_map/ppermute | solution.py:865
  181.3 1.0 collective-permute-done.39.refs_1_
  183.0 1.6 collective-permute-start.41
  184.5 1.2 collective-permute-start.42
  186.2 2.2 %update_mlp.1 = (f32[48,6144]{1,0:T(8,128)}, f32[48,6144]{1,0:T(8,128)}, f32[48,6144]{1,0:T(8,128)}, bf16[48,6144]{1,0:T(8,128)(2,1)}) custom-call(s32[4]{0:T(128)S(1)} %copy-done.8, f32[48,6144]{1,0:T(8,128)S(1)} %copy-done, f32[48,6144]{1,0:T(8,128)S(1)} %copy-done.2, f32[48,6144]{1,0:T(8,128)S(1)} %copy-done.3, ...), custom_call_target="tpu_custom_call" | custom-call | flops 1048576 | bytes 1048576 | tf_op jit(solution)/shard_map/update_mlp/pallas_call | solution.py:970
  188.5 1.4 collective-permute-done.43
  189.9 2.2 %collective-permute-done.42.refs_1_ = bf16[48,1536]{1,0:T(8,128)(2,1)S(1)} collective-permute-done((bf16[48,1536]{1,0:T(8,128)(2,1)S(1)}, bf16[48,1536]{1,0:T(8,128)(2,1)S(1)}, u32[]{:S(2)}, u32[]{:S(2)}) %collective-permute-start.42) | collective-permute-done | bytes 147488 | tf_op jit(solution)/shard_map/ppermute | solution.py:865
  193.3 1.5 collective-permute-start.44
  194.8 2.0 %update_both.1 = (f32[48,6144]{1,0:T(8,128)}, f32[48,6144]{1,0:T(8,128)}, f32[48,6144]{1,0:T(8,128)}, bf16[48,6144]{1,0:T(8,128)(2,1)}, f32[48,3072]{1,0:T(8,128...) custom-call(s32[4]{0:T(128)S(1)} %copy-done.8, ...), custom_call_target="tpu_custom_call", output_to_operand_aliasing={{0}: (9, {}), {1}: (10, {}), {2}: (11, {}), {3}: (12, {})} | custom-call | flops 1048576 | bytes 1048576 | tf_op jit(solution)/shard_map/update_both/pallas_call | solution.py:970
  199.3 1.9 update_attn.1
  (146 shorter events, 28.7 us)
Async XLA Ops:
  2.9 28.2 %copy-start = (f32[48,6144]{1,0:T(8,128)S(1)}, f32[48,6144]{1,0:T(8,128)}, u32[]{:S(2)}) copy-start(f32[48,6144]{1,0:T(8,128)} %refs_0_.15) | copy-start | bytes 3538948
  2.9 28.2 %copy-start.8 = (s32[4]{0:T(128)S(1)}, s32[4]{0:T(128)}, u32[]{:S(2)}) copy-start(s32[4]{0:T(128)} %pad_add_fusion.co_ref.co) | copy-start | bytes 52
  28.1 24.3 %collective-permute-start.3 = (bf16[192,2304]{1,0:T(8,128)(2,1)S(1)}, bf16[192,2304]{1,0:T(8,128)(2,1)S(1)}, u32[]{:S(2)}, u32[]{:S(2)}) collective-permute-start(bf16[192,2304]{1,0:T(8,128)(2,1)S(1)} %all_gather.9.refs_0_), channel_id=1, source_target_pairs={{0,1},{1,0},{2,3},{3,2},{4,5},{5,4},{6,7},{7,6},{8,9},{9,8},{10,11... | collective-permute-start | bytes 2654216 | tf_op jit(solution)/shard_map/ppermute | solution.py:865
  28.1 24.3 %collective-permute-start.2 = (bf16[192,2304]{1,0:T(8,128)(2,1)S(1)}, bf16[192,2304]{1,0:T(8,128)(2,1)S(1)}, u32[]{:S(2)}, u32[]{:S(2)}) collective-permute-start(bf16[192,2304]{1,0:T(8,128)(2,1)S(1)} %all_gather.9.refs_0_), channel_id=1, source_target_pairs={{0,16},{1,17},{2,18},{3,19},{4,20},{5,21},{6,22},{7,23},{8,24},{9,... | collective-permute-start | bytes 2654216 | tf_op jit(solution)/shard_map/ppermute | solution.py:865
  29.6 22.9 %collective-permute-start.1 = (bf16[192,2304]{1,0:T(8,128)(2,1)S(1)}, bf16[192,2304]{1,0:T(8,128)(2,1)S(1)}, u32[]{:S(2)}, u32[]{:S(2)}) collective-permute-start(bf16[192,2304]{1,0:T(8,128)(2,1)S(1)} %all_gather.9.refs_0_), channel_id=1, source_target_pairs={{0,2},{1,3},{2,0},{3,1},{4,6},{5,7},{6,4},{7,5},{8,10},{9,11},{10,... | collective-permute-start | bytes 2654216 | tf_op jit(solution)/shard_map/ppermute | solution.py:865
  31.1 1.2 collective-permute-start
  32.4 20.1 %collective-permute-start.4 = (f32[16,768]{1,0:T(8,128)S(1)}, f32[16,768]{1,0:T(8,128)S(1)}, u32[]{:S(2)}, u32[]{:S(2)}) collective-permute-start(f32[16,768]{1,0:T(8,128)S(1)} %add.74), channel_id=1, source_target_pairs={{0,2},{1,3},{2,0},{3,1},{4,6},{5,7},{6,4},{7,5},{8,10},{9,11},{10,... | collective-permute-start | bytes 147464 | tf_op jit(solution)/shard_map/ppermute | solution.py:865
  52.5 23.9 %collective-permute-start.9 = (bf16[192,2304]{1,0:T(8,128)(2,1)S(1)}, bf16[192,2304]{1,0:T(8,128)(2,1)S(1)}, u32[]{:S(2)}, u32[]{:S(2)}) collective-permute-start(bf16[192,2304]{1,0:T(8,128)(2,1)S(1)} %collective-permute-done.2.refs_2_), channel_id=1, source_target_pairs={{0,1},{1,0},{2,3},{3,2},{4,5},{5,4},{6,7},{7,6},{8,9},{9,8},{10,11... | collective-permute-start | bytes 2654216 | tf_op jit(solution)/shard_map/ppermute | solution.py:865
  52.5 23.8 %collective-permute-start.6 = (bf16[192,2304]{1,0:T(8,128)(2,1)S(1)}, bf16[192,2304]{1,0:T(8,128)(2,1)S(1)}, u32[]{:S(2)}, u32[]{:S(2)}) collective-permute-start(bf16[192,2304]{1,0:T(8,128)(2,1)S(1)} %all_gather.10.refs_0_), channel_id=1, source_target_pairs={{0,2},{1,3},{2,0},{3,1},{4,6},{5,7},{6,4},{7,5},{8,10},{9,11},{10,... | collective-permute-start | bytes 2654216 | tf_op jit(solution)/shard_map/ppermute | solution.py:865
  54.1 22.2 %collective-permute-start.8 = (bf16[192,2304]{1,0:T(8,128)(2,1)S(1)}, bf16[192,2304]{1,0:T(8,128)(2,1)S(1)}, u32[]{:S(2)}, u32[]{:S(2)}) collective-permute-start(bf16[192,2304]{1,0:T(8,128)(2,1)S(1)} %collective-permute-done.1.refs_1_), channel_id=1, source_target_pairs={{0,1},{1,0},{2,3},{3,2},{4,5},{5,4},{6,7},{7,6},{8,9},{9,8},{10,11... | collective-permute-start | bytes 2654216 | tf_op jit(solution)/shard_map/ppermute | solution.py:865
  54.3 22.1 %collective-permute-start.7 = (bf16[192,2304]{1,0:T(8,128)(2,1)S(1)}, bf16[192,2304]{1,0:T(8,128)(2,1)S(1)}, u32[]{:S(2)}, u32[]{:S(2)}) collective-permute-start(bf16[192,2304]{1,0:T(8,128)(2,1)S(1)} %collective-permute-done.1.refs_1_), channel_id=1, source_target_pairs={{0,16},{1,17},{2,18},{3,19},{4,20},{5,21},{6,22},{7,23},{8,24},{9,... | collective-permute-start | bytes 2654216 | tf_op jit(solution)/shard_map/ppermute | solution.py:865
  54.8 4.1 %collective-permute-start.5 = (f32[16,768]{1,0:T(8,128)S(1)}, f32[16,768]{1,0:T(8,128)S(1)}, u32[]{:S(2)}, u32[]{:S(2)}) collective-permute-start(f32[16,768]{1,0:T(8,128)S(1)} %add.75), channel_id=1, source_target_pairs={{0,4},{1,5},{2,6},{3,7},{4,0},{5,1},{6,2},{7,3},{8,12},{9,13},{10,... | collective-permute-start | bytes 147464 | tf_op jit(solution)/shard_map/ppermute | solution.py:865
  58.9 17.4 %collective-permute-start.10 = (f32[16,768]{1,0:T(8,128)S(1)}, f32[16,768]{1,0:T(8,128)S(1)}, u32[]{:S(2)}, u32[]{:S(2)}) collective-permute-start(f32[16,768]{1,0:T(8,128)S(1)} %add.76), channel_id=1, source_target_pairs={{0,8},{1,9},{2,10},{3,11},{4,12},{5,13},{6,14},{7,15},{8,0},{9,1},... | collective-permute-start | bytes 147464 | tf_op jit(solution)/shard_map/ppermute | solution.py:865
  76.4 4.2 %collective-permute-start.11 = (bf16[192,2304]{1,0:T(8,128)(2,1)S(1)}, bf16[192,2304]{1,0:T(8,128)(2,1)S(1)}, u32[]{:S(2)}, u32[]{:S(2)}) collective-permute-start(bf16[192,2304]{1,0:T(8,128)(2,1)S(1)} %collective-permute-done.7.refs_3_), channel_id=1, source_target_pairs={{0,1},{1,0},{2,3},{3,2},{4,5},{5,4},{6,7},{7,6},{8,9},{9,8},{10,11... | collective-permute-start | bytes 2654216 | tf_op jit(solution)/shard_map/ppermute | solution.py:865
  76.5 11.1 %collective-permute-start.12 = (bf16[192,2304]{1,0:T(8,128)(2,1)S(1)}, bf16[192,2304]{1,0:T(8,128)(2,1)S(1)}, u32[]{:S(2)}, u32[]{:S(2)}) collective-permute-start(bf16[192,2304]{1,0:T(8,128)(2,1)S(1)} %all_gather.10.refs_0_), channel_id=1, source_target_pairs={{0,1},{1,0},{2,3},{3,2},{4,5},{5,4},{6,7},{7,6},{8,9},{9,8},{10,11... | collective-permute-start | bytes 2654216 | tf_op jit(solution)/shard_map/ppermute | solution.py:865
  77.0 10.6 %collective-permute-start.13 = (bf16[192,2304]{1,0:T(8,128)(2,1)S(1)}, bf16[192,2304]{1,0:T(8,128)(2,1)S(1)}, u32[]{:S(2)}, u32[]{:S(2)}) collective-permute-start(bf16[192,2304]{1,0:T(8,128)(2,1)S(1)} %collective-permute-done.6.refs_1_), channel_id=1, source_target_pairs={{0,1},{1,0},{2,3},{3,2},{4,5},{5,4},{6,7},{7,6},{8,9},{9,8},{10,11... | collective-permute-start | bytes 2654216 | tf_op jit(solution)/shard_map/ppermute | solution.py:865
  77.1 15.7 %collective-permute-start.15 = (bf16[384,768]{1,0:T(8,128)(2,1)S(1)}, bf16[384,768]{1,0:T(8,128)(2,1)S(1)}, u32[]{:S(2)}, u32[]{:S(2)}) collective-permute-start(bf16[384,768]{1,0:T(8,128)(2,1)S(1)} %pad_maximum_fusion), channel_id=1, source_target_pairs={{0,16},{1,17},{2,18},{3,19},{4,20},{5,21},{6,22},{7,23},{8,24},{9,... | collective-permute-start | bytes 1769480 | tf_op jit(solution)/shard_map/ppermute | solution.py:865
  78.7 15.4 %collective-permute-start.14 = (bf16[192,1536]{1,0:T(8,128)(2,1)S(1)}, bf16[192,1536]{1,0:T(8,128)(2,1)S(1)}, u32[]{:S(2)}, u32[]{:S(2)}) collective-permute-start(bf16[192,1536]{1,0:T(8,128)(2,1)S(1)} %all_gather.11.refs_0_), channel_id=1, source_target_pairs={{0,2},{1,3},{2,0},{3,1},{4,6},{5,7},{6,4},{7,5},{8,10},{9,11},{10,... | collective-permute-start | bytes 1769480 | tf_op jit(solution)/shard_map/ppermute | solution.py:865
  80.5 16.0 %collective-permute-start.16 = (bf16[192,1536]{1,0:T(8,128)(2,1)S(1)}, bf16[192,1536]{1,0:T(8,128)(2,1)S(1)}, u32[]{:S(2)}, u32[]{:S(2)}) collective-permute-start(bf16[192,1536]{1,0:T(8,128)(2,1)S(1)} %all_gather.11.refs_0_), channel_id=1, source_target_pairs={{0,1},{1,0},{2,3},{3,2},{4,5},{5,4},{6,7},{7,6},{8,9},{9,8},{10,11... | collective-permute-start | bytes 1769480 | tf_op jit(solution)/shard_map/ppermute | solution.py:865
  94.1 2.5 %collective-permute-start.17 = (bf16[192,1536]{1,0:T(8,128)(2,1)S(1)}, bf16[192,1536]{1,0:T(8,128)(2,1)S(1)}, u32[]{:S(2)}, u32[]{:S(2)}) collective-permute-start(bf16[192,1536]{1,0:T(8,128)(2,1)S(1)} %collective-permute-done.14.refs_1_), channel_id=1, source_target_pairs={{0,1},{1,0},{2,3},{3,2},{4,5},{5,4},{6,7},{7,6},{8,9},{9,8},{10,11... | collective-permute-start | bytes 1769480 | tf_op jit(solution)/shard_map/ppermute | solution.py:865
  94.1 2.8 %collective-permute-start.18 = (bf16[384,768]{1,0:T(8,128)(2,1)S(1)}, bf16[384,768]{1,0:T(8,128)(2,1)S(1)}, u32[]{:S(2)}, u32[]{:S(2)}) collective-permute-start(bf16[384,768]{1,0:T(8,128)(2,1)S(1)} %collective-permute-done.15.refs_0_), channel_id=1, source_target_pairs={{0,1},{1,0},{2,3},{3,2},{4,5},{5,4},{6,7},{7,6},{8,9},{9,8},{10,11... | collective-permute-start | bytes 1769480 | tf_op jit(solution)/shard_map/ppermute | solution.py:865
  96.9 6.7 %collective-permute-start.19 = (bf16[384,3072]{1,0:T(8,128)(2,1)S(1)}, bf16[384,3072]{1,0:T(8,128)(2,1)S(1)}, u32[]{:S(2)}, u32[]{:S(2)}) collective-permute-start(bf16[384,3072]{1,0:T(8,128)(2,1)S(1)} %get-tuple-element.275), channel_id=1, source_target_pairs={{0,1},{1,0},{2,3},{3,2},{4,5},{5,4},{6,7},{7,6},{8,9},{9,8},{10,11... | collective-permute-start | bytes 7077896 | tf_op jit(solution)/shard_map/ppermute | solution.py:865
  104.4 16.1 %collective-permute-start.22 = (bf16[384,3072]{1,0:T(8,128)(2,1)S(1)}, bf16[384,3072]{1,0:T(8,128)(2,1)S(1)}, u32[]{:S(2)}, u32[]{:S(2)}) collective-permute-start(bf16[384,3072]{1,0:T(8,128)(2,1)S(1)} %get-tuple-element.291), channel_id=1, source_target_pairs={{0,1},{1,0},{2,3},{3,2},{4,5},{5,4},{6,7},{7,6},{8,9},{9,8},{10,11... | collective-permute-start | bytes 7077896 | tf_op jit(solution)/shard_map/ppermute | solution.py:865
  104.9 15.4 %collective-permute-start.20 = (bf16[192,1536]{1,0:T(8,128)(2,1)S(1)}, bf16[192,1536]{1,0:T(8,128)(2,1)S(1)}, u32[]{:S(2)}, u32[]{:S(2)}) collective-permute-start(bf16[192,1536]{1,0:T(8,128)(2,1)S(1)} %get-tuple-element.289), channel_id=1, source_target_pairs={{0,2},{1,3},{2,0},{3,1},{4,6},{5,7},{6,4},{7,5},{8,10},{9,11},{10,... | collective-permute-start | bytes 1769480 | tf_op jit(solution)/shard_map/ppermute | solution.py:865
  105.4 15.1 %collective-permute-start.21 = (bf16[4,2,48,768]{3,2,1,0:T(8,128)(2,1)S(1)}, bf16[4,2,48,768]{3,2,1,0:T(8,128)(2,1)S(1)}, u32[]{:S(2)}, u32[]{:S(2)}) collective-permute-start(bf16[4,2,48,768]{3,2,1,0:T(8,128)(2,1)S(1)} %get-tuple-element.290), channel_id=1, source_target_pairs={{0,16},{1,17},{2,18},{3,19},{4,20},{5,21},{6,22},{7,23},{8,24},{9,... | collective-permute-start | bytes 1769480 | tf_op jit(solution)/shard_map/ppermute | solution.py:865
  120.5 18.0 %collective-permute-start.26 = (bf16[384,3072]{1,0:T(8,128)(2,1)S(1)}, bf16[384,3072]{1,0:T(8,128)(2,1)S(1)}, u32[]{:S(2)}, u32[]{:S(2)}) collective-permute-start(bf16[384,3072]{1,0:T(8,128)(2,1)S(1)} %get-tuple-element.311), channel_id=1, source_target_pairs={{0,1},{1,0},{2,3},{3,2},{4,5},{5,4},{6,7},{7,6},{8,9},{9,8},{10,11... | collective-permute-start | bytes 7077896 | tf_op jit(solution)/shard_map/ppermute | solution.py:865
  121.3 15.8 %collective-permute-start.23 = (bf16[384,768]{1,0:T(8,128)(2,1)S(1)}, bf16[384,768]{1,0:T(8,128)(2,1)S(1)}, u32[]{:S(2)}, u32[]{:S(2)}) collective-permute-start(bf16[384,768]{1,0:T(8,128)(2,1)S(1)} %get-tuple-element.308), channel_id=1, source_target_pairs={{0,4},{1,5},{2,6},{3,7},{4,0},{5,1},{6,2},{7,3},{8,12},{9,13},{10,... | collective-permute-start | bytes 1769480 | tf_op jit(solution)/shard_map/ppermute | solution.py:865
  121.4 15.8 %collective-permute-start.24 = (bf16[192,1536]{1,0:T(8,128)(2,1)S(1)}, bf16[192,1536]{1,0:T(8,128)(2,1)S(1)}, u32[]{:S(2)}, u32[]{:S(2)}) collective-permute-start(bf16[192,1536]{1,0:T(8,128)(2,1)S(1)} %get-tuple-element.309), channel_id=1, source_target_pairs={{0,2},{1,3},{2,0},{3,1},{4,6},{5,7},{6,4},{7,5},{8,10},{9,11},{10,... | collective-permute-start | bytes 1769480 | tf_op jit(solution)/shard_map/ppermute | solution.py:865
  123.0 15.5 %collective-permute-start.25 = (bf16[4,2,48,768]{3,2,1,0:T(8,128)(2,1)S(1)}, bf16[4,2,48,768]{3,2,1,0:T(8,128)(2,1)S(1)}, u32[]{:S(2)}, u32[]{:S(2)}) collective-permute-start(bf16[4,2,48,768]{3,2,1,0:T(8,128)(2,1)S(1)} %get-tuple-element.310), channel_id=1, source_target_pairs={{0,16},{1,17},{2,18},{3,19},{4,20},{5,21},{6,22},{7,23},{8,24},{9,... | collective-permute-start | bytes 1769480 | tf_op jit(solution)/shard_map/ppermute | solution.py:865
  139.8 16.2 %collective-permute-start.30 = (bf16[4,2,48,768]{3,2,1,0:T(8,128)(2,1)S(1)}, bf16[4,2,48,768]{3,2,1,0:T(8,128)(2,1)S(1)}, u32[]{:S(2)}, u32[]{:S(2)}) collective-permute-start(bf16[4,2,48,768]{3,2,1,0:T(8,128)(2,1)S(1)} %get-tuple-element.329), channel_id=1, source_target_pairs={{0,16},{1,17},{2,18},{3,19},{4,20},{5,21},{6,22},{7,23},{8,24},{9,... | collective-permute-start | bytes 1769480 | tf_op jit(solution)/shard_map/ppermute | solution.py:865
  140.4 15.6 %collective-permute-start.29 = (bf16[192,1536]{1,0:T(8,128)(2,1)S(1)}, bf16[192,1536]{1,0:T(8,128)(2,1)S(1)}, u32[]{:S(2)}, u32[]{:S(2)}) collective-permute-start(bf16[192,1536]{1,0:T(8,128)(2,1)S(1)} %get-tuple-element.325), channel_id=1, source_target_pairs={{0,2},{1,3},{2,0},{3,1},{4,6},{5,7},{6,4},{7,5},{8,10},{9,11},{10,... | collective-permute-start | bytes 1769480 | tf_op jit(solution)/shard_map/ppermute | solution.py:865
  140.9 15.1 %collective-permute-start.27 = (bf16[192,768]{1,0:T(8,128)(2,1)S(1)}, bf16[192,768]{1,0:T(8,128)(2,1)S(1)}, u32[]{:S(2)}, u32[]{:S(2)}) collective-permute-start(bf16[192,768]{1,0:T(8,128)(2,1)S(1)} %split_far.2), channel_id=1, source_target_pairs={{0,8},{1,9},{2,10},{3,11},{4,12},{5,13},{6,14},{7,15},{8,0},{9,1},... | collective-permute-start | bytes 884744 | tf_op jit(solution)/shard_map/ppermute | solution.py:865
  143.2 12.8 %collective-permute-start.28 = (bf16[96,1536]{1,0:T(8,128)(2,1)S(1)}, bf16[96,1536]{1,0:T(8,128)(2,1)S(1)}, u32[]{:S(2)}, u32[]{:S(2)}) collective-permute-start(bf16[96,1536]{1,0:T(8,128)(2,1)S(1)} %split_near.2), channel_id=1, source_target_pairs={{0,4},{1,5},{2,6},{3,7},{4,0},{5,1},{6,2},{7,3},{8,12},{9,13},{10,... | collective-permute-start | bytes 884744 | tf_op jit(solution)/shard_map/ppermute | solution.py:865
  144.0 3.6 %collective-permute-start.31 = (f32[16,768]{1,0:T(8,128)S(1)}, f32[16,768]{1,0:T(8,128)S(1)}, u32[]{:S(2)}, u32[]{:S(2)}) collective-permute-start(f32[16,768]{1,0:T(8,128)S(1)} %get-tuple-element.330), channel_id=1, source_target_pairs={{0,1},{1,0},{2,3},{3,2},{4,5},{5,4},{6,7},{7,6},{8,9},{9,8},{10,11... | collective-permute-start | bytes 147464 | tf_op jit(solution)/shard_map/ppermute | solution.py:865
  156.8 15.6 %collective-permute-start.35 = (bf16[192,1536]{1,0:T(8,128)(2,1)S(1)}, bf16[192,1536]{1,0:T(8,128)(2,1)S(1)}, u32[]{:S(2)}, u32[]{:S(2)}) collective-permute-start(bf16[192,1536]{1,0:T(8,128)(2,1)S(1)} %get-tuple-element.352), channel_id=1, source_target_pairs={{0,2},{1,3},{2,0},{3,1},{4,6},{5,7},{6,4},{7,5},{8,10},{9,11},{10,... | collective-permute-start | bytes 1769480 | tf_op jit(solution)/shard_map/ppermute | solution.py:865
  158.9 13.4 %collective-permute-start.34 = (bf16[96,1536]{1,0:T(8,128)(2,1)S(1)}, bf16[96,1536]{1,0:T(8,128)(2,1)S(1)}, u32[]{:S(2)}, u32[]{:S(2)}) collective-permute-start(bf16[96,1536]{1,0:T(8,128)(2,1)S(1)} %get-tuple-element.354), channel_id=1, source_target_pairs={{0,4},{1,5},{2,6},{3,7},{4,0},{5,1},{6,2},{7,3},{8,12},{9,13},{10,... | collective-permute-start | bytes 884744 | tf_op jit(solution)/shard_map/ppermute | solution.py:865
  160.7 11.6 %collective-permute-start.32 = (bf16[48,1536]{1,0:T(8,128)(2,1)S(1)}, bf16[48,1536]{1,0:T(8,128)(2,1)S(1)}, u32[]{:S(2)}, u32[]{:S(2)}) collective-permute-start(bf16[48,1536]{1,0:T(8,128)(2,1)S(1)} %get-tuple-element.358.refs_3_), channel_id=1, source_target_pairs={{0,16},{1,17},{2,18},{3,19},{4,20},{5,21},{6,22},{7,23},{8,24},{9,... | collective-permute-start | bytes 442376 | tf_op jit(solution)/shard_map/ppermute | solution.py:865
  162.0 10.3 %collective-permute-start.33 = (bf16[48,1536]{1,0:T(8,128)(2,1)S(1)}, bf16[48,1536]{1,0:T(8,128)(2,1)S(1)}, u32[]{:S(2)}, u32[]{:S(2)}) collective-permute-start(bf16[48,1536]{1,0:T(8,128)(2,1)S(1)} %get-tuple-element.356), channel_id=1, source_target_pairs={{0,8},{1,9},{2,10},{3,11},{4,12},{5,13},{6,14},{7,15},{8,0},{9,1},... | collective-permute-start | bytes 442376 | tf_op jit(solution)/shard_map/ppermute | solution.py:865
  164.9 7.4 %collective-permute-start.36 = (f32[16,768]{1,0:T(8,128)S(1)}, f32[16,768]{1,0:T(8,128)S(1)}, u32[]{:S(2)}, u32[]{:S(2)}) collective-permute-start(f32[16,768]{1,0:T(8,128)S(1)} %add.78), channel_id=1, source_target_pairs={{0,8},{1,9},{2,10},{3,11},{4,12},{5,13},{6,14},{7,15},{8,0},{9,1},... | collective-permute-start | bytes 147464 | tf_op jit(solution)/shard_map/ppermute | solution.py:865
  173.1 9.2 %collective-permute-start.39 = (bf16[96,1536]{1,0:T(8,128)(2,1)S(1)}, bf16[96,1536]{1,0:T(8,128)(2,1)S(1)}, u32[]{:S(2)}, u32[]{:S(2)}) collective-permute-start(bf16[96,1536]{1,0:T(8,128)(2,1)S(1)} %get-tuple-element.370), channel_id=1, source_target_pairs={{0,4},{1,5},{2,6},{3,7},{4,0},{5,1},{6,2},{7,3},{8,12},{9,13},{10,... | collective-permute-start | bytes 884744 | tf_op jit(solution)/shard_map/ppermute | solution.py:865
  173.2 8.1 %collective-permute-start.38 = (bf16[48,1536]{1,0:T(8,128)(2,1)S(1)}, bf16[48,1536]{1,0:T(8,128)(2,1)S(1)}, u32[]{:S(2)}, u32[]{:S(2)}) collective-permute-start(bf16[48,1536]{1,0:T(8,128)(2,1)S(1)} %get-tuple-element.369), channel_id=1, source_target_pairs={{0,8},{1,9},{2,10},{3,11},{4,12},{5,13},{6,14},{7,15},{8,0},{9,1},... | collective-permute-start | bytes 442376 | tf_op jit(solution)/shard_map/ppermute | solution.py:865
  175.8 5.5 %collective-permute-start.37 = (bf16[48,1536]{1,0:T(8,128)(2,1)S(1)}, bf16[48,1536]{1,0:T(8,128)(2,1)S(1)}, u32[]{:S(2)}, u32[]{:S(2)}) collective-permute-start(bf16[48,1536]{1,0:T(8,128)(2,1)S(1)} %get-tuple-element.368.refs_5_), channel_id=1, source_target_pairs={{0,16},{1,17},{2,18},{3,19},{4,20},{5,21},{6,22},{7,23},{8,24},{9,... | collective-permute-start | bytes 442376 | tf_op jit(solution)/shard_map/ppermute | solution.py:865
  176.7 4.6 %collective-permute-start.40 = (bf16[64,768]{1,0:T(8,128)(2,1)S(1)}, bf16[64,768]{1,0:T(8,128)(2,1)S(1)}, u32[]{:S(2)}, u32[]{:S(2)}) collective-permute-start(bf16[64,768]{1,0:T(8,128)(2,1)S(1)} %get-tuple-element.371), channel_id=1, source_target_pairs={{0,2},{1,3},{2,0},{3,1},{4,6},{5,7},{6,4},{7,5},{8,10},{9,11},{10,... | collective-permute-start | bytes 294920 | tf_op jit(solution)/shard_map/ppermute | solution.py:865
  183.0 9.1 %collective-permute-start.41 = (bf16[48,2304]{1,0:T(8,128)(2,1)S(1)}, bf16[48,2304]{1,0:T(8,128)(2,1)S(1)}, u32[]{:S(2)}, u32[]{:S(2)}) collective-permute-start(bf16[48,2304]{1,0:T(8,128)(2,1)S(1)} %get-tuple-element.378.refs_6_), channel_id=1, source_target_pairs={{0,16},{1,17},{2,18},{3,19},{4,20},{5,21},{6,22},{7,23},{8,24},{9,... | collective-permute-start | bytes 663560 | tf_op jit(solution)/shard_map/ppermute | solution.py:865
  184.5 7.5 %collective-permute-start.42 = (bf16[48,1536]{1,0:T(8,128)(2,1)S(1)}, bf16[48,1536]{1,0:T(8,128)(2,1)S(1)}, u32[]{:S(2)}, u32[]{:S(2)}) collective-permute-start(bf16[48,1536]{1,0:T(8,128)(2,1)S(1)} %get-tuple-element.379), channel_id=1, source_target_pairs={{0,8},{1,9},{2,10},{3,11},{4,12},{5,13},{6,14},{7,15},{8,0},{9,1},... | collective-permute-start | bytes 442376 | tf_op jit(solution)/shard_map/ppermute | solution.py:865
  185.7 4.1 %collective-permute-start.43 = (f32[16,768]{1,0:T(8,128)S(1)}, f32[16,768]{1,0:T(8,128)S(1)}, u32[]{:S(2)}, u32[]{:S(2)}) collective-permute-start(f32[16,768]{1,0:T(8,128)S(1)} %get-tuple-element.380), channel_id=1, source_target_pairs={{0,4},{1,5},{2,6},{3,7},{4,0},{5,1},{6,2},{7,3},{8,12},{9,13},{10,... | collective-permute-start | bytes 147464 | tf_op jit(solution)/shard_map/ppermute | solution.py:865
  192.1 4.8 %collective-permute-start.45 = (f32[16,768]{1,0:T(8,128)S(1)}, f32[16,768]{1,0:T(8,128)S(1)}, u32[]{:S(2)}, u32[]{:S(2)}) collective-permute-start(f32[16,768]{1,0:T(8,128)S(1)} %add.80), channel_id=1, source_target_pairs={{0,16},{1,17},{2,18},{3,19},{4,20},{5,21},{6,22},{7,23},{8,24},{9,... | collective-permute-start | bytes 147464 | tf_op jit(solution)/shard_map/ppermute | solution.py:865
  193.3 6.0 %collective-permute-start.44 = (bf16[48,1536]{1,0:T(8,128)(2,1)S(1)}, bf16[48,1536]{1,0:T(8,128)(2,1)S(1)}, u32[]{:S(2)}, u32[]{:S(2)}) collective-permute-start(bf16[48,1536]{1,0:T(8,128)(2,1)S(1)} %sum_far.3.refs_3_), channel_id=1, source_target_pairs={{0,16},{1,17},{2,18},{3,19},{4,20},{5,21},{6,22},{7,23},{8,24},{9,... | collective-permute-start | bytes 442376 | tf_op jit(solution)/shard_map/ppermute | solution.py:865
  (18 other events, 99.7 us)
